TPU v7x, 128 devices: a whole 4x4x4 slice. The times are simulated.
128 devices in a mesh: node: 64 (over z, y_lo, x, core), head: 2 (over y_hi).
Axes of the slice: x: 4, y: 4 (y_hi: 2, y_lo: 2; y = y_hi * 2 + y_lo), z: 4, core: 2. Of those that a mesh axis runs over, the one named last changes fastest.
Arguments:
- features: bfloat16 [8192, 1024], P('node', 'head'), may hold values from -6 to 6
- queries: bfloat16 [8192, 1024], P('node', 'head'), may hold values from -6 to 6
- keys: bfloat16 [8192, 1024], P('node', 'head'), may hold values from -6 to 6
- values: bfloat16 [8192, 1024], P('node', 'head'), may hold values from -6 to 6
- attn_mix: bfloat16 [8192, 1024], P('node', 'head'), may hold values from -6 to 6
- log_sums: float32 [16, 8192], P('head', 'node'), as said below
- out_weight: bfloat16 [1024, 1024], P('head'), may hold values from -0.1875 to 0.1875
- msg_weight: bfloat16 [1024, 1024], P('head'), may hold values from -0.1875 to 0.1875
- edge_tiles: bfloat16 [64, 8, 128, 128], P('node'), may hold values from -0.25 to 0.25
- edge_source: int32 [64, 8], P('node'), may hold values from 0 to 63, as said below
- edge_count: int32 [64], P('node'), may hold values from 1 to 8, as said below
- out_grad: bfloat16 [8192, 1024], P('node', 'head'), may hold values from -6 to 6
Outputs:
- grad_features: bfloat16 [8192, 1024], P('node', 'head')
- grad_queries: bfloat16 [8192, 1024], P('node', 'head')
- grad_keys: bfloat16 [8192, 1024], P('node', 'head')
- grad_values: bfloat16 [8192, 1024], P('node', 'head')
- out_weight_grad: float32 [1024, 1024], P('head')
- msg_weight_grad: float32 [1024, 1024], P('head')
Inputs may be any that keep to these rules, and one draw needn't show every extreme that they name: `log_sums`: the saved statistic of each row, of the size of the log of 8192. The partition of edge_source[b, e] lies at most 3 partitions before or after the partition of b, counted cyclically over the partitions; some slot lies exactly 3 partitions after and some exactly 3 before; slots that are not live hold valid block numbers too. `edge_count`: some block has all 8 slots live.
All inputs are finite; a program needn't handle non-finite values.
Results may differ from a plain program's by a relative error of at most 0.012.
Values may be sent and summed in bfloat16 or wider, within the bound.
No kernel may reach another device: no remote copies, remote signals or barrier semaphores. Data moves between devices by JAX's collectives and lax.ppermute only.
A program may use at most 256 MiB of HBM per device.

v0:
```python
import math

import jax
import jax.numpy as jnp
from jax import lax
from jax.sharding import PartitionSpec as P

HEAD_DIM = 64
BLOCK = 128
REACH = 3


def from_behind(value, axis, steps):
    count = lax.axis_size(axis)
    pairs = [(source, (source + steps) % count) for source in range(count)]
    return lax.ppermute(value, axis, pairs)


def split_heads(array):
    return array.reshape(array.shape[0], array.shape[1] // HEAD_DIM, HEAD_DIM)


def query_side(query, grad_rows, key_rows, value_rows, log_rows, spread_rows):
    scale = 1.0 / math.sqrt(HEAD_DIM)
    scores = jnp.einsum("ihd,jhd->hij", query, key_rows, preferred_element_type=jnp.float32) * scale
    softmax_rows = jnp.exp(scores - log_rows[:, :, None])
    grad_scores = jnp.einsum(
        "ihd,jhd->hij", grad_rows, value_rows, preferred_element_type=jnp.float32
    )
    score_grad = (softmax_rows * (grad_scores - spread_rows[:, :, None])).astype(jnp.bfloat16)
    return (
        jnp.einsum("hij,jhd->ihd", score_grad, key_rows, preferred_element_type=jnp.float32) * scale
    )


def key_side(query, grad_rows, log_rows, spread_rows, key_rows, value_rows):
    scale = 1.0 / math.sqrt(HEAD_DIM)
    scores = jnp.einsum("ihd,jhd->hij", query, key_rows, preferred_element_type=jnp.float32) * scale
    softmax_rows = jnp.exp(scores - log_rows[:, :, None])
    grad_scores = jnp.einsum(
        "ihd,jhd->hij", grad_rows, value_rows, preferred_element_type=jnp.float32
    )
    score_grad = (softmax_rows * (grad_scores - spread_rows[:, :, None])).astype(jnp.bfloat16)
    softmax_low = softmax_rows.astype(jnp.bfloat16)
    grad_value = jnp.einsum(
        "hij,ihd->jhd", softmax_low, grad_rows, preferred_element_type=jnp.float32
    )
    grad_key = (
        jnp.einsum("hij,ihd->jhd", score_grad, query, preferred_element_type=jnp.float32) * scale
    )
    return (grad_key, grad_value)


def stats_table(log_sums, spread):
    return (
        lax.all_gather(log_sums, "node", axis=1, tiled=True),
        lax.all_gather(spread, "node", axis=1, tiled=True),
    )


def attention(queries, keys, values, grad_mix, log_sums, spread):
    rows = queries.shape[0]
    columns = queries.shape[1]
    local_query = split_heads(queries)
    local_keys = split_heads(keys)
    local_values = split_heads(values)
    local_grad = split_heads(grad_mix)
    all_logs, all_spread = stats_table(log_sums, spread)
    key_piece = lax.all_gather(keys, "node", axis=0, tiled=True)
    value_piece = lax.all_gather(values, "node", axis=0, tiled=True)
    grad_query = query_side(
        local_query, local_grad, split_heads(key_piece), split_heads(value_piece), log_sums, spread
    )
    query_piece = lax.all_gather(queries, "node", axis=0, tiled=True)
    grad_piece = lax.all_gather(grad_mix, "node", axis=0, tiled=True)
    grad_key, grad_value = key_side(
        split_heads(query_piece),
        split_heads(grad_piece),
        all_logs,
        all_spread,
        local_keys,
        local_values,
    )
    grad_key, grad_value = (grad_key, grad_value)
    return (
        grad_query.reshape(rows, columns).astype(jnp.bfloat16),
        grad_key.reshape(rows, columns).astype(jnp.bfloat16),
        grad_value.reshape(rows, columns).astype(jnp.bfloat16),
    )


def messages(features, edge_tiles, edge_source, edge_count, full_grad, msg_weight):
    parts = lax.axis_size("node")
    home = lax.axis_index("node")
    rows = features.shape[0]
    columns = features.shape[1]
    per_part = rows // BLOCK
    window = 2 * REACH + 1
    beside_all = []
    for offset in range(-REACH, REACH + 1):
        if offset == 0:
            beside_all.append(features)
        else:
            beside_all.append(from_behind(features, "node", -offset))
    nearby = jnp.stack(beside_all)
    distance = (edge_source // per_part - home) % parts
    distance = jnp.where(distance > REACH, distance - parts, distance)
    place = (distance + REACH) * per_part + edge_source % per_part
    live = lax.broadcasted_iota(jnp.int32, edge_source.shape, 1) < edge_count[:, None]
    tiles = jnp.where(live[:, :, None, None], edge_tiles, jnp.zeros((), jnp.bfloat16))
    picked = nearby[place]
    aggregate = jnp.einsum("beij,bejd->bid", tiles, picked, preferred_element_type=jnp.float32)
    aggregate = aggregate.astype(jnp.bfloat16).reshape(rows, columns)
    grad_aggregate = jnp.einsum(
        "id,kd->ik", full_grad, msg_weight, preferred_element_type=jnp.float32
    ).astype(jnp.bfloat16)
    weight_grad = jnp.einsum("ik,id->kd", aggregate, full_grad, preferred_element_type=jnp.float32)
    back_terms = jnp.einsum(
        "beij,bid->bejd",
        tiles,
        grad_aggregate.reshape(per_part, BLOCK, columns),
        preferred_element_type=jnp.float32,
    )
    slot_table = (
        place[:, :, None] == lax.broadcasted_iota(jnp.int32, (1, 1, window * per_part), 2)
    ).astype(jnp.float32)
    outgoing = jnp.einsum("bek,bejd->kjd", slot_table, back_terms).astype(jnp.bfloat16)
    total = jnp.zeros((rows, columns), jnp.float32)
    for offset in range(-REACH, REACH + 1):
        share = outgoing[offset + REACH]
        if offset != 0:
            share = from_behind(share, "node", offset)
        total = total + share.astype(jnp.float32)
    return (total.astype(jnp.bfloat16), weight_grad)


def body(
    features,
    queries,
    keys,
    values,
    attn_mix,
    log_sums,
    out_weight,
    msg_weight,
    edge_tiles,
    edge_source,
    edge_count,
    out_grad,
):
    full_grad = lax.all_gather(out_grad, "head", axis=1, tiled=True)
    grad_mix = jnp.einsum(
        "id,kd->ik", full_grad, out_weight, preferred_element_type=jnp.float32
    ).astype(jnp.bfloat16)
    spread = jnp.sum(
        split_heads(grad_mix).astype(jnp.float32) * split_heads(attn_mix).astype(jnp.float32),
        axis=2,
    ).T
    out_weight_grad = jnp.einsum(
        "ik,id->kd", attn_mix, full_grad, preferred_element_type=jnp.float32
    )
    grad_query, grad_key, grad_value = attention(queries, keys, values, grad_mix, log_sums, spread)
    grad_features, msg_weight_grad = messages(
        features, edge_tiles, edge_source, edge_count, full_grad, msg_weight
    )
    out_weight_grad, msg_weight_grad = lax.psum((out_weight_grad, msg_weight_grad), "node")
    return (grad_features, grad_query, grad_key, grad_value, out_weight_grad, msg_weight_grad)


def solution(mesh):
    placed = (
        P("node", "head"),
        P("node", "head"),
        P("node", "head"),
        P("node", "head"),
        P("node", "head"),
        P("head", "node"),
        P("head", None),
        P("head", None),
        P("node", None, None, None),
        P("node", None),
        P("node"),
        P("node", "head"),
    )
    return jax.shard_map(
        body,
        mesh=mesh,
        in_specs=placed,
        out_specs=(
            P("node", "head"),
            P("node", "head"),
            P("node", "head"),
            P("node", "head"),
            P("head", None),
            P("head", None),
        ),
        check_vma=False,
    )
```

profile of v0, /device:TPU:1, one launch (start us, length us, event | category | flops | bytes accessed | tf_op | source)
XLA Modules:
  0.0 1067.8 jit_solution(9798110362631429057)
XLA Ops:
  7.2 0.7 all-gather.5.cloned.1.call-update
  7.9 0.0 all-gather.9.cloned.1.call-start
  8.0 0.7 all-gather.9.cloned.1.call-update
  8.7 0.0 all-gather.7.cloned.1.call-start
  8.7 1.7 copy.72
  10.4 0.0 all-gather.11.cloned.1.call-start
  10.4 7.7 all_gather.21
  18.1 1.1 convolution_convert_fusion
  19.3 0.0 all-reduce.3.cloned.1.call-start
  19.3 4.2 collective-permute-start.6
  23.5 0.3 collective-permute-start.7
  23.8 0.5 collective-permute-start.9
  24.3 5.4 collective-permute-start.10
  29.7 1.0 copy.71
  31.4 1.0 select_bitcast_fusion
  32.4 0.2 copy.65
  32.6 1.0 copy.73
  33.7 84.6 %all_gather.27 = f32[8,8192]{1,0:T(8,128)} all-gather(f32[8,128]{1,0:T(8,128)S(1)} %bitcast.128), channel_id=1, replica_groups=mesh['node'=64,'head'=2] {'node'}, dimensions={1}, use_global_device_ids=true | all-gather | bytes 266240 | tf_op jit(solution)/shard_map/all_gather | solution.py:57
  118.3 1.7 fusion.25
  120.0 0.7 fusion.36
  120.7 0.7 fusion.14
  121.4 2.7 fusion.43
  124.1 1.3 fusion.40
  125.4 1.7 copy.69
  127.1 1.0 copy.75
  128.1 0.7 copy.98
  128.8 0.7 copy.99
  129.5 0.7 copy.100
  130.1 0.7 copy.95
  130.9 77.8 %all_gather.25 = f32[8,8192]{1,0:T(8,128)S(1)} all-gather(f32[8,128]{1,0:T(8,128)} %param.17), channel_id=1, replica_groups=mesh['node'=64,'head'=2] {'node'}, dimensions={1}, use_global_device_ids=true | all-gather | bytes 266240 | tf_op jit(solution)/shard_map/all_gather | solution.py:56
  208.6 1.4 collective-permute-start.11
  210.0 0.9 bitcast_dynamic-update-slice_fusion.6
  211.0 1.9 collective-permute-start.5
  212.9 0.9 bitcast_dynamic-update-slice_fusion.5
  213.8 1.4 collective-permute-start.4
  215.2 0.9 bitcast_dynamic-update-slice_fusion.4
  216.1 0.9 bitcast_dynamic-update-slice_fusion.3
  217.1 0.1 collective-permute-start.3
  217.2 0.9 bitcast_dynamic-update-slice_fusion.2
  218.1 0.6 collective-permute-start.2
  218.6 0.9 bitcast_dynamic-update-slice_fusion.1
  219.6 4.4 collective-permute-start.1
  224.0 0.6 gather_fusion
  224.6 1.9 collective-permute-start
  226.6 2.1 fusion.26
  228.7 2.4 collective-permute-done
  231.1 1.9 fusion.30
  233.1 12.0 %copy.70 = bf16[8192,512]{0,1:T(8,128)(2,1)} copy(bf16[8192,512]{1,0:T(8,128)(2,1)} %all-gather.5.cloned.1.call-done) | data formatting | bytes 16777216 | tf_op jit(solution)/shard_map/all_gather | solution.py:69
  245.1 19.1 %fusion.41 = f32[8,128,8192]{2,1,0:T(8,128)} fusion(bf16[128,8,64]{0,2,1:T(8,128)(2,1)S(1)} %bitcast.120, bf16[8192,8,64]{0,2,1:T(8,128)(2,1)} %bitcast.115), kind=kOutput, calls=%fused_computation.65 | convolution fusion | flops 1073741824 | bytes 42074112 | tf_op jit(solution)/shard_map/ihd,jhd->hij/dot_general | solution.py:25
  264.1 12.0 %copy.74 = bf16[8192,512]{0,1:T(8,128)(2,1)} copy(bf16[8192,512]{1,0:T(8,128)(2,1)} %all-gather.9.cloned.1.call-done) | data formatting | bytes 16777216 | tf_op jit(solution)/shard_map/all_gather | solution.py:74
  276.2 16.1 %fusion.42 = f32[8,8192,128]{2,1,0:T(8,128)} fusion(bf16[8192,8,64]{0,2,1:T(8,128)(2,1)} %bitcast.113, bf16[128,8,64]{0,2,1:T(8,128)(2,1)S(1)} %bitcast.119), kind=kOutput, calls=%fused_computation.66 | convolution fusion | flops 1073741824 | bytes 42074112 | tf_op jit(solution)/shard_map/ihd,jhd->hij/dot_general | solution.py:38
  292.3 89.6 %all-gather.7.cloned.1.call-done = bf16[8192,512]{0,1:T(8,128)(2,1)} async-done(((bf16[128,512]{0,1:T(8,128)(2,1)}), bf16[8192,512]{0,1:T(8,128)(2,1)}) %all-gather.7.cloned.1.call-update) | async-done | bytes 8388624 | tf_op jit(solution)/shard_map/all_gather | solution.py:70
  381.9 20.5 %fusion.20 = bf16[8,128,64]{1,2,0:T(8,128)(2,1)S(1)} fusion(bf16[8192,8,64]{0,2,1:T(8,128)(2,1)} %bitcast.116, f32[8,128,8192]{2,1,0:T(8,128)} %fusion.41, f32[8,128]{1,0:T(8,128)S(1)} %bitcast.129, f32[8,128]{1,0:T(8,128)S(1)} %copy-done.7, bf16[128,8,64]{0,2,1:T(8,128)(2,1)S(1)} %bitcast.124, bf16[8192,8,64]{0,2,1:T(8,128)(2,1)} %bitcast.130), kind=kOutput, calls=%fused_computation.21 | convolution fusion | flops 2189557760 | bytes 50601984 | tf_op jit(solution)/shard_map/hij,jhd->ihd/dot_general | solution.py:32
  402.4 91.5 %all-gather.11.cloned.1.call-done = bf16[8192,512]{1,0:T(8,128)(2,1)} async-done(((bf16[128,512]{1,0:T(8,128)(2,1)}), bf16[8192,512]{1,0:T(8,128)(2,1)}) %all-gather.11.cloned.1.call-update) | async-done | bytes 8388624 | tf_op jit(solution)/shard_map/all_gather | solution.py:75
  493.9 12.0 %copy.76 = bf16[8192,512]{0,1:T(8,128)(2,1)} copy(bf16[8192,512]{1,0:T(8,128)(2,1)} %all-gather.11.cloned.1.call-done) | data formatting | bytes 16777216 | tf_op jit(solution)/shard_map/all_gather | solution.py:75
  505.9 26.4 %multiply_convert_fusion.14 = bf16[8,8192,128]{2,1,0:T(8,128)(2,1)} fusion(f32[8,8192,128]{2,1,0:T(8,128)} %fusion.42, f32[8,8192]{1,0:T(8,128)S(1)} %copy-done.6, f32[8,8192]{1,0:T(8,128)S(1)} %all_gather.25, bf16[8192,8,64]{0,2,1:T(8,128)(2,1)} %bitcast.117, bf16[128,8,64]{0,2,1:T(8,128)(2,1)S(1)} %bitcast.123), kind=kOutput, calls=%fused_computation.1.clone.clone.clone.clone.clone.clone.1 | convolution fusion | flops 1115684864 | bytes 59375616 | tf_op jit(solution)/shard_map/ihd,jhd->hij/dot_general | solution.py:40
  532.3 0.8 copy.78
  533.1 11.2 %fusion.21 = bf16[8,128,64]{1,2,0:T(8,128)(2,1)S(1)} fusion(bf16[8192,8,64]{0,2,1:T(8,128)(2,1)} %bitcast.114, bf16[8,8192,128]{2,1,0:T(8,128)(2,1)} %multiply_convert_fusion.14), kind=kOutput, calls=%fused_computation.22 | convolution fusion | flops 1073872896 | bytes 25296896 | tf_op jit(solution)/shard_map/hij,ihd->jhd/dot_general | solution.py:49
  544.4 0.8 copy.79
  545.1 14.8 %fusion.22 = bf16[8,64,128]{2,1,0:T(8,128)(2,1)S(1)} fusion(bf16[8192,8,64]{0,2,1:T(8,128)(2,1)} %bitcast.118, f32[8,8192,128]{2,1,0:T(8,128)} %fusion.42, f32[8,8192]{1,0:T(8,128)S(1)} %all_gather.25), kind=kOutput, calls=%fused_computation.23 | convolution fusion | flops 1098973184 | bytes 42336256 | tf_op jit(solution)/shard_map/hij,ihd->jhd/dot_general | solution.py:45
  559.9 0.8 copy.80
  560.7 494.2 %all-reduce.3.cloned.1.call-done = (f32[512,1024]{1,0:T(8,128)}, f32[512,1024]{1,0:T(8,128)}) async-done(((f32[512,1024]{1,0:T(8,128)}, f32[512,1024]{1,0:T(8,128)}), (f32[512,1024]{1,0:T(8,128)}, f32[512,1024]{1,0:T(8,128)})) %all-reduce.3.cloned.1.call-update) | async-done | bytes 4194320 | tf_op jit(solution)/shard_map/psum | solution.py:166
  1054.9 3.2 copy.110
  1058.1 3.2 copy.111
  (41 shorter events, 0.3 us)
Async XLA Ops:
  7.2 10.9 %copy-start = (bf16[512,1024]{1,0:T(8,128)(2,1)S(1)}, bf16[512,1024]{1,0:T(8,128)(2,1)}, u32[]{:S(2)}) copy-start(bf16[512,1024]{1,0:T(8,128)(2,1)} %param.18) | copy-start | bytes 3145732
  7.2 225.9 %all-gather.5.cloned.1.call-start = ((), (), s32[]{:S(2)}) async-start(), calls=%async_computation | async-start | bytes 8519680 | tf_op jit(solution)/shard_map/all_gather | solution.py:69
  7.9 256.2 %all-gather.9.cloned.1.call-start = ((), (), s32[]{:S(2)}) async-start(), calls=%async_computation.2 | async-start | bytes 8519680 | tf_op jit(solution)/shard_map/all_gather | solution.py:74
  8.7 373.2 %all-gather.7.cloned.1.call-start = ((), (), s32[]{:S(2)}) async-start(), calls=%async_computation.1 | async-start | bytes 8519680 | tf_op jit(solution)/shard_map/all_gather | solution.py:70
  10.4 483.5 %all-gather.11.cloned.1.call-start = ((), (), s32[]{:S(2)}) async-start(), calls=%async_computation.3 | async-start | bytes 8519680 | tf_op jit(solution)/shard_map/all_gather | solution.py:75
  19.3 1035.6 %all-reduce.3.cloned.1.call-start = ((), (), s32[]{:S(2)}) async-start(), calls=%async_computation.4 | async-start | bytes 8388608 | tf_op jit(solution)/shard_map/psum | solution.py:166
  19.3 189.3 %collective-permute-start.6 = (bf16[128,512]{1,0:T(8,128)(2,1)}, bf16[128,512]{1,0:T(8,128)(2,1)}, u32[]{:S(2)}, u32[]{:S(2)}) collective-permute-start(bf16[128,512]{1,0:T(8,128)(2,1)} %param.12), channel_id=1, source_target_pairs={{0,6},{2,8},{4,10},{6,12},{8,14},{10,16},{12,18},{14,20},{16,22},{... | collective-permute-start | bytes 393224 | tf_op jit(solution)/shard_map/ppermute | solution.py:16
  23.5 187.5 %collective-permute-start.7 = (bf16[128,512]{1,0:T(8,128)(2,1)}, bf16[128,512]{1,0:T(8,128)(2,1)}, u32[]{:S(2)}, u32[]{:S(2)}) collective-permute-start(bf16[128,512]{1,0:T(8,128)(2,1)} %param.12), channel_id=1, source_target_pairs={{0,4},{2,6},{4,8},{6,10},{8,12},{10,14},{12,16},{14,18},{16,20},{1... | collective-permute-start | bytes 393224 | tf_op jit(solution)/shard_map/ppermute | solution.py:16
  23.8 190.0 %collective-permute-start.8 = (bf16[128,512]{1,0:T(8,128)(2,1)}, bf16[128,512]{1,0:T(8,128)(2,1)}, u32[]{:S(2)}, u32[]{:S(2)}) collective-permute-start(bf16[128,512]{1,0:T(8,128)(2,1)} %param.12), channel_id=1, source_target_pairs={{0,2},{2,4},{4,6},{6,8},{8,10},{10,12},{12,14},{14,16},{16,18},{18... | collective-permute-start | bytes 393224 | tf_op jit(solution)/shard_map/ppermute | solution.py:16
  23.8 193.3 %collective-permute-start.9 = (bf16[128,512]{1,0:T(8,128)(2,1)}, bf16[128,512]{1,0:T(8,128)(2,1)}, u32[]{:S(2)}, u32[]{:S(2)}) collective-permute-start(bf16[128,512]{1,0:T(8,128)(2,1)} %param.12), channel_id=1, source_target_pairs={{0,126},{2,0},{4,2},{6,4},{8,6},{10,8},{12,10},{14,12},{16,14},{18... | collective-permute-start | bytes 393224 | tf_op jit(solution)/shard_map/ppermute | solution.py:16
  24.3 193.8 %collective-permute-start.10 = (bf16[128,512]{1,0:T(8,128)(2,1)}, bf16[128,512]{1,0:T(8,128)(2,1)}, u32[]{:S(2)}, u32[]{:S(2)}) collective-permute-start(bf16[128,512]{1,0:T(8,128)(2,1)} %param.12), channel_id=1, source_target_pairs={{0,124},{2,126},{4,0},{6,2},{8,4},{10,6},{12,8},{14,10},{16,12},{1... | collective-permute-start | bytes 393224 | tf_op jit(solution)/shard_map/ppermute | solution.py:16
  30.7 90.0 %copy-start.4 = (bf16[128,512]{0,1:T(8,128)(2,1)}, bf16[128,512]{0,1:T(8,128)(2,1)S(1)}, u32[]{:S(2)}) copy-start(bf16[128,512]{0,1:T(8,128)(2,1)S(1)} %copy.71) | copy-start | bytes 393220
  128.8 116.3 %copy-start.2 = (bf16[128,512]{0,1:T(8,128)(2,1)S(1)}, bf16[128,512]{0,1:T(8,128)(2,1)}, u32[]{:S(2)}) copy-start(bf16[128,512]{0,1:T(8,128)(2,1)} %copy.69) | copy-start | bytes 393220
  208.6 10.9 %collective-permute-start.11 = (bf16[128,512]{1,0:T(8,128)(2,1)}, bf16[128,512]{1,0:T(8,128)(2,1)S(1)}, u32[]{:S(2)}, u32[]{:S(2)}) collective-permute-start(bf16[128,512]{1,0:T(8,128)(2,1)} %param.12), channel_id=1, source_target_pairs={{0,122},{2,124},{4,126},{6,0},{8,2},{10,4},{12,6},{14,8},{16,10},{... | collective-permute-start | bytes 393224 | tf_op jit(solution)/shard_map/ppermute | solution.py:16
  211.0 13.7 %collective-permute-start.5 = (bf16[128,512]{1,0:T(8,128)(2,1)}, bf16[128,512]{1,0:T(8,128)(2,1)}, u32[]{:S(2)}, u32[]{:S(2)}) collective-permute-start(bf16[128,512]{1,0:T(8,128)(2,1)} %bitcast.109), channel_id=1, source_target_pairs={{0,6},{2,8},{4,10},{6,12},{8,14},{10,16},{12,18},{14,20},{16,22},{... | collective-permute-start | bytes 393224 | tf_op jit(solution)/shard_map/ppermute | solution.py:16
  213.8 14.8 %collective-permute-start.4 = (bf16[128,512]{1,0:T(8,128)(2,1)}, bf16[128,512]{1,0:T(8,128)(2,1)}, u32[]{:S(2)}, u32[]{:S(2)}) collective-permute-start(bf16[128,512]{1,0:T(8,128)(2,1)} %bitcast.110), channel_id=1, source_target_pairs={{0,4},{2,6},{4,8},{6,10},{8,12},{10,14},{12,16},{14,18},{16,20},{1... | collective-permute-start | bytes 393224 | tf_op jit(solution)/shard_map/ppermute | solution.py:16
  217.1 11.6 %collective-permute-start.3 = (bf16[128,512]{1,0:T(8,128)(2,1)}, bf16[128,512]{1,0:T(8,128)(2,1)}, u32[]{:S(2)}, u32[]{:S(2)}) collective-permute-start(bf16[128,512]{1,0:T(8,128)(2,1)} %bitcast.111), channel_id=1, source_target_pairs={{0,2},{2,4},{4,6},{6,8},{8,10},{10,12},{12,14},{14,16},{16,18},{18... | collective-permute-start | bytes 393224 | tf_op jit(solution)/shard_map/ppermute | solution.py:16
  218.1 10.6 collective-permute-start.2
  219.6 9.1 collective-permute-start.1
  224.6 6.5 collective-permute-start
  276.2 105.7 %copy-start.5 = (bf16[128,512]{0,1:T(8,128)(2,1)S(1)}, bf16[128,512]{0,1:T(8,128)(2,1)}, u32[]{:S(2)}) copy-start(bf16[128,512]{0,1:T(8,128)(2,1)} %copy-done.4) | copy-start | bytes 393220
  276.2 105.7 %copy-start.7 = (f32[8,128]{1,0:T(8,128)S(1)}, f32[8,128]{1,0:T(8,128)}, u32[]{:S(2)}) copy-start(f32[8,128]{1,0:T(8,128)} %param.17) | copy-start | bytes 12292
  402.4 103.5 %copy-start.3 = (bf16[128,512]{0,1:T(8,128)(2,1)S(1)}, bf16[128,512]{0,1:T(8,128)(2,1)}, u32[]{:S(2)}) copy-start(bf16[128,512]{0,1:T(8,128)(2,1)} %copy.72) | copy-start | bytes 393220
  402.4 103.5 %copy-start.6 = (f32[8,8192]{1,0:T(8,128)S(1)}, f32[8,8192]{1,0:T(8,128)}, u32[]{:S(2)}) copy-start(f32[8,8192]{1,0:T(8,128)} %all_gather.27) | copy-start | bytes 786436
  544.3 516.9 %copy-start.1 = (bf16[512,1024]{1,0:T(8,128)(2,1)S(1)}, bf16[512,1024]{1,0:T(8,128)(2,1)}, u32[]{:S(2)}) copy-start(bf16[512,1024]{1,0:T(8,128)(2,1)} %param.18) | copy-start | bytes 3145732
Sparse Core Ops, SparseCore 0:
  9.7 119.8 all-gather.4
  131.4 122.5 all-gather.8
  255.6 126.1 all-gather.6
  383.4 110.3 all-gather.10
  496.8 558.0 all-reduce.2
where the time goes:
time: 1070 us
  waiting for transfers between devices  679 us (63%)
  blocking collectives  170 us (16%)
  matrix products  116 us (11%)
  local copies, waits for them, and re-layouts  60.1 us (6%)
  starting transfers between devices  22.3 us (2%)
  between operations  14.7 us (1%)
    psum x1, waiting for transfers between devices, body(): lax.psum((out_weight_grad, msg_weight_grad), 'node')  494 us
    all_gather x1, waiting for transfers between devices, attention(): grad_piece = lax.all_gather(grad_mix, 'node', axis=0, tiled=True)  91.5 us
    all_gather x1, waiting for transfers between devices, attention(): value_piece = lax.all_gather(values, 'node', axis=0, tiled=True)  89.6 us
    all_gather x1, blocking collectives, stats_table(): lax.all_gather(spread, 'node', axis=1, tiled=True)  84.6 us
    all_gather x1, blocking collectives, stats_table(): lax.all_gather(log_sums, 'node', axis=1, tiled=True)  77.8 us
    dot_general x1, matrix products, key_side(): jnp.einsum('ihd,jhd->hij', grad_rows, value_rows, preferred_element_type=...  26.4 us
    unnamed x37, local copies, waits for them, and re-layouts  22.3 us
    ppermute x12, starting transfers between devices, from_behind(): return lax.ppermute(value, axis, pairs)  22.1 us
  transfers between devices with their start and end apart: 17, of which 4 were waited for; matrix products, arithmetic and copies ran while one was open for 16% of the time, Pallas kernels for 0%

commit v1 on v0

v1 whole, which is shorter than its diff:
```python
import functools
import math

import jax
import jax.numpy as jnp
from jax import lax
from jax.experimental import pallas as pl
from jax.experimental.pallas import tpu as pltpu
from jax.sharding import Mesh
from jax.sharding import PartitionSpec as P

BLOCK = 128
REACH = 3
LANES = 128
PAIRS = 4
STAT = 16
NODE = ("z", "y", "x", "c")
BF16 = jnp.bfloat16
F32 = jnp.float32
VMEM_LIMIT = 48 * 1024 * 1024

NT = (((1,), (1,)), ((), ()))
NN = (((1,), (0,)), ((), ()))
TN = (((0,), (0,)), ((), ()))


def dot(a, b, dims):
    return lax.dot_general(a, b, dims, preferred_element_type=F32)


def shift(value, axis, steps):
    count = lax.axis_size(axis)
    return lax.ppermute(value, axis, [(i, (i + steps) % count) for i in range(count)])


def swap(value, axes, mask):
    count = lax.axis_size(axes)
    return lax.ppermute(value, axes, [(i, i ^ mask) for i in range(count)])


def place_in_group():
    return lax.axis_index("y") * 2 + lax.axis_index("c")


def call(kernel, outs, *args, scratch=(), smem=0, flops=0, name=None):
    specs = [pl.BlockSpec(memory_space=pltpu.SMEM)] * smem
    specs += [pl.BlockSpec(memory_space=pltpu.VMEM)] * (len(args) - smem)
    size = sum(math.prod(a.shape) * a.dtype.itemsize for a in (*args, *outs))
    return pl.pallas_call(
        kernel,
        out_shape=outs,
        in_specs=specs,
        out_specs=[pl.BlockSpec(memory_space=pltpu.VMEM)] * len(outs),
        scratch_shapes=list(scratch),
        cost_estimate=pl.CostEstimate(flops=flops, bytes_accessed=size, transcendentals=0),
        compiler_params=pltpu.CompilerParams(vmem_limit_bytes=VMEM_LIMIT),
        name=name,
    )(*args)


def shaped(shape, dtype=BF16):
    return jax.ShapeDtypeStruct(shape, dtype)


def three_pieces(value):
    high = value.astype(BF16)
    rest = value - high.astype(F32)
    middle = rest.astype(BF16)
    low = (rest - middle.astype(F32)).astype(BF16)
    return jnp.concatenate(
        [high.astype(F32), middle.astype(F32), low.astype(F32), jnp.zeros((STAT - 6, LANES), F32)],
        axis=0,
    ).astype(BF16)


def pair_rows(table, pair):
    rows = table[0:2]
    for other in range(1, PAIRS):
        rows = jnp.where(pair == other, table[2 * other : 2 * other + 2], rows)
    return rows


def outgoing_kernel(q_ref, k_ref, v_ref, log_ref, *pay_refs):
    me = place_in_group()
    logs = log_ref[...]
    for j, pay in enumerate(pay_refs):
        pair = me ^ j
        columns = pl.ds(pl.multiple_of(pair * LANES, LANES), LANES)
        pay[0:128] = q_ref[:, columns]
        pay[128:144] = three_pieces(pair_rows(logs, pair))
        pay[144:272] = k_ref[:, columns]
        pay[272:400] = v_ref[:, columns]


def join_kernel(*refs):
    q_out, kv_out = refs[4:]
    for j, pay in enumerate(refs[:4]):
        q_out[j * 144 : (j + 1) * 144] = pay[0:144]
        kv_out[j * 256 : (j + 1) * 256] = pay[144:400]


def mix_kernel(own_ref, other_ref, weight_ref, mix_ref, *pay_refs):
    side = lax.axis_index("h")
    half = own_ref.shape[1]
    own_columns = pl.ds(pl.multiple_of(side * half, half), half)
    other_columns = pl.ds(pl.multiple_of((1 - side) * half, half), half)
    grad = dot(own_ref[...], weight_ref[:, own_columns], NT)
    grad = (grad + dot(other_ref[...], weight_ref[:, other_columns], NT)).astype(BF16)
    product = grad.astype(F32) * mix_ref[...].astype(F32)
    turned = product.T
    rows = [jnp.sum(turned[64 * i : 64 * (i + 1)], axis=0, keepdims=True) for i in range(8)]
    spread = jnp.concatenate(rows, axis=0)
    me = place_in_group()
    for j, pay in enumerate(pay_refs):
        pair = me ^ j
        block = grad[:, 0:LANES]
        for other in range(1, PAIRS):
            block = jnp.where(pair == other, grad[:, other * LANES : (other + 1) * LANES], block)
        pay[0:128] = block
        pay[128:144] = three_pieces(pair_rows(spread, pair))


def join_grad_kernel(*refs):
    for j, pay in enumerate(refs[:4]):
        refs[4][j * 144 : (j + 1) * 144] = pay[...]


TILE = 512


def attention_kernel(*refs):
    q_in, do_in, kv_in = refs[0:4], refs[4:8], refs[8:12]
    dq_out, dkv_out = refs[12:16], refs[16:20]
    keys, values, keys_t, query, grad, logs, spread, dq, dk, dv = refs[20:]
    lane = lax.broadcasted_iota(jnp.int32, (128, LANES), 1)
    for k in range(4):
        for j in range(4):
            rows = slice((k * 4 + j) * 128, (k * 4 + j + 1) * 128)
            block = kv_in[k][j * 256 : j * 256 + 128]
            keys[rows] = block
            keys_t[:, rows] = block.astype(F32).T.astype(BF16)
            values[rows] = kv_in[k][j * 256 + 128 : (j + 1) * 256]
            for source, table, stat, factor in (
                (q_in[k], query, logs, 0.125),
                (do_in[k], grad, spread, 1.0),
            ):
                block = source[j * 144 : j * 144 + 128].astype(F32) * factor
                table[0, rows] = jnp.where(lane < 64, block, 0.0).astype(BF16)
                table[1, rows] = jnp.where(lane < 64, 0.0, block).astype(BF16)
                pieces = source[j * 144 + 128 : (j + 1) * 144].astype(F32)
                stat[:, rows] = pieces[0:2] + pieces[2:4] + pieces[4:6]
    dq[...] = jnp.zeros_like(dq)
    steps = keys.shape[0] // TILE

    @pl.loop(0, steps)
    def _(kb):
        krows = pl.ds(pl.multiple_of(kb * TILE, TILE), TILE)
        dk[krows] = jnp.zeros((TILE, LANES), F32)
        dv[krows] = jnp.zeros((TILE, LANES), F32)
        key_tile, value_tile = keys[krows], values[krows]

        @pl.loop(0, steps)
        def _(qb):
            qrows = pl.ds(pl.multiple_of(qb * TILE, TILE), TILE)
            for h in range(2):
                query_tile, grad_tile = query[h, qrows], grad[h, qrows]
                scores = dot(key_tile, query_tile, NT) - logs[h : h + 1, qrows]
                soft = jnp.exp(scores)
                change = dot(value_tile, grad_tile, NT) - spread[h : h + 1, qrows]
                score_grad = (soft * change).astype(BF16)
                dv[krows] += dot(soft.astype(BF16), grad_tile, NN)
                dk[krows] += dot(score_grad, query_tile, NN)
                head = slice(64 * h, 64 * (h + 1))
                dq[head, qrows] += dot(keys_t[head, krows], score_grad, NN)

    for k in range(4):
        for j in range(4):
            rows = slice((k * 4 + j) * 128, (k * 4 + j + 1) * 128)
            dq_out[k][j * 128 : (j + 1) * 128] = (dq[:, rows].T * 0.125).astype(BF16)
            dkv_out[k][j * 256 : j * 256 + 128] = dk[rows].astype(BF16)
            dkv_out[k][j * 256 + 128 : (j + 1) * 256] = dv[rows].astype(BF16)


def sum_kernel(*refs):
    dq = [r[...].astype(F32) for r in refs[0:4]]
    dkv = [r[...].astype(F32) for r in refs[4:8]]
    dq = (dq[0] + dq[1] + dq[2] + dq[3]).astype(BF16)
    dkv = (dkv[0] + dkv[1] + dkv[2] + dkv[3]).astype(BF16)
    for j, pay in enumerate(refs[8:12]):
        pay[0:128] = dq[j * 128 : (j + 1) * 128]
        pay[128:384] = dkv[j * 256 : (j + 1) * 256]


def place_kernel(*refs):
    me = place_in_group()
    dq, dk, dv = refs[4:]
    for j, pay in enumerate(refs[:4]):
        columns = pl.ds(pl.multiple_of((me ^ j) * LANES, LANES), LANES)
        dq[:, columns] = pay[0:128]
        dk[:, columns] = pay[128:256]
        dv[:, columns] = pay[256:384]


def share_kernel(source_ref, count_ref, tiles_ref, grad_ref, *refs):
    outs, total = refs[:-1], refs[-1]
    window = 2 * REACH + 1
    parts = lax.axis_size(NODE)
    home = lax.axis_index(NODE)
    total[...] = jnp.zeros_like(total)
    grad = grad_ref[...]
    for e in range(tiles_ref.shape[1]):

        @pl.when(e < count_ref[0])
        def _():
            distance = lax.rem(source_ref[0, e] - home + REACH + 2 * parts, parts)
            slot = jnp.clip(distance, 0, window - 1)
            total[slot] += dot(tiles_ref[0, e], grad, TN)

    for o, out in enumerate(outs):
        out[...] = total[o].astype(out.dtype)


def weights_kernel(own_ref, other_ref, g_own_ref, g_other_ref, mix_ref, feat_ref, weight_ref, gf_ref, keep_ref, send_ref):
    side = lax.axis_index("h")
    core = lax.axis_index("c")
    half = own_ref.shape[1]
    own_columns = pl.ds(pl.multiple_of(side * half, half), half)
    other_columns = pl.ds(pl.multiple_of((1 - side) * half, half), half)
    features = dot(g_own_ref[...], weight_ref[:, own_columns], NT)
    features = features + dot(g_other_ref[...], weight_ref[:, other_columns], NT)
    gf_ref[...] = features.astype(BF16)
    mix = mix_ref[...].astype(F32).T.astype(BF16)
    feat = feat_ref[...].astype(F32).T.astype(BF16)

    def put(out_refs):
        for left, rights, out in zip((mix, feat), ((own_ref, other_ref), (g_own_ref, g_other_ref)), out_refs):
            out[:, own_columns] = dot(left, rights[0][...], NN).astype(BF16)
            out[:, other_columns] = dot(left, rights[1][...], NN).astype(BF16)

    @pl.when(core == 0)
    def _():
        put((keep_ref, send_ref))

    @pl.when(core == 1)
    def _():
        put((send_ref, keep_ref))


def scatter_kernel(axis, received, *refs):
    me = lax.axis_index(axis)
    outs = refs[received:]
    count = len(outs)
    rows = outs[0].shape[0]
    for k, out in enumerate(outs):
        at = pl.ds(pl.multiple_of(lax.rem(me + k, count) * rows, rows), rows)
        total = refs[0][at].astype(F32)
        for ref in refs[1:received]:
            total = total + ref[at].astype(F32)
        out[...] = total.astype(BF16)


def gather_kernel(axis, *refs):
    me = lax.axis_index(axis)
    out = refs[-1]
    count = len(refs) - 1
    rows = refs[0].shape[0]
    for k in range(count):
        at = pl.ds(pl.multiple_of(lax.rem(me - k + count, count) * rows, rows), rows)
        out[at] = refs[k][...]


def final_kernel(own_ref, other_ref, first_ref, second_ref):
    core = lax.axis_index("c")

    @pl.when(core == 0)
    def _():
        first_ref[...] = own_ref[...].astype(F32)
        second_ref[...] = other_ref[...].astype(F32)

    @pl.when(core == 1)
    def _():
        first_ref[...] = other_ref[...].astype(F32)
        second_ref[...] = own_ref[...].astype(F32)


def reduce_weights(keep, send):
    rows, columns = keep.shape
    parts = [keep, swap(send, "c", 1)]
    for axis, count in (("x", 4), ("z", 4), ("y", 2)):
        rows = rows // count
        blocks = call(
            functools.partial(scatter_kernel, axis, len(parts)),
            [shaped((rows, columns))] * count,
            *parts,
            name="scatter_" + axis,
        )
        parts = [blocks[0]] + [shift(blocks[k], axis, k) for k in range(1, count)]
    whole = (parts[0].astype(F32) + parts[1].astype(F32)).astype(BF16)
    for axis, count in (("y", 2), ("z", 4), ("x", 4)):
        blocks = [whole] + [shift(whole, axis, k) for k in range(1, count)]
        rows = rows * count
        (whole,) = call(
            functools.partial(gather_kernel, axis),
            [shaped((rows, columns))],
            *blocks,
            name="gather_" + axis,
        )
    other = swap(whole, "c", 1)
    return call(final_kernel, [shaped(whole.shape, F32)] * 2, whole, other, name="final")


def body(
    features,
    queries,
    keys,
    values,
    attn_mix,
    log_sums,
    out_weight,
    msg_weight,
    edge_tiles,
    edge_source,
    edge_count,
    out_grad,
):
    rows, columns = out_grad.shape
    other_grad = swap(out_grad, "h", 1)
    pays = call(
        outgoing_kernel, [shaped((400, LANES))] * 4, queries, keys, values, log_sums, name="outgoing"
    )
    pays = [pays[0]] + [swap(pays[j], ("y", "c"), j) for j in range(1, 4)]
    near_q, near_kv = call(
        join_kernel, [shaped((576, LANES)), shaped((1024, LANES))], *pays, name="join"
    )
    all_kv = [near_kv] + [shift(near_kv, "x", k) for k in range(1, 4)]
    all_q = [near_q] + [shift(near_q, "z", k) for k in range(1, 4)]

    pays = call(
        mix_kernel,
        [shaped((144, LANES))] * 4,
        out_grad,
        other_grad,
        out_weight,
        attn_mix,
        name="mix",
    )
    pays = [pays[0]] + [swap(pays[j], ("y", "c"), j) for j in range(1, 4)]
    (near_do,) = call(join_grad_kernel, [shaped((576, LANES))], *pays, name="join_grad")
    all_do = [near_do] + [shift(near_do, "z", k) for k in range(1, 4)]

    shares = call(
        share_kernel,
        [shaped((rows, columns), F32 if o == REACH else BF16) for o in range(2 * REACH + 1)],
        edge_source,
        edge_count,
        edge_tiles,
        out_grad,
        smem=2,
        scratch=[pltpu.VMEM((2 * REACH + 1, rows, columns), F32)],
        name="shares",
    )
    total = shares[REACH]
    for o in range(2 * REACH + 1):
        if o != REACH:
            total = total + shift(shares[o], NODE, o - REACH).astype(F32)
    near_g = total.astype(BF16)
    other_g = swap(near_g, "h", 1)
    grad_features, keep, send = call(
        weights_kernel,
        [shaped((rows, columns)), shaped((columns, 2 * columns)), shaped((columns, 2 * columns))],
        out_grad,
        other_grad,
        near_g,
        other_g,
        attn_mix,
        features,
        msg_weight,
        name="weights",
    )
    out_weight_grad, msg_weight_grad = reduce_weights(keep, send)

    big = 2048
    results = call(
        attention_kernel,
        [shaped((512, LANES))] * 4 + [shaped((1024, LANES))] * 4,
        *all_q,
        *all_do,
        *all_kv,
        scratch=[
            pltpu.VMEM((big, LANES), BF16),
            pltpu.VMEM((big, LANES), BF16),
            pltpu.VMEM((LANES, big), BF16),
            pltpu.VMEM((2, big, LANES), BF16),
            pltpu.VMEM((2, big, LANES), BF16),
            pltpu.VMEM((2, big), F32),
            pltpu.VMEM((2, big), F32),
            pltpu.VMEM((LANES, big), F32),
            pltpu.VMEM((big, LANES), F32),
            pltpu.VMEM((big, LANES), F32),
        ],
        flops=8 * 10 * big * big * 64,
        name="attention",
    )
    parts = [results[0]] + [shift(results[k], "z", -k) for k in range(1, 4)]
    parts += [results[4]] + [shift(results[4 + k], "x", -k) for k in range(1, 4)]
    pays = call(sum_kernel, [shaped((384, LANES))] * 4, *parts, name="sum")
    pays = [pays[0]] + [swap(pays[j], ("y", "c"), j) for j in range(1, 4)]
    grad_query, grad_key, grad_value = call(
        place_kernel, [shaped((rows, columns))] * 3, *pays, name="place"
    )
    return (grad_features, grad_query, grad_key, grad_value, out_weight_grad, msg_weight_grad)


def solution(mesh):
    fine = Mesh(mesh.devices.reshape(4, 2, 4, 2, 2), NODE + ("h",))
    both = P(NODE, "h")
    placed = (
        both,
        both,
        both,
        both,
        both,
        P("h", NODE),
        P("h", None),
        P("h", None),
        P(NODE, None, None, None),
        P(NODE, None),
        P(NODE),
        both,
    )
    return jax.shard_map(
        body,
        mesh=fine,
        in_specs=placed,
        out_specs=(both, both, both, both, P("h", None), P("h", None)),
        check_vma=False,
    )
```

time: 1070 us -> 170 us (0.16)
  waiting for transfers between devices: 679 us -> 74.7 us
  blocking collectives: 170 us -> 0 us
  matrix products: 116 us -> 0 us
  local copies, waits for them, and re-layouts: 60.1 us -> 5.25 us
  starting transfers between devices: 22.3 us -> 57 us
  Pallas kernels: 0 us -> 31.3 us
  between operations: 14.7 us -> 1.48 us
    psum x1 -> x0, waiting for transfers between devices: 494 us -> none  [body(): lax.psum((out_weight_grad, msg_weight_grad), 'node')]
    all_gather x4 -> x0, waiting for transfers between devices: 181 us -> none  [the longest x1 91.5 us: attention(): grad_piece = lax.all_gather(grad_mix, 'node', axis=0, tiled=True)]
    all_gather x3 -> x0, blocking collectives: 170 us -> none  [the longest x1 84.6 us: stats_table(): lax.all_gather(spread, 'node', axis=1, tiled=True)]
    dot_general x11 -> x0, matrix products: 116 us -> none  [the longest x1 26.4 us: key_side(): jnp.einsum('ihd,jhd->hij', grad_rows, value_rows, preferred_element_type=...]
    ppermute x12 -> x48, waiting for transfers between devices: 2.47 us -> 74.7 us  [the longest x35 62 us: shift(): lax.ppermute(value, axis, [(i, (i + steps) % count) for i in range(count)])]
    all_gather x3 -> x0, local copies, waits for them, and re-layouts: 36 us -> none  [the longest x1 12 us: attention(): query_piece = lax.all_gather(queries, 'node', axis=0, tiled=True)]
    ppermute x12 -> x48, starting transfers between devices: 22.1 us -> 57 us  [the longest x35 36.8 us: shift(): lax.ppermute(value, axis, [(i, (i + steps) % count) for i in range(count)])]
    pallas_call x0 -> x16, Pallas kernels: none -> 31.3 us  [call(): pl.pallas_call(kernel, out_shape=outs, in_specs=specs, out_specs=[pl.Bloc...]
  transfers between devices with their start and end apart: 17 -> 48, of which waited for: 4 -> 27; matrix products, arithmetic and copies ran while one was open for 16% -> 0% of each run, Pallas kernels for 0% -> 15%
where the time goes in v1:
time: 170 us
  waiting for transfers between devices  74.7 us (44%)
  starting transfers between devices  57 us (34%)
  Pallas kernels  31.3 us (18%)
  local copies, waits for them, and re-layouts  5.25 us (3%)
    ppermute x35, waiting for transfers between devices, shift(): lax.ppermute(value, axis, [(i, (i + steps) % count) for i in range(count)])  62 us
    ppermute x35, starting transfers between devices, shift(): lax.ppermute(value, axis, [(i, (i + steps) % count) for i in range(count)])  36.8 us
    pallas_call x16, Pallas kernels, call(): pl.pallas_call(kernel, out_shape=outs, in_specs=specs, out_specs=[pl.Bloc...  31.3 us
    ppermute x13, starting transfers between devices, swap(): return lax.ppermute(value, axes, [(i, i ^ mask) for i in range(count)])  20.2 us
    ppermute x13, waiting for transfers between devices, swap(): return lax.ppermute(value, axes, [(i, i ^ mask) for i in range(count)])  12.6 us
    unnamed x28, local copies, waits for them, and re-layouts  5.25 us
  transfers between devices with their start and end apart: 48, of which 27 were waited for; matrix products, arithmetic and copies ran while one was open for 0% of the time, Pallas kernels for 15%

profile of v1, /device:TPU:1, one launch (start us, length us, event | category | flops | bytes accessed | tf_op | source)
XLA Modules:
  0.0 169.9 jit_solution(6910736118312046122)
XLA Ops:
  1.3 0.9 copy-done
  2.2 0.9 copy-done.7
  3.1 0.7 copy-done.13
  3.8 1.4 shares.1
  5.2 8.0 %collective-permute-start.1 = (bf16[128,512]{1,0:T(8,128)(2,1)S(1)}, bf16[128,512]{1,0:T(8,128)(2,1)S(1)}, u32[]{:S(2)}, u32[]{:S(2)}) collective-permute-start(bf16[128,512]{1,0:T(8,128)(2,1)S(1)} %get-tuple-element.54), channel_id=1, source_target_pairs={{0,122},{2,124},{4,126},{6,0},{8,2},{10,4},{12,6},{14,8},{16,10},{... | collective-permute-start | bytes 393224 | tf_op jit(solution)/shard_map/ppermute | solution.py:33
  13.2 1.2 collective-permute-start.2
  14.3 0.7 collective-permute-start.3
  15.0 1.1 collective-permute-start.4
  16.8 2.5 %collective-permute-done.2 = bf16[128,512]{1,0:T(8,128)(2,1)S(1)} collective-permute-done((bf16[128,512]{1,0:T(8,128)(2,1)S(1)}, bf16[128,512]{1,0:T(8,128)(2,1)S(1)}, u32[]{:S(2)}, u32[]{:S(2)}) %collective-permute-start.2) | collective-permute-done | bytes 131104 | tf_op jit(solution)/shard_map/ppermute | solution.py:33
  19.3 2.6 %collective-permute-start = (bf16[128,512]{1,0:T(8,128)(2,1)S(1)}, bf16[128,512]{1,0:T(8,128)(2,1)S(1)}, u32[]{:S(2)}, u32[]{:S(2)}) collective-permute-start(bf16[128,512]{1,0:T(8,128)(2,1)S(1)} %copy-done), channel_id=1, source_target_pairs={{0,1},{1,0},{2,3},{3,2},{4,5},{5,4},{6,7},{7,6},{8,9},{9,8},{10,11... | collective-permute-start | bytes 393224 | tf_op jit(solution)/shard_map/ppermute | solution.py:38
  21.9 7.0 %collective-permute-done.5 = bf16[128,512]{1,0:T(8,128)(2,1)S(1)} collective-permute-done((bf16[128,512]{1,0:T(8,128)(2,1)S(1)}, bf16[128,512]{1,0:T(8,128)(2,1)S(1)}, u32[]{:S(2)}, u32[]{:S(2)}) %collective-permute-start.5) | collective-permute-done | bytes 131104 | tf_op jit(solution)/shard_map/ppermute | solution.py:33
  29.6 2.7 %collective-permute-start.7 = (bf16[128,512]{1,0:T(8,128)(2,1)S(1)}, bf16[128,512]{1,0:T(8,128)(2,1)S(1)}, u32[]{:S(2)}, u32[]{:S(2)}) collective-permute-start(bf16[128,512]{1,0:T(8,128)(2,1)S(1)} %add_convert_fusion.g_own_ref), channel_id=1, source_target_pairs={{0,1},{1,0},{2,3},{3,2},{4,5},{5,4},{6,7},{7,6},{8,9},{9,8},{10,11... | collective-permute-start | bytes 393224 | tf_op jit(solution)/shard_map/ppermute | solution.py:38
  32.3 3.0 %collective-permute-done.7.g_other_ref = bf16[128,512]{1,0:T(8,128)(2,1)S(1)} collective-permute-done((bf16[128,512]{1,0:T(8,128)(2,1)S(1)}, bf16[128,512]{1,0:T(8,128)(2,1)S(1)}, u32[]{:S(2)}, u32[]{:S(2)}) %collective-permute-start.7) | collective-permute-done | bytes 131104 | tf_op jit(solution)/shard_map/ppermute | solution.py:38
  35.3 0.9 copy-done.1
  36.2 0.9 copy-done.5
  37.1 0.9 copy-done.8
  38.0 1.8 %weights.1 = (bf16[128,512]{1,0:T(8,128)(2,1)}, bf16[512,1024]{1,0:T(8,128)(2,1)S(1)}, bf16[512,1024]{1,0:T(8,128)(2,1)S(1)}) custom-call(bf16[128,512]{1,0:T(8,128)(2,1)S(1)} %copy-done.1, bf16[128,512]{1,0:T(8,128)(2,1)S(1)} %collective-permute-done.other_ref, bf16[128,512]{1,0:T(8,128)(2,1)S(1)} %add_convert_fusion.g_own_ref, ...), custom_call_target="tpu_custom_call" | custom-call | bytes 4063232 | tf_op jit(solution)/shard_map/weights/pallas_call | solution.py:49
  39.9 2.6 %collective-permute-done.32.refs_1_ = bf16[512,1024]{1,0:T(8,128)(2,1)S(1)} collective-permute-done((bf16[512,1024]{1,0:T(8,128)(2,1)S(1)}, bf16[512,1024]{1,0:T(8,128)(2,1)S(1)}, u32[]{:S(2)}, u32[]{:S(2)}) %collective-permute-start.32) | collective-permute-done | bytes 1048608 | tf_op jit(solution)/shard_map/ppermute | solution.py:38
  43.0 2.6 %collective-permute-start.35 = (bf16[128,1024]{1,0:T(8,128)(2,1)S(1)}, bf16[128,1024]{1,0:T(8,128)(2,1)S(1)}, u32[]{:S(2)}, u32[]{:S(2)}) collective-permute-start(bf16[128,1024]{1,0:T(8,128)(2,1)S(1)} %get-tuple-element.91), channel_id=1, source_target_pairs={{0,12},{4,0},{8,4},{12,8},{1,13},{5,1},{9,5},{13,9},{2,14},{6,2},{... | collective-permute-start | bytes 786440 | tf_op jit(solution)/shard_map/ppermute | solution.py:33
  45.6 11.9 %collective-permute-done.33.refs_1_ = bf16[128,1024]{1,0:T(8,128)(2,1)S(1)} collective-permute-done((bf16[128,1024]{1,0:T(8,128)(2,1)S(1)}, bf16[128,1024]{1,0:T(8,128)(2,1)S(1)}, u32[]{:S(2)}, u32[]{:S(2)}) %collective-permute-start.33) | collective-permute-done | bytes 262176 | tf_op jit(solution)/shard_map/ppermute | solution.py:33
  58.0 0.7 collective-permute-start.37
  58.7 1.9 %collective-permute-start.38 = (bf16[32,1024]{1,0:T(8,128)(2,1)S(1)}, bf16[32,1024]{1,0:T(8,128)(2,1)S(1)}, u32[]{:S(2)}, u32[]{:S(2)}) collective-permute-start(bf16[32,1024]{1,0:T(8,128)(2,1)S(1)} %get-tuple-element.95), channel_id=1, source_target_pairs={{0,96},{32,0},{64,32},{96,64},{1,97},{33,1},{65,33},{97,65},{2,98}... | collective-permute-start | bytes 196616 | tf_op jit(solution)/shard_map/ppermute | solution.py:33
  60.7 2.0 %collective-permute-done.36.refs_1_ = bf16[32,1024]{1,0:T(8,128)(2,1)S(1)} collective-permute-done((bf16[32,1024]{1,0:T(8,128)(2,1)S(1)}, bf16[32,1024]{1,0:T(8,128)(2,1)S(1)}, u32[]{:S(2)}, u32[]{:S(2)}) %collective-permute-start.36) | collective-permute-done | bytes 65568 | tf_op jit(solution)/shard_map/ppermute | solution.py:33
  63.0 0.9 collective-permute-done.38.refs_3_
  63.9 1.5 collective-permute-start.39
  65.6 2.6 %collective-permute-start.8 = (bf16[400,128]{1,0:T(8,128)(2,1)S(1)}, bf16[400,128]{1,0:T(8,128)(2,1)S(1)}, u32[]{:S(2)}, u32[]{:S(2)}) collective-permute-start(bf16[400,128]{1,0:T(8,128)(2,1)S(1)} %get-tuple-element.62), channel_id=1, source_target_pairs={{0,2},{2,0},{16,18},{18,16},{1,3},{3,1},{17,19},{19,17},{4,6},{6,4... | collective-permute-start | bytes 307208 | tf_op jit(solution)/shard_map/ppermute | solution.py:38
  68.4 1.5 collective-permute-start.10
  70.2 5.0 %collective-permute-done.40.refs_1_ = bf16[16,1024]{1,0:T(8,128)(2,1)S(1)} collective-permute-done((bf16[16,1024]{1,0:T(8,128)(2,1)S(1)}, bf16[16,1024]{1,0:T(8,128)(2,1)S(1)}, u32[]{:S(2)}, u32[]{:S(2)}) %collective-permute-start.40) | collective-permute-done | bytes 32800 | tf_op jit(solution)/shard_map/ppermute | solution.py:33
  75.2 1.3 collective-permute-start.43
  76.5 1.1 collective-permute-start.42
  77.7 2.7 %collective-permute-start.13 = (bf16[576,128]{1,0:T(8,128)(2,1)S(1)}, bf16[576,128]{1,0:T(8,128)(2,1)S(1)}, u32[]{:S(2)}, u32[]{:S(2)}) collective-permute-start(bf16[576,128]{1,0:T(8,128)(2,1)S(1)} %get-tuple-element.65.refs_0_), channel_id=1, source_target_pairs={{0,96},{32,0},{64,32},{96,64},{1,97},{33,1},{65,33},{97,65},{2,98}... | collective-permute-start | bytes 442376 | tf_op jit(solution)/shard_map/ppermute | solution.py:33
  80.4 0.7 collective-permute-start.12
  81.2 0.8 collective-permute-done.41.refs_1_
  82.0 2.6 %collective-permute-start.46 = (bf16[128,1024]{1,0:T(8,128)(2,1)S(1)}, bf16[128,1024]{1,0:T(8,128)(2,1)S(1)}, u32[]{:S(2)}, u32[]{:S(2)}) collective-permute-start(bf16[128,1024]{1,0:T(8,128)(2,1)S(1)} %gather_z.1.refs_0_), channel_id=1, source_target_pairs={{0,12},{4,0},{8,4},{12,8},{1,13},{5,1},{9,5},{13,9},{2,14},{6,2},{... | collective-permute-start | bytes 786440 | tf_op jit(solution)/shard_map/ppermute | solution.py:33
  85.2 2.5 %collective-permute-start.14 = (bf16[144,128]{1,0:T(8,128)(2,1)S(1)}, bf16[144,128]{1,0:T(8,128)(2,1)S(1)}, u32[]{:S(2)}, u32[]{:S(2)}) collective-permute-start(bf16[144,128]{1,0:T(8,128)(2,1)S(1)} %get-tuple-element.67), channel_id=1, source_target_pairs={{0,2},{2,0},{16,18},{18,16},{1,3},{3,1},{17,19},{19,17},{4,6},{6,4... | collective-permute-start | bytes 110600 | tf_op jit(solution)/shard_map/ppermute | solution.py:38
  87.7 1.2 collective-permute-start.15
  88.9 1.1 collective-permute-start.16
  90.0 0.7 collective-permute-done.15.refs_2_
  90.9 1.4 collective-permute-done.16.refs_3_
  93.1 0.9 collective-permute-start.19
  93.9 1.9 %collective-permute-done.11.refs_1_ = bf16[576,128]{1,0:T(8,128)(2,1)S(1)} collective-permute-done((bf16[576,128]{1,0:T(8,128)(2,1)S(1)}, bf16[576,128]{1,0:T(8,128)(2,1)S(1)}, u32[]{:S(2)}, u32[]{:S(2)}) %collective-permute-start.11) | collective-permute-done | bytes 147488 | tf_op jit(solution)/shard_map/ppermute | solution.py:33
  96.2 1.6 collective-permute-done.19.refs_7_
  97.8 2.1 %collective-permute-start.21 = (bf16[1024,128]{1,0:T(8,128)(2,1)S(1)}, bf16[1024,128]{1,0:T(8,128)(2,1)S(1)}, u32[]{:S(2)}, u32[]{:S(2)}) collective-permute-start(bf16[1024,128]{1,0:T(8,128)(2,1)S(1)} %get-tuple-element.70.refs_8_), channel_id=1, source_target_pairs={{0,8},{4,12},{8,0},{12,4},{1,9},{5,13},{9,1},{13,5},{2,10},{6,14},... | collective-permute-start | bytes 786440 | tf_op jit(solution)/shard_map/ppermute | solution.py:33
  100.6 0.9 collective-permute-done.45.refs_2_
  101.5 1.0 collective-permute-start.18
  102.5 5.3 %collective-permute-done.44.refs_1_ = bf16[128,1024]{1,0:T(8,128)(2,1)S(1)} collective-permute-done((bf16[128,1024]{1,0:T(8,128)(2,1)S(1)}, bf16[128,1024]{1,0:T(8,128)(2,1)S(1)}, u32[]{:S(2)}, u32[]{:S(2)}) %collective-permute-start.44) | collective-permute-done | bytes 262176 | tf_op jit(solution)/shard_map/ppermute | solution.py:33
  107.9 2.2 %collective-permute-start.47 = (bf16[512,1024]{1,0:T(8,128)(2,1)S(1)}, bf16[512,1024]{1,0:T(8,128)(2,1)S(1)}, u32[]{:S(2)}, u32[]{:S(2)}) collective-permute-start(bf16[512,1024]{1,0:T(8,128)(2,1)S(1)} %gather_x.1.own_ref), channel_id=1, source_target_pairs={{0,2},{2,0},{1,3},{3,1},{4,6},{6,4},{5,7},{7,5},{8,10},{10,8},{9,1... | collective-permute-start | bytes 3145736 | tf_op jit(solution)/shard_map/ppermute | solution.py:38
  110.1 3.2 %collective-permute-done.17.refs_5_ = bf16[576,128]{1,0:T(8,128)(2,1)S(1)} collective-permute-done((bf16[576,128]{1,0:T(8,128)(2,1)S(1)}, bf16[576,128]{1,0:T(8,128)(2,1)S(1)}, u32[]{:S(2)}, u32[]{:S(2)}) %collective-permute-start.17) | collective-permute-done | bytes 147488 | tf_op jit(solution)/shard_map/ppermute | solution.py:33
  113.3 5.4 %collective-permute-done.20.refs_9_ = bf16[1024,128]{1,0:T(8,128)(2,1)S(1)} collective-permute-done((bf16[1024,128]{1,0:T(8,128)(2,1)S(1)}, bf16[1024,128]{1,0:T(8,128)(2,1)S(1)}, u32[]{:S(2)}, u32[]{:S(2)}) %collective-permute-start.20) | collective-permute-done | bytes 262176 | tf_op jit(solution)/shard_map/ppermute | solution.py:33
  118.7 23.6 %attention.1 = (bf16[512,128]{1,0:T(8,128)(2,1)S(1)}, bf16[512,128]{1,0:T(8,128)(2,1)S(1)}, bf16[512,128]{1,0:T(8,128)(2,1)S(1)}, bf16[512,128]{1,0:T(8,128)(2,1...) custom-call(bf16[576,128]{1,0:T(8,128)(2,1)S(1)} %get-tuple-element., ...), custom_call_target="tpu_custom_call" | custom-call | flops 21474836480 | bytes 3801088 | tf_op jit(solution)/shard_map/attention/pallas_call | solution.py:49
  142.3 1.0 collective-permute-start.23
  143.3 0.8 collective-permute-start.24
  144.5 2.3 %collective-permute-done.23.refs_1_ = bf16[512,128]{1,0:T(8,128)(2,1)S(1)} collective-permute-done((bf16[512,128]{1,0:T(8,128)(2,1)S(1)}, bf16[512,128]{1,0:T(8,128)(2,1)S(1)}, u32[]{:S(2)}, u32[]{:S(2)}) %collective-permute-start.23) | collective-permute-done | bytes 131104 | tf_op jit(solution)/shard_map/ppermute | solution.py:33
  146.8 1.8 %collective-permute-done.24.refs_2_ = bf16[512,128]{1,0:T(8,128)(2,1)S(1)} collective-permute-done((bf16[512,128]{1,0:T(8,128)(2,1)S(1)}, bf16[512,128]{1,0:T(8,128)(2,1)S(1)}, u32[]{:S(2)}, u32[]{:S(2)}) %collective-permute-start.24) | collective-permute-done | bytes 131104 | tf_op jit(solution)/shard_map/ppermute | solution.py:33
  148.6 1.4 collective-permute-start.25
  149.9 4.7 %collective-permute-done.25.refs_3_ = bf16[512,128]{1,0:T(8,128)(2,1)S(1)} collective-permute-done((bf16[512,128]{1,0:T(8,128)(2,1)S(1)}, bf16[512,128]{1,0:T(8,128)(2,1)S(1)}, u32[]{:S(2)}, u32[]{:S(2)}) %collective-permute-start.25) | collective-permute-done | bytes 131104 | tf_op jit(solution)/shard_map/ppermute | solution.py:33
  154.6 3.5 %collective-permute-done.28.refs_7_ = bf16[1024,128]{1,0:T(8,128)(2,1)S(1)} collective-permute-done((bf16[1024,128]{1,0:T(8,128)(2,1)S(1)}, bf16[1024,128]{1,0:T(8,128)(2,1)S(1)}, u32[]{:S(2)}, u32[]{:S(2)}) %collective-permute-start.28) | collective-permute-done | bytes 262176 | tf_op jit(solution)/shard_map/ppermute | solution.py:33
  158.4 1.8 %collective-permute-start.29 = (bf16[384,128]{1,0:T(8,128)(2,1)S(1)}, bf16[384,128]{1,0:T(8,128)(2,1)S(1)}, u32[]{:S(2)}, u32[]{:S(2)}) collective-permute-start(bf16[384,128]{1,0:T(8,128)(2,1)S(1)} %get-tuple-element.80), channel_id=1, source_target_pairs={{0,2},{2,0},{16,18},{18,16},{1,3},{3,1},{17,19},{19,17},{4,6},{6,4... | collective-permute-start | bytes 294920 | tf_op jit(solution)/shard_map/ppermute | solution.py:38
  160.2 0.6 collective-permute-start.30
  160.8 1.1 collective-permute-start.31
  161.9 2.6 %collective-permute-done.30.refs_2_ = bf16[384,128]{1,0:T(8,128)(2,1)S(1)} collective-permute-done((bf16[384,128]{1,0:T(8,128)(2,1)S(1)}, bf16[384,128]{1,0:T(8,128)(2,1)S(1)}, u32[]{:S(2)}, u32[]{:S(2)}) %collective-permute-start.30) | collective-permute-done | bytes 98336 | tf_op jit(solution)/shard_map/ppermute | solution.py:38
  164.5 2.3 %collective-permute-done.31.refs_3_ = bf16[384,128]{1,0:T(8,128)(2,1)S(1)} collective-permute-done((bf16[384,128]{1,0:T(8,128)(2,1)S(1)}, bf16[384,128]{1,0:T(8,128)(2,1)S(1)}, u32[]{:S(2)}, u32[]{:S(2)}) %collective-permute-start.31) | collective-permute-done | bytes 98336 | tf_op jit(solution)/shard_map/ppermute | solution.py:38
  166.8 0.8 place.1
  167.6 2.3 %final.1 = (f32[512,1024]{1,0:T(8,128)}, f32[512,1024]{1,0:T(8,128)}) custom-call(bf16[512,1024]{1,0:T(8,128)(2,1)S(1)} %gather_x.1.own_ref, bf16[512,1024]{1,0:T(8,128)(2,1)S(1)} %collective-permute-done.47.other_ref), custom_call_target="tpu_custom_call" | custom-call | bytes 6291456 | tf_op jit(solution)/shard_map/final/pallas_call | solution.py:49
  (78 shorter events, 6.9 us)
Async XLA Ops:
  1.3 0.9 copy-start
  2.2 0.9 copy-start.7
  3.1 0.7 copy-start.13
  3.8 31.5 %copy-start.3 = (bf16[512,1024]{1,0:T(8,128)(2,1)S(1)}, bf16[512,1024]{1,0:T(8,128)(2,1)}, u32[]{:S(2)}) copy-start(bf16[512,1024]{1,0:T(8,128)(2,1)} %weight_ref.2) | copy-start | bytes 3145732
  5.2 11.2 %collective-permute-start.1 = (bf16[128,512]{1,0:T(8,128)(2,1)S(1)}, bf16[128,512]{1,0:T(8,128)(2,1)S(1)}, u32[]{:S(2)}, u32[]{:S(2)}) collective-permute-start(bf16[128,512]{1,0:T(8,128)(2,1)S(1)} %get-tuple-element.54), channel_id=1, source_target_pairs={{0,122},{2,124},{4,126},{6,0},{8,2},{10,4},{12,6},{14,8},{16,10},{... | collective-permute-start | bytes 393224 | tf_op jit(solution)/shard_map/ppermute | solution.py:33
  13.2 6.1 %collective-permute-start.2 = (bf16[128,512]{1,0:T(8,128)(2,1)S(1)}, bf16[128,512]{1,0:T(8,128)(2,1)S(1)}, u32[]{:S(2)}, u32[]{:S(2)}) collective-permute-start(bf16[128,512]{1,0:T(8,128)(2,1)S(1)} %get-tuple-element.55), channel_id=1, source_target_pairs={{0,124},{2,126},{4,0},{6,2},{8,4},{10,6},{12,8},{14,10},{16,12},{1... | collective-permute-start | bytes 393224 | tf_op jit(solution)/shard_map/ppermute | solution.py:33
  14.3 7.6 %collective-permute-start.3 = (bf16[128,512]{1,0:T(8,128)(2,1)S(1)}, bf16[128,512]{1,0:T(8,128)(2,1)S(1)}, u32[]{:S(2)}, u32[]{:S(2)}) collective-permute-start(bf16[128,512]{1,0:T(8,128)(2,1)S(1)} %get-tuple-element.56), channel_id=1, source_target_pairs={{0,126},{2,0},{4,2},{6,4},{8,6},{10,8},{12,10},{14,12},{16,14},{18... | collective-permute-start | bytes 393224 | tf_op jit(solution)/shard_map/ppermute | solution.py:33
  15.0 6.9 %collective-permute-start.4 = (bf16[128,512]{1,0:T(8,128)(2,1)S(1)}, bf16[128,512]{1,0:T(8,128)(2,1)S(1)}, u32[]{:S(2)}, u32[]{:S(2)}) collective-permute-start(bf16[128,512]{1,0:T(8,128)(2,1)S(1)} %get-tuple-element.57), channel_id=1, source_target_pairs={{0,2},{2,4},{4,6},{6,8},{8,10},{10,12},{12,14},{14,16},{16,18},{18... | collective-permute-start | bytes 393224 | tf_op jit(solution)/shard_map/ppermute | solution.py:33
  16.1 12.8 %collective-permute-start.5 = (bf16[128,512]{1,0:T(8,128)(2,1)S(1)}, bf16[128,512]{1,0:T(8,128)(2,1)S(1)}, u32[]{:S(2)}, u32[]{:S(2)}) collective-permute-start(bf16[128,512]{1,0:T(8,128)(2,1)S(1)} %get-tuple-element.58), channel_id=1, source_target_pairs={{0,4},{2,6},{4,8},{6,10},{8,12},{10,14},{12,16},{14,18},{16,20},{1... | collective-permute-start | bytes 393224 | tf_op jit(solution)/shard_map/ppermute | solution.py:33
  16.4 13.0 %collective-permute-start.6 = (bf16[128,512]{1,0:T(8,128)(2,1)S(1)}, bf16[128,512]{1,0:T(8,128)(2,1)S(1)}, u32[]{:S(2)}, u32[]{:S(2)}) collective-permute-start(bf16[128,512]{1,0:T(8,128)(2,1)S(1)} %get-tuple-element.59), channel_id=1, source_target_pairs={{0,6},{2,8},{4,10},{6,12},{8,14},{10,16},{12,18},{14,20},{16,22},{... | collective-permute-start | bytes 393224 | tf_op jit(solution)/shard_map/ppermute | solution.py:33
  19.3 13.0 %collective-permute-start = (bf16[128,512]{1,0:T(8,128)(2,1)S(1)}, bf16[128,512]{1,0:T(8,128)(2,1)S(1)}, u32[]{:S(2)}, u32[]{:S(2)}) collective-permute-start(bf16[128,512]{1,0:T(8,128)(2,1)S(1)} %copy-done), channel_id=1, source_target_pairs={{0,1},{1,0},{2,3},{3,2},{4,5},{5,4},{6,7},{7,6},{8,9},{9,8},{10,11... | collective-permute-start | bytes 393224 | tf_op jit(solution)/shard_map/ppermute | solution.py:38
  29.6 5.7 %collective-permute-start.7 = (bf16[128,512]{1,0:T(8,128)(2,1)S(1)}, bf16[128,512]{1,0:T(8,128)(2,1)S(1)}, u32[]{:S(2)}, u32[]{:S(2)}) collective-permute-start(bf16[128,512]{1,0:T(8,128)(2,1)S(1)} %add_convert_fusion.g_own_ref), channel_id=1, source_target_pairs={{0,1},{1,0},{2,3},{3,2},{4,5},{5,4},{6,7},{7,6},{8,9},{9,8},{10,11... | collective-permute-start | bytes 393224 | tf_op jit(solution)/shard_map/ppermute | solution.py:38
  35.3 0.9 copy-start.1
  36.2 0.9 copy-start.5
  37.1 0.9 copy-start.8
  39.8 25.6 %copy-start.9 = (bf16[128,512]{1,0:T(8,128)(2,1)S(1)}, bf16[128,512]{1,0:T(8,128)(2,1)}, u32[]{:S(2)}) copy-start(bf16[128,512]{1,0:T(8,128)(2,1)} %q_ref.1) | copy-start | bytes 393220
  39.8 25.6 %copy-start.10 = (bf16[128,512]{1,0:T(8,128)(2,1)S(1)}, bf16[128,512]{1,0:T(8,128)(2,1)}, u32[]{:S(2)}) copy-start(bf16[128,512]{1,0:T(8,128)(2,1)} %k_ref.1) | copy-start | bytes 393220
  39.8 25.6 %copy-start.11 = (bf16[128,512]{1,0:T(8,128)(2,1)S(1)}, bf16[128,512]{1,0:T(8,128)(2,1)}, u32[]{:S(2)}) copy-start(bf16[128,512]{1,0:T(8,128)(2,1)} %v_ref.1) | copy-start | bytes 393220
  39.8 25.6 %copy-start.12 = (f32[8,128]{1,0:T(8,128)S(1)}, f32[8,128]{1,0:T(8,128)}, u32[]{:S(2)}) copy-start(f32[8,128]{1,0:T(8,128)} %log_ref.1) | copy-start | bytes 12292
  39.8 2.7 %collective-permute-start.32 = (bf16[512,1024]{1,0:T(8,128)(2,1)S(1)}, bf16[512,1024]{1,0:T(8,128)(2,1)S(1)}, u32[]{:S(2)}, u32[]{:S(2)}) collective-permute-start(bf16[512,1024]{1,0:T(8,128)(2,1)S(1)} %get-tuple-element.87), channel_id=1, source_target_pairs={{0,2},{2,0},{1,3},{3,1},{4,6},{6,4},{5,7},{7,5},{8,10},{10,8},{9,1... | collective-permute-start | bytes 3145736 | tf_op jit(solution)/shard_map/ppermute | solution.py:38
  42.6 42.0 %copy-start.2 = (bf16[128,512]{1,0:T(8,128)(2,1)S(1)}, bf16[128,512]{1,0:T(8,128)(2,1)}, u32[]{:S(2)}) copy-start(bf16[128,512]{1,0:T(8,128)(2,1)} %own_ref.3) | copy-start | bytes 393220
  42.6 42.0 %copy-start.4 = (bf16[512,1024]{1,0:T(8,128)(2,1)S(1)}, bf16[512,1024]{1,0:T(8,128)(2,1)}, u32[]{:S(2)}) copy-start(bf16[512,1024]{1,0:T(8,128)(2,1)} %weight_ref.3) | copy-start | bytes 3145732
  42.6 42.0 %copy-start.6 = (bf16[128,512]{1,0:T(8,128)(2,1)S(1)}, bf16[128,512]{1,0:T(8,128)(2,1)}, u32[]{:S(2)}) copy-start(bf16[128,512]{1,0:T(8,128)(2,1)} %mix_ref.3) | copy-start | bytes 393220
  42.8 14.7 %collective-permute-start.33 = (bf16[128,1024]{1,0:T(8,128)(2,1)S(1)}, bf16[128,1024]{1,0:T(8,128)(2,1)S(1)}, u32[]{:S(2)}, u32[]{:S(2)}) collective-permute-start(bf16[128,1024]{1,0:T(8,128)(2,1)S(1)} %get-tuple-element.89), channel_id=1, source_target_pairs={{0,4},{4,8},{8,12},{12,0},{1,5},{5,9},{9,13},{13,1},{2,6},{6,10},{... | collective-permute-start | bytes 786440 | tf_op jit(solution)/shard_map/ppermute | solution.py:33
  42.9 14.6 %collective-permute-start.34 = (bf16[128,1024]{1,0:T(8,128)(2,1)S(1)}, bf16[128,1024]{1,0:T(8,128)(2,1)S(1)}, u32[]{:S(2)}, u32[]{:S(2)}) collective-permute-start(bf16[128,1024]{1,0:T(8,128)(2,1)S(1)} %get-tuple-element.90), channel_id=1, source_target_pairs={{0,8},{4,12},{8,0},{12,4},{1,9},{5,13},{9,1},{13,5},{2,10},{6,14},... | collective-permute-start | bytes 786440 | tf_op jit(solution)/shard_map/ppermute | solution.py:33
  43.0 14.8 %collective-permute-start.35 = (bf16[128,1024]{1,0:T(8,128)(2,1)S(1)}, bf16[128,1024]{1,0:T(8,128)(2,1)S(1)}, u32[]{:S(2)}, u32[]{:S(2)}) collective-permute-start(bf16[128,1024]{1,0:T(8,128)(2,1)S(1)} %get-tuple-element.91), channel_id=1, source_target_pairs={{0,12},{4,0},{8,4},{12,8},{1,13},{5,1},{9,5},{13,9},{2,14},{6,2},{... | collective-permute-start | bytes 786440 | tf_op jit(solution)/shard_map/ppermute | solution.py:33
  57.9 4.8 %collective-permute-start.36 = (bf16[32,1024]{1,0:T(8,128)(2,1)S(1)}, bf16[32,1024]{1,0:T(8,128)(2,1)S(1)}, u32[]{:S(2)}, u32[]{:S(2)}) collective-permute-start(bf16[32,1024]{1,0:T(8,128)(2,1)S(1)} %get-tuple-element.93), channel_id=1, source_target_pairs={{0,32},{32,64},{64,96},{96,0},{1,33},{33,65},{65,97},{97,1},{2,34}... | collective-permute-start | bytes 196616 | tf_op jit(solution)/shard_map/ppermute | solution.py:33
  58.0 5.0 %collective-permute-start.37 = (bf16[32,1024]{1,0:T(8,128)(2,1)S(1)}, bf16[32,1024]{1,0:T(8,128)(2,1)S(1)}, u32[]{:S(2)}, u32[]{:S(2)}) collective-permute-start(bf16[32,1024]{1,0:T(8,128)(2,1)S(1)} %get-tuple-element.94), channel_id=1, source_target_pairs={{0,64},{32,96},{64,0},{96,32},{1,65},{33,97},{65,1},{97,33},{2,66}... | collective-permute-start | bytes 196616 | tf_op jit(solution)/shard_map/ppermute | solution.py:33
  58.7 5.2 %collective-permute-start.38 = (bf16[32,1024]{1,0:T(8,128)(2,1)S(1)}, bf16[32,1024]{1,0:T(8,128)(2,1)S(1)}, u32[]{:S(2)}, u32[]{:S(2)}) collective-permute-start(bf16[32,1024]{1,0:T(8,128)(2,1)S(1)} %get-tuple-element.95), channel_id=1, source_target_pairs={{0,96},{32,0},{64,32},{96,64},{1,97},{33,1},{65,33},{97,65},{2,98}... | collective-permute-start | bytes 196616 | tf_op jit(solution)/shard_map/ppermute | solution.py:33
  63.9 6.0 %collective-permute-start.39 = (bf16[16,1024]{1,0:T(8,128)(2,1)S(1)}, bf16[16,1024]{1,0:T(8,128)(2,1)S(1)}, u32[]{:S(2)}, u32[]{:S(2)}) collective-permute-start(bf16[16,1024]{1,0:T(8,128)(2,1)S(1)} %get-tuple-element.97), channel_id=1, source_target_pairs={{0,16},{16,0},{1,17},{17,1},{2,18},{18,2},{3,19},{19,3},{4,20},{20... | collective-permute-start | bytes 98312 | tf_op jit(solution)/shard_map/ppermute | solution.py:33
  65.6 12.0 %collective-permute-start.8 = (bf16[400,128]{1,0:T(8,128)(2,1)S(1)}, bf16[400,128]{1,0:T(8,128)(2,1)S(1)}, u32[]{:S(2)}, u32[]{:S(2)}) collective-permute-start(bf16[400,128]{1,0:T(8,128)(2,1)S(1)} %get-tuple-element.62), channel_id=1, source_target_pairs={{0,2},{2,0},{16,18},{18,16},{1,3},{3,1},{17,19},{19,17},{4,6},{6,4... | collective-permute-start | bytes 307208 | tf_op jit(solution)/shard_map/ppermute | solution.py:38
  68.2 9.5 %collective-permute-start.9 = (bf16[400,128]{1,0:T(8,128)(2,1)S(1)}, bf16[400,128]{1,0:T(8,128)(2,1)S(1)}, u32[]{:S(2)}, u32[]{:S(2)}) collective-permute-start(bf16[400,128]{1,0:T(8,128)(2,1)S(1)} %get-tuple-element.63), channel_id=1, source_target_pairs={{0,16},{2,18},{16,0},{18,2},{1,17},{3,19},{17,1},{19,3},{4,20},{6,... | collective-permute-start | bytes 307208 | tf_op jit(solution)/shard_map/ppermute | solution.py:38
  68.4 9.2 %collective-permute-start.10 = (bf16[400,128]{1,0:T(8,128)(2,1)S(1)}, bf16[400,128]{1,0:T(8,128)(2,1)S(1)}, u32[]{:S(2)}, u32[]{:S(2)}) collective-permute-start(bf16[400,128]{1,0:T(8,128)(2,1)S(1)} %get-tuple-element.64), channel_id=1, source_target_pairs={{0,18},{2,16},{16,2},{18,0},{1,19},{3,17},{17,3},{19,1},{4,22},{6,... | collective-permute-start | bytes 307208 | tf_op jit(solution)/shard_map/ppermute | solution.py:38
  69.9 5.3 %collective-permute-start.40 = (bf16[16,1024]{1,0:T(8,128)(2,1)S(1)}, bf16[16,1024]{1,0:T(8,128)(2,1)S(1)}, u32[]{:S(2)}, u32[]{:S(2)}) collective-permute-start(bf16[16,1024]{1,0:T(8,128)(2,1)S(1)} %add_convert_fusion.1.refs_0_), channel_id=1, source_target_pairs={{0,16},{16,0},{1,17},{17,1},{2,18},{18,2},{3,19},{19,3},{4,20},{20... | collective-permute-start | bytes 98312 | tf_op jit(solution)/shard_map/ppermute | solution.py:33
  75.2 5.9 %collective-permute-start.43 = (bf16[32,1024]{1,0:T(8,128)(2,1)S(1)}, bf16[32,1024]{1,0:T(8,128)(2,1)S(1)}, u32[]{:S(2)}, u32[]{:S(2)}) collective-permute-start(bf16[32,1024]{1,0:T(8,128)(2,1)S(1)} %gather_y.1.refs_0_), channel_id=1, source_target_pairs={{0,96},{32,0},{64,32},{96,64},{1,97},{33,1},{65,33},{97,65},{2,98}... | collective-permute-start | bytes 196616 | tf_op jit(solution)/shard_map/ppermute | solution.py:33
  76.5 4.6 %collective-permute-start.42 = (bf16[32,1024]{1,0:T(8,128)(2,1)S(1)}, bf16[32,1024]{1,0:T(8,128)(2,1)S(1)}, u32[]{:S(2)}, u32[]{:S(2)}) collective-permute-start(bf16[32,1024]{1,0:T(8,128)(2,1)S(1)} %gather_y.1.refs_0_), channel_id=1, source_target_pairs={{0,64},{32,96},{64,0},{96,32},{1,65},{33,97},{65,1},{97,33},{2,66}... | collective-permute-start | bytes 196616 | tf_op jit(solution)/shard_map/ppermute | solution.py:33
  77.6 4.3 %collective-permute-start.41 = (bf16[32,1024]{1,0:T(8,128)(2,1)S(1)}, bf16[32,1024]{1,0:T(8,128)(2,1)S(1)}, u32[]{:S(2)}, u32[]{:S(2)}) collective-permute-start(bf16[32,1024]{1,0:T(8,128)(2,1)S(1)} %gather_y.1.refs_0_), channel_id=1, source_target_pairs={{0,32},{32,64},{64,96},{96,0},{1,33},{33,65},{65,97},{97,1},{2,34}... | collective-permute-start | bytes 196616 | tf_op jit(solution)/shard_map/ppermute | solution.py:33
  77.7 14.9 %collective-permute-start.13 = (bf16[576,128]{1,0:T(8,128)(2,1)S(1)}, bf16[576,128]{1,0:T(8,128)(2,1)S(1)}, u32[]{:S(2)}, u32[]{:S(2)}) collective-permute-start(bf16[576,128]{1,0:T(8,128)(2,1)S(1)} %get-tuple-element.65.refs_0_), channel_id=1, source_target_pairs={{0,96},{32,0},{64,32},{96,64},{1,97},{33,1},{65,33},{97,65},{2,98}... | collective-permute-start | bytes 442376 | tf_op jit(solution)/shard_map/ppermute | solution.py:33
  80.4 12.7 %collective-permute-start.12 = (bf16[576,128]{1,0:T(8,128)(2,1)S(1)}, bf16[576,128]{1,0:T(8,128)(2,1)S(1)}, u32[]{:S(2)}, u32[]{:S(2)}) collective-permute-start(bf16[576,128]{1,0:T(8,128)(2,1)S(1)} %get-tuple-element.65.refs_0_), channel_id=1, source_target_pairs={{0,64},{32,96},{64,0},{96,32},{1,65},{33,97},{65,1},{97,33},{2,66}... | collective-permute-start | bytes 442376 | tf_op jit(solution)/shard_map/ppermute | solution.py:33
  82.0 18.0 %collective-permute-start.46 = (bf16[128,1024]{1,0:T(8,128)(2,1)S(1)}, bf16[128,1024]{1,0:T(8,128)(2,1)S(1)}, u32[]{:S(2)}, u32[]{:S(2)}) collective-permute-start(bf16[128,1024]{1,0:T(8,128)(2,1)S(1)} %gather_z.1.refs_0_), channel_id=1, source_target_pairs={{0,12},{4,0},{8,4},{12,8},{1,13},{5,1},{9,5},{13,9},{2,14},{6,2},{... | collective-permute-start | bytes 786440 | tf_op jit(solution)/shard_map/ppermute | solution.py:33
  85.2 3.7 %collective-permute-start.14 = (bf16[144,128]{1,0:T(8,128)(2,1)S(1)}, bf16[144,128]{1,0:T(8,128)(2,1)S(1)}, u32[]{:S(2)}, u32[]{:S(2)}) collective-permute-start(bf16[144,128]{1,0:T(8,128)(2,1)S(1)} %get-tuple-element.67), channel_id=1, source_target_pairs={{0,2},{2,0},{16,18},{18,16},{1,3},{3,1},{17,19},{19,17},{4,6},{6,4... | collective-permute-start | bytes 110600 | tf_op jit(solution)/shard_map/ppermute | solution.py:38
  87.7 2.9 %collective-permute-start.15 = (bf16[144,128]{1,0:T(8,128)(2,1)S(1)}, bf16[144,128]{1,0:T(8,128)(2,1)S(1)}, u32[]{:S(2)}, u32[]{:S(2)}) collective-permute-start(bf16[144,128]{1,0:T(8,128)(2,1)S(1)} %get-tuple-element.68), channel_id=1, source_target_pairs={{0,16},{2,18},{16,0},{18,2},{1,17},{3,19},{17,1},{19,3},{4,20},{6,... | collective-permute-start | bytes 110600 | tf_op jit(solution)/shard_map/ppermute | solution.py:38
  88.9 3.4 %collective-permute-start.16 = (bf16[144,128]{1,0:T(8,128)(2,1)S(1)}, bf16[144,128]{1,0:T(8,128)(2,1)S(1)}, u32[]{:S(2)}, u32[]{:S(2)}) collective-permute-start(bf16[144,128]{1,0:T(8,128)(2,1)S(1)} %get-tuple-element.69), channel_id=1, source_target_pairs={{0,18},{2,16},{16,2},{18,0},{1,19},{3,17},{17,3},{19,1},{4,22},{6,... | collective-permute-start | bytes 110600 | tf_op jit(solution)/shard_map/ppermute | solution.py:38
  90.7 5.2 %collective-permute-start.11 = (bf16[576,128]{1,0:T(8,128)(2,1)S(1)}, bf16[576,128]{1,0:T(8,128)(2,1)S(1)}, u32[]{:S(2)}, u32[]{:S(2)}) collective-permute-start(bf16[576,128]{1,0:T(8,128)(2,1)S(1)} %get-tuple-element.65.refs_0_), channel_id=1, source_target_pairs={{0,32},{32,64},{64,96},{96,0},{1,33},{33,65},{65,97},{97,1},{2,34}... | collective-permute-start | bytes 442376 | tf_op jit(solution)/shard_map/ppermute | solution.py:33
  92.3 9.2 %collective-permute-start.45 = (bf16[128,1024]{1,0:T(8,128)(2,1)S(1)}, bf16[128,1024]{1,0:T(8,128)(2,1)S(1)}, u32[]{:S(2)}, u32[]{:S(2)}) collective-permute-start(bf16[128,1024]{1,0:T(8,128)(2,1)S(1)} %gather_z.1.refs_0_), channel_id=1, source_target_pairs={{0,8},{4,12},{8,0},{12,4},{1,9},{5,13},{9,1},{13,5},{2,10},{6,14},... | collective-permute-start | bytes 786440 | tf_op jit(solution)/shard_map/ppermute | solution.py:33
  92.6 15.2 %collective-permute-start.44 = (bf16[128,1024]{1,0:T(8,128)(2,1)S(1)}, bf16[128,1024]{1,0:T(8,128)(2,1)S(1)}, u32[]{:S(2)}, u32[]{:S(2)}) collective-permute-start(bf16[128,1024]{1,0:T(8,128)(2,1)S(1)} %gather_z.1.refs_0_), channel_id=1, source_target_pairs={{0,4},{4,8},{8,12},{12,0},{1,5},{5,9},{9,13},{13,1},{2,6},{6,10},{... | collective-permute-start | bytes 786440 | tf_op jit(solution)/shard_map/ppermute | solution.py:33
  93.1 4.8 %collective-permute-start.19 = (bf16[576,128]{1,0:T(8,128)(2,1)S(1)}, bf16[576,128]{1,0:T(8,128)(2,1)S(1)}, u32[]{:S(2)}, u32[]{:S(2)}) collective-permute-start(bf16[576,128]{1,0:T(8,128)(2,1)S(1)} %join_grad.1.refs_4_), channel_id=1, source_target_pairs={{0,96},{32,0},{64,32},{96,64},{1,97},{33,1},{65,33},{97,65},{2,98}... | collective-permute-start | bytes 442376 | tf_op jit(solution)/shard_map/ppermute | solution.py:33
  95.9 17.4 %collective-permute-start.22 = (bf16[1024,128]{1,0:T(8,128)(2,1)S(1)}, bf16[1024,128]{1,0:T(8,128)(2,1)S(1)}, u32[]{:S(2)}, u32[]{:S(2)}) collective-permute-start(bf16[1024,128]{1,0:T(8,128)(2,1)S(1)} %get-tuple-element.70.refs_8_), channel_id=1, source_target_pairs={{0,12},{4,0},{8,4},{12,8},{1,13},{5,1},{9,5},{13,9},{2,14},{6,2},{... | collective-permute-start | bytes 786440 | tf_op jit(solution)/shard_map/ppermute | solution.py:33
  97.8 15.5 %collective-permute-start.21 = (bf16[1024,128]{1,0:T(8,128)(2,1)S(1)}, bf16[1024,128]{1,0:T(8,128)(2,1)S(1)}, u32[]{:S(2)}, u32[]{:S(2)}) collective-permute-start(bf16[1024,128]{1,0:T(8,128)(2,1)S(1)} %get-tuple-element.70.refs_8_), channel_id=1, source_target_pairs={{0,8},{4,12},{8,0},{12,4},{1,9},{5,13},{9,1},{13,5},{2,10},{6,14},... | collective-permute-start | bytes 786440 | tf_op jit(solution)/shard_map/ppermute | solution.py:33
  100.0 18.7 %collective-permute-start.20 = (bf16[1024,128]{1,0:T(8,128)(2,1)S(1)}, bf16[1024,128]{1,0:T(8,128)(2,1)S(1)}, u32[]{:S(2)}, u32[]{:S(2)}) collective-permute-start(bf16[1024,128]{1,0:T(8,128)(2,1)S(1)} %get-tuple-element.70.refs_8_), channel_id=1, source_target_pairs={{0,4},{4,8},{8,12},{12,0},{1,5},{5,9},{9,13},{13,1},{2,6},{6,10},{... | collective-permute-start | bytes 786440 | tf_op jit(solution)/shard_map/ppermute | solution.py:33
  101.5 6.4 %collective-permute-start.18 = (bf16[576,128]{1,0:T(8,128)(2,1)S(1)}, bf16[576,128]{1,0:T(8,128)(2,1)S(1)}, u32[]{:S(2)}, u32[]{:S(2)}) collective-permute-start(bf16[576,128]{1,0:T(8,128)(2,1)S(1)} %join_grad.1.refs_4_), channel_id=1, source_target_pairs={{0,64},{32,96},{64,0},{96,32},{1,65},{33,97},{65,1},{97,33},{2,66}... | collective-permute-start | bytes 442376 | tf_op jit(solution)/shard_map/ppermute | solution.py:33
  107.8 5.5 %collective-permute-start.17 = (bf16[576,128]{1,0:T(8,128)(2,1)S(1)}, bf16[576,128]{1,0:T(8,128)(2,1)S(1)}, u32[]{:S(2)}, u32[]{:S(2)}) collective-permute-start(bf16[576,128]{1,0:T(8,128)(2,1)S(1)} %join_grad.1.refs_4_), channel_id=1, source_target_pairs={{0,32},{32,64},{64,96},{96,0},{1,33},{33,65},{65,97},{97,1},{2,34}... | collective-permute-start | bytes 442376 | tf_op jit(solution)/shard_map/ppermute | solution.py:33
  107.9 59.7 %collective-permute-start.47 = (bf16[512,1024]{1,0:T(8,128)(2,1)S(1)}, bf16[512,1024]{1,0:T(8,128)(2,1)S(1)}, u32[]{:S(2)}, u32[]{:S(2)}) collective-permute-start(bf16[512,1024]{1,0:T(8,128)(2,1)S(1)} %gather_x.1.own_ref), channel_id=1, source_target_pairs={{0,2},{2,0},{1,3},{3,1},{4,6},{6,4},{5,7},{7,5},{8,10},{10,8},{9,1... | collective-permute-start | bytes 3145736 | tf_op jit(solution)/shard_map/ppermute | solution.py:38
  142.3 4.5 %collective-permute-start.23 = (bf16[512,128]{1,0:T(8,128)(2,1)S(1)}, bf16[512,128]{1,0:T(8,128)(2,1)S(1)}, u32[]{:S(2)}, u32[]{:S(2)}) collective-permute-start(bf16[512,128]{1,0:T(8,128)(2,1)S(1)} %get-tuple-element.72), channel_id=1, source_target_pairs={{0,96},{32,0},{64,32},{96,64},{1,97},{33,1},{65,33},{97,65},{2,98}... | collective-permute-start | bytes 393224 | tf_op jit(solution)/shard_map/ppermute | solution.py:33
  143.3 5.3 %collective-permute-start.24 = (bf16[512,128]{1,0:T(8,128)(2,1)S(1)}, bf16[512,128]{1,0:T(8,128)(2,1)S(1)}, u32[]{:S(2)}, u32[]{:S(2)}) collective-permute-start(bf16[512,128]{1,0:T(8,128)(2,1)S(1)} %get-tuple-element.73), channel_id=1, source_target_pairs={{0,64},{32,96},{64,0},{96,32},{1,65},{33,97},{65,1},{97,33},{2,66}... | collective-permute-start | bytes 393224 | tf_op jit(solution)/shard_map/ppermute | solution.py:33
  144.0 10.6 %collective-permute-start.26 = (bf16[1024,128]{1,0:T(8,128)(2,1)S(1)}, bf16[1024,128]{1,0:T(8,128)(2,1)S(1)}, u32[]{:S(2)}, u32[]{:S(2)}) collective-permute-start(bf16[1024,128]{1,0:T(8,128)(2,1)S(1)} %get-tuple-element.76), channel_id=1, source_target_pairs={{0,12},{4,0},{8,4},{12,8},{1,13},{5,1},{9,5},{13,9},{2,14},{6,2},{... | collective-permute-start | bytes 786440 | tf_op jit(solution)/shard_map/ppermute | solution.py:33
  144.0 10.6 %collective-permute-start.27 = (bf16[1024,128]{1,0:T(8,128)(2,1)S(1)}, bf16[1024,128]{1,0:T(8,128)(2,1)S(1)}, u32[]{:S(2)}, u32[]{:S(2)}) collective-permute-start(bf16[1024,128]{1,0:T(8,128)(2,1)S(1)} %get-tuple-element.77), channel_id=1, source_target_pairs={{0,8},{4,12},{8,0},{12,4},{1,9},{5,13},{9,1},{13,5},{2,10},{6,14},... | collective-permute-start | bytes 786440 | tf_op jit(solution)/shard_map/ppermute | solution.py:33
  146.8 11.4 %collective-permute-start.28 = (bf16[1024,128]{1,0:T(8,128)(2,1)S(1)}, bf16[1024,128]{1,0:T(8,128)(2,1)S(1)}, u32[]{:S(2)}, u32[]{:S(2)}) collective-permute-start(bf16[1024,128]{1,0:T(8,128)(2,1)S(1)} %get-tuple-element.78), channel_id=1, source_target_pairs={{0,4},{4,8},{8,12},{12,0},{1,5},{5,9},{9,13},{13,1},{2,6},{6,10},{... | collective-permute-start | bytes 786440 | tf_op jit(solution)/shard_map/ppermute | solution.py:33
  148.6 6.0 %collective-permute-start.25 = (bf16[512,128]{1,0:T(8,128)(2,1)S(1)}, bf16[512,128]{1,0:T(8,128)(2,1)S(1)}, u32[]{:S(2)}, u32[]{:S(2)}) collective-permute-start(bf16[512,128]{1,0:T(8,128)(2,1)S(1)} %get-tuple-element.74), channel_id=1, source_target_pairs={{0,32},{32,64},{64,96},{96,0},{1,33},{33,65},{65,97},{97,1},{2,34}... | collective-permute-start | bytes 393224 | tf_op jit(solution)/shard_map/ppermute | solution.py:33
  158.4 3.5 %collective-permute-start.29 = (bf16[384,128]{1,0:T(8,128)(2,1)S(1)}, bf16[384,128]{1,0:T(8,128)(2,1)S(1)}, u32[]{:S(2)}, u32[]{:S(2)}) collective-permute-start(bf16[384,128]{1,0:T(8,128)(2,1)S(1)} %get-tuple-element.80), channel_id=1, source_target_pairs={{0,2},{2,0},{16,18},{18,16},{1,3},{3,1},{17,19},{19,17},{4,6},{6,4... | collective-permute-start | bytes 294920 | tf_op jit(solution)/shard_map/ppermute | solution.py:38
  160.2 4.4 %collective-permute-start.30 = (bf16[384,128]{1,0:T(8,128)(2,1)S(1)}, bf16[384,128]{1,0:T(8,128)(2,1)S(1)}, u32[]{:S(2)}, u32[]{:S(2)}) collective-permute-start(bf16[384,128]{1,0:T(8,128)(2,1)S(1)} %get-tuple-element.81), channel_id=1, source_target_pairs={{0,16},{2,18},{16,0},{18,2},{1,17},{3,19},{17,1},{19,3},{4,20},{6,... | collective-permute-start | bytes 294920 | tf_op jit(solution)/shard_map/ppermute | solution.py:38
  160.8 6.0 %collective-permute-start.31 = (bf16[384,128]{1,0:T(8,128)(2,1)S(1)}, bf16[384,128]{1,0:T(8,128)(2,1)S(1)}, u32[]{:S(2)}, u32[]{:S(2)}) collective-permute-start(bf16[384,128]{1,0:T(8,128)(2,1)S(1)} %get-tuple-element.82), channel_id=1, source_target_pairs={{0,18},{2,16},{16,2},{18,0},{1,19},{3,17},{17,3},{19,1},{4,22},{6,... | collective-permute-start | bytes 294920 | tf_op jit(solution)/shard_map/ppermute | solution.py:38

commit v2 on v1

v2 whole, which is shorter than its diff:
```python
import functools
import math

import jax
import jax.numpy as jnp
from jax import lax
from jax.experimental import pallas as pl
from jax.experimental.pallas import tpu as pltpu
from jax.sharding import Mesh
from jax.sharding import PartitionSpec as P

BLOCK = 128
REACH = 3
LANES = 128
PAIRS = 4
STAT = 16
GROUP = 512
NODE = ("z", "y", "x", "c")
BF16 = jnp.bfloat16
F32 = jnp.float32
VMEM_LIMIT = 48 * 1024 * 1024

NT = (((1,), (1,)), ((), ()))
NN = (((1,), (0,)), ((), ()))
TN = (((0,), (0,)), ((), ()))


def dot(a, b, dims):
    return lax.dot_general(a, b, dims, preferred_element_type=F32)


def swap(value, axes, mask):
    count = lax.axis_size(axes)
    return lax.ppermute(value, axes, [(i, i ^ mask) for i in range(count)])


NEXT = ((1, 0, 3, 2), (3, 2, 1, 0))


def meet(value, axis, step):
    pairs = [
        (2 * i + core, 2 * NEXT[(step + core) % 2][i] + core) for i in range(4) for core in range(2)
    ]
    return lax.ppermute(value, (axis, "c"), pairs)


def side_at(axis, step):
    place, core = lax.axis_index(axis), lax.axis_index("c")
    first = jnp.where((place == 1) | (place == 2), 1, 0)
    second = jnp.where(place >= 2, 1, 0)
    return jnp.where(core == step, first, second)


def place_in_group():
    return lax.axis_index("y") * 2 + lax.axis_index("c")


class Order:
    def __init__(self):
        self.token = None

    def call(self, kernel, outs, *args, scratch=(), smem=0, anywhere=0, flops=0, name=None):
        count, first = len(args), self.token is None
        tokens = [] if first else [self.token]
        results = len(outs)

        def whole(*refs):
            token_out = refs[count + len(tokens) + results]
            token_out[...] = jnp.zeros_like(token_out) if first else refs[count][...]
            outputs = refs[count + len(tokens) : count + len(tokens) + results]
            kernel(*refs[:count], *outputs, *refs[count + len(tokens) + results + 1 :])

        specs = [pl.BlockSpec(memory_space=pltpu.SMEM)] * smem
        specs += [pl.BlockSpec(memory_space=pl.ANY)] * anywhere
        specs += [pl.BlockSpec(memory_space=pltpu.VMEM)] * (count - smem - anywhere + len(tokens))
        size = sum(math.prod(a.shape) * a.dtype.itemsize for a in (*args, *outs))
        *values, self.token = pl.pallas_call(
            whole,
            out_shape=[*outs, shaped((8, LANES), F32)],
            in_specs=specs,
            out_specs=[pl.BlockSpec(memory_space=pltpu.VMEM)] * (results + 1),
            scratch_shapes=list(scratch),
            cost_estimate=pl.CostEstimate(flops=flops, bytes_accessed=size, transcendentals=0),
            compiler_params=pltpu.CompilerParams(vmem_limit_bytes=VMEM_LIMIT),
            name=name,
        )(*args, *tokens)
        return values


def shaped(shape, dtype=BF16):
    return jax.ShapeDtypeStruct(shape, dtype)


def three_pieces(value):
    high = value.astype(BF16)
    rest = value - high.astype(F32)
    middle = rest.astype(BF16)
    low = (rest - middle.astype(F32)).astype(BF16)
    return jnp.concatenate(
        [high.astype(F32), middle.astype(F32), low.astype(F32), jnp.zeros((STAT - 6, LANES), F32)],
        axis=0,
    ).astype(BF16)


def pair_rows(table, pair):
    rows = table[0:2]
    for other in range(1, PAIRS):
        rows = jnp.where(pair == other, table[2 * other : 2 * other + 2], rows)
    return rows


PAY = 544
Q_ROWS = 2 * (GROUP + PAIRS * STAT)
KV_ROWS = 2 * GROUP


def load_kernel(count, source_ref, count_ref, *refs):
    sources, refs = refs[:count], refs[count:]
    loaded, refs = refs[:count], refs[count:]
    send, far, keep, local, total, sem = refs
    copies = [
        pltpu.make_async_copy(source, target, sem.at[i])
        for i, (source, target) in enumerate(zip(sources, loaded))
    ]
    for copy in copies:
        copy.start()
    total[...] = jnp.zeros_like(total)
    copies[0].wait()
    copies[1].wait()
    tiles, grad = loaded[0], loaded[1][...]
    parts = lax.axis_size(NODE)
    home = lax.axis_index(NODE)
    for e in range(tiles.shape[1]):

        @pl.when(e < count_ref[0])
        def _():
            distance = lax.rem(source_ref[0, e] - home + REACH + 2 * parts, parts)
            slot = jnp.clip(distance, 0, 2 * REACH)
            total[slot] += dot(tiles[0, e], grad, TN)

    core = lax.axis_index("c")

    def share(on_first, on_second):
        return total[jnp.where(core == 0, on_first + REACH, on_second + REACH)]

    for i, (on_first, on_second) in enumerate(((-2, 1), (-1, 2), (1, -1))):
        send[i * 128 : (i + 1) * 128] = share(on_first, on_second).astype(BF16)
    for i, (on_first, on_second) in enumerate(((2, -3), (3, -2))):
        keep[i * 128 : (i + 1) * 128] = share(on_first, on_second)
    far[...] = share(-3, 3).astype(BF16)
    local[...] = total[REACH]
    for copy in copies[2:]:
        copy.wait()


def near_kernel(keep, local, received, near, local_out):
    near[...] = (keep[...] + received[0:256].astype(F32)).astype(BF16)
    local_out[...] = local[...] + received[256:384].astype(F32)


def cross_kernel(local, near, far, send, local_out):
    core = lax.axis_index("c")
    mine = pl.ds(pl.multiple_of(core * 128, 128), 128)
    other = pl.ds(pl.multiple_of((1 - core) * 128, 128), 128)
    send[...] = near[other]
    local_out[...] = local[...] + near[mine].astype(F32) + far[...].astype(F32)


def mix_kernel(own_ref, other_ref, weight_ref, mix_ref, q_ref, k_ref, v_ref, log_ref, send, keep, through):
    side = lax.axis_index("h")
    half = own_ref.shape[1]
    own_columns = pl.ds(pl.multiple_of(side * half, half), half)
    other_columns = pl.ds(pl.multiple_of((1 - side) * half, half), half)
    grad = dot(own_ref[...], weight_ref[:, own_columns], NT)
    grad = (grad + dot(other_ref[...], weight_ref[:, other_columns], NT)).astype(BF16)
    product = grad.astype(F32) * mix_ref[...].astype(F32)
    turned_product = product.T
    rows = [jnp.sum(turned_product[64 * i : 64 * (i + 1)], axis=0, keepdims=True) for i in range(8)]
    spread = jnp.concatenate(rows, axis=0)
    logs = log_ref[...]
    me = place_in_group()
    for j, (pay, base) in enumerate(((keep, 0), (send, 0), (through, 0), (send, PAY))):
        pair = me ^ j
        columns = pl.ds(pl.multiple_of(pair * LANES, LANES), LANES)
        block = grad[:, 0:LANES]
        for other in range(1, PAIRS):
            block = jnp.where(pair == other, grad[:, other * LANES : (other + 1) * LANES], block)
        pay[base : base + 128] = q_ref[:, columns]
        pay[base + 128 : base + 144] = three_pieces(pair_rows(logs, pair))
        pay[base + 144 : base + 272] = block
        pay[base + 272 : base + 288] = three_pieces(pair_rows(spread, pair))
        pay[base + 288 : base + 416] = k_ref[:, columns]
        pay[base + 416 : base + 544] = v_ref[:, columns]


def forward_kernel(own, received, out):
    rows = own.shape[0]
    out[0:rows] = own[...]
    out[rows : 2 * rows] = received[rows : 2 * rows]


def join_kernel(own, near, far, q_out, kv_out):
    for j, (pay, base) in enumerate(((own, 0), (near, 0), (far, 0), (far, PAY))):
        for part in range(2):
            at, start = part * (Q_ROWS // 2), base + part * 144
            q_out[at + j * 128 : at + (j + 1) * 128] = pay[start : start + 128]
            stats = at + GROUP + j * STAT
            q_out[stats : stats + STAT] = pay[start + 128 : start + 144]
            start = base + 288 + part * 128
            kv_out[part * GROUP + j * 128 : part * GROUP + (j + 1) * 128] = pay[start : start + 128]


def pair_kernel(first, second, out):
    out[0] = first[...]
    out[1] = second[...]


def masked(block, head):
    lane = lax.broadcasted_iota(jnp.int32, block.shape, 1)
    keep = lane < 64 if head == 0 else lane >= 64
    return jnp.where(keep, block, 0.0).astype(BF16)


def unpack_rows(source, factor, table, stat):
    block = source[0:GROUP].astype(F32) * factor
    for h in range(2):
        table[h] = masked(block, h)
    for j in range(PAIRS):
        pieces = source[GROUP + STAT * j : GROUP + STAT * (j + 1)].astype(F32)
        stat[:, j * LANES : (j + 1) * LANES] = pieces[0:2] + pieces[2:4] + pieces[4:6]


def tile_step(key_tile, value_tile, keys_t, query, grad, logs, spread, dk, dv, dq):
    for h in range(2):
        query_tile, grad_tile = query[h], grad[h]
        scores = dot(key_tile, query_tile, NT) - logs[h : h + 1]
        soft = jnp.exp(scores)
        change = dot(value_tile, grad_tile, NT) - spread[h : h + 1]
        score_grad = (soft * change).astype(BF16)
        dv[...] += dot(soft.astype(BF16), grad_tile, NN)
        dk[...] += dot(score_grad, query_tile, NN)
        head = slice(64 * h, 64 * (h + 1))
        dq[head] += dot(keys_t[head], score_grad, NN)


def turned(block):
    return block.astype(F32).T.astype(BF16)


def attention_kernel(has_dq, has_dkv, dq_last, dkv_last, qdo, kv, *refs):
    if has_dq:
        dq_in, refs = refs[0], refs[1:]
    if has_dkv:
        dkv_in, refs = refs[0], refs[1:]
    dq_out, dkv_out, keys_t, query, grad, logs, spread, dq, dkv = refs
    for i in range(2):
        unpack_rows(qdo.at[i, 0 : Q_ROWS // 2], 0.125, query.at[i], logs.at[i])
        unpack_rows(qdo.at[i, Q_ROWS // 2 : Q_ROWS], 1.0, grad.at[i], spread.at[i])
        keys_t[i] = turned(kv[i, 0:GROUP])
    dq[...] = dq_in[...] if has_dq else jnp.zeros_like(dq)
    dkv[...] = dkv_in[...] if has_dkv else jnp.zeros_like(dkv)

    @pl.loop(0, 4)
    def _(step):
        i, k = step % 2, step // 2
        tile_step(
            kv[k, 0:GROUP],
            kv[k, GROUP : 2 * GROUP],
            keys_t.at[k],
            query.at[i],
            grad.at[i],
            logs.at[i],
            spread.at[i],
            dkv.at[k, pl.ds(0, GROUP)],
            dkv.at[k, pl.ds(GROUP, GROUP)],
            dq.at[i],
        )

    if dq_last:
        for i in range(2):
            dq_out[i] = (dq[i].T * 0.125).astype(dq_out.dtype)
    else:
        dq_out[...] = dq[...]
    dkv_out[...] = dkv[...].astype(dkv_out.dtype)


TILE_FLOPS = 2 * 10 * GROUP * GROUP * 64


def attention(order, name, qdo, kv, dq, dkv, dq_last=None, dkv_last=None):
    carry = [a for a in (dq, dkv) if a is not None]
    dq_shape = (2, LANES, GROUP) if dq_last is None else (2, GROUP, LANES)
    return order.call(
        functools.partial(
            attention_kernel, dq is not None, dkv is not None, dq_last is not None, dkv_last is not None
        ),
        [shaped(dq_shape, dq_last or F32), shaped((2, KV_ROWS, LANES), dkv_last or F32)],
        qdo,
        kv,
        *carry,
        scratch=[
            pltpu.VMEM((2, LANES, GROUP), BF16),
            pltpu.VMEM((2, 2, GROUP, LANES), BF16),
            pltpu.VMEM((2, 2, GROUP, LANES), BF16),
            pltpu.VMEM((2, 2, GROUP), F32),
            pltpu.VMEM((2, 2, GROUP), F32),
            pltpu.VMEM((2, LANES, GROUP), F32),
            pltpu.VMEM((2, KV_ROWS, LANES), F32),
        ],
        flops=4 * TILE_FLOPS,
        name="attention_" + name,
    )


def half_sum_kernel(totals, received, out):
    out[...] = (totals[1].astype(F32) + received[1].astype(F32)).astype(BF16)


def back_kernel(dq, dq_far, dq_near, dkv, dkv_far, dkv_near, send, keep, through):
    dq_sum = (dq[0] + dq_far[0].astype(F32) + dq_near[...].astype(F32)).astype(BF16)
    dkv_sum = (dkv[0] + dkv_far[0].astype(F32) + dkv_near[...].astype(F32)).astype(BF16)
    for j, (pay, base) in enumerate(((keep, 0), (send, 0), (through, 0), (send, 384))):
        pay[base : base + 128] = dq_sum[j * 128 : (j + 1) * 128]
        pay[base + 128 : base + 256] = dkv_sum[j * 128 : (j + 1) * 128]
        pay[base + 256 : base + 384] = dkv_sum[GROUP + j * 128 : GROUP + (j + 1) * 128]


def place_kernel(own, near, far, dq, dk, dv):
    me = place_in_group()
    for j, (pay, base) in enumerate(((own, 0), (near, 0), (far, 0), (far, 384))):
        columns = pl.ds(pl.multiple_of((me ^ j) * LANES, LANES), LANES)
        dq[:, columns] = pay[base : base + 128]
        dk[:, columns] = pay[base + 128 : base + 256]
        dv[:, columns] = pay[base + 256 : base + 384]


def turn_kernel(dq, out):
    for i in range(2):
        out[i] = dq[i].T * 0.125


def weights_kernel(own_ref, other_ref, g_own_ref, g_other_ref, mix_ref, feat_ref, weight_ref, gf_ref, keep_ref, send_ref):
    side = lax.axis_index("h")
    core = lax.axis_index("c")
    half = own_ref.shape[1]
    own_columns = pl.ds(pl.multiple_of(side * half, half), half)
    other_columns = pl.ds(pl.multiple_of((1 - side) * half, half), half)
    features = dot(g_own_ref[...], weight_ref[:, own_columns], NT)
    features = features + dot(g_other_ref[...], weight_ref[:, other_columns], NT)
    gf_ref[...] = features.astype(BF16)
    mix = mix_ref[...].astype(F32).T.astype(BF16)
    feat = feat_ref[...].astype(F32).T.astype(BF16)

    def put(out_refs):
        for left, rights, out in zip((mix, feat), ((own_ref, other_ref), (g_own_ref, g_other_ref)), out_refs):
            out[:, own_columns] = dot(left, rights[0][...], NN).astype(BF16)
            out[:, other_columns] = dot(left, rights[1][...], NN).astype(BF16)

    @pl.when(core == 0)
    def _():
        put((keep_ref, send_ref))

    @pl.when(core == 1)
    def _():
        put((send_ref, keep_ref))


def final_kernel(own_ref, other_ref, first_ref, second_ref):
    core = lax.axis_index("c")

    @pl.when(core == 0)
    def _():
        first_ref[...] = own_ref[...].astype(F32)
        second_ref[...] = other_ref[...].astype(F32)

    @pl.when(core == 1)
    def _():
        first_ref[...] = other_ref[...].astype(F32)
        second_ref[...] = own_ref[...].astype(F32)


def add_kernel(*refs):
    total = refs[0][...].astype(F32)
    for ref in refs[1:-1]:
        total = total + ref[...].astype(F32)
    refs[-1][...] = total.astype(BF16)


def halve_kernel(step, first, second, keep, send):
    rows = keep.shape[0]
    side = side_at("z", step)
    for out, which in ((keep, side), (send, 1 - side)):
        at = pl.ds(pl.multiple_of(which * rows, rows), rows)
        out[...] = (first[at].astype(F32) + second[at].astype(F32)).astype(BF16)


def double_kernel(step, own, received, out):
    rows = own.shape[0]
    side = side_at("z", step)
    out[pl.ds(pl.multiple_of(side * rows, rows), rows)] = own[...]
    out[pl.ds(pl.multiple_of((1 - side) * rows, rows), rows)] = received[...]


def halve(order, step, first, second):
    rows, columns = first.shape
    return order.call(
        functools.partial(halve_kernel, step),
        [shaped((rows // 2, columns))] * 2,
        first,
        second,
        name="halve_%d" % step,
    )


def double(order, step, own, received):
    rows, columns = own.shape
    (out,) = order.call(
        functools.partial(double_kernel, step),
        [shaped((2 * rows, columns))],
        own,
        received,
        name="double_%d" % step,
    )
    return out


def add(order, name, *terms):
    (out,) = order.call(add_kernel, [shaped(terms[0].shape)], *terms, name="add_" + name)
    return out


def pair(order, first, second):
    (out,) = order.call(pair_kernel, [shaped((2,) + first.shape)], first, second, name="pair")
    return out


def body(
    features,
    queries,
    keys,
    values,
    attn_mix,
    log_sums,
    out_weight,
    msg_weight,
    edge_tiles,
    edge_source,
    edge_count,
    out_grad,
):
    rows, columns = out_grad.shape
    order = Order()
    other_grad = swap(out_grad, "h", 1)
    arguments = [edge_tiles, out_grad, queries, keys, values, log_sums, out_weight, attn_mix, features, msg_weight]
    *loaded, share_send, share_far, share_keep, local = order.call(
        functools.partial(load_kernel, len(arguments)),
        [shaped(a.shape, a.dtype) for a in arguments]
        + [
            shaped((3 * rows, columns)),
            shaped((rows, columns)),
            shaped((2 * rows, columns), F32),
            shaped((rows, columns), F32),
        ],
        edge_source,
        edge_count,
        *arguments,
        smem=2,
        anywhere=len(arguments),
        scratch=[
            pltpu.VMEM((2 * REACH + 1, rows, columns), F32),
            pltpu.SemaphoreType.DMA((len(arguments),)),
        ],
        name="load",
    )
    _, out_grad, queries, keys, values, log_sums, out_weight, attn_mix, features, msg_weight = loaded
    share_received = swap(share_send, "c", 1)

    pay_send, pay_own, pay_through = order.call(
        mix_kernel,
        [shaped((2 * PAY, LANES)), shaped((PAY, LANES)), shaped((PAY, LANES))],
        out_grad,
        other_grad,
        out_weight,
        attn_mix,
        queries,
        keys,
        values,
        log_sums,
        name="mix",
    )
    pay_near = swap(pay_send, "c", 1)

    share_near, local = order.call(
        near_kernel,
        [shaped((2 * rows, columns)), shaped((rows, columns), F32)],
        share_keep,
        local,
        share_received,
        name="near",
    )
    parts = lax.axis_size(NODE)
    share_near = lax.ppermute(
        share_near, NODE, [(i, (i + (2 if i % 2 == 0 else -2)) % parts) for i in range(parts)]
    )
    share_far = lax.ppermute(
        share_far, NODE, [(i, (i + (-3 if i % 2 == 0 else 3)) % parts) for i in range(parts)]
    )
    (pay_forward,) = order.call(
        forward_kernel, [shaped((2 * PAY, LANES))], pay_through, pay_near, name="forward"
    )
    pay_far = swap(pay_forward, "y", 1)

    share_cross, local = order.call(
        cross_kernel,
        [shaped((rows, columns)), shaped((rows, columns), F32)],
        local,
        share_near,
        share_far,
        name="cross",
    )
    share_cross = swap(share_cross, "c", 1)

    qdo, kv = order.call(
        join_kernel,
        [shaped((Q_ROWS, LANES)), shaped((KV_ROWS, LANES))],
        pay_own,
        pay_near,
        pay_far,
        name="join",
    )
    qdo_met, kv_met = meet(qdo, "z", 0), meet(kv, "x", 0)

    near_g = add(order, "shares", local, share_cross)
    other_g = swap(near_g, "h", 1)

    qdo_near, kv_near = pair(order, qdo, qdo_met), pair(order, kv, kv_met)
    qdo_far, kv_far = meet(qdo_near, "z", 1), meet(kv_near, "x", 1)

    grad_features, keep, send = order.call(
        weights_kernel,
        [shaped((rows, columns)), shaped((columns, 2 * columns)), shaped((columns, 2 * columns))],
        out_grad,
        other_grad,
        near_g,
        other_g,
        attn_mix,
        features,
        msg_weight,
        name="weights",
    )
    received = swap(send, "c", 1)

    dq_near, dkv_near = attention(order, "near", qdo_near, kv_near, None, None)

    keep, send = halve(order, 0, keep, received)
    received = meet(send, "z", 0)

    dq_far, dkv_far = attention(order, "far", qdo_far, kv_far, None, None)

    keep, send = halve(order, 1, keep, received)
    received = meet(send, "z", 1)

    dq_near, dkv_far = attention(order, "far_keys", qdo_near, kv_far, dq_near, dkv_far, None, BF16)
    dkv_met = meet(dkv_far, "x", 1)

    part = add(order, "z", keep, received)
    received = meet(part, "x", 0)

    dq_far, dkv_near = attention(order, "far_queries", qdo_far, kv_near, dq_far, dkv_near, BF16, F32)
    dq_met = meet(dq_far, "z", 1)
    (dq_near,) = order.call(
        turn_kernel, [shaped((2, GROUP, LANES), F32)], dq_near, name="turn"
    )

    part = add(order, "x0", part, received)
    received = meet(part, "x", 1)
    (half,) = order.call(
        half_sum_kernel, [shaped((KV_ROWS, LANES))], dkv_near, dkv_met, name="half_dkv"
    )
    dkv_last = meet(half, "x", 0)
    part = add(order, "x1", part, received)
    received = swap(part, "y", 1)
    (half,) = order.call(half_sum_kernel, [shaped((GROUP, LANES))], dq_near, dq_met, name="half_dq")
    dq_last = meet(half, "z", 0)
    part = add(order, "y", part, received)
    received = meet(part, "z", 1)

    back_send, back_own, back_through = order.call(
        back_kernel,
        [shaped((768, LANES)), shaped((384, LANES)), shaped((384, LANES))],
        dq_near,
        dq_met,
        dq_last,
        dkv_near,
        dkv_met,
        dkv_last,
        name="back",
    )
    back_near = swap(back_send, "c", 1)
    whole = double(order, 1, part, received)
    received = meet(whole, "z", 0)
    (back_forward,) = order.call(
        forward_kernel, [shaped((768, LANES))], back_through, back_near, name="forward_back"
    )
    back_far = swap(back_forward, "y", 1)
    grad_query, grad_key, grad_value = order.call(
        place_kernel, [shaped((rows, columns))] * 3, back_own, back_near, back_far, name="place"
    )
    whole = double(order, 0, whole, received)
    other = swap(whole, "c", 1)
    out_weight_grad, msg_weight_grad = order.call(
        final_kernel, [shaped(whole.shape, F32)] * 2, whole, other, name="final"
    )
    return (grad_features, grad_query, grad_key, grad_value, out_weight_grad, msg_weight_grad)


def solution(mesh):
    fine = Mesh(mesh.devices.reshape(4, 2, 4, 2, 2), NODE + ("h",))
    both = P(NODE, "h")
    placed = (
        both,
        both,
        both,
        both,
        both,
        P("h", NODE),
        P("h", None),
        P("h", None),
        P(NODE, None, None, None),
        P(NODE, None),
        P(NODE),
        both,
    )
    return jax.shard_map(
        body,
        mesh=fine,
        in_specs=placed,
        out_specs=(both, both, both, both, P("h", None), P("h", None)),
        check_vma=False,
    )
```

time: 170 us -> 124 us (0.73)
  waiting for transfers between devices: 74.7 us -> 31.8 us
  starting transfers between devices: 57 us -> 47.3 us
  Pallas kernels: 31.3 us -> 35.5 us
  local copies, waits for them, and re-layouts: 5.25 us -> 7.71 us
    ppermute x35 -> x16, waiting for transfers between devices: 62 us -> 17 us  [the longest x14 10.9 us: meet(): return lax.ppermute(value, (axis, 'c'), pairs)]
    ppermute x35 -> x16, starting transfers between devices: 36.8 us -> 26.6 us  [the longest x14 19.9 us: meet(): return lax.ppermute(value, (axis, 'c'), pairs)]
    pallas_call x16 -> x29, Pallas kernels: 31.3 us -> 35.5 us  [call(): pl.pallas_call(whole, out_shape=[*outs, shaped((8, LANES), F32)], in_spec...]
    unnamed x28 -> x18, local copies, waits for them, and re-layouts: 5.25 us -> 7.71 us
    ppermute x13 -> x11, waiting for transfers between devices: 12.6 us -> 14.7 us  [swap(): return lax.ppermute(value, axes, [(i, i ^ mask) for i in range(count)])]
    ppermute x13 -> x11, starting transfers between devices: 20.2 us -> 20.7 us  [swap(): return lax.ppermute(value, axes, [(i, i ^ mask) for i in range(count)])]
  transfers between devices with their start and end apart: 48 -> 27, of which waited for: 27 -> 14; matrix products, arithmetic and copies ran while one was open for 0% -> 0% of each run, Pallas kernels for 15% -> 25%
where the time goes in v2:
time: 124 us
  starting transfers between devices  47.3 us (38%)
  Pallas kernels  35.5 us (29%)
  waiting for transfers between devices  31.8 us (26%)
  local copies, waits for them, and re-layouts  7.71 us (6%)
  between operations  1.51 us (1%)
    pallas_call x29, Pallas kernels, call(): pl.pallas_call(whole, out_shape=[*outs, shaped((8, LANES), F32)], in_spec...  35.5 us
    ppermute x11, starting transfers between devices, swap(): return lax.ppermute(value, axes, [(i, i ^ mask) for i in range(count)])  20.7 us
    ppermute x14, starting transfers between devices, meet(): return lax.ppermute(value, (axis, 'c'), pairs)  19.9 us
    ppermute x11, waiting for transfers between devices, swap(): return lax.ppermute(value, axes, [(i, i ^ mask) for i in range(count)])  14.7 us
    ppermute x14, waiting for transfers between devices, meet(): return lax.ppermute(value, (axis, 'c'), pairs)  10.9 us
    unnamed x18, local copies, waits for them, and re-layouts  7.71 us
    ppermute x1, starting transfers between devices, body(): lax.ppermute(share_near, NODE, [(i, (i + (2 if i % 2 == 0 else -2)) % par...  6.74 us
    ppermute x1, waiting for transfers between devices, body(): lax.ppermute(share_far, NODE, [(i, (i + (-3 if i % 2 == 0 else 3)) % part...  6.11 us
  transfers between devices with their start and end apart: 27, of which 14 were waited for; matrix products, arithmetic and copies ran while one was open for 0% of the time, Pallas kernels for 25%

profile of v2, /device:TPU:1, one launch (start us, length us, event | category | flops | bytes accessed | tf_op | source)
XLA Modules:
  0.0 123.8 jit_solution(8210297252486537825)
XLA Ops:
  0.6 3.8 %collective-permute-start = (bf16[128,512]{1,0:T(8,128)(2,1)}, bf16[128,512]{1,0:T(8,128)(2,1)S(1)}, u32[]{:S(2)}, u32[]{:S(2)}) collective-permute-start(bf16[128,512]{1,0:T(8,128)(2,1)} %refs_3_.1), channel_id=1, source_target_pairs={{0,1},{1,0},{2,3},{3,2},{4,5},{5,4},{6,7},{7,6},{8,9},{9,8},{10,11... | collective-permute-start | bytes 393224 | tf_op jit(solution)/shard_map/ppermute | solution.py:34
  5.1 0.9 copy-done
  6.1 0.9 copy-done.1
  7.0 0.9 copy-done.2
  7.9 0.9 copy-done.3
  8.8 0.9 copy-done.4
  9.7 0.9 copy-done.5
  10.6 0.9 copy-done.6
  11.5 0.7 copy-done.7
  12.2 0.7 copy-done.8
  12.8 3.9 %load.1 = (bf16[1,8,128,128]{3,2,1,0:T(8,128)(2,1)}, bf16[128,512]{1,0:T(8,128)(2,1)S(1)}, bf16[128,512]{1,0:T(8,128)(2,1)S(1)}, bf16[128,512]{1,0:T(8,128)(2,1)...) custom-call(s32[1,8]{1,0:T(1,128)S(1)} %copy-done.8, ...), custom_call_target="tpu_custom_call" | custom-call | bytes 7610404 | tf_op jit(solution)/shard_map/load/pallas_call | solution.py:77
  16.7 1.0 collective-permute-start.1
  17.8 0.6 mix.1
  18.4 0.1 collective-permute-start.4
  18.5 0.6 collective-permute-done.1.refs_2_
  19.2 0.8 collective-permute-done.4.refs_1_
  20.0 0.5 collective-permute-start.6
  20.5 6.7 %collective-permute-start.2 = (bf16[256,512]{1,0:T(8,128)(2,1)S(1)}, bf16[256,512]{1,0:T(8,128)(2,1)S(1)}, u32[]{:S(2)}, u32[]{:S(2)}) collective-permute-start(bf16[256,512]{1,0:T(8,128)(2,1)S(1)} %get-tuple-element.106), channel_id=1, source_target_pairs={{0,4},{2,126},{4,8},{6,2},{8,12},{10,6},{12,16},{14,10},{16,20},{1... | collective-permute-start | bytes 786440 | tf_op jit(solution)/shard_map/ppermute | solution.py:502
  27.3 6.1 %collective-permute-done.3.refs_2_ = bf16[128,512]{1,0:T(8,128)(2,1)S(1)} collective-permute-done((bf16[128,512]{1,0:T(8,128)(2,1)S(1)}, bf16[128,512]{1,0:T(8,128)(2,1)S(1)}, u32[]{:S(2)}, u32[]{:S(2)}) %collective-permute-start.3) | collective-permute-done | bytes 131104 | tf_op jit(solution)/shard_map/ppermute | solution.py:505
  33.5 3.0 %collective-permute-start.9 = (bf16[1152,128]{1,0:T(8,128)(2,1)S(1)}, bf16[1152,128]{1,0:T(8,128)(2,1)S(1)}, u32[]{:S(2)}, u32[]{:S(2)}) collective-permute-start(bf16[1152,128]{1,0:T(8,128)(2,1)S(1)} %get-tuple-element.122.refs_0_), channel_id=1, source_target_pairs={{0,32},{2,98},{32,0},{34,66},{64,96},{66,34},{96,64},{98,2},{1,33}... | collective-permute-start | bytes 884744 | tf_op jit(solution)/shard_map/ppermute | solution.py:44
  36.5 2.3 %collective-permute-start.8 = (bf16[1024,128]{1,0:T(8,128)(2,1)S(1)}, bf16[1024,128]{1,0:T(8,128)(2,1)S(1)}, u32[]{:S(2)}, u32[]{:S(2)}) collective-permute-start(bf16[1024,128]{1,0:T(8,128)(2,1)S(1)} %get-tuple-element.121.refs_0_), channel_id=1, source_target_pairs={{0,4},{2,14},{4,0},{6,10},{8,12},{10,6},{12,8},{14,2},{1,5},{3,15}... | collective-permute-start | bytes 786440 | tf_op jit(solution)/shard_map/ppermute | solution.py:44
  38.9 1.4 %collective-permute-start.7 = (bf16[128,512]{1,0:T(8,128)(2,1)S(1)}, bf16[128,512]{1,0:T(8,128)(2,1)S(1)}, u32[]{:S(2)}, u32[]{:S(2)}) collective-permute-start(bf16[128,512]{1,0:T(8,128)(2,1)S(1)} %get-tuple-element.118.refs_2_), channel_id=1, source_target_pairs={{0,1},{1,0},{2,3},{3,2},{4,5},{5,4},{6,7},{7,6},{8,9},{9,8},{10,11... | collective-permute-start | bytes 393224 | tf_op jit(solution)/shard_map/ppermute | solution.py:34
  40.3 0.3 collective-permute-done.9.refs_1_
  40.7 2.6 %collective-permute-done.8.refs_1_ = bf16[1024,128]{1,0:T(8,128)(2,1)S(1)} collective-permute-done((bf16[1024,128]{1,0:T(8,128)(2,1)S(1)}, bf16[1024,128]{1,0:T(8,128)(2,1)S(1)}, u32[]{:S(2)}, u32[]{:S(2)}) %collective-permute-start.8) | collective-permute-done | bytes 262176 | tf_op jit(solution)/shard_map/ppermute | solution.py:44
  43.3 2.1 %collective-permute-done.7.refs_3_ = bf16[128,512]{1,0:T(8,128)(2,1)S(1)} collective-permute-done((bf16[128,512]{1,0:T(8,128)(2,1)S(1)}, bf16[128,512]{1,0:T(8,128)(2,1)S(1)}, u32[]{:S(2)}, u32[]{:S(2)}) %collective-permute-start.7) | collective-permute-done | bytes 131104 | tf_op jit(solution)/shard_map/ppermute | solution.py:34
  45.4 1.8 %weights.1 = (bf16[128,512]{1,0:T(8,128)(2,1)}, bf16[512,1024]{1,0:T(8,128)(2,1)S(1)}, bf16[512,1024]{1,0:T(8,128)(2,1)S(1)}, f32[8,128]{1,0:T(8,128)S(1)}) custom-call(bf16[128,512]{1,0:T(8,128)(2,1)S(1)} %get-tuple-element.93.refs_0_, bf16[128,512]{1,0:T(8,128)(2,1)S(1)} %collective-permute-done.refs_1_, bf16[128,512]{1,0:T(8,128)(2,1)S(1)} %get-tuple-element.118.refs_2_, ...), custom_call_target="tpu_custom_call" | custom-call | bytes 4063232 | tf_op jit(solution)/shard_map/weights/pallas_call | solution.py:77
  47.2 0.4 collective-permute-start.12
  47.6 0.1 collective-permute-start.11
  47.7 1.0 collective-permute-start.10
  48.6 6.1 %attention_near.1 = (f32[2,128,512]{2,1,0:T(8,128)S(1)}, f32[2,1024,128]{2,1,0:T(8,128)S(1)}, f32[8,128]{1,0:T(8,128)S(1)}) custom-call(bf16[2,1152,128]{2,1,0:T(8,128)(2,1)S(1)} %get-tuple-element.127.refs_0_, bf16[2,1024,128]{2,1,0:T(8,128)(2,1)S(1)} %get-tuple-element.128.refs_1_, f32[8,128]{1,0:T(8,128)S(1)} %get-tuple-element.129.refs_2_), custom_call_target="tpu_custom_call" | custom-call | flops 1342177280 | bytes 2686976 | tf_op jit(solution)/shard_map/attention_near/pallas_call | solution.py:77
  54.8 0.3 halve_0.1
  55.1 1.0 collective-permute-start.13
  56.1 0.5 collective-permute-done.11.refs_0_
  56.6 6.2 %attention_far.1 = (f32[2,128,512]{2,1,0:T(8,128)S(1)}, f32[2,1024,128]{2,1,0:T(8,128)S(1)}, f32[8,128]{1,0:T(8,128)S(1)}) custom-call(bf16[2,1152,128]{2,1,0:T(8,128)(2,1)S(1)} %collective-permute-done.11.refs_0_, bf16[2,1024,128]{2,1,0:T(8,128)(2,1)S(1)} %collective-permute-done.10.refs_1_, f32[8,128]{1,0:T(8,128)S(1)} %get-tuple-element.134.refs_2_), custom_call_target="tpu_custom_call" | custom-call | flops 1342177280 | bytes 2686976 | tf_op jit(solution)/shard_map/attention_far/pallas_call | solution.py:77
  62.8 1.6 %collective-permute-done.13.refs_1_ = bf16[256,1024]{1,0:T(8,128)(2,1)S(1)} collective-permute-done((bf16[256,1024]{1,0:T(8,128)(2,1)S(1)}, bf16[256,1024]{1,0:T(8,128)(2,1)S(1)}, u32[]{:S(2)}, u32[]{:S(2)}) %collective-permute-start.13) | collective-permute-done | bytes 524320 | tf_op jit(solution)/shard_map/ppermute | solution.py:44
  64.4 0.1 halve_1.1
  64.5 0.3 collective-permute-start.14
  64.8 6.1 %attention_far_keys.1 = (f32[2,128,512]{2,1,0:T(8,128)S(1)}, bf16[2,1024,128]{2,1,0:T(8,128)(2,1)S(1)}, f32[8,128]{1,0:T(8,128)S(1)}) custom-call(bf16[2,1152,128]{2,1,0:T(8,128)(2,1)S(1)} %get-tuple-element.127.refs_0_, bf16[2,1024,128]{2,1,0:T(8,128)(2,1)S(1)} %collective-permute-done.10.refs_1_, f32[2,128,512]{2,1,0:T(8,128)S(1)} %get-tuple-element.130.refs_2_, ...), custom_call_target="tpu_custom_call" | custom-call | flops 1342177280 | bytes 3735552 | tf_op jit(solution)/shard_map/attention_far_keys/pallas_call | solution.py:77
  70.9 1.0 collective-permute-start.18
  71.9 0.1 add_z.1
  72.0 1.7 %collective-permute-start.16 = (bf16[128,1024]{1,0:T(8,128)(2,1)S(1)}, bf16[128,1024]{1,0:T(8,128)(2,1)S(1)}, u32[]{:S(2)}, u32[]{:S(2)}) collective-permute-start(bf16[128,1024]{1,0:T(8,128)(2,1)S(1)} %get-tuple-element.150.refs_0_), channel_id=1, source_target_pairs={{0,4},{2,14},{4,0},{6,10},{8,12},{10,6},{12,8},{14,2},{1,5},{3,15}... | collective-permute-start | bytes 786440 | tf_op jit(solution)/shard_map/ppermute | solution.py:44
  73.7 6.2 %attention_far_queries.1 = (bf16[2,512,128]{2,1,0:T(8,128)(2,1)S(1)}, f32[2,1024,128]{2,1,0:T(8,128)S(1)}, f32[8,128]{1,0:T(8,128)S(1)}) custom-call(bf16[2,1152,128]{2,1,0:T(8,128)(2,1)S(1)} %collective-permute-done.11.refs_0_, bf16[2,1024,128]{2,1,0:T(8,128)(2,1)S(1)} %get-tuple-element.128.refs_1_, f32[2,128,512]{2,1,0:T(8,128)S(1)} %get-tuple-element.141.refs_2_, ...), custom_call_target="tpu_custom_call" | custom-call | flops 1342177280 | bytes 3997696 | tf_op jit(solution)/shard_map/attention_far_queries/pallas_call | solution.py:77
  80.0 0.2 turn.1
  80.2 0.1 add_x0.1
  80.3 0.1 collective-permute-start.17
  80.3 2.0 %collective-permute-start.15 = (bf16[2,512,128]{2,1,0:T(8,128)(2,1)S(1)}, bf16[2,512,128]{2,1,0:T(8,128)(2,1)S(1)}, u32[]{:S(2)}, u32[]{:S(2)}) collective-permute-start(bf16[2,512,128]{2,1,0:T(8,128)(2,1)S(1)} %get-tuple-element.149), channel_id=1, source_target_pairs={{0,96},{2,34},{32,64},{34,2},{64,32},{66,98},{96,0},{98,66},{1,97}... | collective-permute-start | bytes 786440 | tf_op jit(solution)/shard_map/ppermute | solution.py:44
  82.4 3.2 %collective-permute-done.17.refs_1_ = bf16[128,1024]{1,0:T(8,128)(2,1)S(1)} collective-permute-done((bf16[128,1024]{1,0:T(8,128)(2,1)S(1)}, bf16[128,1024]{1,0:T(8,128)(2,1)S(1)}, u32[]{:S(2)}, u32[]{:S(2)}) %collective-permute-start.17) | collective-permute-done | bytes 262176 | tf_op jit(solution)/shard_map/ppermute | solution.py:44
  85.6 1.1 collective-permute-start.21
  86.7 1.6 %collective-permute-start.20 = (bf16[1024,128]{1,0:T(8,128)(2,1)S(1)}, bf16[1024,128]{1,0:T(8,128)(2,1)S(1)}, u32[]{:S(2)}, u32[]{:S(2)}) collective-permute-start(bf16[1024,128]{1,0:T(8,128)(2,1)S(1)} %get-tuple-element.159), channel_id=1, source_target_pairs={{0,4},{2,14},{4,0},{6,10},{8,12},{10,6},{12,8},{14,2},{1,5},{3,15}... | collective-permute-start | bytes 786440 | tf_op jit(solution)/shard_map/ppermute | solution.py:44
  88.4 2.8 %collective-permute-done.21.refs_1_ = bf16[128,1024]{1,0:T(8,128)(2,1)S(1)} collective-permute-done((bf16[128,1024]{1,0:T(8,128)(2,1)S(1)}, bf16[128,1024]{1,0:T(8,128)(2,1)S(1)}, u32[]{:S(2)}, u32[]{:S(2)}) %collective-permute-start.21) | collective-permute-done | bytes 262176 | tf_op jit(solution)/shard_map/ppermute | solution.py:34
  91.3 1.0 collective-permute-start.23
  92.3 2.3 %collective-permute-start.19 = (bf16[512,128]{1,0:T(8,128)(2,1)S(1)}, bf16[512,128]{1,0:T(8,128)(2,1)S(1)}, u32[]{:S(2)}, u32[]{:S(2)}) collective-permute-start(bf16[512,128]{1,0:T(8,128)(2,1)S(1)} %get-tuple-element.158), channel_id=1, source_target_pairs={{0,32},{2,98},{32,0},{34,66},{64,96},{66,34},{96,64},{98,2},{1,33}... | collective-permute-start | bytes 393224 | tf_op jit(solution)/shard_map/ppermute | solution.py:44
  94.6 2.7 %collective-permute-done.19.refs_2_ = bf16[512,128]{1,0:T(8,128)(2,1)S(1)} collective-permute-done((bf16[512,128]{1,0:T(8,128)(2,1)S(1)}, bf16[512,128]{1,0:T(8,128)(2,1)S(1)}, u32[]{:S(2)}, u32[]{:S(2)}) %collective-permute-start.19) | collective-permute-done | bytes 131104 | tf_op jit(solution)/shard_map/ppermute | solution.py:44
  97.3 0.1 back.1
  97.5 2.4 %collective-permute-start.25 = (bf16[256,1024]{1,0:T(8,128)(2,1)S(1)}, bf16[256,1024]{1,0:T(8,128)(2,1)S(1)}, u32[]{:S(2)}, u32[]{:S(2)}) collective-permute-start(bf16[256,1024]{1,0:T(8,128)(2,1)S(1)} %get-tuple-element.174.refs_0_), channel_id=1, source_target_pairs={{0,32},{2,98},{32,0},{34,66},{64,96},{66,34},{96,64},{98,2},{1,33}... | collective-permute-start | bytes 1572872 | tf_op jit(solution)/shard_map/ppermute | solution.py:44
  99.9 9.5 %collective-permute-start.22 = (bf16[768,128]{1,0:T(8,128)(2,1)S(1)}, bf16[768,128]{1,0:T(8,128)(2,1)S(1)}, u32[]{:S(2)}, u32[]{:S(2)}) collective-permute-start(bf16[768,128]{1,0:T(8,128)(2,1)S(1)} %get-tuple-element.164), channel_id=1, source_target_pairs={{0,2},{2,0},{1,3},{3,1},{4,6},{6,4},{5,7},{7,5},{8,10},{10,8},{9,1... | collective-permute-start | bytes 589832 | tf_op jit(solution)/shard_map/ppermute | solution.py:34
  109.5 1.1 collective-permute-done.22.refs_1_
  110.5 1.8 %collective-permute-start.24 = (bf16[768,128]{1,0:T(8,128)(2,1)S(1)}, bf16[768,128]{1,0:T(8,128)(2,1)S(1)}, u32[]{:S(2)}, u32[]{:S(2)}) collective-permute-start(bf16[768,128]{1,0:T(8,128)(2,1)S(1)} %get-tuple-element.169), channel_id=1, source_target_pairs={{0,16},{16,0},{1,17},{17,1},{2,18},{18,2},{3,19},{19,3},{4,20},{20... | collective-permute-start | bytes 589832 | tf_op jit(solution)/shard_map/ppermute | solution.py:34
  112.4 5.0 %collective-permute-done.24.refs_2_ = bf16[768,128]{1,0:T(8,128)(2,1)S(1)} collective-permute-done((bf16[768,128]{1,0:T(8,128)(2,1)S(1)}, bf16[768,128]{1,0:T(8,128)(2,1)S(1)}, u32[]{:S(2)}, u32[]{:S(2)}) %collective-permute-start.24) | collective-permute-done | bytes 196640 | tf_op jit(solution)/shard_map/ppermute | solution.py:34
  117.3 0.8 place.1
  118.2 0.1 double_0.1
  118.2 1.0 collective-permute-start.26
  119.2 2.3 %collective-permute-done.26.refs_1_ = bf16[512,1024]{1,0:T(8,128)(2,1)S(1)} collective-permute-done((bf16[512,1024]{1,0:T(8,128)(2,1)S(1)}, bf16[512,1024]{1,0:T(8,128)(2,1)S(1)}, u32[]{:S(2)}, u32[]{:S(2)}) %collective-permute-start.26) | collective-permute-done | bytes 1048608 | tf_op jit(solution)/shard_map/ppermute | solution.py:34
  121.5 2.3 %final.1 = (f32[512,1024]{1,0:T(8,128)}, f32[512,1024]{1,0:T(8,128)}, f32[8,128]{1,0:T(8,128)}) custom-call(bf16[512,1024]{1,0:T(8,128)(2,1)S(1)} %get-tuple-element.176.refs_0_, bf16[512,1024]{1,0:T(8,128)(2,1)S(1)} %collective-permute-done.26.refs_1_, f32[8,128]{1,0:T(8,128)S(1)} %get-tuple-element.177.refs_2_), custom_call_target="tpu_custom_call" | custom-call | bytes 6291456 | tf_op jit(solution)/shard_map/final/pallas_call | solution.py:77
  (37 shorter events, 0.6 us)
Async XLA Ops:
  0.6 17.1 %collective-permute-start = (bf16[128,512]{1,0:T(8,128)(2,1)}, bf16[128,512]{1,0:T(8,128)(2,1)S(1)}, u32[]{:S(2)}, u32[]{:S(2)}) collective-permute-start(bf16[128,512]{1,0:T(8,128)(2,1)} %refs_3_.1), channel_id=1, source_target_pairs={{0,1},{1,0},{2,3},{3,2},{4,5},{5,4},{6,7},{7,6},{8,9},{9,8},{10,11... | collective-permute-start | bytes 393224 | tf_op jit(solution)/shard_map/ppermute | solution.py:34
  5.1 1.0 copy-start
  6.1 0.9 copy-start.1
  7.0 0.9 copy-start.2
  7.9 0.9 copy-start.3
  8.8 0.9 copy-start.4
  9.7 0.9 copy-start.5
  10.6 0.9 copy-start.6
  11.5 0.7 copy-start.7
  12.2 0.7 copy-start.8
  16.7 2.4 %collective-permute-start.1 = (bf16[384,512]{1,0:T(8,128)(2,1)S(1)}, bf16[384,512]{1,0:T(8,128)(2,1)S(1)}, u32[]{:S(2)}, u32[]{:S(2)}) collective-permute-start(bf16[384,512]{1,0:T(8,128)(2,1)S(1)} %get-tuple-element.96), channel_id=1, source_target_pairs={{0,2},{2,0},{1,3},{3,1},{4,6},{6,4},{5,7},{7,5},{8,10},{10,8},{9,1... | collective-permute-start | bytes 1179656 | tf_op jit(solution)/shard_map/ppermute | solution.py:34
  18.4 1.6 %collective-permute-start.4 = (bf16[1088,128]{1,0:T(8,128)(2,1)S(1)}, bf16[1088,128]{1,0:T(8,128)(2,1)S(1)}, u32[]{:S(2)}, u32[]{:S(2)}) collective-permute-start(bf16[1088,128]{1,0:T(8,128)(2,1)S(1)} %get-tuple-element.109), channel_id=1, source_target_pairs={{0,2},{2,0},{1,3},{3,1},{4,6},{6,4},{5,7},{7,5},{8,10},{10,8},{9,1... | collective-permute-start | bytes 835592 | tf_op jit(solution)/shard_map/ppermute | solution.py:34
  20.0 13.4 %collective-permute-start.6 = (bf16[1088,128]{1,0:T(8,128)(2,1)S(1)}, bf16[1088,128]{1,0:T(8,128)(2,1)S(1)}, u32[]{:S(2)}, u32[]{:S(2)}) collective-permute-start(bf16[1088,128]{1,0:T(8,128)(2,1)S(1)} %get-tuple-element.115), channel_id=1, source_target_pairs={{0,16},{16,0},{1,17},{17,1},{2,18},{18,2},{3,19},{19,3},{4,20},{20... | collective-permute-start | bytes 835592 | tf_op jit(solution)/shard_map/ppermute | solution.py:34
  20.5 12.9 %collective-permute-start.2 = (bf16[256,512]{1,0:T(8,128)(2,1)S(1)}, bf16[256,512]{1,0:T(8,128)(2,1)S(1)}, u32[]{:S(2)}, u32[]{:S(2)}) collective-permute-start(bf16[256,512]{1,0:T(8,128)(2,1)S(1)} %get-tuple-element.106), channel_id=1, source_target_pairs={{0,4},{2,126},{4,8},{6,2},{8,12},{10,6},{12,16},{14,10},{16,20},{1... | collective-permute-start | bytes 786440 | tf_op jit(solution)/shard_map/ppermute | solution.py:502
  27.3 6.1 %collective-permute-start.3 = (bf16[128,512]{1,0:T(8,128)(2,1)S(1)}, bf16[128,512]{1,0:T(8,128)(2,1)S(1)}, u32[]{:S(2)}, u32[]{:S(2)}) collective-permute-start(bf16[128,512]{1,0:T(8,128)(2,1)S(1)} %get-tuple-element.107), channel_id=1, source_target_pairs={{0,122},{2,8},{4,126},{6,12},{8,2},{10,16},{12,6},{14,20},{16,10},... | collective-permute-start | bytes 393224 | tf_op jit(solution)/shard_map/ppermute | solution.py:505
  33.5 7.1 %collective-permute-start.9 = (bf16[1152,128]{1,0:T(8,128)(2,1)S(1)}, bf16[1152,128]{1,0:T(8,128)(2,1)S(1)}, u32[]{:S(2)}, u32[]{:S(2)}) collective-permute-start(bf16[1152,128]{1,0:T(8,128)(2,1)S(1)} %get-tuple-element.122.refs_0_), channel_id=1, source_target_pairs={{0,32},{2,98},{32,0},{34,66},{64,96},{66,34},{96,64},{98,2},{1,33}... | collective-permute-start | bytes 884744 | tf_op jit(solution)/shard_map/ppermute | solution.py:44
  36.5 2.3 %collective-permute-start.5 = (bf16[128,512]{1,0:T(8,128)(2,1)S(1)}, bf16[128,512]{1,0:T(8,128)(2,1)S(1)}, u32[]{:S(2)}, u32[]{:S(2)}) collective-permute-start(bf16[128,512]{1,0:T(8,128)(2,1)S(1)} %get-tuple-element.113), channel_id=1, source_target_pairs={{0,2},{2,0},{1,3},{3,1},{4,6},{6,4},{5,7},{7,5},{8,10},{10,8},{9,1... | collective-permute-start | bytes 393224 | tf_op jit(solution)/shard_map/ppermute | solution.py:34
  36.5 6.7 %collective-permute-start.8 = (bf16[1024,128]{1,0:T(8,128)(2,1)S(1)}, bf16[1024,128]{1,0:T(8,128)(2,1)S(1)}, u32[]{:S(2)}, u32[]{:S(2)}) collective-permute-start(bf16[1024,128]{1,0:T(8,128)(2,1)S(1)} %get-tuple-element.121.refs_0_), channel_id=1, source_target_pairs={{0,4},{2,14},{4,0},{6,10},{8,12},{10,6},{12,8},{14,2},{1,5},{3,15}... | collective-permute-start | bytes 786440 | tf_op jit(solution)/shard_map/ppermute | solution.py:44
  38.9 6.5 %collective-permute-start.7 = (bf16[128,512]{1,0:T(8,128)(2,1)S(1)}, bf16[128,512]{1,0:T(8,128)(2,1)S(1)}, u32[]{:S(2)}, u32[]{:S(2)}) collective-permute-start(bf16[128,512]{1,0:T(8,128)(2,1)S(1)} %get-tuple-element.118.refs_2_), channel_id=1, source_target_pairs={{0,1},{1,0},{2,3},{3,2},{4,5},{5,4},{6,7},{7,6},{8,9},{9,8},{10,11... | collective-permute-start | bytes 393224 | tf_op jit(solution)/shard_map/ppermute | solution.py:34
  47.2 7.6 %collective-permute-start.12 = (bf16[512,1024]{1,0:T(8,128)(2,1)S(1)}, bf16[512,1024]{1,0:T(8,128)(2,1)S(1)}, u32[]{:S(2)}, u32[]{:S(2)}) collective-permute-start(bf16[512,1024]{1,0:T(8,128)(2,1)S(1)} %get-tuple-element.132), channel_id=1, source_target_pairs={{0,2},{2,0},{1,3},{3,1},{4,6},{6,4},{5,7},{7,5},{8,10},{10,8},{9,1... | collective-permute-start | bytes 3145736 | tf_op jit(solution)/shard_map/ppermute | solution.py:34
  47.6 9.0 %collective-permute-start.11 = (bf16[2,1152,128]{2,1,0:T(8,128)(2,1)S(1)}, bf16[2,1152,128]{2,1,0:T(8,128)(2,1)S(1)}, u32[]{:S(2)}, u32[]{:S(2)}) collective-permute-start(bf16[2,1152,128]{2,1,0:T(8,128)(2,1)S(1)} %get-tuple-element.127.refs_0_), channel_id=1, source_target_pairs={{0,96},{2,34},{32,64},{34,2},{64,32},{66,98},{96,0},{98,66},{1,97}... | collective-permute-start | bytes 1769480 | tf_op jit(solution)/shard_map/ppermute | solution.py:44
  47.7 8.4 %collective-permute-start.10 = (bf16[2,1024,128]{2,1,0:T(8,128)(2,1)S(1)}, bf16[2,1024,128]{2,1,0:T(8,128)(2,1)S(1)}, u32[]{:S(2)}, u32[]{:S(2)}) collective-permute-start(bf16[2,1024,128]{2,1,0:T(8,128)(2,1)S(1)} %get-tuple-element.128.refs_1_), channel_id=1, source_target_pairs={{0,12},{2,6},{4,8},{6,2},{8,4},{10,14},{12,0},{14,10},{1,13},{3,7}... | collective-permute-start | bytes 1572872 | tf_op jit(solution)/shard_map/ppermute | solution.py:44
  55.1 9.3 %collective-permute-start.13 = (bf16[256,1024]{1,0:T(8,128)(2,1)S(1)}, bf16[256,1024]{1,0:T(8,128)(2,1)S(1)}, u32[]{:S(2)}, u32[]{:S(2)}) collective-permute-start(bf16[256,1024]{1,0:T(8,128)(2,1)S(1)} %get-tuple-element.137), channel_id=1, source_target_pairs={{0,32},{2,98},{32,0},{34,66},{64,96},{66,34},{96,64},{98,2},{1,33}... | collective-permute-start | bytes 1572872 | tf_op jit(solution)/shard_map/ppermute | solution.py:44
  64.5 7.4 %collective-permute-start.14 = (bf16[128,1024]{1,0:T(8,128)(2,1)S(1)}, bf16[128,1024]{1,0:T(8,128)(2,1)S(1)}, u32[]{:S(2)}, u32[]{:S(2)}) collective-permute-start(bf16[128,1024]{1,0:T(8,128)(2,1)S(1)} %get-tuple-element.144), channel_id=1, source_target_pairs={{0,96},{2,34},{32,64},{34,2},{64,32},{66,98},{96,0},{98,66},{1,97}... | collective-permute-start | bytes 786440 | tf_op jit(solution)/shard_map/ppermute | solution.py:44
  70.9 11.4 %collective-permute-start.18 = (bf16[2,1024,128]{2,1,0:T(8,128)(2,1)S(1)}, bf16[2,1024,128]{2,1,0:T(8,128)(2,1)S(1)}, u32[]{:S(2)}, u32[]{:S(2)}) collective-permute-start(bf16[2,1024,128]{2,1,0:T(8,128)(2,1)S(1)} %get-tuple-element.154), channel_id=1, source_target_pairs={{0,12},{2,6},{4,8},{6,2},{8,4},{10,14},{12,0},{14,10},{1,13},{3,7}... | collective-permute-start | bytes 1572872 | tf_op jit(solution)/shard_map/ppermute | solution.py:44
  72.0 8.2 %collective-permute-start.16 = (bf16[128,1024]{1,0:T(8,128)(2,1)S(1)}, bf16[128,1024]{1,0:T(8,128)(2,1)S(1)}, u32[]{:S(2)}, u32[]{:S(2)}) collective-permute-start(bf16[128,1024]{1,0:T(8,128)(2,1)S(1)} %get-tuple-element.150.refs_0_), channel_id=1, source_target_pairs={{0,4},{2,14},{4,0},{6,10},{8,12},{10,6},{12,8},{14,2},{1,5},{3,15}... | collective-permute-start | bytes 786440 | tf_op jit(solution)/shard_map/ppermute | solution.py:44
  80.3 5.3 %collective-permute-start.17 = (bf16[128,1024]{1,0:T(8,128)(2,1)S(1)}, bf16[128,1024]{1,0:T(8,128)(2,1)S(1)}, u32[]{:S(2)}, u32[]{:S(2)}) collective-permute-start(bf16[128,1024]{1,0:T(8,128)(2,1)S(1)} %get-tuple-element.152.refs_0_), channel_id=1, source_target_pairs={{0,12},{2,6},{4,8},{6,2},{8,4},{10,14},{12,0},{14,10},{1,13},{3,7}... | collective-permute-start | bytes 786440 | tf_op jit(solution)/shard_map/ppermute | solution.py:44
  80.3 8.0 %collective-permute-start.15 = (bf16[2,512,128]{2,1,0:T(8,128)(2,1)S(1)}, bf16[2,512,128]{2,1,0:T(8,128)(2,1)S(1)}, u32[]{:S(2)}, u32[]{:S(2)}) collective-permute-start(bf16[2,512,128]{2,1,0:T(8,128)(2,1)S(1)} %get-tuple-element.149), channel_id=1, source_target_pairs={{0,96},{2,34},{32,64},{34,2},{64,32},{66,98},{96,0},{98,66},{1,97}... | collective-permute-start | bytes 786440 | tf_op jit(solution)/shard_map/ppermute | solution.py:44
  85.6 5.6 %collective-permute-start.21 = (bf16[128,1024]{1,0:T(8,128)(2,1)S(1)}, bf16[128,1024]{1,0:T(8,128)(2,1)S(1)}, u32[]{:S(2)}, u32[]{:S(2)}) collective-permute-start(bf16[128,1024]{1,0:T(8,128)(2,1)S(1)} %get-tuple-element.160.refs_0_), channel_id=1, source_target_pairs={{0,16},{16,0},{1,17},{17,1},{2,18},{18,2},{3,19},{19,3},{4,20},{20... | collective-permute-start | bytes 786440 | tf_op jit(solution)/shard_map/ppermute | solution.py:34
  86.7 7.9 %collective-permute-start.20 = (bf16[1024,128]{1,0:T(8,128)(2,1)S(1)}, bf16[1024,128]{1,0:T(8,128)(2,1)S(1)}, u32[]{:S(2)}, u32[]{:S(2)}) collective-permute-start(bf16[1024,128]{1,0:T(8,128)(2,1)S(1)} %get-tuple-element.159), channel_id=1, source_target_pairs={{0,4},{2,14},{4,0},{6,10},{8,12},{10,6},{12,8},{14,2},{1,5},{3,15}... | collective-permute-start | bytes 786440 | tf_op jit(solution)/shard_map/ppermute | solution.py:44
  91.3 6.2 %collective-permute-start.23 = (bf16[128,1024]{1,0:T(8,128)(2,1)S(1)}, bf16[128,1024]{1,0:T(8,128)(2,1)S(1)}, u32[]{:S(2)}, u32[]{:S(2)}) collective-permute-start(bf16[128,1024]{1,0:T(8,128)(2,1)S(1)} %get-tuple-element.166.refs_0_), channel_id=1, source_target_pairs={{0,96},{2,34},{32,64},{34,2},{64,32},{66,98},{96,0},{98,66},{1,97}... | collective-permute-start | bytes 786440 | tf_op jit(solution)/shard_map/ppermute | solution.py:44
  92.3 5.0 %collective-permute-start.19 = (bf16[512,128]{1,0:T(8,128)(2,1)S(1)}, bf16[512,128]{1,0:T(8,128)(2,1)S(1)}, u32[]{:S(2)}, u32[]{:S(2)}) collective-permute-start(bf16[512,128]{1,0:T(8,128)(2,1)S(1)} %get-tuple-element.158), channel_id=1, source_target_pairs={{0,32},{2,98},{32,0},{34,66},{64,96},{66,34},{96,64},{98,2},{1,33}... | collective-permute-start | bytes 393224 | tf_op jit(solution)/shard_map/ppermute | solution.py:44
  97.5 20.6 %collective-permute-start.25 = (bf16[256,1024]{1,0:T(8,128)(2,1)S(1)}, bf16[256,1024]{1,0:T(8,128)(2,1)S(1)}, u32[]{:S(2)}, u32[]{:S(2)}) collective-permute-start(bf16[256,1024]{1,0:T(8,128)(2,1)S(1)} %get-tuple-element.174.refs_0_), channel_id=1, source_target_pairs={{0,32},{2,98},{32,0},{34,66},{64,96},{66,34},{96,64},{98,2},{1,33}... | collective-permute-start | bytes 1572872 | tf_op jit(solution)/shard_map/ppermute | solution.py:44
  99.9 10.6 %collective-permute-start.22 = (bf16[768,128]{1,0:T(8,128)(2,1)S(1)}, bf16[768,128]{1,0:T(8,128)(2,1)S(1)}, u32[]{:S(2)}, u32[]{:S(2)}) collective-permute-start(bf16[768,128]{1,0:T(8,128)(2,1)S(1)} %get-tuple-element.164), channel_id=1, source_target_pairs={{0,2},{2,0},{1,3},{3,1},{4,6},{6,4},{5,7},{7,5},{8,10},{10,8},{9,1... | collective-permute-start | bytes 589832 | tf_op jit(solution)/shard_map/ppermute | solution.py:34
  110.5 6.8 %collective-permute-start.24 = (bf16[768,128]{1,0:T(8,128)(2,1)S(1)}, bf16[768,128]{1,0:T(8,128)(2,1)S(1)}, u32[]{:S(2)}, u32[]{:S(2)}) collective-permute-start(bf16[768,128]{1,0:T(8,128)(2,1)S(1)} %get-tuple-element.169), channel_id=1, source_target_pairs={{0,16},{16,0},{1,17},{17,1},{2,18},{18,2},{3,19},{19,3},{4,20},{20... | collective-permute-start | bytes 589832 | tf_op jit(solution)/shard_map/ppermute | solution.py:34
  118.2 3.2 %collective-permute-start.26 = (bf16[512,1024]{1,0:T(8,128)(2,1)S(1)}, bf16[512,1024]{1,0:T(8,128)(2,1)S(1)}, u32[]{:S(2)}, u32[]{:S(2)}) collective-permute-start(bf16[512,1024]{1,0:T(8,128)(2,1)S(1)} %get-tuple-element.176.refs_0_), channel_id=1, source_target_pairs={{0,2},{2,0},{1,3},{3,1},{4,6},{6,4},{5,7},{7,5},{8,10},{10,8},{9,1... | collective-permute-start | bytes 3145736 | tf_op jit(solution)/shard_map/ppermute | solution.py:34

commit v3 on v2

v3 whole, which is shorter than its diff:
```python
import functools
import math

import jax
import jax.numpy as jnp
from jax import lax
from jax.experimental import pallas as pl
from jax.experimental.pallas import tpu as pltpu
from jax.sharding import Mesh
from jax.sharding import PartitionSpec as P

BLOCK = 128
REACH = 3
LANES = 128
PAIRS = 4
STAT = 16
GROUP = 512
NODE = ("z", "y", "x", "c")
BF16 = jnp.bfloat16
F32 = jnp.float32
VMEM_LIMIT = 48 * 1024 * 1024

NT = (((1,), (1,)), ((), ()))
NN = (((1,), (0,)), ((), ()))
TN = (((0,), (0,)), ((), ()))


def dot(a, b, dims):
    return lax.dot_general(a, b, dims, preferred_element_type=F32)


def swap(value, axes, mask):
    count = lax.axis_size(axes)
    return lax.ppermute(value, axes, [(i, i ^ mask) for i in range(count)])


NEXT = ((1, 0, 3, 2), (3, 2, 1, 0))


def meet(value, axis, step):
    pairs = [
        (2 * i + core, 2 * NEXT[(step + core) % 2][i] + core) for i in range(4) for core in range(2)
    ]
    return lax.ppermute(value, (axis, "c"), pairs)


def x_near(value):
    pairs = [(2 * i + c, 2 * ((i + (1 if c == 0 else 3)) % 4) + c) for i in range(4) for c in range(2)]
    return lax.ppermute(value, ("x", "c"), pairs)


def x_far(value):
    return swap(value, "x", 2)


def place_in_group():
    return lax.axis_index("y") * 2 + lax.axis_index("c")


class Order:
    def __init__(self):
        self.token = None

    def call(self, kernel, outs, *args, scratch=(), smem=0, anywhere=0, flops=0, name=None):
        count, first = len(args), self.token is None
        tokens = [] if first else [self.token]
        results = len(outs)

        def whole(*refs):
            token_out = refs[count + len(tokens) + results]
            token_out[...] = jnp.zeros_like(token_out) if first else refs[count][...]
            outputs = refs[count + len(tokens) : count + len(tokens) + results]
            kernel(*refs[:count], *outputs, *refs[count + len(tokens) + results + 1 :])

        specs = [pl.BlockSpec(memory_space=pltpu.SMEM)] * smem
        specs += [pl.BlockSpec(memory_space=pltpu.HBM)] * anywhere
        specs += [pl.BlockSpec(memory_space=pltpu.VMEM)] * (count - smem - anywhere + len(tokens))
        size = sum(math.prod(a.shape) * a.dtype.itemsize for a in (*args, *outs))
        *values, self.token = pl.pallas_call(
            whole,
            out_shape=[*outs, shaped((8, LANES), F32)],
            in_specs=specs,
            out_specs=[pl.BlockSpec(memory_space=pltpu.VMEM)] * (results + 1),
            scratch_shapes=list(scratch),
            cost_estimate=pl.CostEstimate(flops=flops, bytes_accessed=size, transcendentals=0),
            compiler_params=pltpu.CompilerParams(vmem_limit_bytes=VMEM_LIMIT),
            name=name,
        )(*args, *tokens)
        return values


def shaped(shape, dtype=BF16):
    return jax.ShapeDtypeStruct(shape, dtype)


def three_pieces(value):
    high = value.astype(BF16)
    rest = value - high.astype(F32)
    middle = rest.astype(BF16)
    low = (rest - middle.astype(F32)).astype(BF16)
    return jnp.concatenate(
        [high.astype(F32), middle.astype(F32), low.astype(F32), jnp.zeros((STAT - 6, LANES), F32)],
        axis=0,
    ).astype(BF16)


def pair_rows(table, pair):
    rows = table[0:2]
    for other in range(1, PAIRS):
        rows = jnp.where(pair == other, table[2 * other : 2 * other + 2], rows)
    return rows


Q_PAY = 288
KV_PAY = 256
Q_ROWS = 2 * (GROUP + PAIRS * STAT)
KV_ROWS = 2 * GROUP


def load_kernel(count, *refs):
    sem = refs[-1]
    copies = [
        pltpu.make_async_copy(source, target, sem.at[i])
        for i, (source, target) in enumerate(zip(refs[:count], refs[count : 2 * count]))
    ]
    for copy in copies:
        copy.start()
    for copy in copies:
        copy.wait()


def whole_rows(own, other, out):
    side, half = lax.axis_index("h"), own.shape[1]
    out[:, pl.ds(pl.multiple_of(side * half, half), half)] = own[...]
    out[:, pl.ds(pl.multiple_of((1 - side) * half, half), half)] = other[...]


def slot_of(source_ref, e):
    parts = lax.axis_size(NODE)
    distance = lax.rem(source_ref[0, e] - lax.axis_index(NODE) + REACH + 2 * parts, parts)
    return jnp.clip(distance, 0, 2 * REACH)


def chip_kernel(own, other, out):
    core = lax.axis_index("c")
    out[pl.ds(pl.multiple_of(core * 128, 128), 128)] = own[...]
    out[pl.ds(pl.multiple_of((1 - core) * 128, 128), 128)] = other[...]


def share_kernel(source_ref, count_ref, tiles, grad, weight, send, far, keep, local, total):
    total[...] = jnp.zeros_like(total)
    grad_aggregate = dot(grad[...], weight[...], NT).astype(BF16)
    for e in range(tiles.shape[1]):

        @pl.when(e < count_ref[0])
        def _():
            total[slot_of(source_ref, e)] += dot(tiles[0, e], grad_aggregate, TN)

    core = lax.axis_index("c")

    def share(on_first, on_second):
        return total[jnp.where(core == 0, on_first + REACH, on_second + REACH)]

    for i, (on_first, on_second) in enumerate(((-2, 1), (-1, 2), (1, -1))):
        send[i * 128 : (i + 1) * 128] = share(on_first, on_second).astype(BF16)
    for i, (on_first, on_second) in enumerate(((2, -3), (3, -2))):
        keep[i * 128 : (i + 1) * 128] = share(on_first, on_second)
    far[...] = share(-3, 3).astype(BF16)
    local[...] = total[REACH]


def near_kernel(keep, local, received, near, local_out):
    near[...] = (keep[...] + received[0:256].astype(F32)).astype(BF16)
    local_out[...] = local[...] + received[256:384].astype(F32)


def cross_kernel(local, near, far, send, local_out):
    core = lax.axis_index("c")
    mine = pl.ds(pl.multiple_of(core * 128, 128), 128)
    other = pl.ds(pl.multiple_of((1 - core) * 128, 128), 128)
    send[...] = near[other]
    local_out[...] = local[...] + near[mine].astype(F32) + far[...].astype(F32)


def pay_kernel(k_ref, v_ref, *pays):
    me = place_in_group()
    for j, pay in enumerate(pays):
        columns = pl.ds(pl.multiple_of((me ^ j) * LANES, LANES), LANES)
        pay[0:128] = k_ref[:, columns]
        pay[128:256] = v_ref[:, columns]


def mix_kernel(own, other, weight_ref, mix_ref, q_ref, log_ref, whole, *pays):
    whole_rows(own, other, whole)
    grad = dot(whole[...], weight_ref[...], NT).astype(BF16)
    product = grad.astype(F32) * mix_ref[...].astype(F32)
    turned_product = product.T
    rows = [jnp.sum(turned_product[64 * i : 64 * (i + 1)], axis=0, keepdims=True) for i in range(8)]
    spread = jnp.concatenate(rows, axis=0)
    logs = log_ref[...]
    me = place_in_group()
    for j, pay in enumerate(pays):
        pair = me ^ j
        columns = pl.ds(pl.multiple_of(pair * LANES, LANES), LANES)
        block = grad[:, 0:LANES]
        for other in range(1, PAIRS):
            block = jnp.where(pair == other, grad[:, other * LANES : (other + 1) * LANES], block)
        pay[0:128] = q_ref[:, columns]
        pay[128:144] = three_pieces(pair_rows(logs, pair))
        pay[144:272] = block
        pay[272:288] = three_pieces(pair_rows(spread, pair))


def forward_kernel(own, received, out):
    rows = own.shape[0]
    out[0:rows] = own[...]
    out[rows : 2 * rows] = received[...]


def join_rows_kernel(own, near, far, out):
    for j, (pay, base) in enumerate(((own, 0), (near, 0), (far, 0), (far, Q_PAY))):
        for part in range(2):
            at, start = part * (Q_ROWS // 2), base + part * 144
            out[at + j * 128 : at + (j + 1) * 128] = pay[start : start + 128]
            stats = at + GROUP + j * STAT
            out[stats : stats + STAT] = pay[start + 128 : start + 144]


def join_keys_kernel(own, near, far, out):
    for j, (pay, base) in enumerate(((own, 0), (near, 0), (far, 0), (far, KV_PAY))):
        for part in range(2):
            start = base + part * 128
            out[part * GROUP + j * 128 : part * GROUP + (j + 1) * 128] = pay[start : start + 128]


def pair_kernel(first, second, out):
    out[0] = first[...]
    out[1] = second[...]


def masked(block, head):
    lane = lax.broadcasted_iota(jnp.int32, block.shape, 1)
    keep = lane < 64 if head == 0 else lane >= 64
    return jnp.where(keep, block, 0.0).astype(BF16)


def unpack_rows(source, factor, table, stat):
    block = source[0:GROUP].astype(F32) * factor
    for h in range(2):
        table[h] = masked(block, h)
    for j in range(PAIRS):
        pieces = source[GROUP + STAT * j : GROUP + STAT * (j + 1)].astype(F32)
        stat[:, j * LANES : (j + 1) * LANES] = pieces[0:2] + pieces[2:4] + pieces[4:6]


def tile_step(key_tile, value_tile, keys_t, query, grad, logs, spread, dk, dv, dq):
    for h in range(2):
        query_tile, grad_tile = query[h], grad[h]
        scores = dot(key_tile, query_tile, NT) - logs[h : h + 1]
        soft = jnp.exp(scores)
        change = dot(value_tile, grad_tile, NT) - spread[h : h + 1]
        score_grad = (soft * change).astype(BF16)
        dv[...] += dot(soft.astype(BF16), grad_tile, NN)
        dk[...] += dot(score_grad, query_tile, NN)
        head = slice(64 * h, 64 * (h + 1))
        dq[head] += dot(keys_t[head], score_grad, NN)


def turned(block):
    return block.astype(F32).T.astype(BF16)


def attention_kernel(has_dq, has_dkv, dq_last, dkv_last, qdo, kv, *refs):
    if has_dq:
        dq_in, refs = refs[0], refs[1:]
    if has_dkv:
        dkv_in, refs = refs[0], refs[1:]
    dq_out, dkv_out, keys_t, query, grad, logs, spread, dq, dkv = refs
    for i in range(2):
        unpack_rows(qdo.at[i, 0 : Q_ROWS // 2], 0.125, query.at[i], logs.at[i])
        unpack_rows(qdo.at[i, Q_ROWS // 2 : Q_ROWS], 1.0, grad.at[i], spread.at[i])
        keys_t[i] = turned(kv[i, 0:GROUP])
    dq[...] = dq_in[...] if has_dq else jnp.zeros_like(dq)
    dkv[...] = dkv_in[...] if has_dkv else jnp.zeros_like(dkv)

    @pl.loop(0, 4)
    def _(step):
        i, k = step % 2, step // 2
        tile_step(
            kv[k, 0:GROUP],
            kv[k, GROUP : 2 * GROUP],
            keys_t.at[k],
            query.at[i],
            grad.at[i],
            logs.at[i],
            spread.at[i],
            dkv.at[k, pl.ds(0, GROUP)],
            dkv.at[k, pl.ds(GROUP, GROUP)],
            dq.at[i],
        )

    if dq_last:
        for i in range(2):
            dq_out[i] = (dq[i].T * 0.125).astype(dq_out.dtype)
    else:
        dq_out[...] = dq[...]
    dkv_out[...] = dkv[...].astype(dkv_out.dtype)


SLOW = 10**10
MIX = SLOW
JOIN = SLOW
JOIN_KEYS = 1 * 10**9
FORWARD = 0
PAIR = SLOW
WEIGHTS = 0
TILE_FLOPS = 2 * 10 * GROUP * GROUP * 64


def attention(order, name, qdo, kv, dq, dkv, dq_last=None, dkv_last=None):
    carry = [a for a in (dq, dkv) if a is not None]
    dq_shape = (2, LANES, GROUP) if dq_last is None else (2, GROUP, LANES)
    return order.call(
        functools.partial(
            attention_kernel, dq is not None, dkv is not None, dq_last is not None, dkv_last is not None
        ),
        [shaped(dq_shape, dq_last or F32), shaped((2, KV_ROWS, LANES), dkv_last or F32)],
        qdo,
        kv,
        *carry,
        scratch=[
            pltpu.VMEM((2, LANES, GROUP), BF16),
            pltpu.VMEM((2, 2, GROUP, LANES), BF16),
            pltpu.VMEM((2, 2, GROUP, LANES), BF16),
            pltpu.VMEM((2, 2, GROUP), F32),
            pltpu.VMEM((2, 2, GROUP), F32),
            pltpu.VMEM((2, LANES, GROUP), F32),
            pltpu.VMEM((2, KV_ROWS, LANES), F32),
        ],
        flops=4 * TILE_FLOPS,
        name="attention_" + name,
    )


def half_sum_kernel(totals, received, out):
    out[...] = (totals[1].astype(F32) + received[1].astype(F32)).astype(BF16)


def back_kernel(dq, dq_far, dq_near, dkv, dkv_far, dkv_near, keep, near, through, far):
    dq_sum = (dq[0] + dq_far[0].astype(F32) + dq_near[...].astype(F32)).astype(BF16)
    dkv_sum = (dkv[0] + dkv_far[0].astype(F32) + dkv_near[...].astype(F32)).astype(BF16)
    for j, (pay, base) in enumerate(((keep, 0), (near, 0), (through, 0), (far, 0))):
        pay[base : base + 128] = dq_sum[j * 128 : (j + 1) * 128]
        pay[base + 128 : base + 256] = dkv_sum[j * 128 : (j + 1) * 128]
        pay[base + 256 : base + 384] = dkv_sum[GROUP + j * 128 : GROUP + (j + 1) * 128]


def place_kernel(own, near, far, dq, dk, dv):
    me = place_in_group()
    for j, (pay, base) in enumerate(((own, 0), (near, 0), (far, 0), (far, 384))):
        columns = pl.ds(pl.multiple_of((me ^ j) * LANES, LANES), LANES)
        dq[:, columns] = pay[base : base + 128]
        dk[:, columns] = pay[base + 128 : base + 256]
        dv[:, columns] = pay[base + 256 : base + 384]


def turn_kernel(dq, out):
    for i in range(2):
        out[i] = dq[i].T * 0.125


def weights_kernel(source_ref, count_ref, tiles, grad, mix_ref, own, partner, near, crossed, far, keep_ref, send_ref, window, total, left_ref):
    core = lax.axis_index("c")
    place = lax.axis_index("x")
    window[REACH] = own[...]
    window[jnp.where(core == 0, 4, 2)] = partner[...]
    for block, first in ((near, jnp.where(core == 0, 1, 4)), (crossed, jnp.where(core == 0, 5, 0))):
        window[first] = block[0:128]
        window[first + 1] = block[128:256]
    window[6 * core] = far[...]
    total[...] = jnp.zeros_like(total)
    for e in range(tiles.shape[1]):

        @pl.when(e < count_ref[0])
        def _():
            total[...] += dot(tiles[0, e], window[slot_of(source_ref, e)], NN)

    left_ref[0] = turned(mix_ref[...])
    left_ref[1] = turned(total[...].astype(BF16))

    def put(out, slot, which, distance):
        rows = pl.ds(pl.multiple_of(lax.rem(place + distance, 4) * 128, 128), 128)
        out[slot * 128 : (slot + 1) * 128] = dot(left_ref[which, rows], grad[...], NN).astype(BF16)

    for out, turn in ((keep_ref, core), (send_ref, 1 - core)):
        ahead = jnp.where(turn == 0, 1, 3)
        put(out, 0, 0, ahead)
        put(out, 1, 1, ahead)
        put(out, 2, turn, 2)
        put(out, 3, turn, 0)


def core_sum_kernel(keep, received, near, far, local):
    near[...] = (keep[0:256].astype(F32) + received[0:256].astype(F32)).astype(BF16)
    far[...] = (keep[256:384].astype(F32) + received[256:384].astype(F32)).astype(BF16)
    local[...] = keep[384:512].astype(F32) + received[384:512].astype(F32)


def core_split_kernel(local, near, far, send, local_out):
    core = lax.axis_index("c")
    mine = pl.ds(pl.multiple_of(core * 128, 128), 128)
    other = pl.ds(pl.multiple_of((1 - core) * 128, 128), 128)
    send[...] = near[other]
    local_out[...] = local[...] + near[mine].astype(F32) + far[...].astype(F32)


def core_pack_kernel(own, received, out):
    core = lax.axis_index("c")
    out[pl.ds(pl.multiple_of(core * 128, 128), 128)] = own[...]
    out[pl.ds(pl.multiple_of((1 - core) * 128, 128), 128)] = received[...]


def core_send_kernel(near, far, out):
    out[0:256] = near[...]
    out[256:384] = far[...]


def final_kernel(local, near, received, first_ref, second_ref):
    core = lax.axis_index("c")
    place = lax.axis_index("x")

    def rows(distance):
        return pl.ds(pl.multiple_of(lax.rem(place + distance, 4) * 128, 128), 128)

    before = jnp.where(core == 0, 3, 1)
    outs = (first_ref, second_ref)
    for i, out in enumerate(outs):
        block = slice(i * 128, (i + 1) * 128)
        out[rows(0)] = local[block].astype(F32)
        out[rows(before)] = near[block].astype(F32)
        out[rows(4 - before)] = received[block].astype(F32)

    @pl.when(core == 0)
    def _():
        first_ref[rows(2)] = near[256:384].astype(F32)
        second_ref[rows(2)] = received[256:384].astype(F32)

    @pl.when(core == 1)
    def _():
        second_ref[rows(2)] = near[256:384].astype(F32)
        first_ref[rows(2)] = received[256:384].astype(F32)


def add_kernel(*refs):
    total = refs[0][...].astype(F32)
    for ref in refs[1:-1]:
        total = total + ref[...].astype(F32)
    refs[-1][...] = total.astype(BF16)


def add(order, name, *terms):
    (out,) = order.call(add_kernel, [shaped(terms[0].shape)], *terms, name="add_" + name)
    return out


def pair(order, first, second):
    (out,) = order.call(pair_kernel, [shaped((2,) + first.shape)], first, second, flops=PAIR, name="pair")
    return out


def body(
    features,
    queries,
    keys,
    values,
    attn_mix,
    log_sums,
    out_weight,
    msg_weight,
    edge_tiles,
    edge_source,
    edge_count,
    out_grad,
):
    rows, columns = out_grad.shape
    order = Order()
    other_grad = swap(out_grad, "h", 1)
    parts = lax.axis_size(NODE)
    to_near = [(i, (i + (2 if i % 2 == 0 else -2)) % parts) for i in range(parts)]
    to_far = [(i, (i + (-3 if i % 2 == 0 else 3)) % parts) for i in range(parts)]
    partner_features = swap(features, "c", 1)
    far_features = lax.ppermute(features, NODE, to_far)
    arguments = [features, edge_tiles, out_grad, queries, keys, values, log_sums, out_weight, attn_mix, msg_weight]
    arguments = [pltpu.with_memory_space_constraint(a, pltpu.HBM) for a in arguments]
    loaded = order.call(
        functools.partial(load_kernel, len(arguments)),
        [shaped(a.shape, a.dtype) for a in arguments],
        *arguments,
        anywhere=len(arguments),
        scratch=[pltpu.SemaphoreType.DMA((len(arguments),))],
        name="load",
    )
    features, edge_tiles, out_grad, queries, keys, values, log_sums, out_weight, attn_mix, msg_weight = loaded
    wide = (rows, 2 * columns)
    key_pays = order.call(
        pay_kernel, [shaped((KV_PAY, LANES))] * 4, keys, values, name="pay"
    )
    key_near, key_cross = swap(key_pays[1], "c", 1), swap(key_pays[3], "c", 1)
    (near_features,) = order.call(
        chip_kernel, [shaped((2 * rows, columns))], features, partner_features, name="chip"
    )
    near_features = lax.ppermute(near_features, NODE, to_near)
    (key_far,) = order.call(
        forward_kernel, [shaped((2 * KV_PAY, LANES))], key_pays[2], key_cross, name="forward_keys"
    )
    key_far = swap(key_far, "y", 1)
    out_grad, *pays = order.call(
        mix_kernel,
        [shaped(wide)] + [shaped((Q_PAY, LANES))] * 4,
        out_grad,
        other_grad,
        out_weight,
        attn_mix,
        queries,
        log_sums,
        flops=MIX,
        name="mix",
    )
    pay_near, pay_cross = swap(pays[1], "c", 1), swap(pays[3], "c", 1)
    (pay_far,) = order.call(
        forward_kernel, [shaped((2 * Q_PAY, LANES))], pays[2], pay_cross, flops=FORWARD, name="forward"
    )
    pay_far = swap(pay_far, "y", 1)
    (kv,) = order.call(
        join_keys_kernel,
        [shaped((KV_ROWS, LANES))],
        key_pays[0],
        key_near,
        key_far,
        flops=JOIN_KEYS,
        name="join_keys",
    )
    kv_met = meet(kv, "x", 0)
    (qdo,) = order.call(
        join_rows_kernel,
        [shaped((Q_ROWS, LANES))],
        pays[0],
        pay_near,
        pay_far,
        flops=JOIN,
        name="join",
    )
    qdo_met = meet(qdo, "z", 0)
    crossed_features = swap(near_features, "c", 1)
    keep, send = order.call(
        weights_kernel,
        [shaped((columns, 2 * columns)), shaped((columns, 2 * columns))],
        edge_source,
        edge_count,
        edge_tiles,
        out_grad,
        attn_mix,
        features,
        partner_features,
        near_features,
        crossed_features,
        far_features,
        smem=2,
        scratch=[
            pltpu.VMEM((2 * REACH + 1, rows, columns), BF16),
            pltpu.VMEM((rows, columns), F32),
            pltpu.VMEM((2, columns, rows), BF16),
        ],
        flops=WEIGHTS,
        name="weights",
    )
    received = swap(send, "c", 1)
    kv_near = pair(order, kv, kv_met)
    kv_far = meet(kv_near, "x", 1)
    qdo_near = pair(order, qdo, qdo_met)
    qdo_far = meet(qdo_near, "z", 1)
    near, far, local = order.call(
        core_sum_kernel,
        [shaped((2 * rows, 2 * columns)), shaped(wide), shaped(wide, F32)],
        keep,
        received,
        name="core_sum",
    )
    far, near = x_far(far), x_near(near)

    share_send, share_far, share_keep, share_local = order.call(
        share_kernel,
        [
            shaped((3 * rows, columns)),
            shaped((rows, columns)),
            shaped((2 * rows, columns), F32),
            shaped((rows, columns), F32),
        ],
        edge_source,
        edge_count,
        edge_tiles,
        out_grad,
        msg_weight,
        smem=2,
        scratch=[pltpu.VMEM((2 * REACH + 1, rows, columns), F32)],
        name="shares",
    )
    share_received = swap(share_send, "c", 1)
    dq_near, dkv_near = attention(order, "near", qdo_near, kv_near, None, None)
    dq_far, dkv_far = attention(order, "far", qdo_far, kv_far, None, None)
    send, local = order.call(
        core_split_kernel, [shaped(wide), shaped(wide, F32)], local, near, far, name="core_split"
    )
    received = swap(send, "c", 1)
    part = add(order, "x", local, received)
    received = meet(part, "z", 0)
    share_near, share_local = order.call(
        near_kernel,
        [shaped((2 * rows, columns)), shaped((rows, columns), F32)],
        share_keep,
        share_local,
        share_received,
        name="near",
    )
    share_far, share_near = lax.ppermute(share_far, NODE, to_far), lax.ppermute(share_near, NODE, to_near)
    dq_near, dkv_far = attention(order, "far_keys", qdo_near, kv_far, dq_near, dkv_far, None, BF16)
    dkv_met = meet(dkv_far, "x", 1)
    part = add(order, "z0", part, received)
    received = meet(part, "z", 1)
    share_cross, share_local = order.call(
        cross_kernel,
        [shaped((rows, columns)), shaped((rows, columns), F32)],
        share_local,
        share_near,
        share_far,
        flops=SLOW,
        name="cross",
    )
    share_cross = swap(share_cross, "c", 1)
    dq_far, dkv_near = attention(order, "far_queries", qdo_far, kv_near, dq_far, dkv_near, BF16, F32)
    dq_met = meet(dq_far, "z", 1)
    part = add(order, "z1", part, received)
    received = swap(part, "y", 1)
    grad_features = add(order, "shares", share_local, share_cross)
    (half,) = order.call(
        half_sum_kernel, [shaped((KV_ROWS, LANES))], dkv_near, dkv_met, name="half_dkv"
    )
    dkv_last = meet(half, "x", 0)
    (dq_near,) = order.call(
        turn_kernel, [shaped((2, GROUP, LANES), F32)], dq_near, name="turn"
    )
    part = add(order, "y", part, received)
    far, received = x_far(part), swap(part, "c", 1)
    (half,) = order.call(half_sum_kernel, [shaped((GROUP, LANES))], dq_near, dq_met, name="half_dq")
    dq_last = meet(half, "z", 0)
    (local,) = order.call(
        core_pack_kernel, [shaped((2 * rows, 2 * columns))], part, received, name="core_pack"
    )
    near = x_near(local)

    back_own, back_near, back_through, back_cross = order.call(
        back_kernel,
        [shaped((384, LANES))] * 4,
        dq_near,
        dq_met,
        dq_last,
        dkv_near,
        dkv_met,
        dkv_last,
        name="back",
    )
    back_near, back_cross = swap(back_near, "c", 1), swap(back_cross, "c", 1)
    (back_forward,) = order.call(
        forward_kernel, [shaped((768, LANES))], back_through, back_cross, name="forward_back"
    )
    back_far = swap(back_forward, "y", 1)
    grad_query, grad_key, grad_value = order.call(
        place_kernel, [shaped((rows, columns))] * 3, back_own, back_near, back_far, name="place"
    )
    (near,) = order.call(
        core_send_kernel, [shaped((3 * rows, 2 * columns))], near, far, name="core_send"
    )
    out_weight_grad, msg_weight_grad = order.call(
        final_kernel,
        [shaped((columns, 2 * columns), F32)] * 2,
        local,
        near,
        swap(near, "c", 1),
        name="final",
    )
    return (grad_features, grad_query, grad_key, grad_value, out_weight_grad, msg_weight_grad)


def solution(mesh):
    fine = Mesh(mesh.devices.reshape(4, 2, 4, 2, 2), NODE + ("h",))
    both = P(NODE, "h")
    placed = (
        both,
        both,
        both,
        both,
        both,
        P("h", NODE),
        P("h", None),
        P("h", None),
        P(NODE, None, None, None),
        P(NODE, None),
        P(NODE),
        both,
    )
    return jax.shard_map(
        body,
        mesh=fine,
        in_specs=placed,
        out_specs=(both, both, both, both, P("h", None), P("h", None)),
        check_vma=False,
    )
```

time: 124 us -> 111 us (0.90)
  waiting for transfers between devices: 31.8 us -> 24.3 us
  local copies, waits for them, and re-layouts: 7.71 us -> 0.52 us
  Pallas kernels: 35.5 us -> 36.8 us
    ppermute x14 -> x10, starting transfers between devices: 19.9 us -> 9.81 us  [meet(): return lax.ppermute(value, (axis, 'c'), pairs)]
    unnamed x18 -> x4, local copies, waits for them, and re-layouts: 7.71 us -> 0.52 us
    ppermute x2 -> x6, waiting for transfers between devices: 6.11 us -> 0.02 us  [the longest x2 0.01 us: x_near(): return lax.ppermute(value, ('x', 'c'), pairs)]
    ppermute x2 -> x6, starting transfers between devices: 6.74 us -> 12.5 us  [the longest x1 6.74 us: body(): near_features = lax.ppermute(near_features, NODE, to_near)]
    ppermute x11 -> x21, starting transfers between devices: 20.7 us -> 25.9 us  [swap(): return lax.ppermute(value, axes, [(i, i ^ mask) for i in range(count)])]
    ppermute x14 -> x10, waiting for transfers between devices: 10.9 us -> 6.21 us  [meet(): return lax.ppermute(value, (axis, 'c'), pairs)]
    ppermute x11 -> x21, waiting for transfers between devices: 14.7 us -> 18 us  [swap(): return lax.ppermute(value, axes, [(i, i ^ mask) for i in range(count)])]
    pallas_call x29 -> x34, Pallas kernels: 35.5 us -> 36.8 us  [call(): pl.pallas_call(whole, out_shape=[*outs, shaped((8, LANES), F32)], in_spec...]
  transfers between devices with their start and end apart: 27 -> 37, of which waited for: 14 -> 14; matrix products, arithmetic and copies ran while one was open for 0% -> 0% of each run, Pallas kernels for 25% -> 31%
where the time goes in v3:
time: 111 us
  starting transfers between devices  48.1 us (43%)
  Pallas kernels  36.8 us (33%)
  waiting for transfers between devices  24.3 us (22%)
  between operations  1.66 us (1%)
    pallas_call x34, Pallas kernels, call(): pl.pallas_call(whole, out_shape=[*outs, shaped((8, LANES), F32)], in_spec...  36.8 us
    ppermute x21, starting transfers between devices, swap(): return lax.ppermute(value, axes, [(i, i ^ mask) for i in range(count)])  25.9 us
    ppermute x21, waiting for transfers between devices, swap(): return lax.ppermute(value, axes, [(i, i ^ mask) for i in range(count)])  18 us
    ppermute x10, starting transfers between devices, meet(): return lax.ppermute(value, (axis, 'c'), pairs)  9.81 us
    ppermute x1, starting transfers between devices, body(): near_features = lax.ppermute(near_features, NODE, to_near)  6.74 us
    ppermute x10, waiting for transfers between devices, meet(): return lax.ppermute(value, (axis, 'c'), pairs)  6.21 us
    ppermute x1, starting transfers between devices, body(): lax.ppermute(share_near, NODE, to_near)  3.95 us
  transfers between devices with their start and end apart: 37, of which 14 were waited for; matrix products, arithmetic and copies ran while one was open for 0% of the time, Pallas kernels for 31%

profile of v3, /device:TPU:1, one launch (start us, length us, event | category | flops | bytes accessed | tf_op | source)
XLA Modules:
  0.0 111.3 jit_solution(4955152932803778740)
XLA Ops:
  0.6 1.5 %collective-permute-start.2 = (bf16[128,512]{1,0:T(8,128)(2,1)}, bf16[128,512]{1,0:T(8,128)(2,1)S(1)}, u32[]{:S(2)}, u32[]{:S(2)}) collective-permute-start(bf16[128,512]{1,0:T(8,128)(2,1)} %refs_0_.3), channel_id=1, source_target_pairs={{0,2},{2,0},{1,3},{3,1},{4,6},{6,4},{5,7},{7,5},{8,10},{10,8},{9,1... | collective-permute-start | bytes 393224 | tf_op jit(solution)/shard_map/ppermute | solution.py:34
  2.1 3.0 %collective-permute-start = (bf16[128,512]{1,0:T(8,128)(2,1)}, bf16[128,512]{1,0:T(8,128)(2,1)S(1)}, u32[]{:S(2)}, u32[]{:S(2)}) collective-permute-start(bf16[128,512]{1,0:T(8,128)(2,1)} %refs_2_.1), channel_id=1, source_target_pairs={{0,1},{1,0},{2,3},{3,2},{4,5},{5,4},{6,7},{7,6},{8,9},{9,8},{10,11... | collective-permute-start | bytes 393224 | tf_op jit(solution)/shard_map/ppermute | solution.py:34
  5.1 2.0 %load.1 = (bf16[128,512]{1,0:T(8,128)(2,1)S(1)}, bf16[1,8,128,128]{3,2,1,0:T(8,128)(2,1)S(1)}, bf16[128,512]{1,0:T(8,128)(2,1)S(1)}, bf16[128,512]{1,0:T(8,128)(...) custom-call(bf16[128,512]{1,0:T(8,128)(2,1)} %refs_0_.3, ...), custom_call_target="tpu_custom_call" | custom-call | bytes 6299648 | tf_op jit(solution)/shard_map/load/pallas_call | solution.py:79
  7.2 0.4 collective-permute-start.1
  7.7 0.9 collective-permute-done.1.refs_1_
  8.6 0.5 collective-permute-start.10
  9.1 6.7 %collective-permute-start.3 = (bf16[256,512]{1,0:T(8,128)(2,1)S(1)}, bf16[256,512]{1,0:T(8,128)(2,1)S(1)}, u32[]{:S(2)}, u32[]{:S(2)}) collective-permute-start(bf16[256,512]{1,0:T(8,128)(2,1)S(1)} %get-tuple-element.125), channel_id=1, source_target_pairs={{0,4},{2,126},{4,8},{6,2},{8,12},{10,6},{12,16},{14,10},{16,20},{1... | collective-permute-start | bytes 786440 | tf_op jit(solution)/shard_map/ppermute | solution.py:512
  15.8 0.6 mix.1
  16.5 0.1 collective-permute-start.7
  16.6 0.5 collective-permute-start.9
  17.0 0.8 collective-permute-done.7.refs_1_
  17.8 0.1 collective-permute-start.8
  17.9 0.1 collective-permute-start.5
  18.7 2.5 %collective-permute-start.6 = (bf16[288,128]{1,0:T(8,128)(2,1)S(1)}, bf16[288,128]{1,0:T(8,128)(2,1)S(1)}, u32[]{:S(2)}, u32[]{:S(2)}) collective-permute-start(bf16[288,128]{1,0:T(8,128)(2,1)S(1)} %get-tuple-element.127), channel_id=1, source_target_pairs={{0,2},{2,0},{1,3},{3,1},{4,6},{6,4},{5,7},{7,5},{8,10},{10,8},{9,1... | collective-permute-start | bytes 221192 | tf_op jit(solution)/shard_map/ppermute | solution.py:34
  21.2 0.1 collective-permute-start.13
  21.3 0.7 collective-permute-start.4
  22.0 0.1 collective-permute-done.6.refs_1_
  22.1 2.5 %collective-permute-done.8.refs_2_ = bf16[576,128]{1,0:T(8,128)(2,1)S(1)} collective-permute-done((bf16[576,128]{1,0:T(8,128)(2,1)S(1)}, bf16[576,128]{1,0:T(8,128)(2,1)S(1)}, u32[]{:S(2)}, u32[]{:S(2)}) %collective-permute-start.8) | collective-permute-done | bytes 147488 | tf_op jit(solution)/shard_map/ppermute | solution.py:34
  24.6 0.1 collective-permute-start.12
  24.7 0.5 copy-done
  25.3 2.2 %weights.1 = (bf16[512,1024]{1,0:T(8,128)(2,1)S(1)}, bf16[512,1024]{1,0:T(8,128)(2,1)S(1)}, f32[8,128]{1,0:T(8,128)S(1)}) custom-call(s32[1,8]{1,0:T(1,128)S(1)} %copy-done, s32[1]{0:T(128)S(6)} %copy.18.refs_1_, bf16[1,8,128,128]{3,2,1,0:T(8,128)(2,1)S(1)} %get-tuple-element.108.refs_2_, bf16[128,1024]{1,0:T(8,128)(2,1)S(1)} %get-tuple-element.123.refs_3_, ...), custom_call_target="tpu_custom_call" | custom-call | bytes 3670052 | tf_op jit(solution)/shard_map/weights/pallas_call | solution.py:79
  27.4 1.4 %collective-permute-start.11 = (bf16[512,1024]{1,0:T(8,128)(2,1)S(1)}, bf16[512,1024]{1,0:T(8,128)(2,1)S(1)}, u32[]{:S(2)}, u32[]{:S(2)}) collective-permute-start(bf16[512,1024]{1,0:T(8,128)(2,1)S(1)} %get-tuple-element.139), channel_id=1, source_target_pairs={{0,2},{2,0},{1,3},{3,1},{4,6},{6,4},{5,7},{7,5},{8,10},{10,8},{9,1... | collective-permute-start | bytes 3145736 | tf_op jit(solution)/shard_map/ppermute | solution.py:34
  28.9 2.6 %collective-permute-done.12.refs_1_ = bf16[1152,128]{1,0:T(8,128)(2,1)S(1)} collective-permute-done((bf16[1152,128]{1,0:T(8,128)(2,1)S(1)}, bf16[1152,128]{1,0:T(8,128)(2,1)S(1)}, u32[]{:S(2)}, u32[]{:S(2)}) %collective-permute-start.12) | collective-permute-done | bytes 294944 | tf_op jit(solution)/shard_map/ppermute | solution.py:44
  31.5 0.1 collective-permute-start.17
  31.6 0.1 collective-permute-start.18
  31.7 0.2 core_sum.1
  32.0 0.5 collective-permute-start.15
  32.5 2.8 %collective-permute-start.16 = (bf16[128,1024]{1,0:T(8,128)(2,1)S(1)}, bf16[128,1024]{1,0:T(8,128)(2,1)S(1)}, u32[]{:S(2)}, u32[]{:S(2)}) collective-permute-start(bf16[128,1024]{1,0:T(8,128)(2,1)S(1)} %get-tuple-element.151), channel_id=1, source_target_pairs={{0,8},{4,12},{8,0},{12,4},{1,9},{5,13},{9,1},{13,5},{2,10},{6,14},... | collective-permute-start | bytes 786440 | tf_op jit(solution)/shard_map/ppermute | solution.py:34
  35.3 2.0 %shares.1 = (bf16[384,512]{1,0:T(8,128)(2,1)S(1)}, bf16[128,512]{1,0:T(8,128)(2,1)S(1)}, f32[256,512]{1,0:T(8,128)S(1)}, f32[128,512]{1,0:T(8,128)S(1)}, f32[8,128]{1,0:T(8,128)S(1)}) custom-call(s32[1,8]{1,0:T(1,128)S(1)} %copy-done, s32[1]{0:T(128)S(6)} %copy.18.refs_1_, bf16[1,8,128,128]{3,2,1,0:T(8,128)(2,1)S(1)} %get-tuple-element.108.refs_2_, ...), custom_call_target="tpu_custom_call" | custom-call | bytes 2883620 | tf_op jit(solution)/shard_map/shares/pallas_call | solution.py:79
  37.3 2.6 %collective-permute-start.14 = (bf16[384,512]{1,0:T(8,128)(2,1)S(1)}, bf16[384,512]{1,0:T(8,128)(2,1)S(1)}, u32[]{:S(2)}, u32[]{:S(2)}) collective-permute-start(bf16[384,512]{1,0:T(8,128)(2,1)S(1)} %get-tuple-element.148), channel_id=1, source_target_pairs={{0,2},{2,0},{1,3},{3,1},{4,6},{6,4},{5,7},{7,5},{8,10},{10,8},{9,1... | collective-permute-start | bytes 1179656 | tf_op jit(solution)/shard_map/ppermute | solution.py:34
  39.9 6.2 %attention_near.1 = (f32[2,128,512]{2,1,0:T(8,128)S(1)}, f32[2,1024,128]{2,1,0:T(8,128)S(1)}, f32[8,128]{1,0:T(8,128)S(1)}) custom-call(bf16[2,1152,128]{2,1,0:T(8,128)(2,1)S(1)} %get-tuple-element.152.refs_0_, bf16[2,1024,128]{2,1,0:T(8,128)(2,1)S(1)} %get-tuple-element.153.refs_1_, f32[8,128]{1,0:T(8,128)S(1)} %get-tuple-element.154.refs_2_), custom_call_target="tpu_custom_call" | custom-call | flops 1342177280 | bytes 2686976 | tf_op jit(solution)/shard_map/attention_near/pallas_call | solution.py:79
  46.1 6.2 %attention_far.1 = (f32[2,128,512]{2,1,0:T(8,128)S(1)}, f32[2,1024,128]{2,1,0:T(8,128)S(1)}, f32[8,128]{1,0:T(8,128)S(1)}) custom-call(bf16[2,1152,128]{2,1,0:T(8,128)(2,1)S(1)} %collective-permute-done.17.refs_0_, bf16[2,1024,128]{2,1,0:T(8,128)(2,1)S(1)} %collective-permute-done.18.refs_1_, f32[8,128]{1,0:T(8,128)S(1)} %get-tuple-element.155.refs_2_), custom_call_target="tpu_custom_call" | custom-call | flops 1342177280 | bytes 2686976 | tf_op jit(solution)/shard_map/attention_far/pallas_call | solution.py:79
  52.3 0.1 core_split.1
  52.4 2.6 %collective-permute-start.19 = (bf16[128,1024]{1,0:T(8,128)(2,1)S(1)}, bf16[128,1024]{1,0:T(8,128)(2,1)S(1)}, u32[]{:S(2)}, u32[]{:S(2)}) collective-permute-start(bf16[128,1024]{1,0:T(8,128)(2,1)S(1)} %get-tuple-element.158), channel_id=1, source_target_pairs={{0,2},{2,0},{1,3},{3,1},{4,6},{6,4},{5,7},{7,5},{8,10},{10,8},{9,1... | collective-permute-start | bytes 786440 | tf_op jit(solution)/shard_map/ppermute | solution.py:34
  55.0 1.2 %collective-permute-done.19.refs_1_ = bf16[128,1024]{1,0:T(8,128)(2,1)S(1)} collective-permute-done((bf16[128,1024]{1,0:T(8,128)(2,1)S(1)}, bf16[128,1024]{1,0:T(8,128)(2,1)S(1)}, u32[]{:S(2)}, u32[]{:S(2)}) %collective-permute-start.19) | collective-permute-done | bytes 262176 | tf_op jit(solution)/shard_map/ppermute | solution.py:34
  56.2 4.4 %collective-permute-start.22 = (bf16[128,1024]{1,0:T(8,128)(2,1)S(1)}, bf16[128,1024]{1,0:T(8,128)(2,1)S(1)}, u32[]{:S(2)}, u32[]{:S(2)}) collective-permute-start(bf16[128,1024]{1,0:T(8,128)(2,1)S(1)} %get-tuple-element.164.refs_0_), channel_id=1, source_target_pairs={{0,32},{2,98},{32,0},{34,66},{64,96},{66,34},{96,64},{98,2},{1,33}... | collective-permute-start | bytes 786440 | tf_op jit(solution)/shard_map/ppermute | solution.py:44
  60.6 4.0 %collective-permute-start.20 = (bf16[256,512]{1,0:T(8,128)(2,1)S(1)}, bf16[256,512]{1,0:T(8,128)(2,1)S(1)}, u32[]{:S(2)}, u32[]{:S(2)}) collective-permute-start(bf16[256,512]{1,0:T(8,128)(2,1)S(1)} %get-tuple-element.162), channel_id=1, source_target_pairs={{0,4},{2,126},{4,8},{6,2},{8,12},{10,6},{12,16},{14,10},{16,20},{1... | collective-permute-start | bytes 786440 | tf_op jit(solution)/shard_map/ppermute | solution.py:625
  64.6 6.1 %attention_far_keys.1 = (f32[2,128,512]{2,1,0:T(8,128)S(1)}, bf16[2,1024,128]{2,1,0:T(8,128)(2,1)S(1)}, f32[8,128]{1,0:T(8,128)S(1)}) custom-call(bf16[2,1152,128]{2,1,0:T(8,128)(2,1)S(1)} %get-tuple-element.152.refs_0_, bf16[2,1024,128]{2,1,0:T(8,128)(2,1)S(1)} %collective-permute-done.18.refs_1_, f32[2,128,512]{2,1,0:T(8,128)S(1)} %get-tuple-element.165.refs_2_, ...), custom_call_target="tpu_custom_call" | custom-call | flops 1342177280 | bytes 3735552 | tf_op jit(solution)/shard_map/attention_far_keys/pallas_call | solution.py:79
  70.7 0.1 collective-permute-start.25
  70.9 1.1 %collective-permute-start.24 = (bf16[128,1024]{1,0:T(8,128)(2,1)S(1)}, bf16[128,1024]{1,0:T(8,128)(2,1)S(1)}, u32[]{:S(2)}, u32[]{:S(2)}) collective-permute-start(bf16[128,1024]{1,0:T(8,128)(2,1)S(1)} %get-tuple-element.172.refs_0_), channel_id=1, source_target_pairs={{0,96},{2,34},{32,64},{34,2},{64,32},{66,98},{96,0},{98,66},{1,97}... | collective-permute-start | bytes 786440 | tf_op jit(solution)/shard_map/ppermute | solution.py:44
  72.1 6.2 %attention_far_queries.1 = (bf16[2,512,128]{2,1,0:T(8,128)(2,1)S(1)}, f32[2,1024,128]{2,1,0:T(8,128)S(1)}, f32[8,128]{1,0:T(8,128)S(1)}) custom-call(bf16[2,1152,128]{2,1,0:T(8,128)(2,1)S(1)} %collective-permute-done.17.refs_0_, bf16[2,1024,128]{2,1,0:T(8,128)(2,1)S(1)} %get-tuple-element.153.refs_1_, f32[2,128,512]{2,1,0:T(8,128)S(1)} %get-tuple-element.173.refs_2_, ...), custom_call_target="tpu_custom_call" | custom-call | flops 1342177280 | bytes 3997696 | tf_op jit(solution)/shard_map/attention_far_queries/pallas_call | solution.py:79
  78.5 0.9 collective-permute-start.27
  79.4 0.9 collective-permute-start.23
  80.3 1.0 collective-permute-done.23.refs_1_
  81.3 0.7 add_shares.1
  82.0 0.2 turn.1
  82.2 3.3 %collective-permute-done.27.refs_1_ = bf16[128,1024]{1,0:T(8,128)(2,1)S(1)} collective-permute-done((bf16[128,1024]{1,0:T(8,128)(2,1)S(1)}, bf16[128,1024]{1,0:T(8,128)(2,1)S(1)}, u32[]{:S(2)}, u32[]{:S(2)}) %collective-permute-start.27) | collective-permute-done | bytes 262176 | tf_op jit(solution)/shard_map/ppermute | solution.py:34
  85.6 1.8 %collective-permute-start.30 = (bf16[128,1024]{1,0:T(8,128)(2,1)S(1)}, bf16[128,1024]{1,0:T(8,128)(2,1)S(1)}, u32[]{:S(2)}, u32[]{:S(2)}) collective-permute-start(bf16[128,1024]{1,0:T(8,128)(2,1)S(1)} %get-tuple-element.191.refs_0_), channel_id=1, source_target_pairs={{0,2},{2,0},{1,3},{3,1},{4,6},{6,4},{5,7},{7,5},{8,10},{10,8},{9,1... | collective-permute-start | bytes 786440 | tf_op jit(solution)/shard_map/ppermute | solution.py:34
  87.4 2.2 %collective-permute-start.29 = (bf16[1024,128]{1,0:T(8,128)(2,1)S(1)}, bf16[1024,128]{1,0:T(8,128)(2,1)S(1)}, u32[]{:S(2)}, u32[]{:S(2)}) collective-permute-start(bf16[1024,128]{1,0:T(8,128)(2,1)S(1)} %get-tuple-element.190), channel_id=1, source_target_pairs={{0,4},{2,14},{4,0},{6,10},{8,12},{10,6},{12,8},{14,2},{1,5},{3,15}... | collective-permute-start | bytes 786440 | tf_op jit(solution)/shard_map/ppermute | solution.py:44
  89.7 1.2 %collective-permute-start.34 = (bf16[256,1024]{1,0:T(8,128)(2,1)S(1)}, bf16[256,1024]{1,0:T(8,128)(2,1)S(1)}, u32[]{:S(2)}, u32[]{:S(2)}) collective-permute-start(bf16[256,1024]{1,0:T(8,128)(2,1)S(1)} %get-tuple-element.204.refs_0_), channel_id=1, source_target_pairs={{0,4},{2,14},{4,8},{6,2},{8,12},{10,6},{12,0},{14,10},{1,5},{3,15}... | collective-permute-start | bytes 1572872 | tf_op jit(solution)/shard_map/ppermute | solution.py:49
  90.9 1.7 %collective-permute-start.28 = (bf16[512,128]{1,0:T(8,128)(2,1)S(1)}, bf16[512,128]{1,0:T(8,128)(2,1)S(1)}, u32[]{:S(2)}, u32[]{:S(2)}) collective-permute-start(bf16[512,128]{1,0:T(8,128)(2,1)S(1)} %get-tuple-element.189), channel_id=1, source_target_pairs={{0,32},{2,98},{32,0},{34,66},{64,96},{66,34},{96,64},{98,2},{1,33}... | collective-permute-start | bytes 393224 | tf_op jit(solution)/shard_map/ppermute | solution.py:44
  92.6 1.9 %collective-permute-done.29.refs_5_ = bf16[1024,128]{1,0:T(8,128)(2,1)S(1)} collective-permute-done((bf16[1024,128]{1,0:T(8,128)(2,1)S(1)}, bf16[1024,128]{1,0:T(8,128)(2,1)S(1)}, u32[]{:S(2)}, u32[]{:S(2)}) %collective-permute-start.29) | collective-permute-done | bytes 262176 | tf_op jit(solution)/shard_map/ppermute | solution.py:44
  94.4 1.7 %collective-permute-done.28.refs_2_ = bf16[512,128]{1,0:T(8,128)(2,1)S(1)} collective-permute-done((bf16[512,128]{1,0:T(8,128)(2,1)S(1)}, bf16[512,128]{1,0:T(8,128)(2,1)S(1)}, u32[]{:S(2)}, u32[]{:S(2)}) %collective-permute-start.28) | collective-permute-done | bytes 131104 | tf_op jit(solution)/shard_map/ppermute | solution.py:44
  96.2 0.1 back.1
  96.4 1.5 %collective-permute-start.35 = (bf16[128,1024]{1,0:T(8,128)(2,1)S(1)}, bf16[128,1024]{1,0:T(8,128)(2,1)S(1)}, u32[]{:S(2)}, u32[]{:S(2)}) collective-permute-start(bf16[128,1024]{1,0:T(8,128)(2,1)S(1)} %get-tuple-element.191.refs_0_), channel_id=1, source_target_pairs={{0,8},{4,12},{8,0},{12,4},{1,9},{5,13},{9,1},{13,5},{2,10},{6,14},... | collective-permute-start | bytes 786440 | tf_op jit(solution)/shard_map/ppermute | solution.py:34
  97.9 0.3 collective-permute-start.33
  98.2 0.6 collective-permute-start.31
  98.8 0.9 collective-permute-done.31.refs_1_
  99.8 4.3 %collective-permute-done.33.refs_2_ = bf16[768,128]{1,0:T(8,128)(2,1)S(1)} collective-permute-done((bf16[768,128]{1,0:T(8,128)(2,1)S(1)}, bf16[768,128]{1,0:T(8,128)(2,1)S(1)}, u32[]{:S(2)}, u32[]{:S(2)}) %collective-permute-start.33) | collective-permute-done | bytes 196640 | tf_op jit(solution)/shard_map/ppermute | solution.py:34
  104.1 0.8 place.1
  104.9 1.1 collective-permute-done.35.refs_1_
  106.1 1.0 collective-permute-start.36
  107.1 1.9 %collective-permute-done.36.refs_2_ = bf16[384,1024]{1,0:T(8,128)(2,1)S(1)} collective-permute-done((bf16[384,1024]{1,0:T(8,128)(2,1)S(1)}, bf16[384,1024]{1,0:T(8,128)(2,1)S(1)}, u32[]{:S(2)}, u32[]{:S(2)}) %collective-permute-start.36) | collective-permute-done | bytes 786464 | tf_op jit(solution)/shard_map/ppermute | solution.py:34
  109.0 2.3 %final.1 = (f32[512,1024]{1,0:T(8,128)}, f32[512,1024]{1,0:T(8,128)}, f32[8,128]{1,0:T(8,128)}) custom-call(bf16[256,1024]{1,0:T(8,128)(2,1)S(1)} %get-tuple-element.204.refs_0_, bf16[384,1024]{1,0:T(8,128)(2,1)S(1)} %get-tuple-element.206.refs_1_, bf16[384,1024]{1,0:T(8,128)(2,1)S(1)} %collective-permute-done.36.refs_2_, ...), custom_call_target="tpu_custom_call" | custom-call | bytes 6291456 | tf_op jit(solution)/shard_map/final/pallas_call | solution.py:79
  (48 shorter events, 0.9 us)
Async XLA Ops:
  0.6 7.1 %collective-permute-start.2 = (bf16[128,512]{1,0:T(8,128)(2,1)}, bf16[128,512]{1,0:T(8,128)(2,1)S(1)}, u32[]{:S(2)}, u32[]{:S(2)}) collective-permute-start(bf16[128,512]{1,0:T(8,128)(2,1)} %refs_0_.3), channel_id=1, source_target_pairs={{0,2},{2,0},{1,3},{3,1},{4,6},{6,4},{5,7},{7,5},{8,10},{10,8},{9,1... | collective-permute-start | bytes 393224 | tf_op jit(solution)/shard_map/ppermute | solution.py:34
  2.1 13.7 %collective-permute-start = (bf16[128,512]{1,0:T(8,128)(2,1)}, bf16[128,512]{1,0:T(8,128)(2,1)S(1)}, u32[]{:S(2)}, u32[]{:S(2)}) collective-permute-start(bf16[128,512]{1,0:T(8,128)(2,1)} %refs_2_.1), channel_id=1, source_target_pairs={{0,1},{1,0},{2,3},{3,2},{4,5},{5,4},{6,7},{7,6},{8,9},{9,8},{10,11... | collective-permute-start | bytes 393224 | tf_op jit(solution)/shard_map/ppermute | solution.py:34
  7.2 1.3 %collective-permute-start.1 = (bf16[256,128]{1,0:T(8,128)(2,1)S(1)}, bf16[256,128]{1,0:T(8,128)(2,1)S(1)}, u32[]{:S(2)}, u32[]{:S(2)}) collective-permute-start(bf16[256,128]{1,0:T(8,128)(2,1)S(1)} %get-tuple-element.118), channel_id=1, source_target_pairs={{0,2},{2,0},{1,3},{3,1},{4,6},{6,4},{5,7},{7,5},{8,10},{10,8},{9,1... | collective-permute-start | bytes 196616 | tf_op jit(solution)/shard_map/ppermute | solution.py:34
  8.6 12.6 %collective-permute-start.10 = (bf16[512,128]{1,0:T(8,128)(2,1)S(1)}, bf16[512,128]{1,0:T(8,128)(2,1)S(1)}, u32[]{:S(2)}, u32[]{:S(2)}) collective-permute-start(bf16[512,128]{1,0:T(8,128)(2,1)S(1)} %get-tuple-element.134), channel_id=1, source_target_pairs={{0,16},{16,0},{1,17},{17,1},{2,18},{18,2},{3,19},{19,3},{4,20},{20... | collective-permute-start | bytes 393224 | tf_op jit(solution)/shard_map/ppermute | solution.py:34
  9.1 12.2 %collective-permute-start.3 = (bf16[256,512]{1,0:T(8,128)(2,1)S(1)}, bf16[256,512]{1,0:T(8,128)(2,1)S(1)}, u32[]{:S(2)}, u32[]{:S(2)}) collective-permute-start(bf16[256,512]{1,0:T(8,128)(2,1)S(1)} %get-tuple-element.125), channel_id=1, source_target_pairs={{0,4},{2,126},{4,8},{6,2},{8,12},{10,6},{12,16},{14,10},{16,20},{1... | collective-permute-start | bytes 786440 | tf_op jit(solution)/shard_map/ppermute | solution.py:512
  15.8 2.1 %copy-start.1 = (bf16[128,512]{1,0:T(8,128)(2,1)S(1)}, bf16[128,512]{1,0:T(8,128)(2,1)}, u32[]{:S(2)}) copy-start(bf16[128,512]{1,0:T(8,128)(2,1)} %refs_0_.3) | copy-start | bytes 393220
  16.5 1.3 %collective-permute-start.7 = (bf16[288,128]{1,0:T(8,128)(2,1)S(1)}, bf16[288,128]{1,0:T(8,128)(2,1)S(1)}, u32[]{:S(2)}, u32[]{:S(2)}) collective-permute-start(bf16[288,128]{1,0:T(8,128)(2,1)S(1)} %get-tuple-element.129), channel_id=1, source_target_pairs={{0,2},{2,0},{1,3},{3,1},{4,6},{6,4},{5,7},{7,5},{8,10},{10,8},{9,1... | collective-permute-start | bytes 221192 | tf_op jit(solution)/shard_map/ppermute | solution.py:34
  16.6 2.1 %collective-permute-start.9 = (bf16[256,128]{1,0:T(8,128)(2,1)S(1)}, bf16[256,128]{1,0:T(8,128)(2,1)S(1)}, u32[]{:S(2)}, u32[]{:S(2)}) collective-permute-start(bf16[256,128]{1,0:T(8,128)(2,1)S(1)} %get-tuple-element.133), channel_id=1, source_target_pairs={{0,2},{2,0},{1,3},{3,1},{4,6},{6,4},{5,7},{7,5},{8,10},{10,8},{9,1... | collective-permute-start | bytes 196616 | tf_op jit(solution)/shard_map/ppermute | solution.py:34
  17.8 6.8 %collective-permute-start.8 = (bf16[576,128]{1,0:T(8,128)(2,1)S(1)}, bf16[576,128]{1,0:T(8,128)(2,1)S(1)}, u32[]{:S(2)}, u32[]{:S(2)}) collective-permute-start(bf16[576,128]{1,0:T(8,128)(2,1)S(1)} %get-tuple-element.131), channel_id=1, source_target_pairs={{0,16},{16,0},{1,17},{17,1},{2,18},{18,2},{3,19},{19,3},{4,20},{20... | collective-permute-start | bytes 442376 | tf_op jit(solution)/shard_map/ppermute | solution.py:34
  17.9 6.8 %collective-permute-start.5 = (bf16[128,512]{1,0:T(8,128)(2,1)S(1)}, bf16[128,512]{1,0:T(8,128)(2,1)S(1)}, u32[]{:S(2)}, u32[]{:S(2)}) collective-permute-start(bf16[128,512]{1,0:T(8,128)(2,1)S(1)} %copy-done.1), channel_id=1, source_target_pairs={{0,122},{2,8},{4,126},{6,12},{8,2},{10,16},{12,6},{14,20},{16,10},... | collective-permute-start | bytes 393224 | tf_op jit(solution)/shard_map/ppermute | solution.py:492
  18.7 3.4 %collective-permute-start.6 = (bf16[288,128]{1,0:T(8,128)(2,1)S(1)}, bf16[288,128]{1,0:T(8,128)(2,1)S(1)}, u32[]{:S(2)}, u32[]{:S(2)}) collective-permute-start(bf16[288,128]{1,0:T(8,128)(2,1)S(1)} %get-tuple-element.127), channel_id=1, source_target_pairs={{0,2},{2,0},{1,3},{3,1},{4,6},{6,4},{5,7},{7,5},{8,10},{10,8},{9,1... | collective-permute-start | bytes 221192 | tf_op jit(solution)/shard_map/ppermute | solution.py:34
  21.2 7.7 %collective-permute-start.13 = (bf16[1024,128]{1,0:T(8,128)(2,1)S(1)}, bf16[1024,128]{1,0:T(8,128)(2,1)S(1)}, u32[]{:S(2)}, u32[]{:S(2)}) collective-permute-start(bf16[1024,128]{1,0:T(8,128)(2,1)S(1)} %get-tuple-element.141.refs_0_), channel_id=1, source_target_pairs={{0,4},{2,14},{4,0},{6,10},{8,12},{10,6},{12,8},{14,2},{1,5},{3,15}... | collective-permute-start | bytes 786440 | tf_op jit(solution)/shard_map/ppermute | solution.py:44
  21.3 3.4 %collective-permute-start.4 = (bf16[256,512]{1,0:T(8,128)(2,1)S(1)}, bf16[256,512]{1,0:T(8,128)(2,1)S(1)}, u32[]{:S(2)}, u32[]{:S(2)}) collective-permute-start(bf16[256,512]{1,0:T(8,128)(2,1)S(1)} %collective-permute-done.3.refs_7_), channel_id=1, source_target_pairs={{0,2},{2,0},{1,3},{3,1},{4,6},{6,4},{5,7},{7,5},{8,10},{10,8},{9,1... | collective-permute-start | bytes 786440 | tf_op jit(solution)/shard_map/ppermute | solution.py:34
  24.6 0.7 copy-start
  24.6 6.9 %collective-permute-start.12 = (bf16[1152,128]{1,0:T(8,128)(2,1)S(1)}, bf16[1152,128]{1,0:T(8,128)(2,1)S(1)}, u32[]{:S(2)}, u32[]{:S(2)}) collective-permute-start(bf16[1152,128]{1,0:T(8,128)(2,1)S(1)} %get-tuple-element.140.refs_0_), channel_id=1, source_target_pairs={{0,32},{2,98},{32,0},{34,66},{64,96},{66,34},{96,64},{98,2},{1,33}... | collective-permute-start | bytes 884744 | tf_op jit(solution)/shard_map/ppermute | solution.py:44
  27.4 4.3 %collective-permute-start.11 = (bf16[512,1024]{1,0:T(8,128)(2,1)S(1)}, bf16[512,1024]{1,0:T(8,128)(2,1)S(1)}, u32[]{:S(2)}, u32[]{:S(2)}) collective-permute-start(bf16[512,1024]{1,0:T(8,128)(2,1)S(1)} %get-tuple-element.139), channel_id=1, source_target_pairs={{0,2},{2,0},{1,3},{3,1},{4,6},{6,4},{5,7},{7,5},{8,10},{10,8},{9,1... | collective-permute-start | bytes 3145736 | tf_op jit(solution)/shard_map/ppermute | solution.py:34
  31.5 14.5 %collective-permute-start.17 = (bf16[2,1152,128]{2,1,0:T(8,128)(2,1)S(1)}, bf16[2,1152,128]{2,1,0:T(8,128)(2,1)S(1)}, u32[]{:S(2)}, u32[]{:S(2)}) collective-permute-start(bf16[2,1152,128]{2,1,0:T(8,128)(2,1)S(1)} %get-tuple-element.152.refs_0_), channel_id=1, source_target_pairs={{0,96},{2,34},{32,64},{34,2},{64,32},{66,98},{96,0},{98,66},{1,97}... | collective-permute-start | bytes 1769480 | tf_op jit(solution)/shard_map/ppermute | solution.py:44
  31.6 14.4 %collective-permute-start.18 = (bf16[2,1024,128]{2,1,0:T(8,128)(2,1)S(1)}, bf16[2,1024,128]{2,1,0:T(8,128)(2,1)S(1)}, u32[]{:S(2)}, u32[]{:S(2)}) collective-permute-start(bf16[2,1024,128]{2,1,0:T(8,128)(2,1)S(1)} %get-tuple-element.153.refs_1_), channel_id=1, source_target_pairs={{0,12},{2,6},{4,8},{6,2},{8,4},{10,14},{12,0},{14,10},{1,13},{3,7}... | collective-permute-start | bytes 1572872 | tf_op jit(solution)/shard_map/ppermute | solution.py:44
  32.0 20.3 %collective-permute-start.15 = (bf16[256,1024]{1,0:T(8,128)(2,1)S(1)}, bf16[256,1024]{1,0:T(8,128)(2,1)S(1)}, u32[]{:S(2)}, u32[]{:S(2)}) collective-permute-start(bf16[256,1024]{1,0:T(8,128)(2,1)S(1)} %get-tuple-element.150), channel_id=1, source_target_pairs={{0,4},{2,14},{4,8},{6,2},{8,12},{10,6},{12,0},{14,10},{1,5},{3,15}... | collective-permute-start | bytes 1572872 | tf_op jit(solution)/shard_map/ppermute | solution.py:49
  32.5 19.8 %collective-permute-start.16 = (bf16[128,1024]{1,0:T(8,128)(2,1)S(1)}, bf16[128,1024]{1,0:T(8,128)(2,1)S(1)}, u32[]{:S(2)}, u32[]{:S(2)}) collective-permute-start(bf16[128,1024]{1,0:T(8,128)(2,1)S(1)} %get-tuple-element.151), channel_id=1, source_target_pairs={{0,8},{4,12},{8,0},{12,4},{1,9},{5,13},{9,1},{13,5},{2,10},{6,14},... | collective-permute-start | bytes 786440 | tf_op jit(solution)/shard_map/ppermute | solution.py:34
  37.3 23.3 %collective-permute-start.14 = (bf16[384,512]{1,0:T(8,128)(2,1)S(1)}, bf16[384,512]{1,0:T(8,128)(2,1)S(1)}, u32[]{:S(2)}, u32[]{:S(2)}) collective-permute-start(bf16[384,512]{1,0:T(8,128)(2,1)S(1)} %get-tuple-element.148), channel_id=1, source_target_pairs={{0,2},{2,0},{1,3},{3,1},{4,6},{6,4},{5,7},{7,5},{8,10},{10,8},{9,1... | collective-permute-start | bytes 1179656 | tf_op jit(solution)/shard_map/ppermute | solution.py:34
  52.4 3.8 %collective-permute-start.19 = (bf16[128,1024]{1,0:T(8,128)(2,1)S(1)}, bf16[128,1024]{1,0:T(8,128)(2,1)S(1)}, u32[]{:S(2)}, u32[]{:S(2)}) collective-permute-start(bf16[128,1024]{1,0:T(8,128)(2,1)S(1)} %get-tuple-element.158), channel_id=1, source_target_pairs={{0,2},{2,0},{1,3},{3,1},{4,6},{6,4},{5,7},{7,5},{8,10},{10,8},{9,1... | collective-permute-start | bytes 786440 | tf_op jit(solution)/shard_map/ppermute | solution.py:34
  56.2 14.6 %collective-permute-start.22 = (bf16[128,1024]{1,0:T(8,128)(2,1)S(1)}, bf16[128,1024]{1,0:T(8,128)(2,1)S(1)}, u32[]{:S(2)}, u32[]{:S(2)}) collective-permute-start(bf16[128,1024]{1,0:T(8,128)(2,1)S(1)} %get-tuple-element.164.refs_0_), channel_id=1, source_target_pairs={{0,32},{2,98},{32,0},{34,66},{64,96},{66,34},{96,64},{98,2},{1,33}... | collective-permute-start | bytes 786440 | tf_op jit(solution)/shard_map/ppermute | solution.py:44
  60.6 11.4 %collective-permute-start.20 = (bf16[256,512]{1,0:T(8,128)(2,1)S(1)}, bf16[256,512]{1,0:T(8,128)(2,1)S(1)}, u32[]{:S(2)}, u32[]{:S(2)}) collective-permute-start(bf16[256,512]{1,0:T(8,128)(2,1)S(1)} %get-tuple-element.162), channel_id=1, source_target_pairs={{0,4},{2,126},{4,8},{6,2},{8,12},{10,6},{12,16},{14,10},{16,20},{1... | collective-permute-start | bytes 786440 | tf_op jit(solution)/shard_map/ppermute | solution.py:625
  64.6 7.5 %collective-permute-start.21 = (bf16[128,512]{1,0:T(8,128)(2,1)S(1)}, bf16[128,512]{1,0:T(8,128)(2,1)S(1)}, u32[]{:S(2)}, u32[]{:S(2)}) collective-permute-start(bf16[128,512]{1,0:T(8,128)(2,1)S(1)} %get-tuple-element.163), channel_id=1, source_target_pairs={{0,122},{2,8},{4,126},{6,12},{8,2},{10,16},{12,6},{14,20},{16,10},... | collective-permute-start | bytes 393224 | tf_op jit(solution)/shard_map/ppermute | solution.py:625
  70.7 11.2 %collective-permute-start.25 = (bf16[2,1024,128]{2,1,0:T(8,128)(2,1)S(1)}, bf16[2,1024,128]{2,1,0:T(8,128)(2,1)S(1)}, u32[]{:S(2)}, u32[]{:S(2)}) collective-permute-start(bf16[2,1024,128]{2,1,0:T(8,128)(2,1)S(1)} %get-tuple-element.181), channel_id=1, source_target_pairs={{0,12},{2,6},{4,8},{6,2},{8,4},{10,14},{12,0},{14,10},{1,13},{3,7}... | collective-permute-start | bytes 1572872 | tf_op jit(solution)/shard_map/ppermute | solution.py:44
  70.9 7.5 %collective-permute-start.24 = (bf16[128,1024]{1,0:T(8,128)(2,1)S(1)}, bf16[128,1024]{1,0:T(8,128)(2,1)S(1)}, u32[]{:S(2)}, u32[]{:S(2)}) collective-permute-start(bf16[128,1024]{1,0:T(8,128)(2,1)S(1)} %get-tuple-element.172.refs_0_), channel_id=1, source_target_pairs={{0,96},{2,34},{32,64},{34,2},{64,32},{66,98},{96,0},{98,66},{1,97}... | collective-permute-start | bytes 786440 | tf_op jit(solution)/shard_map/ppermute | solution.py:44
  78.5 7.1 %collective-permute-start.27 = (bf16[128,1024]{1,0:T(8,128)(2,1)S(1)}, bf16[128,1024]{1,0:T(8,128)(2,1)S(1)}, u32[]{:S(2)}, u32[]{:S(2)}) collective-permute-start(bf16[128,1024]{1,0:T(8,128)(2,1)S(1)} %get-tuple-element.186.refs_0_), channel_id=1, source_target_pairs={{0,16},{16,0},{1,17},{17,1},{2,18},{18,2},{3,19},{19,3},{4,20},{20... | collective-permute-start | bytes 786440 | tf_op jit(solution)/shard_map/ppermute | solution.py:34
  79.4 1.9 %collective-permute-start.23 = (bf16[128,512]{1,0:T(8,128)(2,1)S(1)}, bf16[128,512]{1,0:T(8,128)(2,1)S(1)}, u32[]{:S(2)}, u32[]{:S(2)}) collective-permute-start(bf16[128,512]{1,0:T(8,128)(2,1)S(1)} %get-tuple-element.171), channel_id=1, source_target_pairs={{0,2},{2,0},{1,3},{3,1},{4,6},{6,4},{5,7},{7,5},{8,10},{10,8},{9,1... | collective-permute-start | bytes 393224 | tf_op jit(solution)/shard_map/ppermute | solution.py:34
  80.3 9.3 %collective-permute-start.26 = (bf16[2,512,128]{2,1,0:T(8,128)(2,1)S(1)}, bf16[2,512,128]{2,1,0:T(8,128)(2,1)S(1)}, u32[]{:S(2)}, u32[]{:S(2)}) collective-permute-start(bf16[2,512,128]{2,1,0:T(8,128)(2,1)S(1)} %get-tuple-element.185), channel_id=1, source_target_pairs={{0,96},{2,34},{32,64},{34,2},{64,32},{66,98},{96,0},{98,66},{1,97}... | collective-permute-start | bytes 786440 | tf_op jit(solution)/shard_map/ppermute | solution.py:44
  85.6 4.0 %collective-permute-start.30 = (bf16[128,1024]{1,0:T(8,128)(2,1)S(1)}, bf16[128,1024]{1,0:T(8,128)(2,1)S(1)}, u32[]{:S(2)}, u32[]{:S(2)}) collective-permute-start(bf16[128,1024]{1,0:T(8,128)(2,1)S(1)} %get-tuple-element.191.refs_0_), channel_id=1, source_target_pairs={{0,2},{2,0},{1,3},{3,1},{4,6},{6,4},{5,7},{7,5},{8,10},{10,8},{9,1... | collective-permute-start | bytes 786440 | tf_op jit(solution)/shard_map/ppermute | solution.py:34
  87.4 7.0 %collective-permute-start.29 = (bf16[1024,128]{1,0:T(8,128)(2,1)S(1)}, bf16[1024,128]{1,0:T(8,128)(2,1)S(1)}, u32[]{:S(2)}, u32[]{:S(2)}) collective-permute-start(bf16[1024,128]{1,0:T(8,128)(2,1)S(1)} %get-tuple-element.190), channel_id=1, source_target_pairs={{0,4},{2,14},{4,0},{6,10},{8,12},{10,6},{12,8},{14,2},{1,5},{3,15}... | collective-permute-start | bytes 786440 | tf_op jit(solution)/shard_map/ppermute | solution.py:44
  89.7 16.4 %collective-permute-start.34 = (bf16[256,1024]{1,0:T(8,128)(2,1)S(1)}, bf16[256,1024]{1,0:T(8,128)(2,1)S(1)}, u32[]{:S(2)}, u32[]{:S(2)}) collective-permute-start(bf16[256,1024]{1,0:T(8,128)(2,1)S(1)} %get-tuple-element.204.refs_0_), channel_id=1, source_target_pairs={{0,4},{2,14},{4,8},{6,2},{8,12},{10,6},{12,0},{14,10},{1,5},{3,15}... | collective-permute-start | bytes 1572872 | tf_op jit(solution)/shard_map/ppermute | solution.py:49
  90.9 5.3 %collective-permute-start.28 = (bf16[512,128]{1,0:T(8,128)(2,1)S(1)}, bf16[512,128]{1,0:T(8,128)(2,1)S(1)}, u32[]{:S(2)}, u32[]{:S(2)}) collective-permute-start(bf16[512,128]{1,0:T(8,128)(2,1)S(1)} %get-tuple-element.189), channel_id=1, source_target_pairs={{0,32},{2,98},{32,0},{34,66},{64,96},{66,34},{96,64},{98,2},{1,33}... | collective-permute-start | bytes 393224 | tf_op jit(solution)/shard_map/ppermute | solution.py:44
  96.3 1.6 %collective-permute-start.32 = (bf16[384,128]{1,0:T(8,128)(2,1)S(1)}, bf16[384,128]{1,0:T(8,128)(2,1)S(1)}, u32[]{:S(2)}, u32[]{:S(2)}) collective-permute-start(bf16[384,128]{1,0:T(8,128)(2,1)S(1)} %get-tuple-element.197), channel_id=1, source_target_pairs={{0,2},{2,0},{1,3},{3,1},{4,6},{6,4},{5,7},{7,5},{8,10},{10,8},{9,1... | collective-permute-start | bytes 294920 | tf_op jit(solution)/shard_map/ppermute | solution.py:34
  96.4 9.6 %collective-permute-start.35 = (bf16[128,1024]{1,0:T(8,128)(2,1)S(1)}, bf16[128,1024]{1,0:T(8,128)(2,1)S(1)}, u32[]{:S(2)}, u32[]{:S(2)}) collective-permute-start(bf16[128,1024]{1,0:T(8,128)(2,1)S(1)} %get-tuple-element.191.refs_0_), channel_id=1, source_target_pairs={{0,8},{4,12},{8,0},{12,4},{1,9},{5,13},{9,1},{13,5},{2,10},{6,14},... | collective-permute-start | bytes 786440 | tf_op jit(solution)/shard_map/ppermute | solution.py:34
  97.9 6.2 %collective-permute-start.33 = (bf16[768,128]{1,0:T(8,128)(2,1)S(1)}, bf16[768,128]{1,0:T(8,128)(2,1)S(1)}, u32[]{:S(2)}, u32[]{:S(2)}) collective-permute-start(bf16[768,128]{1,0:T(8,128)(2,1)S(1)} %get-tuple-element.199), channel_id=1, source_target_pairs={{0,16},{16,0},{1,17},{17,1},{2,18},{18,2},{3,19},{19,3},{4,20},{20... | collective-permute-start | bytes 589832 | tf_op jit(solution)/shard_map/ppermute | solution.py:34
  98.2 1.6 %collective-permute-start.31 = (bf16[384,128]{1,0:T(8,128)(2,1)S(1)}, bf16[384,128]{1,0:T(8,128)(2,1)S(1)}, u32[]{:S(2)}, u32[]{:S(2)}) collective-permute-start(bf16[384,128]{1,0:T(8,128)(2,1)S(1)} %get-tuple-element.195), channel_id=1, source_target_pairs={{0,2},{2,0},{1,3},{3,1},{4,6},{6,4},{5,7},{7,5},{8,10},{10,8},{9,1... | collective-permute-start | bytes 294920 | tf_op jit(solution)/shard_map/ppermute | solution.py:34
  106.1 3.0 %collective-permute-start.36 = (bf16[384,1024]{1,0:T(8,128)(2,1)S(1)}, bf16[384,1024]{1,0:T(8,128)(2,1)S(1)}, u32[]{:S(2)}, u32[]{:S(2)}) collective-permute-start(bf16[384,1024]{1,0:T(8,128)(2,1)S(1)} %get-tuple-element.206.refs_1_), channel_id=1, source_target_pairs={{0,2},{2,0},{1,3},{3,1},{4,6},{6,4},{5,7},{7,5},{8,10},{10,8},{9,1... | collective-permute-start | bytes 2359304 | tf_op jit(solution)/shard_map/ppermute | solution.py:34

commit v4 on v3

--- a/solution.py
+++ b/solution.py
@@ -44,13 +44,29 @@
     return lax.ppermute(value, (axis, "c"), pairs)
 
 
-def x_near(value):
-    pairs = [(2 * i + c, 2 * ((i + (1 if c == 0 else 3)) % 4) + c) for i in range(4) for c in range(2)]
-    return lax.ppermute(value, ("x", "c"), pairs)
-
-
-def x_far(value):
-    return swap(value, "x", 2)
+def ring_place():
+    return jnp.where(lax.axis_index("c") == 0, lax.axis_index("x"), lax.axis_index("z"))
+
+
+def ring(value, to_first, to_second):
+    pairs = []
+    for z in range(4):
+        for x in range(4):
+            pairs.append((8 * z + 2 * x, 8 * to_first[1][z] + 2 * to_first[0][x]))
+            pairs.append((8 * z + 2 * x + 1, 8 * to_second[1][z] + 2 * to_second[0][x] + 1))
+    return lax.ppermute(value, ("z", "x", "c"), pairs)
+
+
+STAY = (0, 1, 2, 3)
+
+
+def around(value, steps):
+    turn = tuple((i + steps) % 4 for i in range(4))
+    return ring(value, (turn, STAY), (STAY, turn))
+
+
+def across(value, step):
+    return ring(value, (STAY, NEXT[step]), (NEXT[step], STAY))
 
 
 def place_in_group():
@@ -61,7 +77,7 @@
     def __init__(self):
         self.token = None
 
-    def call(self, kernel, outs, *args, scratch=(), smem=0, anywhere=0, flops=0, name=None):
+    def call(self, kernel, outs, *args, scratch=(), smem=0, anywhere=0, aliases={}, flops=0, name=None):
         count, first = len(args), self.token is None
         tokens = [] if first else [self.token]
         results = len(outs)
@@ -82,6 +98,7 @@
             in_specs=specs,
             out_specs=[pl.BlockSpec(memory_space=pltpu.VMEM)] * (results + 1),
             scratch_shapes=list(scratch),
+            input_output_aliases=aliases,
             cost_estimate=pl.CostEstimate(flops=flops, bytes_accessed=size, transcendentals=0),
             compiler_params=pltpu.CompilerParams(vmem_limit_bytes=VMEM_LIMIT),
             name=name,
@@ -270,7 +287,7 @@
     return block.astype(F32).T.astype(BF16)
 
 
-def attention_kernel(has_dq, has_dkv, dq_last, dkv_last, qdo, kv, *refs):
+def attention_kernel(first, count, has_dq, has_dkv, dq_last, dkv_last, qdo, kv, *refs):
     if has_dq:
         dq_in, refs = refs[0], refs[1:]
     if has_dkv:
@@ -279,13 +296,20 @@
     for i in range(2):
         unpack_rows(qdo.at[i, 0 : Q_ROWS // 2], 0.125, query.at[i], logs.at[i])
         unpack_rows(qdo.at[i, Q_ROWS // 2 : Q_ROWS], 1.0, grad.at[i], spread.at[i])
-        keys_t[i] = turned(kv[i, 0:GROUP])
-    dq[...] = dq_in[...] if has_dq else jnp.zeros_like(dq)
-    dkv[...] = dkv_in[...] if has_dkv else jnp.zeros_like(dkv)
-
-    @pl.loop(0, 4)
+    for k in range(first, first + count):
+        keys_t[k] = turned(kv[k, 0:GROUP])
+    if not dq_last:
+        dq = dq_out
+    if not dkv_last:
+        dkv = dkv_out
+    if dq_last or not has_dq:
+        dq[...] = dq_in[...] if has_dq else jnp.zeros_like(dq)
+    if dkv_last or not has_dkv:
+        dkv[...] = dkv_in[...] if has_dkv else jnp.zeros_like(dkv)
+
+    @pl.loop(0, 2 * count)
     def _(step):
-        i, k = step % 2, step // 2
+        i, k = step % 2, first + step // 2
         tile_step(
             kv[k, 0:GROUP],
             kv[k, GROUP : 2 * GROUP],
@@ -302,9 +326,8 @@
     if dq_last:
         for i in range(2):
             dq_out[i] = (dq[i].T * 0.125).astype(dq_out.dtype)
-    else:
-        dq_out[...] = dq[...]
-    dkv_out[...] = dkv[...].astype(dkv_out.dtype)
+    if dkv_last:
+        dkv_out[...] = dkv[...].astype(dkv_out.dtype)
 
 
 SLOW = 10**10
@@ -317,12 +340,23 @@
 TILE_FLOPS = 2 * 10 * GROUP * GROUP * 64
 
 
-def attention(order, name, qdo, kv, dq, dkv, dq_last=None, dkv_last=None):
+def attention(order, name, qdo, kv, dq, dkv, dq_last=None, dkv_last=None, first=0, count=2):
     carry = [a for a in (dq, dkv) if a is not None]
     dq_shape = (2, LANES, GROUP) if dq_last is None else (2, GROUP, LANES)
+    aliases = {}
+    if dq is not None and dq_last is None:
+        aliases[2] = 0
+    if dkv is not None and dkv_last is None:
+        aliases[1 + len(carry)] = 1
     return order.call(
         functools.partial(
-            attention_kernel, dq is not None, dkv is not None, dq_last is not None, dkv_last is not None
+            attention_kernel,
+            first,
+            count,
+            dq is not None,
+            dkv is not None,
+            dq_last is not None,
+            dkv_last is not None,
         ),
         [shaped(dq_shape, dq_last or F32), shaped((2, KV_ROWS, LANES), dkv_last or F32)],
         qdo,
@@ -337,7 +371,8 @@
             pltpu.VMEM((2, LANES, GROUP), F32),
             pltpu.VMEM((2, KV_ROWS, LANES), F32),
         ],
-        flops=4 * TILE_FLOPS,
+        aliases=aliases,
+        flops=2 * count * TILE_FLOPS,
         name="attention_" + name,
     )
 
@@ -371,7 +406,6 @@
 
 def weights_kernel(source_ref, count_ref, tiles, grad, mix_ref, own, partner, near, crossed, far, keep_ref, send_ref, window, total, left_ref):
     core = lax.axis_index("c")
-    place = lax.axis_index("x")
     window[REACH] = own[...]
     window[jnp.where(core == 0, 4, 2)] = partner[...]
     for block, first in ((near, jnp.where(core == 0, 1, 4)), (crossed, jnp.where(core == 0, 5, 0))):
@@ -388,67 +422,37 @@
     left_ref[0] = turned(mix_ref[...])
     left_ref[1] = turned(total[...].astype(BF16))
 
-    def put(out, slot, which, distance):
-        rows = pl.ds(pl.multiple_of(lax.rem(place + distance, 4) * 128, 128), 128)
-        out[slot * 128 : (slot + 1) * 128] = dot(left_ref[which, rows], grad[...], NN).astype(BF16)
-
-    for out, turn in ((keep_ref, core), (send_ref, 1 - core)):
-        ahead = jnp.where(turn == 0, 1, 3)
-        put(out, 0, 0, ahead)
-        put(out, 1, 1, ahead)
-        put(out, 2, turn, 2)
-        put(out, 3, turn, 0)
-
-
-def core_sum_kernel(keep, received, near, far, local):
-    near[...] = (keep[0:256].astype(F32) + received[0:256].astype(F32)).astype(BF16)
-    far[...] = (keep[256:384].astype(F32) + received[256:384].astype(F32)).astype(BF16)
-    local[...] = keep[384:512].astype(F32) + received[384:512].astype(F32)
-
-
-def core_split_kernel(local, near, far, send, local_out):
+    for out, which in ((keep_ref, core), (send_ref, 1 - core)):
+        out[...] = dot(left_ref[which], grad[...], NN).astype(BF16)
+
+
+def block_rows(distance):
+    return pl.ds(pl.multiple_of(lax.rem(ring_place() + distance, 4) * 128, 128), 128)
+
+
+def core_sum_kernel(keep, received, *outs):
+    for k, out in enumerate(outs):
+        rows = block_rows(k)
+        out[...] = (keep[rows].astype(F32) + received[rows].astype(F32)).astype(out.dtype)
+
+
+def gather_kernel(*refs):
+    for k, block in enumerate(refs[:4]):
+        refs[4][block_rows((4 - k) % 4)] = block[...]
+
+
+def final_kernel(own, other, first, second):
     core = lax.axis_index("c")
-    mine = pl.ds(pl.multiple_of(core * 128, 128), 128)
-    other = pl.ds(pl.multiple_of((1 - core) * 128, 128), 128)
-    send[...] = near[other]
-    local_out[...] = local[...] + near[mine].astype(F32) + far[...].astype(F32)
-
-
-def core_pack_kernel(own, received, out):
-    core = lax.axis_index("c")
-    out[pl.ds(pl.multiple_of(core * 128, 128), 128)] = own[...]
-    out[pl.ds(pl.multiple_of((1 - core) * 128, 128), 128)] = received[...]
-
-
-def core_send_kernel(near, far, out):
-    out[0:256] = near[...]
-    out[256:384] = far[...]
-
-
-def final_kernel(local, near, received, first_ref, second_ref):
-    core = lax.axis_index("c")
-    place = lax.axis_index("x")
-
-    def rows(distance):
-        return pl.ds(pl.multiple_of(lax.rem(place + distance, 4) * 128, 128), 128)
-
-    before = jnp.where(core == 0, 3, 1)
-    outs = (first_ref, second_ref)
-    for i, out in enumerate(outs):
-        block = slice(i * 128, (i + 1) * 128)
-        out[rows(0)] = local[block].astype(F32)
-        out[rows(before)] = near[block].astype(F32)
-        out[rows(4 - before)] = received[block].astype(F32)
 
     @pl.when(core == 0)
     def _():
-        first_ref[rows(2)] = near[256:384].astype(F32)
-        second_ref[rows(2)] = received[256:384].astype(F32)
+        first[...] = own[...].astype(F32)
+        second[...] = other[...].astype(F32)
 
     @pl.when(core == 1)
     def _():
-        second_ref[rows(2)] = near[256:384].astype(F32)
-        first_ref[rows(2)] = received[256:384].astype(F32)
+        first[...] = other[...].astype(F32)
+        second[...] = own[...].astype(F32)
 
 
 def add_kernel(*refs):
@@ -579,15 +583,14 @@
     kv_far = meet(kv_near, "x", 1)
     qdo_near = pair(order, qdo, qdo_met)
     qdo_far = meet(qdo_near, "z", 1)
-    near, far, local = order.call(
+    blocks = order.call(
         core_sum_kernel,
-        [shaped((2 * rows, 2 * columns)), shaped(wide), shaped(wide, F32)],
+        [shaped(wide, F32)] + [shaped(wide)] * 3,
         keep,
         received,
         name="core_sum",
     )
-    far, near = x_far(far), x_near(near)
-
+    blocks = [blocks[0]] + [around(blocks[k], k) for k in range(1, 4)]
     share_send, share_far, share_keep, share_local = order.call(
         share_kernel,
         [
@@ -608,12 +611,8 @@
     share_received = swap(share_send, "c", 1)
     dq_near, dkv_near = attention(order, "near", qdo_near, kv_near, None, None)
     dq_far, dkv_far = attention(order, "far", qdo_far, kv_far, None, None)
-    send, local = order.call(
-        core_split_kernel, [shaped(wide), shaped(wide, F32)], local, near, far, name="core_split"
-    )
-    received = swap(send, "c", 1)
-    part = add(order, "x", local, received)
-    received = meet(part, "z", 0)
+    part = add(order, "ring", *blocks)
+    received = across(part, 0)
     share_near, share_local = order.call(
         near_kernel,
         [shaped((2 * rows, columns)), shaped((rows, columns), F32)],
@@ -623,10 +622,15 @@
         name="near",
     )
     share_far, share_near = lax.ppermute(share_far, NODE, to_far), lax.ppermute(share_near, NODE, to_near)
-    dq_near, dkv_far = attention(order, "far_keys", qdo_near, kv_far, dq_near, dkv_far, None, BF16)
+    dq_near, dkv_far = attention(
+        order, "far_keys0", qdo_near, kv_far, dq_near, dkv_far, first=0, count=1
+    )
+    part = add(order, "across0", part, received)
+    received = across(part, 1)
+    dq_near, dkv_far = attention(
+        order, "far_keys1", qdo_near, kv_far, dq_near, dkv_far, None, BF16, first=1, count=1
+    )
     dkv_met = meet(dkv_far, "x", 1)
-    part = add(order, "z0", part, received)
-    received = meet(part, "z", 1)
     share_cross, share_local = order.call(
         cross_kernel,
         [shaped((rows, columns)), shaped((rows, columns), F32)],
@@ -637,11 +641,17 @@
         name="cross",
     )
     share_cross = swap(share_cross, "c", 1)
-    dq_far, dkv_near = attention(order, "far_queries", qdo_far, kv_near, dq_far, dkv_near, BF16, F32)
+    dq_far, dkv_near = attention(
+        order, "far_queries0", qdo_far, kv_near, dq_far, dkv_near, first=0, count=1
+    )
+    part = add(order, "across1", part, received)
+    received = swap(part, "y", 1)
+    dq_far, dkv_near = attention(
+        order, "far_queries1", qdo_far, kv_near, dq_far, dkv_near, BF16, F32, first=1, count=1
+    )
     dq_met = meet(dq_far, "z", 1)
-    part = add(order, "z1", part, received)
-    received = swap(part, "y", 1)
-    grad_features = add(order, "shares", share_local, share_cross)
+    part = add(order, "y", part, received)
+    blocks = [part] + [around(part, k) for k in range(1, 4)]
     (half,) = order.call(
         half_sum_kernel, [shaped((KV_ROWS, LANES))], dkv_near, dkv_met, name="half_dkv"
     )
@@ -649,15 +659,8 @@
     (dq_near,) = order.call(
         turn_kernel, [shaped((2, GROUP, LANES), F32)], dq_near, name="turn"
     )
-    part = add(order, "y", part, received)
-    far, received = x_far(part), swap(part, "c", 1)
     (half,) = order.call(half_sum_kernel, [shaped((GROUP, LANES))], dq_near, dq_met, name="half_dq")
     dq_last = meet(half, "z", 0)
-    (local,) = order.call(
-        core_pack_kernel, [shaped((2 * rows, 2 * columns))], part, received, name="core_pack"
-    )
-    near = x_near(local)
-
     back_own, back_near, back_through, back_cross = order.call(
         back_kernel,
         [shaped((384, LANES))] * 4,
@@ -674,18 +677,17 @@
         forward_kernel, [shaped((768, LANES))], back_through, back_cross, name="forward_back"
     )
     back_far = swap(back_forward, "y", 1)
+    (whole,) = order.call(gather_kernel, [shaped((columns, 2 * columns))], *blocks, name="gather")
+    received = swap(whole, "c", 1)
+    grad_features = add(order, "shares", share_local, share_cross)
     grad_query, grad_key, grad_value = order.call(
         place_kernel, [shaped((rows, columns))] * 3, back_own, back_near, back_far, name="place"
-    )
-    (near,) = order.call(
-        core_send_kernel, [shaped((3 * rows, 2 * columns))], near, far, name="core_send"
     )
     out_weight_grad, msg_weight_grad = order.call(
         final_kernel,
         [shaped((columns, 2 * columns), F32)] * 2,
-        local,
-        near,
-        swap(near, "c", 1),
+        whole,
+        received,
         name="final",
     )
     return (grad_features, grad_query, grad_key, grad_value, out_weight_grad, msg_weight_grad)

time: 111 us -> 106 us (0.955)
  waiting for transfers between devices: 24.3 us -> 19.9 us
    ppermute x21 -> x17, waiting for transfers between devices: 18 us -> 9.58 us  [swap(): return lax.ppermute(value, axes, [(i, i ^ mask) for i in range(count)])]
    ppermute x2 -> x8, starting transfers between devices: 1.68 us -> 8.9 us  [ring(): return lax.ppermute(value, ('z', 'x', 'c'), pairs)]
    ppermute x21 -> x17, starting transfers between devices: 25.9 us -> 20.5 us  [swap(): return lax.ppermute(value, axes, [(i, i ^ mask) for i in range(count)])]
    ppermute x10 -> x8, waiting for transfers between devices: 6.21 us -> 10.3 us  [meet(): return lax.ppermute(value, (axis, 'c'), pairs)]
    ppermute x1, starting transfers between devices: 3.95 us -> 1.24 us  [body(): lax.ppermute(share_near, NODE, to_near)]
    ppermute x1, starting transfers between devices: 0.01 us -> 1.49 us  [body(): lax.ppermute(share_far, NODE, to_far)]
    ppermute x10 -> x8, starting transfers between devices: 9.81 us -> 8.53 us  [meet(): return lax.ppermute(value, (axis, 'c'), pairs)]
  transfers between devices with their start and end apart: 37 -> 37, of which waited for: 14 -> 12; matrix products, arithmetic and copies ran while one was open for 0% -> 0% of each run, Pallas kernels for 31% -> 32%
where the time goes in v4:
time: 106 us
  starting transfers between devices  47.5 us (45%)
  Pallas kernels  36.1 us (34%)
  waiting for transfers between devices  19.9 us (19%)
  between operations  1.69 us (2%)
    pallas_call x34, Pallas kernels, call(): pl.pallas_call(whole, out_shape=[*outs, shaped((8, LANES), F32)], in_spec...  36.1 us
    ppermute x17, starting transfers between devices, swap(): return lax.ppermute(value, axes, [(i, i ^ mask) for i in range(count)])  20.5 us
    ppermute x8, waiting for transfers between devices, meet(): return lax.ppermute(value, (axis, 'c'), pairs)  10.3 us
    ppermute x17, waiting for transfers between devices, swap(): return lax.ppermute(value, axes, [(i, i ^ mask) for i in range(count)])  9.58 us
    ppermute x8, starting transfers between devices, ring(): return lax.ppermute(value, ('z', 'x', 'c'), pairs)  8.9 us
    ppermute x8, starting transfers between devices, meet(): return lax.ppermute(value, (axis, 'c'), pairs)  8.53 us
    ppermute x1, starting transfers between devices, body(): near_features = lax.ppermute(near_features, NODE, to_near)  6.74 us
  transfers between devices with their start and end apart: 37, of which 12 were waited for; matrix products, arithmetic and copies ran while one was open for 0% of the time, Pallas kernels for 32%

profile of v4, /device:TPU:1, one launch (start us, length us, event | category | flops | bytes accessed | tf_op | source)
XLA Modules:
  0.0 105.8 jit_solution(10455403497659301816)
XLA Ops:
  0.6 1.5 %collective-permute-start.2 = (bf16[128,512]{1,0:T(8,128)(2,1)}, bf16[128,512]{1,0:T(8,128)(2,1)S(1)}, u32[]{:S(2)}, u32[]{:S(2)}) collective-permute-start(bf16[128,512]{1,0:T(8,128)(2,1)} %refs_0_.3), channel_id=1, source_target_pairs={{0,2},{2,0},{1,3},{3,1},{4,6},{6,4},{5,7},{7,5},{8,10},{10,8},{9,1... | collective-permute-start | bytes 393224 | tf_op jit(solution)/shard_map/ppermute | solution.py:34
  2.1 3.0 %collective-permute-start = (bf16[128,512]{1,0:T(8,128)(2,1)}, bf16[128,512]{1,0:T(8,128)(2,1)S(1)}, u32[]{:S(2)}, u32[]{:S(2)}) collective-permute-start(bf16[128,512]{1,0:T(8,128)(2,1)} %refs_2_.1), channel_id=1, source_target_pairs={{0,1},{1,0},{2,3},{3,2},{4,5},{5,4},{6,7},{7,6},{8,9},{9,8},{10,11... | collective-permute-start | bytes 393224 | tf_op jit(solution)/shard_map/ppermute | solution.py:34
  5.1 2.0 %load.1 = (bf16[128,512]{1,0:T(8,128)(2,1)S(1)}, bf16[1,8,128,128]{3,2,1,0:T(8,128)(2,1)S(1)}, bf16[128,512]{1,0:T(8,128)(2,1)S(1)}, bf16[128,512]{1,0:T(8,128)(...) custom-call(bf16[128,512]{1,0:T(8,128)(2,1)} %refs_0_.3, ...), custom_call_target="tpu_custom_call" | custom-call | bytes 6299648 | tf_op jit(solution)/shard_map/load/pallas_call | solution.py:95
  7.2 0.4 collective-permute-start.1
  7.7 0.9 collective-permute-done.1.refs_1_
  8.6 0.5 collective-permute-start.10
  9.1 6.7 %collective-permute-start.3 = (bf16[256,512]{1,0:T(8,128)(2,1)S(1)}, bf16[256,512]{1,0:T(8,128)(2,1)S(1)}, u32[]{:S(2)}, u32[]{:S(2)}) collective-permute-start(bf16[256,512]{1,0:T(8,128)(2,1)S(1)} %get-tuple-element.127), channel_id=1, source_target_pairs={{0,4},{2,126},{4,8},{6,2},{8,12},{10,6},{12,16},{14,10},{16,20},{1... | collective-permute-start | bytes 786440 | tf_op jit(solution)/shard_map/ppermute | solution.py:516
  15.8 0.6 mix.1
  16.5 0.1 collective-permute-start.7
  16.5 0.5 collective-permute-start.9
  17.0 0.8 collective-permute-done.7.refs_1_
  17.8 0.1 collective-permute-start.8
  18.7 2.5 %collective-permute-start.6 = (bf16[288,128]{1,0:T(8,128)(2,1)S(1)}, bf16[288,128]{1,0:T(8,128)(2,1)S(1)}, u32[]{:S(2)}, u32[]{:S(2)}) collective-permute-start(bf16[288,128]{1,0:T(8,128)(2,1)S(1)} %get-tuple-element.129), channel_id=1, source_target_pairs={{0,2},{2,0},{1,3},{3,1},{4,6},{6,4},{5,7},{7,5},{8,10},{10,8},{9,1... | collective-permute-start | bytes 221192 | tf_op jit(solution)/shard_map/ppermute | solution.py:34
  21.3 0.7 collective-permute-start.4
  22.0 0.1 collective-permute-done.6.refs_1_
  22.1 2.5 %collective-permute-done.8.refs_2_ = bf16[576,128]{1,0:T(8,128)(2,1)S(1)} collective-permute-done((bf16[576,128]{1,0:T(8,128)(2,1)S(1)}, bf16[576,128]{1,0:T(8,128)(2,1)S(1)}, u32[]{:S(2)}, u32[]{:S(2)}) %collective-permute-start.8) | collective-permute-done | bytes 147488 | tf_op jit(solution)/shard_map/ppermute | solution.py:34
  24.6 0.1 collective-permute-start.12
  24.7 0.5 copy-done
  25.3 1.8 %weights.1 = (bf16[512,1024]{1,0:T(8,128)(2,1)S(1)}, bf16[512,1024]{1,0:T(8,128)(2,1)S(1)}, f32[8,128]{1,0:T(8,128)S(1)}) custom-call(s32[1,8]{1,0:T(1,128)S(1)} %copy-done, s32[1]{0:T(128)S(6)} %copy.28.refs_1_, bf16[1,8,128,128]{3,2,1,0:T(8,128)(2,1)S(1)} %get-tuple-element.110.refs_2_, bf16[128,1024]{1,0:T(8,128)(2,1)S(1)} %get-tuple-element.125.refs_3_, ...), custom_call_target="tpu_custom_call" | custom-call | bytes 3670052 | tf_op jit(solution)/shard_map/weights/pallas_call | solution.py:95
  27.1 1.0 collective-permute-done.13.refs_1_
  28.1 0.1 collective-permute-start.19
  28.2 1.2 %collective-permute-start.11 = (bf16[512,1024]{1,0:T(8,128)(2,1)S(1)}, bf16[512,1024]{1,0:T(8,128)(2,1)S(1)}, u32[]{:S(2)}, u32[]{:S(2)}) collective-permute-start(bf16[512,1024]{1,0:T(8,128)(2,1)S(1)} %get-tuple-element.141), channel_id=1, source_target_pairs={{0,2},{2,0},{1,3},{3,1},{4,6},{6,4},{5,7},{7,5},{8,10},{10,8},{9,1... | collective-permute-start | bytes 3145736 | tf_op jit(solution)/shard_map/ppermute | solution.py:34
  29.5 2.0 %collective-permute-done.12.refs_1_ = bf16[1152,128]{1,0:T(8,128)(2,1)S(1)} collective-permute-done((bf16[1152,128]{1,0:T(8,128)(2,1)S(1)}, bf16[1152,128]{1,0:T(8,128)(2,1)S(1)}, u32[]{:S(2)}, u32[]{:S(2)}) %collective-permute-start.12) | collective-permute-done | bytes 294944 | tf_op jit(solution)/shard_map/ppermute | solution.py:44
  31.5 0.1 collective-permute-start.18
  31.6 0.1 collective-permute-done.11.refs_1_
  31.8 0.2 core_sum.1
  32.0 1.6 %shares.1 = (bf16[384,512]{1,0:T(8,128)(2,1)S(1)}, bf16[128,512]{1,0:T(8,128)(2,1)S(1)}, f32[256,512]{1,0:T(8,128)S(1)}, f32[128,512]{1,0:T(8,128)S(1)}, f32[8,128]{1,0:T(8,128)S(1)}) custom-call(s32[1,8]{1,0:T(1,128)S(1)} %copy-done, s32[1]{0:T(128)S(6)} %copy.28.refs_1_, bf16[1,8,128,128]{3,2,1,0:T(8,128)(2,1)S(1)} %get-tuple-element.110.refs_2_, ...), custom_call_target="tpu_custom_call" | custom-call | bytes 2883620 | tf_op jit(solution)/shard_map/shares/pallas_call | solution.py:95
  33.6 1.3 %collective-permute-start.14 = (bf16[384,512]{1,0:T(8,128)(2,1)S(1)}, bf16[384,512]{1,0:T(8,128)(2,1)S(1)}, u32[]{:S(2)}, u32[]{:S(2)}) collective-permute-start(bf16[384,512]{1,0:T(8,128)(2,1)S(1)} %get-tuple-element.150), channel_id=1, source_target_pairs={{0,2},{2,0},{1,3},{3,1},{4,6},{6,4},{5,7},{7,5},{8,10},{10,8},{9,1... | collective-permute-start | bytes 1179656 | tf_op jit(solution)/shard_map/ppermute | solution.py:34
  34.9 1.1 %collective-permute-start.15 = (bf16[128,1024]{1,0:T(8,128)(2,1)S(1)}, bf16[128,1024]{1,0:T(8,128)(2,1)S(1)}, u32[]{:S(2)}, u32[]{:S(2)}) collective-permute-start(bf16[128,1024]{1,0:T(8,128)(2,1)S(1)} %get-tuple-element.152), channel_id=1, source_target_pairs={{0,4},{2,34},{4,8},{6,38},{8,12},{10,42},{12,0},{14,46},{32,36},{3... | collective-permute-start | bytes 786440 | tf_op jit(solution)/shard_map/ppermute | solution.py:57
  36.1 2.7 %collective-permute-start.16 = (bf16[128,1024]{1,0:T(8,128)(2,1)S(1)}, bf16[128,1024]{1,0:T(8,128)(2,1)S(1)}, u32[]{:S(2)}, u32[]{:S(2)}) collective-permute-start(bf16[128,1024]{1,0:T(8,128)(2,1)S(1)} %get-tuple-element.153), channel_id=1, source_target_pairs={{0,8},{2,66},{4,12},{6,70},{8,0},{10,74},{12,4},{14,78},{32,40},{3... | collective-permute-start | bytes 786440 | tf_op jit(solution)/shard_map/ppermute | solution.py:57
  38.8 1.9 %collective-permute-start.17 = (bf16[128,1024]{1,0:T(8,128)(2,1)S(1)}, bf16[128,1024]{1,0:T(8,128)(2,1)S(1)}, u32[]{:S(2)}, u32[]{:S(2)}) collective-permute-start(bf16[128,1024]{1,0:T(8,128)(2,1)S(1)} %get-tuple-element.154), channel_id=1, source_target_pairs={{0,12},{2,98},{4,0},{6,102},{8,4},{10,106},{12,8},{14,110},{32,44}... | collective-permute-start | bytes 786440 | tf_op jit(solution)/shard_map/ppermute | solution.py:57
  40.7 6.1 %attention_near.1 = (f32[2,128,512]{2,1,0:T(8,128)S(1)}, f32[2,1024,128]{2,1,0:T(8,128)S(1)}, f32[8,128]{1,0:T(8,128)S(1)}) custom-call(bf16[2,1152,128]{2,1,0:T(8,128)(2,1)S(1)} %get-tuple-element.155.refs_0_, bf16[2,1024,128]{2,1,0:T(8,128)(2,1)S(1)} %get-tuple-element.156.refs_1_, f32[8,128]{1,0:T(8,128)S(1)} %get-tuple-element.157.refs_2_), custom_call_target="tpu_custom_call" | custom-call | flops 1342177280 | bytes 2686976 | tf_op jit(solution)/shard_map/attention_near/pallas_call | solution.py:95
  46.8 6.1 %attention_far.1 = (f32[2,128,512]{2,1,0:T(8,128)S(1)}, f32[2,1024,128]{2,1,0:T(8,128)S(1)}, f32[8,128]{1,0:T(8,128)S(1)}) custom-call(bf16[2,1152,128]{2,1,0:T(8,128)(2,1)S(1)} %collective-permute-done.18.refs_0_, bf16[2,1024,128]{2,1,0:T(8,128)(2,1)S(1)} %collective-permute-done.19.refs_1_, f32[8,128]{1,0:T(8,128)S(1)} %get-tuple-element.158.refs_2_), custom_call_target="tpu_custom_call" | custom-call | flops 1342177280 | bytes 2686976 | tf_op jit(solution)/shard_map/attention_far/pallas_call | solution.py:95
  52.9 0.1 add_ring.1
  53.1 0.1 collective-permute-start.22
  53.2 1.2 %collective-permute-start.20 = (bf16[256,512]{1,0:T(8,128)(2,1)S(1)}, bf16[256,512]{1,0:T(8,128)(2,1)S(1)}, u32[]{:S(2)}, u32[]{:S(2)}) collective-permute-start(bf16[256,512]{1,0:T(8,128)(2,1)S(1)} %get-tuple-element.162), channel_id=1, source_target_pairs={{0,4},{2,126},{4,8},{6,2},{8,12},{10,6},{12,16},{14,10},{16,20},{1... | collective-permute-start | bytes 786440 | tf_op jit(solution)/shard_map/ppermute | solution.py:624
  54.5 1.5 %collective-permute-start.21 = (bf16[128,512]{1,0:T(8,128)(2,1)S(1)}, bf16[128,512]{1,0:T(8,128)(2,1)S(1)}, u32[]{:S(2)}, u32[]{:S(2)}) collective-permute-start(bf16[128,512]{1,0:T(8,128)(2,1)S(1)} %get-tuple-element.163), channel_id=1, source_target_pairs={{0,122},{2,8},{4,126},{6,12},{8,2},{10,16},{12,6},{14,20},{16,10},... | collective-permute-start | bytes 393224 | tf_op jit(solution)/shard_map/ppermute | solution.py:624
  56.0 3.1 %attention_far_keys0.1 = (f32[2,128,512]{2,1,0:T(8,128)S(1)}, f32[2,1024,128]{2,1,0:T(8,128)S(1)}, f32[8,128]{1,0:T(8,128)S(1)}) custom-call(bf16[2,1152,128]{2,1,0:T(8,128)(2,1)S(1)} %get-tuple-element.155.refs_0_, bf16[2,1024,128]{2,1,0:T(8,128)(2,1)S(1)} %collective-permute-done.19.refs_1_, ...), custom_call_target="tpu_custom_call", output_to_operand_aliasing={{0}: (2, {}), {1}: (3, {})} | custom-call | flops 671088640 | bytes 4259840 | tf_op jit(solution)/shard_map/attention_far_keys0/pallas_call | solution.py:95
  59.1 1.6 %collective-permute-start.24 = (bf16[128,1024]{1,0:T(8,128)(2,1)S(1)}, bf16[128,1024]{1,0:T(8,128)(2,1)S(1)}, u32[]{:S(2)}, u32[]{:S(2)}) collective-permute-start(bf16[128,1024]{1,0:T(8,128)(2,1)S(1)} %get-tuple-element.175.refs_0_), channel_id=1, source_target_pairs={{0,96},{2,14},{4,100},{6,10},{8,104},{10,6},{12,108},{14,2},{32,64... | collective-permute-start | bytes 786440 | tf_op jit(solution)/shard_map/ppermute | solution.py:57
  60.7 3.2 %attention_far_keys1.1 = (f32[2,128,512]{2,1,0:T(8,128)S(1)}, bf16[2,1024,128]{2,1,0:T(8,128)(2,1)S(1)}, f32[8,128]{1,0:T(8,128)S(1)}) custom-call(bf16[2,1152,128]{2,1,0:T(8,128)(2,1)S(1)} %get-tuple-element.155.refs_0_, bf16[2,1024,128]{2,1,0:T(8,128)(2,1)S(1)} %collective-permute-done.19.refs_1_, ...), custom_call_target="tpu_custom_call", output_to_operand_aliasing={{0}: (2, {})} | custom-call | flops 671088640 | bytes 3735552 | tf_op jit(solution)/shard_map/attention_far_keys1/pallas_call | solution.py:95
  63.9 0.5 collective-permute-start.29
  64.5 3.1 %attention_far_queries0.1 = (f32[2,128,512]{2,1,0:T(8,128)S(1)}, f32[2,1024,128]{2,1,0:T(8,128)S(1)}, f32[8,128]{1,0:T(8,128)S(1)}) custom-call(bf16[2,1152,128]{2,1,0:T(8,128)(2,1)S(1)} %collective-permute-done.18.refs_0_, bf16[2,1024,128]{2,1,0:T(8,128)(2,1)S(1)} %get-tuple-element.156.refs_1_, ...), custom_call_target="tpu_custom_call", output_to_operand_aliasing={{0}: (2, {}), {1}: (3, {})} | custom-call | flops 671088640 | bytes 4259840 | tf_op jit(solution)/shard_map/attention_far_queries0/pallas_call | solution.py:95
  67.6 4.0 %collective-permute-start.25 = (bf16[128,1024]{1,0:T(8,128)(2,1)S(1)}, bf16[128,1024]{1,0:T(8,128)(2,1)S(1)}, u32[]{:S(2)}, u32[]{:S(2)}) collective-permute-start(bf16[128,1024]{1,0:T(8,128)(2,1)S(1)} %get-tuple-element.180.refs_0_), channel_id=1, source_target_pairs={{0,16},{16,0},{1,17},{17,1},{2,18},{18,2},{3,19},{19,3},{4,20},{20... | collective-permute-start | bytes 786440 | tf_op jit(solution)/shard_map/ppermute | solution.py:34
  71.6 3.4 %attention_far_queries1.1 = (bf16[2,512,128]{2,1,0:T(8,128)(2,1)S(1)}, f32[2,1024,128]{2,1,0:T(8,128)S(1)}, f32[8,128]{1,0:T(8,128)S(1)}) custom-call(bf16[2,1152,128]{2,1,0:T(8,128)(2,1)S(1)} %collective-permute-done.18.refs_0_, bf16[2,1024,128]{2,1,0:T(8,128)(2,1)S(1)} %get-tuple-element.156.refs_1_, f32[2,128,512]{2,1,0:T(8,128)S(1)} %get-tuple-element.181.refs_2_, ...), custom_call_target="tpu_custom_call" | custom-call | flops 671088640 | bytes 3997696 | tf_op jit(solution)/shard_map/attention_far_queries1/pallas_call | solution.py:95
  74.9 0.1 collective-permute-start.30
  75.0 0.3 collective-permute-done.25.refs_1_
  75.5 5.1 %collective-permute-start.32 = (bf16[1024,128]{1,0:T(8,128)(2,1)S(1)}, bf16[1024,128]{1,0:T(8,128)(2,1)S(1)}, u32[]{:S(2)}, u32[]{:S(2)}) collective-permute-start(bf16[1024,128]{1,0:T(8,128)(2,1)S(1)} %get-tuple-element.195), channel_id=1, source_target_pairs={{0,4},{2,14},{4,0},{6,10},{8,12},{10,6},{12,8},{14,2},{1,5},{3,15}... | collective-permute-start | bytes 786440 | tf_op jit(solution)/shard_map/ppermute | solution.py:44
  80.6 0.2 collective-permute-start.28
  80.8 1.3 %collective-permute-start.26 = (bf16[128,1024]{1,0:T(8,128)(2,1)S(1)}, bf16[128,1024]{1,0:T(8,128)(2,1)S(1)}, u32[]{:S(2)}, u32[]{:S(2)}) collective-permute-start(bf16[128,1024]{1,0:T(8,128)(2,1)S(1)} %get-tuple-element.185.refs_0_), channel_id=1, source_target_pairs={{0,4},{2,34},{4,8},{6,38},{8,12},{10,42},{12,0},{14,46},{32,36},{3... | collective-permute-start | bytes 786440 | tf_op jit(solution)/shard_map/ppermute | solution.py:57
  82.1 0.2 turn.1
  82.3 2.5 %collective-permute-start.31 = (bf16[512,128]{1,0:T(8,128)(2,1)S(1)}, bf16[512,128]{1,0:T(8,128)(2,1)S(1)}, u32[]{:S(2)}, u32[]{:S(2)}) collective-permute-start(bf16[512,128]{1,0:T(8,128)(2,1)S(1)} %get-tuple-element.194), channel_id=1, source_target_pairs={{0,32},{2,98},{32,0},{34,66},{64,96},{66,34},{96,64},{98,2},{1,33}... | collective-permute-start | bytes 393224 | tf_op jit(solution)/shard_map/ppermute | solution.py:44
  84.8 7.3 %collective-permute-done.31.refs_2_ = bf16[512,128]{1,0:T(8,128)(2,1)S(1)} collective-permute-done((bf16[512,128]{1,0:T(8,128)(2,1)S(1)}, bf16[512,128]{1,0:T(8,128)(2,1)S(1)}, u32[]{:S(2)}, u32[]{:S(2)}) %collective-permute-start.31) | collective-permute-done | bytes 131104 | tf_op jit(solution)/shard_map/ppermute | solution.py:44
  92.1 0.1 back.1
  92.2 2.0 %collective-permute-start.33 = (bf16[384,128]{1,0:T(8,128)(2,1)S(1)}, bf16[384,128]{1,0:T(8,128)(2,1)S(1)}, u32[]{:S(2)}, u32[]{:S(2)}) collective-permute-start(bf16[384,128]{1,0:T(8,128)(2,1)S(1)} %get-tuple-element.198), channel_id=1, source_target_pairs={{0,2},{2,0},{1,3},{3,1},{4,6},{6,4},{5,7},{7,5},{8,10},{10,8},{9,1... | collective-permute-start | bytes 294920 | tf_op jit(solution)/shard_map/ppermute | solution.py:34
  94.2 0.9 collective-permute-done.33.refs_1_
  95.2 0.1 gather.1
  95.3 0.4 collective-permute-start.36
  95.7 1.8 %collective-permute-start.35 = (bf16[768,128]{1,0:T(8,128)(2,1)S(1)}, bf16[768,128]{1,0:T(8,128)(2,1)S(1)}, u32[]{:S(2)}, u32[]{:S(2)}) collective-permute-start(bf16[768,128]{1,0:T(8,128)(2,1)S(1)} %get-tuple-element.205), channel_id=1, source_target_pairs={{0,16},{16,0},{1,17},{17,1},{2,18},{18,2},{3,19},{19,3},{4,20},{20... | collective-permute-start | bytes 589832 | tf_op jit(solution)/shard_map/ppermute | solution.py:34
  97.5 0.4 collective-permute-start.23
  98.0 0.9 collective-permute-done.23.refs_1_
  99.0 0.7 add_shares.1
  99.7 3.0 %collective-permute-done.35.refs_2_ = bf16[768,128]{1,0:T(8,128)(2,1)S(1)} collective-permute-done((bf16[768,128]{1,0:T(8,128)(2,1)S(1)}, bf16[768,128]{1,0:T(8,128)(2,1)S(1)}, u32[]{:S(2)}, u32[]{:S(2)}) %collective-permute-start.35) | collective-permute-done | bytes 196640 | tf_op jit(solution)/shard_map/ppermute | solution.py:34
  102.7 0.8 place.1
  103.5 2.3 %final.1 = (f32[512,1024]{1,0:T(8,128)}, f32[512,1024]{1,0:T(8,128)}, f32[8,128]{1,0:T(8,128)}) custom-call(bf16[512,1024]{1,0:T(8,128)(2,1)S(1)} %get-tuple-element.210.refs_0_, bf16[512,1024]{1,0:T(8,128)(2,1)S(1)} %collective-permute-done.36.refs_1_, f32[8,128]{1,0:T(8,128)S(1)} %get-tuple-element.211.refs_2_), custom_call_target="tpu_custom_call" | custom-call | bytes 6291456 | tf_op jit(solution)/shard_map/final/pallas_call | solution.py:95
  (48 shorter events, 1.0 us)
Async XLA Ops:
  0.6 7.1 %collective-permute-start.2 = (bf16[128,512]{1,0:T(8,128)(2,1)}, bf16[128,512]{1,0:T(8,128)(2,1)S(1)}, u32[]{:S(2)}, u32[]{:S(2)}) collective-permute-start(bf16[128,512]{1,0:T(8,128)(2,1)} %refs_0_.3), channel_id=1, source_target_pairs={{0,2},{2,0},{1,3},{3,1},{4,6},{6,4},{5,7},{7,5},{8,10},{10,8},{9,1... | collective-permute-start | bytes 393224 | tf_op jit(solution)/shard_map/ppermute | solution.py:34
  2.1 13.7 %collective-permute-start = (bf16[128,512]{1,0:T(8,128)(2,1)}, bf16[128,512]{1,0:T(8,128)(2,1)S(1)}, u32[]{:S(2)}, u32[]{:S(2)}) collective-permute-start(bf16[128,512]{1,0:T(8,128)(2,1)} %refs_2_.1), channel_id=1, source_target_pairs={{0,1},{1,0},{2,3},{3,2},{4,5},{5,4},{6,7},{7,6},{8,9},{9,8},{10,11... | collective-permute-start | bytes 393224 | tf_op jit(solution)/shard_map/ppermute | solution.py:34
  7.2 1.3 %collective-permute-start.1 = (bf16[256,128]{1,0:T(8,128)(2,1)S(1)}, bf16[256,128]{1,0:T(8,128)(2,1)S(1)}, u32[]{:S(2)}, u32[]{:S(2)}) collective-permute-start(bf16[256,128]{1,0:T(8,128)(2,1)S(1)} %get-tuple-element.120), channel_id=1, source_target_pairs={{0,2},{2,0},{1,3},{3,1},{4,6},{6,4},{5,7},{7,5},{8,10},{10,8},{9,1... | collective-permute-start | bytes 196616 | tf_op jit(solution)/shard_map/ppermute | solution.py:34
  8.6 12.6 %collective-permute-start.10 = (bf16[512,128]{1,0:T(8,128)(2,1)S(1)}, bf16[512,128]{1,0:T(8,128)(2,1)S(1)}, u32[]{:S(2)}, u32[]{:S(2)}) collective-permute-start(bf16[512,128]{1,0:T(8,128)(2,1)S(1)} %get-tuple-element.136), channel_id=1, source_target_pairs={{0,16},{16,0},{1,17},{17,1},{2,18},{18,2},{3,19},{19,3},{4,20},{20... | collective-permute-start | bytes 393224 | tf_op jit(solution)/shard_map/ppermute | solution.py:34
  9.1 12.2 %collective-permute-start.3 = (bf16[256,512]{1,0:T(8,128)(2,1)S(1)}, bf16[256,512]{1,0:T(8,128)(2,1)S(1)}, u32[]{:S(2)}, u32[]{:S(2)}) collective-permute-start(bf16[256,512]{1,0:T(8,128)(2,1)S(1)} %get-tuple-element.127), channel_id=1, source_target_pairs={{0,4},{2,126},{4,8},{6,2},{8,12},{10,6},{12,16},{14,10},{16,20},{1... | collective-permute-start | bytes 786440 | tf_op jit(solution)/shard_map/ppermute | solution.py:516
  15.8 2.1 %copy-start.1 = (bf16[128,512]{1,0:T(8,128)(2,1)S(1)}, bf16[128,512]{1,0:T(8,128)(2,1)}, u32[]{:S(2)}) copy-start(bf16[128,512]{1,0:T(8,128)(2,1)} %refs_0_.3) | copy-start | bytes 393220
  16.5 1.3 %collective-permute-start.7 = (bf16[288,128]{1,0:T(8,128)(2,1)S(1)}, bf16[288,128]{1,0:T(8,128)(2,1)S(1)}, u32[]{:S(2)}, u32[]{:S(2)}) collective-permute-start(bf16[288,128]{1,0:T(8,128)(2,1)S(1)} %get-tuple-element.131), channel_id=1, source_target_pairs={{0,2},{2,0},{1,3},{3,1},{4,6},{6,4},{5,7},{7,5},{8,10},{10,8},{9,1... | collective-permute-start | bytes 221192 | tf_op jit(solution)/shard_map/ppermute | solution.py:34
  16.5 2.1 %collective-permute-start.9 = (bf16[256,128]{1,0:T(8,128)(2,1)S(1)}, bf16[256,128]{1,0:T(8,128)(2,1)S(1)}, u32[]{:S(2)}, u32[]{:S(2)}) collective-permute-start(bf16[256,128]{1,0:T(8,128)(2,1)S(1)} %get-tuple-element.135), channel_id=1, source_target_pairs={{0,2},{2,0},{1,3},{3,1},{4,6},{6,4},{5,7},{7,5},{8,10},{10,8},{9,1... | collective-permute-start | bytes 196616 | tf_op jit(solution)/shard_map/ppermute | solution.py:34
  17.8 6.8 %collective-permute-start.8 = (bf16[576,128]{1,0:T(8,128)(2,1)S(1)}, bf16[576,128]{1,0:T(8,128)(2,1)S(1)}, u32[]{:S(2)}, u32[]{:S(2)}) collective-permute-start(bf16[576,128]{1,0:T(8,128)(2,1)S(1)} %get-tuple-element.133), channel_id=1, source_target_pairs={{0,16},{16,0},{1,17},{17,1},{2,18},{18,2},{3,19},{19,3},{4,20},{20... | collective-permute-start | bytes 442376 | tf_op jit(solution)/shard_map/ppermute | solution.py:34
  17.9 6.8 %collective-permute-start.5 = (bf16[128,512]{1,0:T(8,128)(2,1)S(1)}, bf16[128,512]{1,0:T(8,128)(2,1)S(1)}, u32[]{:S(2)}, u32[]{:S(2)}) collective-permute-start(bf16[128,512]{1,0:T(8,128)(2,1)S(1)} %copy-done.1), channel_id=1, source_target_pairs={{0,122},{2,8},{4,126},{6,12},{8,2},{10,16},{12,6},{14,20},{16,10},... | collective-permute-start | bytes 393224 | tf_op jit(solution)/shard_map/ppermute | solution.py:496
  18.7 3.4 %collective-permute-start.6 = (bf16[288,128]{1,0:T(8,128)(2,1)S(1)}, bf16[288,128]{1,0:T(8,128)(2,1)S(1)}, u32[]{:S(2)}, u32[]{:S(2)}) collective-permute-start(bf16[288,128]{1,0:T(8,128)(2,1)S(1)} %get-tuple-element.129), channel_id=1, source_target_pairs={{0,2},{2,0},{1,3},{3,1},{4,6},{6,4},{5,7},{7,5},{8,10},{10,8},{9,1... | collective-permute-start | bytes 221192 | tf_op jit(solution)/shard_map/ppermute | solution.py:34
  21.2 6.9 %collective-permute-start.13 = (bf16[1024,128]{1,0:T(8,128)(2,1)S(1)}, bf16[1024,128]{1,0:T(8,128)(2,1)S(1)}, u32[]{:S(2)}, u32[]{:S(2)}) collective-permute-start(bf16[1024,128]{1,0:T(8,128)(2,1)S(1)} %get-tuple-element.143.refs_0_), channel_id=1, source_target_pairs={{0,4},{2,14},{4,0},{6,10},{8,12},{10,6},{12,8},{14,2},{1,5},{3,15}... | collective-permute-start | bytes 786440 | tf_op jit(solution)/shard_map/ppermute | solution.py:44
  21.3 3.4 %collective-permute-start.4 = (bf16[256,512]{1,0:T(8,128)(2,1)S(1)}, bf16[256,512]{1,0:T(8,128)(2,1)S(1)}, u32[]{:S(2)}, u32[]{:S(2)}) collective-permute-start(bf16[256,512]{1,0:T(8,128)(2,1)S(1)} %collective-permute-done.3.refs_7_), channel_id=1, source_target_pairs={{0,2},{2,0},{1,3},{3,1},{4,6},{6,4},{5,7},{7,5},{8,10},{10,8},{9,1... | collective-permute-start | bytes 786440 | tf_op jit(solution)/shard_map/ppermute | solution.py:34
  24.6 0.7 copy-start
  24.6 6.9 %collective-permute-start.12 = (bf16[1152,128]{1,0:T(8,128)(2,1)S(1)}, bf16[1152,128]{1,0:T(8,128)(2,1)S(1)}, u32[]{:S(2)}, u32[]{:S(2)}) collective-permute-start(bf16[1152,128]{1,0:T(8,128)(2,1)S(1)} %get-tuple-element.142.refs_0_), channel_id=1, source_target_pairs={{0,32},{2,98},{32,0},{34,66},{64,96},{66,34},{96,64},{98,2},{1,33}... | collective-permute-start | bytes 884744 | tf_op jit(solution)/shard_map/ppermute | solution.py:44
  28.1 10.7 %collective-permute-start.19 = (bf16[2,1024,128]{2,1,0:T(8,128)(2,1)S(1)}, bf16[2,1024,128]{2,1,0:T(8,128)(2,1)S(1)}, u32[]{:S(2)}, u32[]{:S(2)}) collective-permute-start(bf16[2,1024,128]{2,1,0:T(8,128)(2,1)S(1)} %get-tuple-element.156.refs_1_), channel_id=1, source_target_pairs={{0,12},{2,6},{4,8},{6,2},{8,4},{10,14},{12,0},{14,10},{1,13},{3,7}... | collective-permute-start | bytes 1572872 | tf_op jit(solution)/shard_map/ppermute | solution.py:44
  28.2 3.5 %collective-permute-start.11 = (bf16[512,1024]{1,0:T(8,128)(2,1)S(1)}, bf16[512,1024]{1,0:T(8,128)(2,1)S(1)}, u32[]{:S(2)}, u32[]{:S(2)}) collective-permute-start(bf16[512,1024]{1,0:T(8,128)(2,1)S(1)} %get-tuple-element.141), channel_id=1, source_target_pairs={{0,2},{2,0},{1,3},{3,1},{4,6},{6,4},{5,7},{7,5},{8,10},{10,8},{9,1... | collective-permute-start | bytes 3145736 | tf_op jit(solution)/shard_map/ppermute | solution.py:34
  31.5 15.3 %collective-permute-start.18 = (bf16[2,1152,128]{2,1,0:T(8,128)(2,1)S(1)}, bf16[2,1152,128]{2,1,0:T(8,128)(2,1)S(1)}, u32[]{:S(2)}, u32[]{:S(2)}) collective-permute-start(bf16[2,1152,128]{2,1,0:T(8,128)(2,1)S(1)} %get-tuple-element.155.refs_0_), channel_id=1, source_target_pairs={{0,96},{2,34},{32,64},{34,2},{64,32},{66,98},{96,0},{98,66},{1,97}... | collective-permute-start | bytes 1769480 | tf_op jit(solution)/shard_map/ppermute | solution.py:44
  33.6 19.5 %collective-permute-start.14 = (bf16[384,512]{1,0:T(8,128)(2,1)S(1)}, bf16[384,512]{1,0:T(8,128)(2,1)S(1)}, u32[]{:S(2)}, u32[]{:S(2)}) collective-permute-start(bf16[384,512]{1,0:T(8,128)(2,1)S(1)} %get-tuple-element.150), channel_id=1, source_target_pairs={{0,2},{2,0},{1,3},{3,1},{4,6},{6,4},{5,7},{7,5},{8,10},{10,8},{9,1... | collective-permute-start | bytes 1179656 | tf_op jit(solution)/shard_map/ppermute | solution.py:34
  34.9 17.9 %collective-permute-start.15 = (bf16[128,1024]{1,0:T(8,128)(2,1)S(1)}, bf16[128,1024]{1,0:T(8,128)(2,1)S(1)}, u32[]{:S(2)}, u32[]{:S(2)}) collective-permute-start(bf16[128,1024]{1,0:T(8,128)(2,1)S(1)} %get-tuple-element.152), channel_id=1, source_target_pairs={{0,4},{2,34},{4,8},{6,38},{8,12},{10,42},{12,0},{14,46},{32,36},{3... | collective-permute-start | bytes 786440 | tf_op jit(solution)/shard_map/ppermute | solution.py:57
  36.1 16.8 %collective-permute-start.16 = (bf16[128,1024]{1,0:T(8,128)(2,1)S(1)}, bf16[128,1024]{1,0:T(8,128)(2,1)S(1)}, u32[]{:S(2)}, u32[]{:S(2)}) collective-permute-start(bf16[128,1024]{1,0:T(8,128)(2,1)S(1)} %get-tuple-element.153), channel_id=1, source_target_pairs={{0,8},{2,66},{4,12},{6,70},{8,0},{10,74},{12,4},{14,78},{32,40},{3... | collective-permute-start | bytes 786440 | tf_op jit(solution)/shard_map/ppermute | solution.py:57
  38.8 14.1 %collective-permute-start.17 = (bf16[128,1024]{1,0:T(8,128)(2,1)S(1)}, bf16[128,1024]{1,0:T(8,128)(2,1)S(1)}, u32[]{:S(2)}, u32[]{:S(2)}) collective-permute-start(bf16[128,1024]{1,0:T(8,128)(2,1)S(1)} %get-tuple-element.154), channel_id=1, source_target_pairs={{0,12},{2,98},{4,0},{6,102},{8,4},{10,106},{12,8},{14,110},{32,44}... | collective-permute-start | bytes 786440 | tf_op jit(solution)/shard_map/ppermute | solution.py:57
  53.1 6.0 %collective-permute-start.22 = (bf16[128,1024]{1,0:T(8,128)(2,1)S(1)}, bf16[128,1024]{1,0:T(8,128)(2,1)S(1)}, u32[]{:S(2)}, u32[]{:S(2)}) collective-permute-start(bf16[128,1024]{1,0:T(8,128)(2,1)S(1)} %get-tuple-element.169.refs_0_), channel_id=1, source_target_pairs={{0,32},{2,6},{4,36},{6,2},{8,40},{10,14},{12,44},{14,10},{32,0},{3... | collective-permute-start | bytes 786440 | tf_op jit(solution)/shard_map/ppermute | solution.py:57
  53.2 11.2 %collective-permute-start.20 = (bf16[256,512]{1,0:T(8,128)(2,1)S(1)}, bf16[256,512]{1,0:T(8,128)(2,1)S(1)}, u32[]{:S(2)}, u32[]{:S(2)}) collective-permute-start(bf16[256,512]{1,0:T(8,128)(2,1)S(1)} %get-tuple-element.162), channel_id=1, source_target_pairs={{0,4},{2,126},{4,8},{6,2},{8,12},{10,6},{12,16},{14,10},{16,20},{1... | collective-permute-start | bytes 786440 | tf_op jit(solution)/shard_map/ppermute | solution.py:624
  54.5 9.9 %collective-permute-start.21 = (bf16[128,512]{1,0:T(8,128)(2,1)S(1)}, bf16[128,512]{1,0:T(8,128)(2,1)S(1)}, u32[]{:S(2)}, u32[]{:S(2)}) collective-permute-start(bf16[128,512]{1,0:T(8,128)(2,1)S(1)} %get-tuple-element.163), channel_id=1, source_target_pairs={{0,122},{2,8},{4,126},{6,12},{8,2},{10,16},{12,6},{14,20},{16,10},... | collective-permute-start | bytes 393224 | tf_op jit(solution)/shard_map/ppermute | solution.py:624
  59.1 8.4 %collective-permute-start.24 = (bf16[128,1024]{1,0:T(8,128)(2,1)S(1)}, bf16[128,1024]{1,0:T(8,128)(2,1)S(1)}, u32[]{:S(2)}, u32[]{:S(2)}) collective-permute-start(bf16[128,1024]{1,0:T(8,128)(2,1)S(1)} %get-tuple-element.175.refs_0_), channel_id=1, source_target_pairs={{0,96},{2,14},{4,100},{6,10},{8,104},{10,6},{12,108},{14,2},{32,64... | collective-permute-start | bytes 786440 | tf_op jit(solution)/shard_map/ppermute | solution.py:57
  63.9 11.6 %collective-permute-start.29 = (bf16[2,1024,128]{2,1,0:T(8,128)(2,1)S(1)}, bf16[2,1024,128]{2,1,0:T(8,128)(2,1)S(1)}, u32[]{:S(2)}, u32[]{:S(2)}) collective-permute-start(bf16[2,1024,128]{2,1,0:T(8,128)(2,1)S(1)} %get-tuple-element.188), channel_id=1, source_target_pairs={{0,12},{2,6},{4,8},{6,2},{8,4},{10,14},{12,0},{14,10},{1,13},{3,7}... | collective-permute-start | bytes 1572872 | tf_op jit(solution)/shard_map/ppermute | solution.py:44
  67.6 7.7 %collective-permute-start.25 = (bf16[128,1024]{1,0:T(8,128)(2,1)S(1)}, bf16[128,1024]{1,0:T(8,128)(2,1)S(1)}, u32[]{:S(2)}, u32[]{:S(2)}) collective-permute-start(bf16[128,1024]{1,0:T(8,128)(2,1)S(1)} %get-tuple-element.180.refs_0_), channel_id=1, source_target_pairs={{0,16},{16,0},{1,17},{17,1},{2,18},{18,2},{3,19},{19,3},{4,20},{20... | collective-permute-start | bytes 786440 | tf_op jit(solution)/shard_map/ppermute | solution.py:34
  74.9 7.3 %collective-permute-start.30 = (bf16[2,512,128]{2,1,0:T(8,128)(2,1)S(1)}, bf16[2,512,128]{2,1,0:T(8,128)(2,1)S(1)}, u32[]{:S(2)}, u32[]{:S(2)}) collective-permute-start(bf16[2,512,128]{2,1,0:T(8,128)(2,1)S(1)} %get-tuple-element.192), channel_id=1, source_target_pairs={{0,96},{2,34},{32,64},{34,2},{64,32},{66,98},{96,0},{98,66},{1,97}... | collective-permute-start | bytes 786440 | tf_op jit(solution)/shard_map/ppermute | solution.py:44
  75.5 16.6 %collective-permute-start.32 = (bf16[1024,128]{1,0:T(8,128)(2,1)S(1)}, bf16[1024,128]{1,0:T(8,128)(2,1)S(1)}, u32[]{:S(2)}, u32[]{:S(2)}) collective-permute-start(bf16[1024,128]{1,0:T(8,128)(2,1)S(1)} %get-tuple-element.195), channel_id=1, source_target_pairs={{0,4},{2,14},{4,0},{6,10},{8,12},{10,6},{12,8},{14,2},{1,5},{3,15}... | collective-permute-start | bytes 786440 | tf_op jit(solution)/shard_map/ppermute | solution.py:44
  80.6 14.6 %collective-permute-start.28 = (bf16[128,1024]{1,0:T(8,128)(2,1)S(1)}, bf16[128,1024]{1,0:T(8,128)(2,1)S(1)}, u32[]{:S(2)}, u32[]{:S(2)}) collective-permute-start(bf16[128,1024]{1,0:T(8,128)(2,1)S(1)} %get-tuple-element.185.refs_0_), channel_id=1, source_target_pairs={{0,12},{2,98},{4,0},{6,102},{8,4},{10,106},{12,8},{14,110},{32,44}... | collective-permute-start | bytes 786440 | tf_op jit(solution)/shard_map/ppermute | solution.py:57
  80.8 14.4 %collective-permute-start.27 = (bf16[128,1024]{1,0:T(8,128)(2,1)S(1)}, bf16[128,1024]{1,0:T(8,128)(2,1)S(1)}, u32[]{:S(2)}, u32[]{:S(2)}) collective-permute-start(bf16[128,1024]{1,0:T(8,128)(2,1)S(1)} %get-tuple-element.185.refs_0_), channel_id=1, source_target_pairs={{0,8},{2,66},{4,12},{6,70},{8,0},{10,74},{12,4},{14,78},{32,40},{3... | collective-permute-start | bytes 786440 | tf_op jit(solution)/shard_map/ppermute | solution.py:57
  80.8 14.4 %collective-permute-start.26 = (bf16[128,1024]{1,0:T(8,128)(2,1)S(1)}, bf16[128,1024]{1,0:T(8,128)(2,1)S(1)}, u32[]{:S(2)}, u32[]{:S(2)}) collective-permute-start(bf16[128,1024]{1,0:T(8,128)(2,1)S(1)} %get-tuple-element.185.refs_0_), channel_id=1, source_target_pairs={{0,4},{2,34},{4,8},{6,38},{8,12},{10,42},{12,0},{14,46},{32,36},{3... | collective-permute-start | bytes 786440 | tf_op jit(solution)/shard_map/ppermute | solution.py:57
  82.3 9.7 %collective-permute-start.31 = (bf16[512,128]{1,0:T(8,128)(2,1)S(1)}, bf16[512,128]{1,0:T(8,128)(2,1)S(1)}, u32[]{:S(2)}, u32[]{:S(2)}) collective-permute-start(bf16[512,128]{1,0:T(8,128)(2,1)S(1)} %get-tuple-element.194), channel_id=1, source_target_pairs={{0,32},{2,98},{32,0},{34,66},{64,96},{66,34},{96,64},{98,2},{1,33}... | collective-permute-start | bytes 393224 | tf_op jit(solution)/shard_map/ppermute | solution.py:44
  92.2 2.9 %collective-permute-start.33 = (bf16[384,128]{1,0:T(8,128)(2,1)S(1)}, bf16[384,128]{1,0:T(8,128)(2,1)S(1)}, u32[]{:S(2)}, u32[]{:S(2)}) collective-permute-start(bf16[384,128]{1,0:T(8,128)(2,1)S(1)} %get-tuple-element.198), channel_id=1, source_target_pairs={{0,2},{2,0},{1,3},{3,1},{4,6},{6,4},{5,7},{7,5},{8,10},{10,8},{9,1... | collective-permute-start | bytes 294920 | tf_op jit(solution)/shard_map/ppermute | solution.py:34
  95.3 8.2 %collective-permute-start.36 = (bf16[512,1024]{1,0:T(8,128)(2,1)S(1)}, bf16[512,1024]{1,0:T(8,128)(2,1)S(1)}, u32[]{:S(2)}, u32[]{:S(2)}) collective-permute-start(bf16[512,1024]{1,0:T(8,128)(2,1)S(1)} %get-tuple-element.210.refs_0_), channel_id=1, source_target_pairs={{0,2},{2,0},{1,3},{3,1},{4,6},{6,4},{5,7},{7,5},{8,10},{10,8},{9,1... | collective-permute-start | bytes 3145736 | tf_op jit(solution)/shard_map/ppermute | solution.py:34
  95.7 6.9 %collective-permute-start.35 = (bf16[768,128]{1,0:T(8,128)(2,1)S(1)}, bf16[768,128]{1,0:T(8,128)(2,1)S(1)}, u32[]{:S(2)}, u32[]{:S(2)}) collective-permute-start(bf16[768,128]{1,0:T(8,128)(2,1)S(1)} %get-tuple-element.205), channel_id=1, source_target_pairs={{0,16},{16,0},{1,17},{17,1},{2,18},{18,2},{3,19},{19,3},{4,20},{20... | collective-permute-start | bytes 589832 | tf_op jit(solution)/shard_map/ppermute | solution.py:34
  97.5 1.4 %collective-permute-start.23 = (bf16[128,512]{1,0:T(8,128)(2,1)S(1)}, bf16[128,512]{1,0:T(8,128)(2,1)S(1)}, u32[]{:S(2)}, u32[]{:S(2)}) collective-permute-start(bf16[128,512]{1,0:T(8,128)(2,1)S(1)} %get-tuple-element.174), channel_id=1, source_target_pairs={{0,2},{2,0},{1,3},{3,1},{4,6},{6,4},{5,7},{7,5},{8,10},{10,8},{9,1... | collective-permute-start | bytes 393224 | tf_op jit(solution)/shard_map/ppermute | solution.py:34
  98.0 1.7 %collective-permute-start.34 = (bf16[384,128]{1,0:T(8,128)(2,1)S(1)}, bf16[384,128]{1,0:T(8,128)(2,1)S(1)}, u32[]{:S(2)}, u32[]{:S(2)}) collective-permute-start(bf16[384,128]{1,0:T(8,128)(2,1)S(1)} %get-tuple-element.204), channel_id=1, source_target_pairs={{0,2},{2,0},{1,3},{3,1},{4,6},{6,4},{5,7},{7,5},{8,10},{10,8},{9,1... | collective-permute-start | bytes 294920 | tf_op jit(solution)/shard_map/ppermute | solution.py:34

commit v5 on v4

--- a/solution.py
+++ b/solution.py
@@ -610,9 +610,6 @@
     )
     share_received = swap(share_send, "c", 1)
     dq_near, dkv_near = attention(order, "near", qdo_near, kv_near, None, None)
-    dq_far, dkv_far = attention(order, "far", qdo_far, kv_far, None, None)
-    part = add(order, "ring", *blocks)
-    received = across(part, 0)
     share_near, share_local = order.call(
         near_kernel,
         [shaped((2 * rows, columns)), shaped((rows, columns), F32)],
@@ -622,15 +619,9 @@
         name="near",
     )
     share_far, share_near = lax.ppermute(share_far, NODE, to_far), lax.ppermute(share_near, NODE, to_near)
-    dq_near, dkv_far = attention(
-        order, "far_keys0", qdo_near, kv_far, dq_near, dkv_far, first=0, count=1
-    )
-    part = add(order, "across0", part, received)
-    received = across(part, 1)
-    dq_near, dkv_far = attention(
-        order, "far_keys1", qdo_near, kv_far, dq_near, dkv_far, None, BF16, first=1, count=1
-    )
-    dkv_met = meet(dkv_far, "x", 1)
+    dq_far, dkv_far = attention(order, "far", qdo_far, kv_far, None, None)
+    part = add(order, "ring", *blocks)
+    received = across(part, 0)
     share_cross, share_local = order.call(
         cross_kernel,
         [shaped((rows, columns)), shaped((rows, columns), F32)],
@@ -641,6 +632,15 @@
         name="cross",
     )
     share_cross = swap(share_cross, "c", 1)
+    dq_near, dkv_far = attention(
+        order, "far_keys0", qdo_near, kv_far, dq_near, dkv_far, first=0, count=1
+    )
+    part = add(order, "across0", part, received)
+    received = across(part, 1)
+    dq_near, dkv_far = attention(
+        order, "far_keys1", qdo_near, kv_far, dq_near, dkv_far, None, BF16, first=1, count=1
+    )
+    dkv_met = meet(dkv_far, "x", 1)
     dq_far, dkv_near = attention(
         order, "far_queries0", qdo_far, kv_near, dq_far, dkv_near, first=0, count=1
     )

time: 106 us -> 103 us (0.972)
  starting transfers between devices: 47.5 us -> 40.4 us
  waiting for transfers between devices: 19.9 us -> 23.2 us
    ppermute x8, starting transfers between devices: 8.53 us -> 3.72 us  [meet(): return lax.ppermute(value, (axis, 'c'), pairs)]
    ppermute x17, starting transfers between devices: 20.5 us -> 16 us  [swap(): return lax.ppermute(value, axes, [(i, i ^ mask) for i in range(count)])]
    ppermute x17, waiting for transfers between devices: 9.58 us -> 12.4 us  [swap(): return lax.ppermute(value, axes, [(i, i ^ mask) for i in range(count)])]
    ppermute x8, starting transfers between devices: 8.9 us -> 10.9 us  [ring(): return lax.ppermute(value, ('z', 'x', 'c'), pairs)]
    ppermute x1, starting transfers between devices: 1.24 us -> 2.89 us  [body(): lax.ppermute(share_near, NODE, to_near)]
    ppermute x1, starting transfers between devices: 1.49 us -> 0.01 us  [body(): lax.ppermute(share_far, NODE, to_far)]
  transfers between devices with their start and end apart: 37 -> 37, of which waited for: 12 -> 12; matrix products, arithmetic and copies ran while one was open for 0% -> 0% of each run, Pallas kernels for 32% -> 34%
where the time goes in v5:
time: 103 us
  starting transfers between devices  40.4 us (39%)
  Pallas kernels  36.9 us (36%)
  waiting for transfers between devices  23.2 us (23%)
  between operations  1.66 us (2%)
    pallas_call x34, Pallas kernels, call(): pl.pallas_call(whole, out_shape=[*outs, shaped((8, LANES), F32)], in_spec...  36.9 us
    ppermute x17, starting transfers between devices, swap(): return lax.ppermute(value, axes, [(i, i ^ mask) for i in range(count)])  16 us
    ppermute x17, waiting for transfers between devices, swap(): return lax.ppermute(value, axes, [(i, i ^ mask) for i in range(count)])  12.4 us
    ppermute x8, starting transfers between devices, ring(): return lax.ppermute(value, ('z', 'x', 'c'), pairs)  10.9 us
    ppermute x8, waiting for transfers between devices, meet(): return lax.ppermute(value, (axis, 'c'), pairs)  9.9 us
    ppermute x1, starting transfers between devices, body(): near_features = lax.ppermute(near_features, NODE, to_near)  6.74 us
    ppermute x8, starting transfers between devices, meet(): return lax.ppermute(value, (axis, 'c'), pairs)  3.72 us
    ppermute x1, starting transfers between devices, body(): lax.ppermute(share_near, NODE, to_near)  2.89 us
  transfers between devices with their start and end apart: 37, of which 12 were waited for; matrix products, arithmetic and copies ran while one was open for 0% of the time, Pallas kernels for 34%

profile of v5, /device:TPU:1, one launch (start us, length us, event | category | flops | bytes accessed | tf_op | source)
XLA Modules:
  0.0 102.7 jit_solution(6590515896952426403)
XLA Ops:
  0.6 1.5 %collective-permute-start.2 = (bf16[128,512]{1,0:T(8,128)(2,1)}, bf16[128,512]{1,0:T(8,128)(2,1)S(1)}, u32[]{:S(2)}, u32[]{:S(2)}) collective-permute-start(bf16[128,512]{1,0:T(8,128)(2,1)} %refs_0_.3), channel_id=1, source_target_pairs={{0,2},{2,0},{1,3},{3,1},{4,6},{6,4},{5,7},{7,5},{8,10},{10,8},{9,1... | collective-permute-start | bytes 393224 | tf_op jit(solution)/shard_map/ppermute | solution.py:34
  2.1 3.0 %collective-permute-start = (bf16[128,512]{1,0:T(8,128)(2,1)}, bf16[128,512]{1,0:T(8,128)(2,1)S(1)}, u32[]{:S(2)}, u32[]{:S(2)}) collective-permute-start(bf16[128,512]{1,0:T(8,128)(2,1)} %refs_2_.1), channel_id=1, source_target_pairs={{0,1},{1,0},{2,3},{3,2},{4,5},{5,4},{6,7},{7,6},{8,9},{9,8},{10,11... | collective-permute-start | bytes 393224 | tf_op jit(solution)/shard_map/ppermute | solution.py:34
  5.1 2.0 %load.1 = (bf16[128,512]{1,0:T(8,128)(2,1)S(1)}, bf16[1,8,128,128]{3,2,1,0:T(8,128)(2,1)S(1)}, bf16[128,512]{1,0:T(8,128)(2,1)S(1)}, bf16[128,512]{1,0:T(8,128)(...) custom-call(bf16[128,512]{1,0:T(8,128)(2,1)} %refs_0_.3, ...), custom_call_target="tpu_custom_call" | custom-call | bytes 6299648 | tf_op jit(solution)/shard_map/load/pallas_call | solution.py:95
  7.2 0.4 collective-permute-start.1
  7.7 0.9 collective-permute-done.1.refs_1_
  8.6 0.5 collective-permute-start.10
  9.1 6.7 %collective-permute-start.3 = (bf16[256,512]{1,0:T(8,128)(2,1)S(1)}, bf16[256,512]{1,0:T(8,128)(2,1)S(1)}, u32[]{:S(2)}, u32[]{:S(2)}) collective-permute-start(bf16[256,512]{1,0:T(8,128)(2,1)S(1)} %get-tuple-element.127), channel_id=1, source_target_pairs={{0,4},{2,126},{4,8},{6,2},{8,12},{10,6},{12,16},{14,10},{16,20},{1... | collective-permute-start | bytes 786440 | tf_op jit(solution)/shard_map/ppermute | solution.py:516
  15.8 0.6 mix.1
  16.5 0.1 collective-permute-start.7
  16.5 0.5 collective-permute-start.9
  17.0 0.8 collective-permute-done.7.refs_1_
  17.8 0.1 collective-permute-start.8
  17.9 0.1 collective-permute-start.5
  18.7 2.5 %collective-permute-start.6 = (bf16[288,128]{1,0:T(8,128)(2,1)S(1)}, bf16[288,128]{1,0:T(8,128)(2,1)S(1)}, u32[]{:S(2)}, u32[]{:S(2)}) collective-permute-start(bf16[288,128]{1,0:T(8,128)(2,1)S(1)} %get-tuple-element.129), channel_id=1, source_target_pairs={{0,2},{2,0},{1,3},{3,1},{4,6},{6,4},{5,7},{7,5},{8,10},{10,8},{9,1... | collective-permute-start | bytes 221192 | tf_op jit(solution)/shard_map/ppermute | solution.py:34
  21.2 0.1 collective-permute-start.13
  21.3 0.7 collective-permute-start.4
  22.0 0.1 collective-permute-done.6.refs_1_
  22.1 2.5 %collective-permute-done.8.refs_2_ = bf16[576,128]{1,0:T(8,128)(2,1)S(1)} collective-permute-done((bf16[576,128]{1,0:T(8,128)(2,1)S(1)}, bf16[576,128]{1,0:T(8,128)(2,1)S(1)}, u32[]{:S(2)}, u32[]{:S(2)}) %collective-permute-start.8) | collective-permute-done | bytes 147488 | tf_op jit(solution)/shard_map/ppermute | solution.py:34
  24.6 0.1 collective-permute-start.12
  24.7 0.5 copy-done
  25.3 2.2 %weights.1 = (bf16[512,1024]{1,0:T(8,128)(2,1)S(1)}, bf16[512,1024]{1,0:T(8,128)(2,1)S(1)}, f32[8,128]{1,0:T(8,128)S(1)}) custom-call(s32[1,8]{1,0:T(1,128)S(1)} %copy-done, s32[1]{0:T(128)S(6)} %copy.28.refs_1_, bf16[1,8,128,128]{3,2,1,0:T(8,128)(2,1)S(1)} %get-tuple-element.110.refs_2_, bf16[128,1024]{1,0:T(8,128)(2,1)S(1)} %get-tuple-element.125.refs_3_, ...), custom_call_target="tpu_custom_call" | custom-call | bytes 3670052 | tf_op jit(solution)/shard_map/weights/pallas_call | solution.py:95
  27.5 1.9 %collective-permute-start.11 = (bf16[512,1024]{1,0:T(8,128)(2,1)S(1)}, bf16[512,1024]{1,0:T(8,128)(2,1)S(1)}, u32[]{:S(2)}, u32[]{:S(2)}) collective-permute-start(bf16[512,1024]{1,0:T(8,128)(2,1)S(1)} %get-tuple-element.141), channel_id=1, source_target_pairs={{0,2},{2,0},{1,3},{3,1},{4,6},{6,4},{5,7},{7,5},{8,10},{10,8},{9,1... | collective-permute-start | bytes 3145736 | tf_op jit(solution)/shard_map/ppermute | solution.py:34
  29.4 0.1 collective-permute-start.21
  29.5 2.0 %collective-permute-done.12.refs_1_ = bf16[1152,128]{1,0:T(8,128)(2,1)S(1)} collective-permute-done((bf16[1152,128]{1,0:T(8,128)(2,1)S(1)}, bf16[1152,128]{1,0:T(8,128)(2,1)S(1)}, u32[]{:S(2)}, u32[]{:S(2)}) %collective-permute-start.12) | collective-permute-done | bytes 294944 | tf_op jit(solution)/shard_map/ppermute | solution.py:44
  31.5 0.1 collective-permute-start.20
  31.7 0.2 core_sum.1
  31.9 2.0 %shares.1 = (bf16[384,512]{1,0:T(8,128)(2,1)S(1)}, bf16[128,512]{1,0:T(8,128)(2,1)S(1)}, f32[256,512]{1,0:T(8,128)S(1)}, f32[128,512]{1,0:T(8,128)S(1)}, f32[8,128]{1,0:T(8,128)S(1)}) custom-call(s32[1,8]{1,0:T(1,128)S(1)} %copy-done, s32[1]{0:T(128)S(6)} %copy.28.refs_1_, bf16[1,8,128,128]{3,2,1,0:T(8,128)(2,1)S(1)} %get-tuple-element.110.refs_2_, ...), custom_call_target="tpu_custom_call" | custom-call | bytes 2883620 | tf_op jit(solution)/shard_map/shares/pallas_call | solution.py:95
  34.0 1.6 %collective-permute-start.14 = (bf16[384,512]{1,0:T(8,128)(2,1)S(1)}, bf16[384,512]{1,0:T(8,128)(2,1)S(1)}, u32[]{:S(2)}, u32[]{:S(2)}) collective-permute-start(bf16[384,512]{1,0:T(8,128)(2,1)S(1)} %get-tuple-element.150), channel_id=1, source_target_pairs={{0,2},{2,0},{1,3},{3,1},{4,6},{6,4},{5,7},{7,5},{8,10},{10,8},{9,1... | collective-permute-start | bytes 1179656 | tf_op jit(solution)/shard_map/ppermute | solution.py:34
  35.6 1.1 %collective-permute-start.17 = (bf16[128,1024]{1,0:T(8,128)(2,1)S(1)}, bf16[128,1024]{1,0:T(8,128)(2,1)S(1)}, u32[]{:S(2)}, u32[]{:S(2)}) collective-permute-start(bf16[128,1024]{1,0:T(8,128)(2,1)S(1)} %get-tuple-element.159), channel_id=1, source_target_pairs={{0,4},{2,34},{4,8},{6,38},{8,12},{10,42},{12,0},{14,46},{32,36},{3... | collective-permute-start | bytes 786440 | tf_op jit(solution)/shard_map/ppermute | solution.py:57
  36.7 1.9 %collective-permute-start.18 = (bf16[128,1024]{1,0:T(8,128)(2,1)S(1)}, bf16[128,1024]{1,0:T(8,128)(2,1)S(1)}, u32[]{:S(2)}, u32[]{:S(2)}) collective-permute-start(bf16[128,1024]{1,0:T(8,128)(2,1)S(1)} %get-tuple-element.160), channel_id=1, source_target_pairs={{0,8},{2,66},{4,12},{6,70},{8,0},{10,74},{12,4},{14,78},{32,40},{3... | collective-permute-start | bytes 786440 | tf_op jit(solution)/shard_map/ppermute | solution.py:57
  38.6 6.1 %attention_near.1 = (f32[2,128,512]{2,1,0:T(8,128)S(1)}, f32[2,1024,128]{2,1,0:T(8,128)S(1)}, f32[8,128]{1,0:T(8,128)S(1)}) custom-call(bf16[2,1152,128]{2,1,0:T(8,128)(2,1)S(1)} %get-tuple-element.151.refs_0_, bf16[2,1024,128]{2,1,0:T(8,128)(2,1)S(1)} %get-tuple-element.152.refs_1_, f32[8,128]{1,0:T(8,128)S(1)} %get-tuple-element.153.refs_2_), custom_call_target="tpu_custom_call" | custom-call | flops 1342177280 | bytes 2686976 | tf_op jit(solution)/shard_map/attention_near/pallas_call | solution.py:95
  44.7 0.5 collective-permute-start.19
  45.2 0.1 near.1
  45.3 2.9 %collective-permute-start.15 = (bf16[256,512]{1,0:T(8,128)(2,1)S(1)}, bf16[256,512]{1,0:T(8,128)(2,1)S(1)}, u32[]{:S(2)}, u32[]{:S(2)}) collective-permute-start(bf16[256,512]{1,0:T(8,128)(2,1)S(1)} %get-tuple-element.156), channel_id=1, source_target_pairs={{0,4},{2,126},{4,8},{6,2},{8,12},{10,6},{12,16},{14,10},{16,20},{1... | collective-permute-start | bytes 786440 | tf_op jit(solution)/shard_map/ppermute | solution.py:621
  48.2 6.1 %attention_far.1 = (f32[2,128,512]{2,1,0:T(8,128)S(1)}, f32[2,1024,128]{2,1,0:T(8,128)S(1)}, f32[8,128]{1,0:T(8,128)S(1)}) custom-call(bf16[2,1152,128]{2,1,0:T(8,128)(2,1)S(1)} %collective-permute-done.20.refs_0_, bf16[2,1024,128]{2,1,0:T(8,128)(2,1)S(1)} %collective-permute-done.21.refs_1_, f32[8,128]{1,0:T(8,128)S(1)} %get-tuple-element.162.refs_2_), custom_call_target="tpu_custom_call" | custom-call | flops 1342177280 | bytes 2686976 | tf_op jit(solution)/shard_map/attention_far/pallas_call | solution.py:95
  54.3 0.1 add_ring.1
  54.5 2.4 %collective-permute-start.23 = (bf16[128,1024]{1,0:T(8,128)(2,1)S(1)}, bf16[128,1024]{1,0:T(8,128)(2,1)S(1)}, u32[]{:S(2)}, u32[]{:S(2)}) collective-permute-start(bf16[128,1024]{1,0:T(8,128)(2,1)S(1)} %get-tuple-element.167.refs_0_), channel_id=1, source_target_pairs={{0,32},{2,6},{4,36},{6,2},{8,40},{10,14},{12,44},{14,10},{32,0},{3... | collective-permute-start | bytes 786440 | tf_op jit(solution)/shard_map/ppermute | solution.py:57
  56.9 3.1 %attention_far_keys0.1 = (f32[2,128,512]{2,1,0:T(8,128)S(1)}, f32[2,1024,128]{2,1,0:T(8,128)S(1)}, f32[8,128]{1,0:T(8,128)S(1)}) custom-call(bf16[2,1152,128]{2,1,0:T(8,128)(2,1)S(1)} %get-tuple-element.151.refs_0_, bf16[2,1024,128]{2,1,0:T(8,128)(2,1)S(1)} %collective-permute-done.21.refs_1_, ...), custom_call_target="tpu_custom_call", output_to_operand_aliasing={{0}: (2, {}), {1}: (3, {})} | custom-call | flops 671088640 | bytes 4259840 | tf_op jit(solution)/shard_map/attention_far_keys0/pallas_call | solution.py:95
  60.0 0.9 collective-permute-done.23.refs_1_
  60.9 2.5 %collective-permute-start.24 = (bf16[128,1024]{1,0:T(8,128)(2,1)S(1)}, bf16[128,1024]{1,0:T(8,128)(2,1)S(1)}, u32[]{:S(2)}, u32[]{:S(2)}) collective-permute-start(bf16[128,1024]{1,0:T(8,128)(2,1)S(1)} %get-tuple-element.172.refs_0_), channel_id=1, source_target_pairs={{0,96},{2,14},{4,100},{6,10},{8,104},{10,6},{12,108},{14,2},{32,64... | collective-permute-start | bytes 786440 | tf_op jit(solution)/shard_map/ppermute | solution.py:57
  63.4 3.2 %attention_far_keys1.1 = (f32[2,128,512]{2,1,0:T(8,128)S(1)}, bf16[2,1024,128]{2,1,0:T(8,128)(2,1)S(1)}, f32[8,128]{1,0:T(8,128)S(1)}) custom-call(bf16[2,1152,128]{2,1,0:T(8,128)(2,1)S(1)} %get-tuple-element.151.refs_0_, bf16[2,1024,128]{2,1,0:T(8,128)(2,1)S(1)} %collective-permute-done.21.refs_1_, ...), custom_call_target="tpu_custom_call", output_to_operand_aliasing={{0}: (2, {})} | custom-call | flops 671088640 | bytes 3735552 | tf_op jit(solution)/shard_map/attention_far_keys1/pallas_call | solution.py:95
  66.6 0.2 collective-permute-start.29
  66.9 3.1 %attention_far_queries0.1 = (f32[2,128,512]{2,1,0:T(8,128)S(1)}, f32[2,1024,128]{2,1,0:T(8,128)S(1)}, f32[8,128]{1,0:T(8,128)S(1)}) custom-call(bf16[2,1152,128]{2,1,0:T(8,128)(2,1)S(1)} %collective-permute-done.20.refs_0_, bf16[2,1024,128]{2,1,0:T(8,128)(2,1)S(1)} %get-tuple-element.152.refs_1_, ...), custom_call_target="tpu_custom_call", output_to_operand_aliasing={{0}: (2, {}), {1}: (3, {})} | custom-call | flops 671088640 | bytes 4259840 | tf_op jit(solution)/shard_map/attention_far_queries0/pallas_call | solution.py:95
  70.0 0.3 collective-permute-start.25
  70.3 3.4 %attention_far_queries1.1 = (bf16[2,512,128]{2,1,0:T(8,128)(2,1)S(1)}, f32[2,1024,128]{2,1,0:T(8,128)S(1)}, f32[8,128]{1,0:T(8,128)S(1)}) custom-call(bf16[2,1152,128]{2,1,0:T(8,128)(2,1)S(1)} %collective-permute-done.20.refs_0_, bf16[2,1024,128]{2,1,0:T(8,128)(2,1)S(1)} %get-tuple-element.152.refs_1_, f32[2,128,512]{2,1,0:T(8,128)S(1)} %get-tuple-element.181.refs_2_, ...), custom_call_target="tpu_custom_call" | custom-call | flops 671088640 | bytes 3997696 | tf_op jit(solution)/shard_map/attention_far_queries1/pallas_call | solution.py:95
  73.7 1.0 collective-permute-start.30
  74.6 3.0 %collective-permute-done.25.refs_1_ = bf16[128,1024]{1,0:T(8,128)(2,1)S(1)} collective-permute-done((bf16[128,1024]{1,0:T(8,128)(2,1)S(1)}, bf16[128,1024]{1,0:T(8,128)(2,1)S(1)}, u32[]{:S(2)}, u32[]{:S(2)}) %collective-permute-start.25) | collective-permute-done | bytes 262176 | tf_op jit(solution)/shard_map/ppermute | solution.py:34
  77.9 1.8 %collective-permute-start.28 = (bf16[128,1024]{1,0:T(8,128)(2,1)S(1)}, bf16[128,1024]{1,0:T(8,128)(2,1)S(1)}, u32[]{:S(2)}, u32[]{:S(2)}) collective-permute-start(bf16[128,1024]{1,0:T(8,128)(2,1)S(1)} %get-tuple-element.185.refs_0_), channel_id=1, source_target_pairs={{0,12},{2,98},{4,0},{6,102},{8,4},{10,106},{12,8},{14,110},{32,44}... | collective-permute-start | bytes 786440 | tf_op jit(solution)/shard_map/ppermute | solution.py:57
  79.6 0.7 collective-permute-start.26
  80.3 0.2 turn.1
  80.6 2.1 %collective-permute-start.31 = (bf16[512,128]{1,0:T(8,128)(2,1)S(1)}, bf16[512,128]{1,0:T(8,128)(2,1)S(1)}, u32[]{:S(2)}, u32[]{:S(2)}) collective-permute-start(bf16[512,128]{1,0:T(8,128)(2,1)S(1)} %get-tuple-element.194), channel_id=1, source_target_pairs={{0,32},{2,98},{32,0},{34,66},{64,96},{66,34},{96,64},{98,2},{1,33}... | collective-permute-start | bytes 393224 | tf_op jit(solution)/shard_map/ppermute | solution.py:44
  82.7 7.9 %collective-permute-done.31.refs_2_ = bf16[512,128]{1,0:T(8,128)(2,1)S(1)} collective-permute-done((bf16[512,128]{1,0:T(8,128)(2,1)S(1)}, bf16[512,128]{1,0:T(8,128)(2,1)S(1)}, u32[]{:S(2)}, u32[]{:S(2)}) %collective-permute-start.31) | collective-permute-done | bytes 131104 | tf_op jit(solution)/shard_map/ppermute | solution.py:44
  90.6 0.1 back.1
  90.7 1.0 collective-permute-start.33
  91.7 0.9 collective-permute-done.33.refs_1_
  92.7 0.1 gather.1
  92.8 0.4 collective-permute-start.36
  93.2 1.0 collective-permute-start.35
  94.2 0.6 collective-permute-start.22
  94.8 1.0 collective-permute-done.22.refs_1_
  95.8 0.7 add_shares.1
  96.5 3.1 %collective-permute-done.35.refs_2_ = bf16[768,128]{1,0:T(8,128)(2,1)S(1)} collective-permute-done((bf16[768,128]{1,0:T(8,128)(2,1)S(1)}, bf16[768,128]{1,0:T(8,128)(2,1)S(1)}, u32[]{:S(2)}, u32[]{:S(2)}) %collective-permute-start.35) | collective-permute-done | bytes 196640 | tf_op jit(solution)/shard_map/ppermute | solution.py:34
  99.6 0.8 place.1
  100.4 2.3 %final.1 = (f32[512,1024]{1,0:T(8,128)}, f32[512,1024]{1,0:T(8,128)}, f32[8,128]{1,0:T(8,128)}) custom-call(bf16[512,1024]{1,0:T(8,128)(2,1)S(1)} %get-tuple-element.210.refs_0_, bf16[512,1024]{1,0:T(8,128)(2,1)S(1)} %collective-permute-done.36.refs_1_, f32[8,128]{1,0:T(8,128)S(1)} %get-tuple-element.211.refs_2_), custom_call_target="tpu_custom_call" | custom-call | bytes 6291456 | tf_op jit(solution)/shard_map/final/pallas_call | solution.py:95
  (48 shorter events, 0.8 us)
Async XLA Ops:
  0.6 7.1 %collective-permute-start.2 = (bf16[128,512]{1,0:T(8,128)(2,1)}, bf16[128,512]{1,0:T(8,128)(2,1)S(1)}, u32[]{:S(2)}, u32[]{:S(2)}) collective-permute-start(bf16[128,512]{1,0:T(8,128)(2,1)} %refs_0_.3), channel_id=1, source_target_pairs={{0,2},{2,0},{1,3},{3,1},{4,6},{6,4},{5,7},{7,5},{8,10},{10,8},{9,1... | collective-permute-start | bytes 393224 | tf_op jit(solution)/shard_map/ppermute | solution.py:34
  2.1 13.7 %collective-permute-start = (bf16[128,512]{1,0:T(8,128)(2,1)}, bf16[128,512]{1,0:T(8,128)(2,1)S(1)}, u32[]{:S(2)}, u32[]{:S(2)}) collective-permute-start(bf16[128,512]{1,0:T(8,128)(2,1)} %refs_2_.1), channel_id=1, source_target_pairs={{0,1},{1,0},{2,3},{3,2},{4,5},{5,4},{6,7},{7,6},{8,9},{9,8},{10,11... | collective-permute-start | bytes 393224 | tf_op jit(solution)/shard_map/ppermute | solution.py:34
  7.2 1.3 %collective-permute-start.1 = (bf16[256,128]{1,0:T(8,128)(2,1)S(1)}, bf16[256,128]{1,0:T(8,128)(2,1)S(1)}, u32[]{:S(2)}, u32[]{:S(2)}) collective-permute-start(bf16[256,128]{1,0:T(8,128)(2,1)S(1)} %get-tuple-element.120), channel_id=1, source_target_pairs={{0,2},{2,0},{1,3},{3,1},{4,6},{6,4},{5,7},{7,5},{8,10},{10,8},{9,1... | collective-permute-start | bytes 196616 | tf_op jit(solution)/shard_map/ppermute | solution.py:34
  8.6 12.6 %collective-permute-start.10 = (bf16[512,128]{1,0:T(8,128)(2,1)S(1)}, bf16[512,128]{1,0:T(8,128)(2,1)S(1)}, u32[]{:S(2)}, u32[]{:S(2)}) collective-permute-start(bf16[512,128]{1,0:T(8,128)(2,1)S(1)} %get-tuple-element.136), channel_id=1, source_target_pairs={{0,16},{16,0},{1,17},{17,1},{2,18},{18,2},{3,19},{19,3},{4,20},{20... | collective-permute-start | bytes 393224 | tf_op jit(solution)/shard_map/ppermute | solution.py:34
  9.1 12.2 %collective-permute-start.3 = (bf16[256,512]{1,0:T(8,128)(2,1)S(1)}, bf16[256,512]{1,0:T(8,128)(2,1)S(1)}, u32[]{:S(2)}, u32[]{:S(2)}) collective-permute-start(bf16[256,512]{1,0:T(8,128)(2,1)S(1)} %get-tuple-element.127), channel_id=1, source_target_pairs={{0,4},{2,126},{4,8},{6,2},{8,12},{10,6},{12,16},{14,10},{16,20},{1... | collective-permute-start | bytes 786440 | tf_op jit(solution)/shard_map/ppermute | solution.py:516
  15.8 2.1 %copy-start.1 = (bf16[128,512]{1,0:T(8,128)(2,1)S(1)}, bf16[128,512]{1,0:T(8,128)(2,1)}, u32[]{:S(2)}) copy-start(bf16[128,512]{1,0:T(8,128)(2,1)} %refs_0_.3) | copy-start | bytes 393220
  16.5 1.3 %collective-permute-start.7 = (bf16[288,128]{1,0:T(8,128)(2,1)S(1)}, bf16[288,128]{1,0:T(8,128)(2,1)S(1)}, u32[]{:S(2)}, u32[]{:S(2)}) collective-permute-start(bf16[288,128]{1,0:T(8,128)(2,1)S(1)} %get-tuple-element.131), channel_id=1, source_target_pairs={{0,2},{2,0},{1,3},{3,1},{4,6},{6,4},{5,7},{7,5},{8,10},{10,8},{9,1... | collective-permute-start | bytes 221192 | tf_op jit(solution)/shard_map/ppermute | solution.py:34
  16.5 2.1 %collective-permute-start.9 = (bf16[256,128]{1,0:T(8,128)(2,1)S(1)}, bf16[256,128]{1,0:T(8,128)(2,1)S(1)}, u32[]{:S(2)}, u32[]{:S(2)}) collective-permute-start(bf16[256,128]{1,0:T(8,128)(2,1)S(1)} %get-tuple-element.135), channel_id=1, source_target_pairs={{0,2},{2,0},{1,3},{3,1},{4,6},{6,4},{5,7},{7,5},{8,10},{10,8},{9,1... | collective-permute-start | bytes 196616 | tf_op jit(solution)/shard_map/ppermute | solution.py:34
  17.8 6.8 %collective-permute-start.8 = (bf16[576,128]{1,0:T(8,128)(2,1)S(1)}, bf16[576,128]{1,0:T(8,128)(2,1)S(1)}, u32[]{:S(2)}, u32[]{:S(2)}) collective-permute-start(bf16[576,128]{1,0:T(8,128)(2,1)S(1)} %get-tuple-element.133), channel_id=1, source_target_pairs={{0,16},{16,0},{1,17},{17,1},{2,18},{18,2},{3,19},{19,3},{4,20},{20... | collective-permute-start | bytes 442376 | tf_op jit(solution)/shard_map/ppermute | solution.py:34
  17.9 6.8 %collective-permute-start.5 = (bf16[128,512]{1,0:T(8,128)(2,1)S(1)}, bf16[128,512]{1,0:T(8,128)(2,1)S(1)}, u32[]{:S(2)}, u32[]{:S(2)}) collective-permute-start(bf16[128,512]{1,0:T(8,128)(2,1)S(1)} %copy-done.1), channel_id=1, source_target_pairs={{0,122},{2,8},{4,126},{6,12},{8,2},{10,16},{12,6},{14,20},{16,10},... | collective-permute-start | bytes 393224 | tf_op jit(solution)/shard_map/ppermute | solution.py:496
  18.7 3.4 %collective-permute-start.6 = (bf16[288,128]{1,0:T(8,128)(2,1)S(1)}, bf16[288,128]{1,0:T(8,128)(2,1)S(1)}, u32[]{:S(2)}, u32[]{:S(2)}) collective-permute-start(bf16[288,128]{1,0:T(8,128)(2,1)S(1)} %get-tuple-element.129), channel_id=1, source_target_pairs={{0,2},{2,0},{1,3},{3,1},{4,6},{6,4},{5,7},{7,5},{8,10},{10,8},{9,1... | collective-permute-start | bytes 221192 | tf_op jit(solution)/shard_map/ppermute | solution.py:34
  21.2 8.2 %collective-permute-start.13 = (bf16[1024,128]{1,0:T(8,128)(2,1)S(1)}, bf16[1024,128]{1,0:T(8,128)(2,1)S(1)}, u32[]{:S(2)}, u32[]{:S(2)}) collective-permute-start(bf16[1024,128]{1,0:T(8,128)(2,1)S(1)} %get-tuple-element.143.refs_0_), channel_id=1, source_target_pairs={{0,4},{2,14},{4,0},{6,10},{8,12},{10,6},{12,8},{14,2},{1,5},{3,15}... | collective-permute-start | bytes 786440 | tf_op jit(solution)/shard_map/ppermute | solution.py:44
  21.3 3.4 %collective-permute-start.4 = (bf16[256,512]{1,0:T(8,128)(2,1)S(1)}, bf16[256,512]{1,0:T(8,128)(2,1)S(1)}, u32[]{:S(2)}, u32[]{:S(2)}) collective-permute-start(bf16[256,512]{1,0:T(8,128)(2,1)S(1)} %collective-permute-done.3.refs_7_), channel_id=1, source_target_pairs={{0,2},{2,0},{1,3},{3,1},{4,6},{6,4},{5,7},{7,5},{8,10},{10,8},{9,1... | collective-permute-start | bytes 786440 | tf_op jit(solution)/shard_map/ppermute | solution.py:34
  24.6 0.7 copy-start
  24.6 6.9 %collective-permute-start.12 = (bf16[1152,128]{1,0:T(8,128)(2,1)S(1)}, bf16[1152,128]{1,0:T(8,128)(2,1)S(1)}, u32[]{:S(2)}, u32[]{:S(2)}) collective-permute-start(bf16[1152,128]{1,0:T(8,128)(2,1)S(1)} %get-tuple-element.142.refs_0_), channel_id=1, source_target_pairs={{0,32},{2,98},{32,0},{34,66},{64,96},{66,34},{96,64},{98,2},{1,33}... | collective-permute-start | bytes 884744 | tf_op jit(solution)/shard_map/ppermute | solution.py:44
  27.5 4.2 %collective-permute-start.11 = (bf16[512,1024]{1,0:T(8,128)(2,1)S(1)}, bf16[512,1024]{1,0:T(8,128)(2,1)S(1)}, u32[]{:S(2)}, u32[]{:S(2)}) collective-permute-start(bf16[512,1024]{1,0:T(8,128)(2,1)S(1)} %get-tuple-element.141), channel_id=1, source_target_pairs={{0,2},{2,0},{1,3},{3,1},{4,6},{6,4},{5,7},{7,5},{8,10},{10,8},{9,1... | collective-permute-start | bytes 3145736 | tf_op jit(solution)/shard_map/ppermute | solution.py:34
  29.4 15.9 %collective-permute-start.21 = (bf16[2,1024,128]{2,1,0:T(8,128)(2,1)S(1)}, bf16[2,1024,128]{2,1,0:T(8,128)(2,1)S(1)}, u32[]{:S(2)}, u32[]{:S(2)}) collective-permute-start(bf16[2,1024,128]{2,1,0:T(8,128)(2,1)S(1)} %get-tuple-element.152.refs_1_), channel_id=1, source_target_pairs={{0,12},{2,6},{4,8},{6,2},{8,4},{10,14},{12,0},{14,10},{1,13},{3,7}... | collective-permute-start | bytes 1572872 | tf_op jit(solution)/shard_map/ppermute | solution.py:44
  31.5 16.7 %collective-permute-start.20 = (bf16[2,1152,128]{2,1,0:T(8,128)(2,1)S(1)}, bf16[2,1152,128]{2,1,0:T(8,128)(2,1)S(1)}, u32[]{:S(2)}, u32[]{:S(2)}) collective-permute-start(bf16[2,1152,128]{2,1,0:T(8,128)(2,1)S(1)} %get-tuple-element.151.refs_0_), channel_id=1, source_target_pairs={{0,96},{2,34},{32,64},{34,2},{64,32},{66,98},{96,0},{98,66},{1,97}... | collective-permute-start | bytes 1769480 | tf_op jit(solution)/shard_map/ppermute | solution.py:44
  34.0 10.7 %collective-permute-start.14 = (bf16[384,512]{1,0:T(8,128)(2,1)S(1)}, bf16[384,512]{1,0:T(8,128)(2,1)S(1)}, u32[]{:S(2)}, u32[]{:S(2)}) collective-permute-start(bf16[384,512]{1,0:T(8,128)(2,1)S(1)} %get-tuple-element.150), channel_id=1, source_target_pairs={{0,2},{2,0},{1,3},{3,1},{4,6},{6,4},{5,7},{7,5},{8,10},{10,8},{9,1... | collective-permute-start | bytes 1179656 | tf_op jit(solution)/shard_map/ppermute | solution.py:34
  35.6 18.7 %collective-permute-start.17 = (bf16[128,1024]{1,0:T(8,128)(2,1)S(1)}, bf16[128,1024]{1,0:T(8,128)(2,1)S(1)}, u32[]{:S(2)}, u32[]{:S(2)}) collective-permute-start(bf16[128,1024]{1,0:T(8,128)(2,1)S(1)} %get-tuple-element.159), channel_id=1, source_target_pairs={{0,4},{2,34},{4,8},{6,38},{8,12},{10,42},{12,0},{14,46},{32,36},{3... | collective-permute-start | bytes 786440 | tf_op jit(solution)/shard_map/ppermute | solution.py:57
  36.7 17.6 %collective-permute-start.18 = (bf16[128,1024]{1,0:T(8,128)(2,1)S(1)}, bf16[128,1024]{1,0:T(8,128)(2,1)S(1)}, u32[]{:S(2)}, u32[]{:S(2)}) collective-permute-start(bf16[128,1024]{1,0:T(8,128)(2,1)S(1)} %get-tuple-element.160), channel_id=1, source_target_pairs={{0,8},{2,66},{4,12},{6,70},{8,0},{10,74},{12,4},{14,78},{32,40},{3... | collective-permute-start | bytes 786440 | tf_op jit(solution)/shard_map/ppermute | solution.py:57
  44.7 9.6 %collective-permute-start.19 = (bf16[128,1024]{1,0:T(8,128)(2,1)S(1)}, bf16[128,1024]{1,0:T(8,128)(2,1)S(1)}, u32[]{:S(2)}, u32[]{:S(2)}) collective-permute-start(bf16[128,1024]{1,0:T(8,128)(2,1)S(1)} %get-tuple-element.161), channel_id=1, source_target_pairs={{0,12},{2,98},{4,0},{6,102},{8,4},{10,106},{12,8},{14,110},{32,44}... | collective-permute-start | bytes 786440 | tf_op jit(solution)/shard_map/ppermute | solution.py:57
  45.3 11.5 %collective-permute-start.15 = (bf16[256,512]{1,0:T(8,128)(2,1)S(1)}, bf16[256,512]{1,0:T(8,128)(2,1)S(1)}, u32[]{:S(2)}, u32[]{:S(2)}) collective-permute-start(bf16[256,512]{1,0:T(8,128)(2,1)S(1)} %get-tuple-element.156), channel_id=1, source_target_pairs={{0,4},{2,126},{4,8},{6,2},{8,12},{10,6},{12,16},{14,10},{16,20},{1... | collective-permute-start | bytes 786440 | tf_op jit(solution)/shard_map/ppermute | solution.py:621
  48.2 8.6 %collective-permute-start.16 = (bf16[128,512]{1,0:T(8,128)(2,1)S(1)}, bf16[128,512]{1,0:T(8,128)(2,1)S(1)}, u32[]{:S(2)}, u32[]{:S(2)}) collective-permute-start(bf16[128,512]{1,0:T(8,128)(2,1)S(1)} %get-tuple-element.157), channel_id=1, source_target_pairs={{0,122},{2,8},{4,126},{6,12},{8,2},{10,16},{12,6},{14,20},{16,10},... | collective-permute-start | bytes 393224 | tf_op jit(solution)/shard_map/ppermute | solution.py:621
  54.5 6.4 %collective-permute-start.23 = (bf16[128,1024]{1,0:T(8,128)(2,1)S(1)}, bf16[128,1024]{1,0:T(8,128)(2,1)S(1)}, u32[]{:S(2)}, u32[]{:S(2)}) collective-permute-start(bf16[128,1024]{1,0:T(8,128)(2,1)S(1)} %get-tuple-element.167.refs_0_), channel_id=1, source_target_pairs={{0,32},{2,6},{4,36},{6,2},{8,40},{10,14},{12,44},{14,10},{32,0},{3... | collective-permute-start | bytes 786440 | tf_op jit(solution)/shard_map/ppermute | solution.py:57
  60.9 9.0 %collective-permute-start.24 = (bf16[128,1024]{1,0:T(8,128)(2,1)S(1)}, bf16[128,1024]{1,0:T(8,128)(2,1)S(1)}, u32[]{:S(2)}, u32[]{:S(2)}) collective-permute-start(bf16[128,1024]{1,0:T(8,128)(2,1)S(1)} %get-tuple-element.172.refs_0_), channel_id=1, source_target_pairs={{0,96},{2,14},{4,100},{6,10},{8,104},{10,6},{12,108},{14,2},{32,64... | collective-permute-start | bytes 786440 | tf_op jit(solution)/shard_map/ppermute | solution.py:57
  66.6 11.1 %collective-permute-start.29 = (bf16[2,1024,128]{2,1,0:T(8,128)(2,1)S(1)}, bf16[2,1024,128]{2,1,0:T(8,128)(2,1)S(1)}, u32[]{:S(2)}, u32[]{:S(2)}) collective-permute-start(bf16[2,1024,128]{2,1,0:T(8,128)(2,1)S(1)} %get-tuple-element.188), channel_id=1, source_target_pairs={{0,12},{2,6},{4,8},{6,2},{8,4},{10,14},{12,0},{14,10},{1,13},{3,7}... | collective-permute-start | bytes 1572872 | tf_op jit(solution)/shard_map/ppermute | solution.py:44
  70.0 7.6 %collective-permute-start.25 = (bf16[128,1024]{1,0:T(8,128)(2,1)S(1)}, bf16[128,1024]{1,0:T(8,128)(2,1)S(1)}, u32[]{:S(2)}, u32[]{:S(2)}) collective-permute-start(bf16[128,1024]{1,0:T(8,128)(2,1)S(1)} %get-tuple-element.180.refs_0_), channel_id=1, source_target_pairs={{0,16},{16,0},{1,17},{17,1},{2,18},{18,2},{3,19},{19,3},{4,20},{20... | collective-permute-start | bytes 786440 | tf_op jit(solution)/shard_map/ppermute | solution.py:34
  73.7 6.9 %collective-permute-start.30 = (bf16[2,512,128]{2,1,0:T(8,128)(2,1)S(1)}, bf16[2,512,128]{2,1,0:T(8,128)(2,1)S(1)}, u32[]{:S(2)}, u32[]{:S(2)}) collective-permute-start(bf16[2,512,128]{2,1,0:T(8,128)(2,1)S(1)} %get-tuple-element.192), channel_id=1, source_target_pairs={{0,96},{2,34},{32,64},{34,2},{64,32},{66,98},{96,0},{98,66},{1,97}... | collective-permute-start | bytes 786440 | tf_op jit(solution)/shard_map/ppermute | solution.py:44
  77.8 12.8 %collective-permute-start.32 = (bf16[1024,128]{1,0:T(8,128)(2,1)S(1)}, bf16[1024,128]{1,0:T(8,128)(2,1)S(1)}, u32[]{:S(2)}, u32[]{:S(2)}) collective-permute-start(bf16[1024,128]{1,0:T(8,128)(2,1)S(1)} %get-tuple-element.195), channel_id=1, source_target_pairs={{0,4},{2,14},{4,0},{6,10},{8,12},{10,6},{12,8},{14,2},{1,5},{3,15}... | collective-permute-start | bytes 786440 | tf_op jit(solution)/shard_map/ppermute | solution.py:44
  77.9 14.8 %collective-permute-start.28 = (bf16[128,1024]{1,0:T(8,128)(2,1)S(1)}, bf16[128,1024]{1,0:T(8,128)(2,1)S(1)}, u32[]{:S(2)}, u32[]{:S(2)}) collective-permute-start(bf16[128,1024]{1,0:T(8,128)(2,1)S(1)} %get-tuple-element.185.refs_0_), channel_id=1, source_target_pairs={{0,12},{2,98},{4,0},{6,102},{8,4},{10,106},{12,8},{14,110},{32,44}... | collective-permute-start | bytes 786440 | tf_op jit(solution)/shard_map/ppermute | solution.py:57
  79.6 13.0 %collective-permute-start.27 = (bf16[128,1024]{1,0:T(8,128)(2,1)S(1)}, bf16[128,1024]{1,0:T(8,128)(2,1)S(1)}, u32[]{:S(2)}, u32[]{:S(2)}) collective-permute-start(bf16[128,1024]{1,0:T(8,128)(2,1)S(1)} %get-tuple-element.185.refs_0_), channel_id=1, source_target_pairs={{0,8},{2,66},{4,12},{6,70},{8,0},{10,74},{12,4},{14,78},{32,40},{3... | collective-permute-start | bytes 786440 | tf_op jit(solution)/shard_map/ppermute | solution.py:57
  79.6 13.0 %collective-permute-start.26 = (bf16[128,1024]{1,0:T(8,128)(2,1)S(1)}, bf16[128,1024]{1,0:T(8,128)(2,1)S(1)}, u32[]{:S(2)}, u32[]{:S(2)}) collective-permute-start(bf16[128,1024]{1,0:T(8,128)(2,1)S(1)} %get-tuple-element.185.refs_0_), channel_id=1, source_target_pairs={{0,4},{2,34},{4,8},{6,38},{8,12},{10,42},{12,0},{14,46},{32,36},{3... | collective-permute-start | bytes 786440 | tf_op jit(solution)/shard_map/ppermute | solution.py:57
  80.6 10.0 %collective-permute-start.31 = (bf16[512,128]{1,0:T(8,128)(2,1)S(1)}, bf16[512,128]{1,0:T(8,128)(2,1)S(1)}, u32[]{:S(2)}, u32[]{:S(2)}) collective-permute-start(bf16[512,128]{1,0:T(8,128)(2,1)S(1)} %get-tuple-element.194), channel_id=1, source_target_pairs={{0,32},{2,98},{32,0},{34,66},{64,96},{66,34},{96,64},{98,2},{1,33}... | collective-permute-start | bytes 393224 | tf_op jit(solution)/shard_map/ppermute | solution.py:44
  90.7 1.9 %collective-permute-start.33 = (bf16[384,128]{1,0:T(8,128)(2,1)S(1)}, bf16[384,128]{1,0:T(8,128)(2,1)S(1)}, u32[]{:S(2)}, u32[]{:S(2)}) collective-permute-start(bf16[384,128]{1,0:T(8,128)(2,1)S(1)} %get-tuple-element.198), channel_id=1, source_target_pairs={{0,2},{2,0},{1,3},{3,1},{4,6},{6,4},{5,7},{7,5},{8,10},{10,8},{9,1... | collective-permute-start | bytes 294920 | tf_op jit(solution)/shard_map/ppermute | solution.py:34
  92.8 7.6 %collective-permute-start.36 = (bf16[512,1024]{1,0:T(8,128)(2,1)S(1)}, bf16[512,1024]{1,0:T(8,128)(2,1)S(1)}, u32[]{:S(2)}, u32[]{:S(2)}) collective-permute-start(bf16[512,1024]{1,0:T(8,128)(2,1)S(1)} %get-tuple-element.210.refs_0_), channel_id=1, source_target_pairs={{0,2},{2,0},{1,3},{3,1},{4,6},{6,4},{5,7},{7,5},{8,10},{10,8},{9,1... | collective-permute-start | bytes 3145736 | tf_op jit(solution)/shard_map/ppermute | solution.py:34
  93.2 6.3 %collective-permute-start.35 = (bf16[768,128]{1,0:T(8,128)(2,1)S(1)}, bf16[768,128]{1,0:T(8,128)(2,1)S(1)}, u32[]{:S(2)}, u32[]{:S(2)}) collective-permute-start(bf16[768,128]{1,0:T(8,128)(2,1)S(1)} %get-tuple-element.205), channel_id=1, source_target_pairs={{0,16},{16,0},{1,17},{17,1},{2,18},{18,2},{3,19},{19,3},{4,20},{20... | collective-permute-start | bytes 589832 | tf_op jit(solution)/shard_map/ppermute | solution.py:34
  94.2 1.6 %collective-permute-start.22 = (bf16[128,512]{1,0:T(8,128)(2,1)S(1)}, bf16[128,512]{1,0:T(8,128)(2,1)S(1)}, u32[]{:S(2)}, u32[]{:S(2)}) collective-permute-start(bf16[128,512]{1,0:T(8,128)(2,1)S(1)} %get-tuple-element.166), channel_id=1, source_target_pairs={{0,2},{2,0},{1,3},{3,1},{4,6},{6,4},{5,7},{7,5},{8,10},{10,8},{9,1... | collective-permute-start | bytes 393224 | tf_op jit(solution)/shard_map/ppermute | solution.py:34
  94.8 1.7 %collective-permute-start.34 = (bf16[384,128]{1,0:T(8,128)(2,1)S(1)}, bf16[384,128]{1,0:T(8,128)(2,1)S(1)}, u32[]{:S(2)}, u32[]{:S(2)}) collective-permute-start(bf16[384,128]{1,0:T(8,128)(2,1)S(1)} %get-tuple-element.204), channel_id=1, source_target_pairs={{0,2},{2,0},{1,3},{3,1},{4,6},{6,4},{5,7},{7,5},{8,10},{10,8},{9,1... | collective-permute-start | bytes 294920 | tf_op jit(solution)/shard_map/ppermute | solution.py:34

commit v6 on v5

--- a/solution.py
+++ b/solution.py
@@ -680,15 +680,15 @@
     (whole,) = order.call(gather_kernel, [shaped((columns, 2 * columns))], *blocks, name="gather")
     received = swap(whole, "c", 1)
     grad_features = add(order, "shares", share_local, share_cross)
-    grad_query, grad_key, grad_value = order.call(
-        place_kernel, [shaped((rows, columns))] * 3, back_own, back_near, back_far, name="place"
-    )
     out_weight_grad, msg_weight_grad = order.call(
         final_kernel,
         [shaped((columns, 2 * columns), F32)] * 2,
         whole,
         received,
         name="final",
+    )
+    grad_query, grad_key, grad_value = order.call(
+        place_kernel, [shaped((rows, columns))] * 3, back_own, back_near, back_far, name="place"
     )
     return (grad_features, grad_query, grad_key, grad_value, out_weight_grad, msg_weight_grad)
 

time: 103 us -> 102 us (level); the launches traced: 103 us -> 100 us
  waiting for transfers between devices: 23.2 us -> 19.3 us
  Pallas kernels: 36.9 us -> 38.4 us
    ppermute x17, waiting for transfers between devices: 12.4 us -> 8.45 us  [swap(): return lax.ppermute(value, axes, [(i, i ^ mask) for i in range(count)])]
    ppermute x1, starting transfers between devices: 2.89 us -> 1.2 us  [body(): lax.ppermute(share_near, NODE, to_near)]
    ppermute x8, starting transfers between devices: 10.9 us -> 12.5 us  [ring(): return lax.ppermute(value, ('z', 'x', 'c'), pairs)]
    pallas_call x34, Pallas kernels: 36.9 us -> 38.4 us  [call(): pl.pallas_call(whole, out_shape=[*outs, shaped((8, LANES), F32)], in_spec...]
  transfers between devices with their start and end apart: 37 -> 37, of which waited for: 12 -> 12; matrix products, arithmetic and copies ran while one was open for 0% -> 0% of each run, Pallas kernels for 34% -> 37%
where the time goes in v6:
time: 102 us; the launch traced here: 100 us
  starting transfers between devices  40.4 us (40%)
  Pallas kernels  38.4 us (38%)
  waiting for transfers between devices  19.3 us (19%)
  between operations  1.66 us (2%)
    pallas_call x34, Pallas kernels, call(): pl.pallas_call(whole, out_shape=[*outs, shaped((8, LANES), F32)], in_spec...  38.4 us
    ppermute x17, starting transfers between devices, swap(): return lax.ppermute(value, axes, [(i, i ^ mask) for i in range(count)])  15.7 us
    ppermute x8, starting transfers between devices, ring(): return lax.ppermute(value, ('z', 'x', 'c'), pairs)  12.5 us
    ppermute x8, waiting for transfers between devices, meet(): return lax.ppermute(value, (axis, 'c'), pairs)  9.9 us
    ppermute x17, waiting for transfers between devices, swap(): return lax.ppermute(value, axes, [(i, i ^ mask) for i in range(count)])  8.45 us
    ppermute x1, starting transfers between devices, body(): near_features = lax.ppermute(near_features, NODE, to_near)  6.74 us
    ppermute x8, starting transfers between devices, meet(): return lax.ppermute(value, (axis, 'c'), pairs)  3.53 us
  transfers between devices with their start and end apart: 37, of which 12 were waited for; matrix products, arithmetic and copies ran while one was open for 0% of the time, Pallas kernels for 37%

profile of v6, /device:TPU:1, one launch (start us, length us, event | category | flops | bytes accessed | tf_op | source)
XLA Modules:
  0.0 100.3 jit_solution(17270006139522679962)
XLA Ops:
  0.6 1.5 %collective-permute-start.2 = (bf16[128,512]{1,0:T(8,128)(2,1)}, bf16[128,512]{1,0:T(8,128)(2,1)S(1)}, u32[]{:S(2)}, u32[]{:S(2)}) collective-permute-start(bf16[128,512]{1,0:T(8,128)(2,1)} %refs_0_.3), channel_id=1, source_target_pairs={{0,2},{2,0},{1,3},{3,1},{4,6},{6,4},{5,7},{7,5},{8,10},{10,8},{9,1... | collective-permute-start | bytes 393224 | tf_op jit(solution)/shard_map/ppermute | solution.py:34
  2.1 3.0 %collective-permute-start = (bf16[128,512]{1,0:T(8,128)(2,1)}, bf16[128,512]{1,0:T(8,128)(2,1)S(1)}, u32[]{:S(2)}, u32[]{:S(2)}) collective-permute-start(bf16[128,512]{1,0:T(8,128)(2,1)} %refs_2_.1), channel_id=1, source_target_pairs={{0,1},{1,0},{2,3},{3,2},{4,5},{5,4},{6,7},{7,6},{8,9},{9,8},{10,11... | collective-permute-start | bytes 393224 | tf_op jit(solution)/shard_map/ppermute | solution.py:34
  5.1 2.0 %load.1 = (bf16[128,512]{1,0:T(8,128)(2,1)S(1)}, bf16[1,8,128,128]{3,2,1,0:T(8,128)(2,1)S(1)}, bf16[128,512]{1,0:T(8,128)(2,1)S(1)}, bf16[128,512]{1,0:T(8,128)(...) custom-call(bf16[128,512]{1,0:T(8,128)(2,1)} %refs_0_.3, ...), custom_call_target="tpu_custom_call" | custom-call | bytes 6299648 | tf_op jit(solution)/shard_map/load/pallas_call | solution.py:95
  7.2 0.4 collective-permute-start.1
  7.7 0.9 collective-permute-done.1.refs_1_
  8.6 0.5 collective-permute-start.10
  9.1 6.7 %collective-permute-start.3 = (bf16[256,512]{1,0:T(8,128)(2,1)S(1)}, bf16[256,512]{1,0:T(8,128)(2,1)S(1)}, u32[]{:S(2)}, u32[]{:S(2)}) collective-permute-start(bf16[256,512]{1,0:T(8,128)(2,1)S(1)} %get-tuple-element.127), channel_id=1, source_target_pairs={{0,4},{2,126},{4,8},{6,2},{8,12},{10,6},{12,16},{14,10},{16,20},{1... | collective-permute-start | bytes 786440 | tf_op jit(solution)/shard_map/ppermute | solution.py:516
  15.8 0.6 mix.1
  16.5 0.1 collective-permute-start.7
  16.5 0.5 collective-permute-start.9
  17.0 0.8 collective-permute-done.7.refs_1_
  17.8 0.1 collective-permute-start.8
  17.9 0.1 collective-permute-start.5
  18.7 2.5 %collective-permute-start.6 = (bf16[288,128]{1,0:T(8,128)(2,1)S(1)}, bf16[288,128]{1,0:T(8,128)(2,1)S(1)}, u32[]{:S(2)}, u32[]{:S(2)}) collective-permute-start(bf16[288,128]{1,0:T(8,128)(2,1)S(1)} %get-tuple-element.129), channel_id=1, source_target_pairs={{0,2},{2,0},{1,3},{3,1},{4,6},{6,4},{5,7},{7,5},{8,10},{10,8},{9,1... | collective-permute-start | bytes 221192 | tf_op jit(solution)/shard_map/ppermute | solution.py:34
  21.2 0.1 collective-permute-start.13
  21.3 0.7 collective-permute-start.4
  22.0 0.1 collective-permute-done.6.refs_1_
  22.1 2.5 %collective-permute-done.8.refs_2_ = bf16[576,128]{1,0:T(8,128)(2,1)S(1)} collective-permute-done((bf16[576,128]{1,0:T(8,128)(2,1)S(1)}, bf16[576,128]{1,0:T(8,128)(2,1)S(1)}, u32[]{:S(2)}, u32[]{:S(2)}) %collective-permute-start.8) | collective-permute-done | bytes 147488 | tf_op jit(solution)/shard_map/ppermute | solution.py:34
  24.6 0.1 collective-permute-start.12
  24.7 0.5 copy-done
  25.3 2.9 %weights.1 = (bf16[512,1024]{1,0:T(8,128)(2,1)S(1)}, bf16[512,1024]{1,0:T(8,128)(2,1)S(1)}, f32[8,128]{1,0:T(8,128)S(1)}) custom-call(s32[1,8]{1,0:T(1,128)S(1)} %copy-done, s32[1]{0:T(128)S(6)} %copy.28.refs_1_, bf16[1,8,128,128]{3,2,1,0:T(8,128)(2,1)S(1)} %get-tuple-element.110.refs_2_, bf16[128,1024]{1,0:T(8,128)(2,1)S(1)} %get-tuple-element.125.refs_3_, ...), custom_call_target="tpu_custom_call" | custom-call | bytes 3670052 | tf_op jit(solution)/shard_map/weights/pallas_call | solution.py:95
  28.2 1.2 %collective-permute-start.11 = (bf16[512,1024]{1,0:T(8,128)(2,1)S(1)}, bf16[512,1024]{1,0:T(8,128)(2,1)S(1)}, u32[]{:S(2)}, u32[]{:S(2)}) collective-permute-start(bf16[512,1024]{1,0:T(8,128)(2,1)S(1)} %get-tuple-element.141), channel_id=1, source_target_pairs={{0,2},{2,0},{1,3},{3,1},{4,6},{6,4},{5,7},{7,5},{8,10},{10,8},{9,1... | collective-permute-start | bytes 3145736 | tf_op jit(solution)/shard_map/ppermute | solution.py:34
  29.5 2.0 %collective-permute-done.12.refs_1_ = bf16[1152,128]{1,0:T(8,128)(2,1)S(1)} collective-permute-done((bf16[1152,128]{1,0:T(8,128)(2,1)S(1)}, bf16[1152,128]{1,0:T(8,128)(2,1)S(1)}, u32[]{:S(2)}, u32[]{:S(2)}) %collective-permute-start.12) | collective-permute-done | bytes 294944 | tf_op jit(solution)/shard_map/ppermute | solution.py:44
  31.5 0.1 collective-permute-start.20
  31.7 0.2 core_sum.1
  31.9 2.8 %shares.1 = (bf16[384,512]{1,0:T(8,128)(2,1)S(1)}, bf16[128,512]{1,0:T(8,128)(2,1)S(1)}, f32[256,512]{1,0:T(8,128)S(1)}, f32[128,512]{1,0:T(8,128)S(1)}, f32[8,128]{1,0:T(8,128)S(1)}) custom-call(s32[1,8]{1,0:T(1,128)S(1)} %copy-done, s32[1]{0:T(128)S(6)} %copy.28.refs_1_, bf16[1,8,128,128]{3,2,1,0:T(8,128)(2,1)S(1)} %get-tuple-element.110.refs_2_, ...), custom_call_target="tpu_custom_call" | custom-call | bytes 2883620 | tf_op jit(solution)/shard_map/shares/pallas_call | solution.py:95
  34.8 0.8 collective-permute-start.14
  35.6 1.9 %collective-permute-start.17 = (bf16[128,1024]{1,0:T(8,128)(2,1)S(1)}, bf16[128,1024]{1,0:T(8,128)(2,1)S(1)}, u32[]{:S(2)}, u32[]{:S(2)}) collective-permute-start(bf16[128,1024]{1,0:T(8,128)(2,1)S(1)} %get-tuple-element.159), channel_id=1, source_target_pairs={{0,4},{2,34},{4,8},{6,38},{8,12},{10,42},{12,0},{14,46},{32,36},{3... | collective-permute-start | bytes 786440 | tf_op jit(solution)/shard_map/ppermute | solution.py:57
  37.5 0.9 collective-permute-start.18
  38.4 6.1 %attention_near.1 = (f32[2,128,512]{2,1,0:T(8,128)S(1)}, f32[2,1024,128]{2,1,0:T(8,128)S(1)}, f32[8,128]{1,0:T(8,128)S(1)}) custom-call(bf16[2,1152,128]{2,1,0:T(8,128)(2,1)S(1)} %get-tuple-element.151.refs_0_, bf16[2,1024,128]{2,1,0:T(8,128)(2,1)S(1)} %get-tuple-element.152.refs_1_, f32[8,128]{1,0:T(8,128)S(1)} %get-tuple-element.153.refs_2_), custom_call_target="tpu_custom_call" | custom-call | flops 1342177280 | bytes 2686976 | tf_op jit(solution)/shard_map/attention_near/pallas_call | solution.py:95
  44.5 1.6 %collective-permute-start.19 = (bf16[128,1024]{1,0:T(8,128)(2,1)S(1)}, bf16[128,1024]{1,0:T(8,128)(2,1)S(1)}, u32[]{:S(2)}, u32[]{:S(2)}) collective-permute-start(bf16[128,1024]{1,0:T(8,128)(2,1)S(1)} %get-tuple-element.161), channel_id=1, source_target_pairs={{0,12},{2,98},{4,0},{6,102},{8,4},{10,106},{12,8},{14,110},{32,44}... | collective-permute-start | bytes 786440 | tf_op jit(solution)/shard_map/ppermute | solution.py:57
  46.0 0.1 near.1
  46.1 1.2 %collective-permute-start.15 = (bf16[256,512]{1,0:T(8,128)(2,1)S(1)}, bf16[256,512]{1,0:T(8,128)(2,1)S(1)}, u32[]{:S(2)}, u32[]{:S(2)}) collective-permute-start(bf16[256,512]{1,0:T(8,128)(2,1)S(1)} %get-tuple-element.156), channel_id=1, source_target_pairs={{0,4},{2,126},{4,8},{6,2},{8,12},{10,6},{12,16},{14,10},{16,20},{1... | collective-permute-start | bytes 786440 | tf_op jit(solution)/shard_map/ppermute | solution.py:621
  47.3 0.7 collective-permute-start.16
  48.0 6.1 %attention_far.1 = (f32[2,128,512]{2,1,0:T(8,128)S(1)}, f32[2,1024,128]{2,1,0:T(8,128)S(1)}, f32[8,128]{1,0:T(8,128)S(1)}) custom-call(bf16[2,1152,128]{2,1,0:T(8,128)(2,1)S(1)} %collective-permute-done.20.refs_0_, bf16[2,1024,128]{2,1,0:T(8,128)(2,1)S(1)} %collective-permute-done.21.refs_1_, f32[8,128]{1,0:T(8,128)S(1)} %get-tuple-element.162.refs_2_), custom_call_target="tpu_custom_call" | custom-call | flops 1342177280 | bytes 2686976 | tf_op jit(solution)/shard_map/attention_far/pallas_call | solution.py:95
  54.1 0.1 add_ring.1
  54.2 2.4 %collective-permute-start.23 = (bf16[128,1024]{1,0:T(8,128)(2,1)S(1)}, bf16[128,1024]{1,0:T(8,128)(2,1)S(1)}, u32[]{:S(2)}, u32[]{:S(2)}) collective-permute-start(bf16[128,1024]{1,0:T(8,128)(2,1)S(1)} %get-tuple-element.167.refs_0_), channel_id=1, source_target_pairs={{0,32},{2,6},{4,36},{6,2},{8,40},{10,14},{12,44},{14,10},{32,0},{3... | collective-permute-start | bytes 786440 | tf_op jit(solution)/shard_map/ppermute | solution.py:57
  56.7 3.1 %attention_far_keys0.1 = (f32[2,128,512]{2,1,0:T(8,128)S(1)}, f32[2,1024,128]{2,1,0:T(8,128)S(1)}, f32[8,128]{1,0:T(8,128)S(1)}) custom-call(bf16[2,1152,128]{2,1,0:T(8,128)(2,1)S(1)} %get-tuple-element.151.refs_0_, bf16[2,1024,128]{2,1,0:T(8,128)(2,1)S(1)} %collective-permute-done.21.refs_1_, ...), custom_call_target="tpu_custom_call", output_to_operand_aliasing={{0}: (2, {}), {1}: (3, {})} | custom-call | flops 671088640 | bytes 4259840 | tf_op jit(solution)/shard_map/attention_far_keys0/pallas_call | solution.py:95
  59.8 0.9 collective-permute-done.23.refs_1_
  60.7 2.7 %collective-permute-start.24 = (bf16[128,1024]{1,0:T(8,128)(2,1)S(1)}, bf16[128,1024]{1,0:T(8,128)(2,1)S(1)}, u32[]{:S(2)}, u32[]{:S(2)}) collective-permute-start(bf16[128,1024]{1,0:T(8,128)(2,1)S(1)} %get-tuple-element.172.refs_0_), channel_id=1, source_target_pairs={{0,96},{2,14},{4,100},{6,10},{8,104},{10,6},{12,108},{14,2},{32,64... | collective-permute-start | bytes 786440 | tf_op jit(solution)/shard_map/ppermute | solution.py:57
  63.4 3.2 %attention_far_keys1.1 = (f32[2,128,512]{2,1,0:T(8,128)S(1)}, bf16[2,1024,128]{2,1,0:T(8,128)(2,1)S(1)}, f32[8,128]{1,0:T(8,128)S(1)}) custom-call(bf16[2,1152,128]{2,1,0:T(8,128)(2,1)S(1)} %get-tuple-element.151.refs_0_, bf16[2,1024,128]{2,1,0:T(8,128)(2,1)S(1)} %collective-permute-done.21.refs_1_, ...), custom_call_target="tpu_custom_call", output_to_operand_aliasing={{0}: (2, {})} | custom-call | flops 671088640 | bytes 3735552 | tf_op jit(solution)/shard_map/attention_far_keys1/pallas_call | solution.py:95
  66.7 3.1 %attention_far_queries0.1 = (f32[2,128,512]{2,1,0:T(8,128)S(1)}, f32[2,1024,128]{2,1,0:T(8,128)S(1)}, f32[8,128]{1,0:T(8,128)S(1)}) custom-call(bf16[2,1152,128]{2,1,0:T(8,128)(2,1)S(1)} %collective-permute-done.20.refs_0_, bf16[2,1024,128]{2,1,0:T(8,128)(2,1)S(1)} %get-tuple-element.152.refs_1_, ...), custom_call_target="tpu_custom_call", output_to_operand_aliasing={{0}: (2, {}), {1}: (3, {})} | custom-call | flops 671088640 | bytes 4259840 | tf_op jit(solution)/shard_map/attention_far_queries0/pallas_call | solution.py:95
  69.9 1.2 %collective-permute-start.25 = (bf16[128,1024]{1,0:T(8,128)(2,1)S(1)}, bf16[128,1024]{1,0:T(8,128)(2,1)S(1)}, u32[]{:S(2)}, u32[]{:S(2)}) collective-permute-start(bf16[128,1024]{1,0:T(8,128)(2,1)S(1)} %get-tuple-element.180.refs_0_), channel_id=1, source_target_pairs={{0,16},{16,0},{1,17},{17,1},{2,18},{18,2},{3,19},{19,3},{4,20},{20... | collective-permute-start | bytes 786440 | tf_op jit(solution)/shard_map/ppermute | solution.py:34
  71.1 3.4 %attention_far_queries1.1 = (bf16[2,512,128]{2,1,0:T(8,128)(2,1)S(1)}, f32[2,1024,128]{2,1,0:T(8,128)S(1)}, f32[8,128]{1,0:T(8,128)S(1)}) custom-call(bf16[2,1152,128]{2,1,0:T(8,128)(2,1)S(1)} %collective-permute-done.20.refs_0_, bf16[2,1024,128]{2,1,0:T(8,128)(2,1)S(1)} %get-tuple-element.152.refs_1_, f32[2,128,512]{2,1,0:T(8,128)S(1)} %get-tuple-element.181.refs_2_, ...), custom_call_target="tpu_custom_call" | custom-call | flops 671088640 | bytes 3997696 | tf_op jit(solution)/shard_map/attention_far_queries1/pallas_call | solution.py:95
  74.5 0.1 collective-permute-start.30
  74.6 1.9 %collective-permute-done.25.refs_1_ = bf16[128,1024]{1,0:T(8,128)(2,1)S(1)} collective-permute-done((bf16[128,1024]{1,0:T(8,128)(2,1)S(1)}, bf16[128,1024]{1,0:T(8,128)(2,1)S(1)}, u32[]{:S(2)}, u32[]{:S(2)}) %collective-permute-start.25) | collective-permute-done | bytes 262176 | tf_op jit(solution)/shard_map/ppermute | solution.py:34
  76.6 0.8 collective-permute-start.32
  77.4 2.4 %collective-permute-start.28 = (bf16[128,1024]{1,0:T(8,128)(2,1)S(1)}, bf16[128,1024]{1,0:T(8,128)(2,1)S(1)}, u32[]{:S(2)}, u32[]{:S(2)}) collective-permute-start(bf16[128,1024]{1,0:T(8,128)(2,1)S(1)} %get-tuple-element.185.refs_0_), channel_id=1, source_target_pairs={{0,12},{2,98},{4,0},{6,102},{8,4},{10,106},{12,8},{14,110},{32,44}... | collective-permute-start | bytes 786440 | tf_op jit(solution)/shard_map/ppermute | solution.py:57
  79.8 0.6 collective-permute-start.26
  80.4 0.2 turn.1
  80.6 2.2 %collective-permute-start.31 = (bf16[512,128]{1,0:T(8,128)(2,1)S(1)}, bf16[512,128]{1,0:T(8,128)(2,1)S(1)}, u32[]{:S(2)}, u32[]{:S(2)}) collective-permute-start(bf16[512,128]{1,0:T(8,128)(2,1)S(1)} %get-tuple-element.194), channel_id=1, source_target_pairs={{0,32},{2,98},{32,0},{34,66},{64,96},{66,34},{96,64},{98,2},{1,33}... | collective-permute-start | bytes 393224 | tf_op jit(solution)/shard_map/ppermute | solution.py:44
  82.8 7.9 %collective-permute-done.31.refs_2_ = bf16[512,128]{1,0:T(8,128)(2,1)S(1)} collective-permute-done((bf16[512,128]{1,0:T(8,128)(2,1)S(1)}, bf16[512,128]{1,0:T(8,128)(2,1)S(1)}, u32[]{:S(2)}, u32[]{:S(2)}) %collective-permute-start.31) | collective-permute-done | bytes 131104 | tf_op jit(solution)/shard_map/ppermute | solution.py:44
  90.8 0.1 back.1
  90.9 0.7 collective-permute-start.33
  91.5 0.9 collective-permute-done.33.refs_1_
  92.5 0.1 gather.1
  92.6 0.4 collective-permute-start.36
  93.1 1.5 %collective-permute-start.35 = (bf16[768,128]{1,0:T(8,128)(2,1)S(1)}, bf16[768,128]{1,0:T(8,128)(2,1)S(1)}, u32[]{:S(2)}, u32[]{:S(2)}) collective-permute-start(bf16[768,128]{1,0:T(8,128)(2,1)S(1)} %get-tuple-element.205), channel_id=1, source_target_pairs={{0,16},{16,0},{1,17},{17,1},{2,18},{18,2},{3,19},{19,3},{4,20},{20... | collective-permute-start | bytes 589832 | tf_op jit(solution)/shard_map/ppermute | solution.py:34
  94.6 0.6 collective-permute-start.22
  95.2 1.0 collective-permute-done.22.refs_1_
  96.2 0.7 add_shares.1
  96.9 2.3 %final.1 = (f32[512,1024]{1,0:T(8,128)}, f32[512,1024]{1,0:T(8,128)}, f32[8,128]{1,0:T(8,128)S(1)}) custom-call(bf16[512,1024]{1,0:T(8,128)(2,1)S(1)} %get-tuple-element.206.refs_0_, bf16[512,1024]{1,0:T(8,128)(2,1)S(1)} %collective-permute-done.36.refs_1_, f32[8,128]{1,0:T(8,128)S(1)} %get-tuple-element.207.refs_2_), custom_call_target="tpu_custom_call" | custom-call | bytes 6291456 | tf_op jit(solution)/shard_map/final/pallas_call | solution.py:95
  99.2 0.3 collective-permute-done.35.refs_2_
  99.4 0.8 place.1
  (48 shorter events, 0.9 us)
Async XLA Ops:
  0.6 7.1 %collective-permute-start.2 = (bf16[128,512]{1,0:T(8,128)(2,1)}, bf16[128,512]{1,0:T(8,128)(2,1)S(1)}, u32[]{:S(2)}, u32[]{:S(2)}) collective-permute-start(bf16[128,512]{1,0:T(8,128)(2,1)} %refs_0_.3), channel_id=1, source_target_pairs={{0,2},{2,0},{1,3},{3,1},{4,6},{6,4},{5,7},{7,5},{8,10},{10,8},{9,1... | collective-permute-start | bytes 393224 | tf_op jit(solution)/shard_map/ppermute | solution.py:34
  2.1 13.7 %collective-permute-start = (bf16[128,512]{1,0:T(8,128)(2,1)}, bf16[128,512]{1,0:T(8,128)(2,1)S(1)}, u32[]{:S(2)}, u32[]{:S(2)}) collective-permute-start(bf16[128,512]{1,0:T(8,128)(2,1)} %refs_2_.1), channel_id=1, source_target_pairs={{0,1},{1,0},{2,3},{3,2},{4,5},{5,4},{6,7},{7,6},{8,9},{9,8},{10,11... | collective-permute-start | bytes 393224 | tf_op jit(solution)/shard_map/ppermute | solution.py:34
  7.2 1.3 %collective-permute-start.1 = (bf16[256,128]{1,0:T(8,128)(2,1)S(1)}, bf16[256,128]{1,0:T(8,128)(2,1)S(1)}, u32[]{:S(2)}, u32[]{:S(2)}) collective-permute-start(bf16[256,128]{1,0:T(8,128)(2,1)S(1)} %get-tuple-element.120), channel_id=1, source_target_pairs={{0,2},{2,0},{1,3},{3,1},{4,6},{6,4},{5,7},{7,5},{8,10},{10,8},{9,1... | collective-permute-start | bytes 196616 | tf_op jit(solution)/shard_map/ppermute | solution.py:34
  8.6 12.6 %collective-permute-start.10 = (bf16[512,128]{1,0:T(8,128)(2,1)S(1)}, bf16[512,128]{1,0:T(8,128)(2,1)S(1)}, u32[]{:S(2)}, u32[]{:S(2)}) collective-permute-start(bf16[512,128]{1,0:T(8,128)(2,1)S(1)} %get-tuple-element.136), channel_id=1, source_target_pairs={{0,16},{16,0},{1,17},{17,1},{2,18},{18,2},{3,19},{19,3},{4,20},{20... | collective-permute-start | bytes 393224 | tf_op jit(solution)/shard_map/ppermute | solution.py:34
  9.1 12.2 %collective-permute-start.3 = (bf16[256,512]{1,0:T(8,128)(2,1)S(1)}, bf16[256,512]{1,0:T(8,128)(2,1)S(1)}, u32[]{:S(2)}, u32[]{:S(2)}) collective-permute-start(bf16[256,512]{1,0:T(8,128)(2,1)S(1)} %get-tuple-element.127), channel_id=1, source_target_pairs={{0,4},{2,126},{4,8},{6,2},{8,12},{10,6},{12,16},{14,10},{16,20},{1... | collective-permute-start | bytes 786440 | tf_op jit(solution)/shard_map/ppermute | solution.py:516
  15.8 2.1 %copy-start.1 = (bf16[128,512]{1,0:T(8,128)(2,1)S(1)}, bf16[128,512]{1,0:T(8,128)(2,1)}, u32[]{:S(2)}) copy-start(bf16[128,512]{1,0:T(8,128)(2,1)} %refs_0_.3) | copy-start | bytes 393220
  16.5 1.3 %collective-permute-start.7 = (bf16[288,128]{1,0:T(8,128)(2,1)S(1)}, bf16[288,128]{1,0:T(8,128)(2,1)S(1)}, u32[]{:S(2)}, u32[]{:S(2)}) collective-permute-start(bf16[288,128]{1,0:T(8,128)(2,1)S(1)} %get-tuple-element.131), channel_id=1, source_target_pairs={{0,2},{2,0},{1,3},{3,1},{4,6},{6,4},{5,7},{7,5},{8,10},{10,8},{9,1... | collective-permute-start | bytes 221192 | tf_op jit(solution)/shard_map/ppermute | solution.py:34
  16.5 2.1 %collective-permute-start.9 = (bf16[256,128]{1,0:T(8,128)(2,1)S(1)}, bf16[256,128]{1,0:T(8,128)(2,1)S(1)}, u32[]{:S(2)}, u32[]{:S(2)}) collective-permute-start(bf16[256,128]{1,0:T(8,128)(2,1)S(1)} %get-tuple-element.135), channel_id=1, source_target_pairs={{0,2},{2,0},{1,3},{3,1},{4,6},{6,4},{5,7},{7,5},{8,10},{10,8},{9,1... | collective-permute-start | bytes 196616 | tf_op jit(solution)/shard_map/ppermute | solution.py:34
  17.8 6.8 %collective-permute-start.8 = (bf16[576,128]{1,0:T(8,128)(2,1)S(1)}, bf16[576,128]{1,0:T(8,128)(2,1)S(1)}, u32[]{:S(2)}, u32[]{:S(2)}) collective-permute-start(bf16[576,128]{1,0:T(8,128)(2,1)S(1)} %get-tuple-element.133), channel_id=1, source_target_pairs={{0,16},{16,0},{1,17},{17,1},{2,18},{18,2},{3,19},{19,3},{4,20},{20... | collective-permute-start | bytes 442376 | tf_op jit(solution)/shard_map/ppermute | solution.py:34
  17.9 6.8 %collective-permute-start.5 = (bf16[128,512]{1,0:T(8,128)(2,1)S(1)}, bf16[128,512]{1,0:T(8,128)(2,1)S(1)}, u32[]{:S(2)}, u32[]{:S(2)}) collective-permute-start(bf16[128,512]{1,0:T(8,128)(2,1)S(1)} %copy-done.1), channel_id=1, source_target_pairs={{0,122},{2,8},{4,126},{6,12},{8,2},{10,16},{12,6},{14,20},{16,10},... | collective-permute-start | bytes 393224 | tf_op jit(solution)/shard_map/ppermute | solution.py:496
  18.7 3.4 %collective-permute-start.6 = (bf16[288,128]{1,0:T(8,128)(2,1)S(1)}, bf16[288,128]{1,0:T(8,128)(2,1)S(1)}, u32[]{:S(2)}, u32[]{:S(2)}) collective-permute-start(bf16[288,128]{1,0:T(8,128)(2,1)S(1)} %get-tuple-element.129), channel_id=1, source_target_pairs={{0,2},{2,0},{1,3},{3,1},{4,6},{6,4},{5,7},{7,5},{8,10},{10,8},{9,1... | collective-permute-start | bytes 221192 | tf_op jit(solution)/shard_map/ppermute | solution.py:34
  21.2 8.2 %collective-permute-start.13 = (bf16[1024,128]{1,0:T(8,128)(2,1)S(1)}, bf16[1024,128]{1,0:T(8,128)(2,1)S(1)}, u32[]{:S(2)}, u32[]{:S(2)}) collective-permute-start(bf16[1024,128]{1,0:T(8,128)(2,1)S(1)} %get-tuple-element.143.refs_0_), channel_id=1, source_target_pairs={{0,4},{2,14},{4,0},{6,10},{8,12},{10,6},{12,8},{14,2},{1,5},{3,15}... | collective-permute-start | bytes 786440 | tf_op jit(solution)/shard_map/ppermute | solution.py:44
  21.3 3.4 %collective-permute-start.4 = (bf16[256,512]{1,0:T(8,128)(2,1)S(1)}, bf16[256,512]{1,0:T(8,128)(2,1)S(1)}, u32[]{:S(2)}, u32[]{:S(2)}) collective-permute-start(bf16[256,512]{1,0:T(8,128)(2,1)S(1)} %collective-permute-done.3.refs_7_), channel_id=1, source_target_pairs={{0,2},{2,0},{1,3},{3,1},{4,6},{6,4},{5,7},{7,5},{8,10},{10,8},{9,1... | collective-permute-start | bytes 786440 | tf_op jit(solution)/shard_map/ppermute | solution.py:34
  24.6 0.7 copy-start
  24.6 6.9 %collective-permute-start.12 = (bf16[1152,128]{1,0:T(8,128)(2,1)S(1)}, bf16[1152,128]{1,0:T(8,128)(2,1)S(1)}, u32[]{:S(2)}, u32[]{:S(2)}) collective-permute-start(bf16[1152,128]{1,0:T(8,128)(2,1)S(1)} %get-tuple-element.142.refs_0_), channel_id=1, source_target_pairs={{0,32},{2,98},{32,0},{34,66},{64,96},{66,34},{96,64},{98,2},{1,33}... | collective-permute-start | bytes 884744 | tf_op jit(solution)/shard_map/ppermute | solution.py:44
  28.2 3.5 %collective-permute-start.11 = (bf16[512,1024]{1,0:T(8,128)(2,1)S(1)}, bf16[512,1024]{1,0:T(8,128)(2,1)S(1)}, u32[]{:S(2)}, u32[]{:S(2)}) collective-permute-start(bf16[512,1024]{1,0:T(8,128)(2,1)S(1)} %get-tuple-element.141), channel_id=1, source_target_pairs={{0,2},{2,0},{1,3},{3,1},{4,6},{6,4},{5,7},{7,5},{8,10},{10,8},{9,1... | collective-permute-start | bytes 3145736 | tf_op jit(solution)/shard_map/ppermute | solution.py:34
  29.4 16.7 %collective-permute-start.21 = (bf16[2,1024,128]{2,1,0:T(8,128)(2,1)S(1)}, bf16[2,1024,128]{2,1,0:T(8,128)(2,1)S(1)}, u32[]{:S(2)}, u32[]{:S(2)}) collective-permute-start(bf16[2,1024,128]{2,1,0:T(8,128)(2,1)S(1)} %get-tuple-element.152.refs_1_), channel_id=1, source_target_pairs={{0,12},{2,6},{4,8},{6,2},{8,4},{10,14},{12,0},{14,10},{1,13},{3,7}... | collective-permute-start | bytes 1572872 | tf_op jit(solution)/shard_map/ppermute | solution.py:44
  31.5 15.8 %collective-permute-start.20 = (bf16[2,1152,128]{2,1,0:T(8,128)(2,1)S(1)}, bf16[2,1152,128]{2,1,0:T(8,128)(2,1)S(1)}, u32[]{:S(2)}, u32[]{:S(2)}) collective-permute-start(bf16[2,1152,128]{2,1,0:T(8,128)(2,1)S(1)} %get-tuple-element.151.refs_0_), channel_id=1, source_target_pairs={{0,96},{2,34},{32,64},{34,2},{64,32},{66,98},{96,0},{98,66},{1,97}... | collective-permute-start | bytes 1769480 | tf_op jit(solution)/shard_map/ppermute | solution.py:44
  34.8 9.7 %collective-permute-start.14 = (bf16[384,512]{1,0:T(8,128)(2,1)S(1)}, bf16[384,512]{1,0:T(8,128)(2,1)S(1)}, u32[]{:S(2)}, u32[]{:S(2)}) collective-permute-start(bf16[384,512]{1,0:T(8,128)(2,1)S(1)} %get-tuple-element.150), channel_id=1, source_target_pairs={{0,2},{2,0},{1,3},{3,1},{4,6},{6,4},{5,7},{7,5},{8,10},{10,8},{9,1... | collective-permute-start | bytes 1179656 | tf_op jit(solution)/shard_map/ppermute | solution.py:34
  35.6 18.5 %collective-permute-start.17 = (bf16[128,1024]{1,0:T(8,128)(2,1)S(1)}, bf16[128,1024]{1,0:T(8,128)(2,1)S(1)}, u32[]{:S(2)}, u32[]{:S(2)}) collective-permute-start(bf16[128,1024]{1,0:T(8,128)(2,1)S(1)} %get-tuple-element.159), channel_id=1, source_target_pairs={{0,4},{2,34},{4,8},{6,38},{8,12},{10,42},{12,0},{14,46},{32,36},{3... | collective-permute-start | bytes 786440 | tf_op jit(solution)/shard_map/ppermute | solution.py:57
  37.5 16.6 %collective-permute-start.18 = (bf16[128,1024]{1,0:T(8,128)(2,1)S(1)}, bf16[128,1024]{1,0:T(8,128)(2,1)S(1)}, u32[]{:S(2)}, u32[]{:S(2)}) collective-permute-start(bf16[128,1024]{1,0:T(8,128)(2,1)S(1)} %get-tuple-element.160), channel_id=1, source_target_pairs={{0,8},{2,66},{4,12},{6,70},{8,0},{10,74},{12,4},{14,78},{32,40},{3... | collective-permute-start | bytes 786440 | tf_op jit(solution)/shard_map/ppermute | solution.py:57
  44.5 9.6 %collective-permute-start.19 = (bf16[128,1024]{1,0:T(8,128)(2,1)S(1)}, bf16[128,1024]{1,0:T(8,128)(2,1)S(1)}, u32[]{:S(2)}, u32[]{:S(2)}) collective-permute-start(bf16[128,1024]{1,0:T(8,128)(2,1)S(1)} %get-tuple-element.161), channel_id=1, source_target_pairs={{0,12},{2,98},{4,0},{6,102},{8,4},{10,106},{12,8},{14,110},{32,44}... | collective-permute-start | bytes 786440 | tf_op jit(solution)/shard_map/ppermute | solution.py:57
  46.1 10.5 %collective-permute-start.15 = (bf16[256,512]{1,0:T(8,128)(2,1)S(1)}, bf16[256,512]{1,0:T(8,128)(2,1)S(1)}, u32[]{:S(2)}, u32[]{:S(2)}) collective-permute-start(bf16[256,512]{1,0:T(8,128)(2,1)S(1)} %get-tuple-element.156), channel_id=1, source_target_pairs={{0,4},{2,126},{4,8},{6,2},{8,12},{10,6},{12,16},{14,10},{16,20},{1... | collective-permute-start | bytes 786440 | tf_op jit(solution)/shard_map/ppermute | solution.py:621
  47.3 9.3 %collective-permute-start.16 = (bf16[128,512]{1,0:T(8,128)(2,1)S(1)}, bf16[128,512]{1,0:T(8,128)(2,1)S(1)}, u32[]{:S(2)}, u32[]{:S(2)}) collective-permute-start(bf16[128,512]{1,0:T(8,128)(2,1)S(1)} %get-tuple-element.157), channel_id=1, source_target_pairs={{0,122},{2,8},{4,126},{6,12},{8,2},{10,16},{12,6},{14,20},{16,10},... | collective-permute-start | bytes 393224 | tf_op jit(solution)/shard_map/ppermute | solution.py:621
  54.2 6.4 %collective-permute-start.23 = (bf16[128,1024]{1,0:T(8,128)(2,1)S(1)}, bf16[128,1024]{1,0:T(8,128)(2,1)S(1)}, u32[]{:S(2)}, u32[]{:S(2)}) collective-permute-start(bf16[128,1024]{1,0:T(8,128)(2,1)S(1)} %get-tuple-element.167.refs_0_), channel_id=1, source_target_pairs={{0,32},{2,6},{4,36},{6,2},{8,40},{10,14},{12,44},{14,10},{32,0},{3... | collective-permute-start | bytes 786440 | tf_op jit(solution)/shard_map/ppermute | solution.py:57
  60.7 9.1 %collective-permute-start.24 = (bf16[128,1024]{1,0:T(8,128)(2,1)S(1)}, bf16[128,1024]{1,0:T(8,128)(2,1)S(1)}, u32[]{:S(2)}, u32[]{:S(2)}) collective-permute-start(bf16[128,1024]{1,0:T(8,128)(2,1)S(1)} %get-tuple-element.172.refs_0_), channel_id=1, source_target_pairs={{0,96},{2,14},{4,100},{6,10},{8,104},{10,6},{12,108},{14,2},{32,64... | collective-permute-start | bytes 786440 | tf_op jit(solution)/shard_map/ppermute | solution.py:57
  66.6 10.0 %collective-permute-start.29 = (bf16[2,1024,128]{2,1,0:T(8,128)(2,1)S(1)}, bf16[2,1024,128]{2,1,0:T(8,128)(2,1)S(1)}, u32[]{:S(2)}, u32[]{:S(2)}) collective-permute-start(bf16[2,1024,128]{2,1,0:T(8,128)(2,1)S(1)} %get-tuple-element.188), channel_id=1, source_target_pairs={{0,12},{2,6},{4,8},{6,2},{8,4},{10,14},{12,0},{14,10},{1,13},{3,7}... | collective-permute-start | bytes 1572872 | tf_op jit(solution)/shard_map/ppermute | solution.py:44
  69.9 6.6 %collective-permute-start.25 = (bf16[128,1024]{1,0:T(8,128)(2,1)S(1)}, bf16[128,1024]{1,0:T(8,128)(2,1)S(1)}, u32[]{:S(2)}, u32[]{:S(2)}) collective-permute-start(bf16[128,1024]{1,0:T(8,128)(2,1)S(1)} %get-tuple-element.180.refs_0_), channel_id=1, source_target_pairs={{0,16},{16,0},{1,17},{17,1},{2,18},{18,2},{3,19},{19,3},{4,20},{20... | collective-permute-start | bytes 786440 | tf_op jit(solution)/shard_map/ppermute | solution.py:34
  74.5 6.1 %collective-permute-start.30 = (bf16[2,512,128]{2,1,0:T(8,128)(2,1)S(1)}, bf16[2,512,128]{2,1,0:T(8,128)(2,1)S(1)}, u32[]{:S(2)}, u32[]{:S(2)}) collective-permute-start(bf16[2,512,128]{2,1,0:T(8,128)(2,1)S(1)} %get-tuple-element.192), channel_id=1, source_target_pairs={{0,96},{2,34},{32,64},{34,2},{64,32},{66,98},{96,0},{98,66},{1,97}... | collective-permute-start | bytes 786440 | tf_op jit(solution)/shard_map/ppermute | solution.py:44
  76.6 14.1 %collective-permute-start.32 = (bf16[1024,128]{1,0:T(8,128)(2,1)S(1)}, bf16[1024,128]{1,0:T(8,128)(2,1)S(1)}, u32[]{:S(2)}, u32[]{:S(2)}) collective-permute-start(bf16[1024,128]{1,0:T(8,128)(2,1)S(1)} %get-tuple-element.195), channel_id=1, source_target_pairs={{0,4},{2,14},{4,0},{6,10},{8,12},{10,6},{12,8},{14,2},{1,5},{3,15}... | collective-permute-start | bytes 786440 | tf_op jit(solution)/shard_map/ppermute | solution.py:44
  77.4 15.1 %collective-permute-start.28 = (bf16[128,1024]{1,0:T(8,128)(2,1)S(1)}, bf16[128,1024]{1,0:T(8,128)(2,1)S(1)}, u32[]{:S(2)}, u32[]{:S(2)}) collective-permute-start(bf16[128,1024]{1,0:T(8,128)(2,1)S(1)} %get-tuple-element.185.refs_0_), channel_id=1, source_target_pairs={{0,12},{2,98},{4,0},{6,102},{8,4},{10,106},{12,8},{14,110},{32,44}... | collective-permute-start | bytes 786440 | tf_op jit(solution)/shard_map/ppermute | solution.py:57
  79.8 12.7 %collective-permute-start.27 = (bf16[128,1024]{1,0:T(8,128)(2,1)S(1)}, bf16[128,1024]{1,0:T(8,128)(2,1)S(1)}, u32[]{:S(2)}, u32[]{:S(2)}) collective-permute-start(bf16[128,1024]{1,0:T(8,128)(2,1)S(1)} %get-tuple-element.185.refs_0_), channel_id=1, source_target_pairs={{0,8},{2,66},{4,12},{6,70},{8,0},{10,74},{12,4},{14,78},{32,40},{3... | collective-permute-start | bytes 786440 | tf_op jit(solution)/shard_map/ppermute | solution.py:57
  79.8 12.7 %collective-permute-start.26 = (bf16[128,1024]{1,0:T(8,128)(2,1)S(1)}, bf16[128,1024]{1,0:T(8,128)(2,1)S(1)}, u32[]{:S(2)}, u32[]{:S(2)}) collective-permute-start(bf16[128,1024]{1,0:T(8,128)(2,1)S(1)} %get-tuple-element.185.refs_0_), channel_id=1, source_target_pairs={{0,4},{2,34},{4,8},{6,38},{8,12},{10,42},{12,0},{14,46},{32,36},{3... | collective-permute-start | bytes 786440 | tf_op jit(solution)/shard_map/ppermute | solution.py:57
  80.6 10.1 %collective-permute-start.31 = (bf16[512,128]{1,0:T(8,128)(2,1)S(1)}, bf16[512,128]{1,0:T(8,128)(2,1)S(1)}, u32[]{:S(2)}, u32[]{:S(2)}) collective-permute-start(bf16[512,128]{1,0:T(8,128)(2,1)S(1)} %get-tuple-element.194), channel_id=1, source_target_pairs={{0,32},{2,98},{32,0},{34,66},{64,96},{66,34},{96,64},{98,2},{1,33}... | collective-permute-start | bytes 393224 | tf_op jit(solution)/shard_map/ppermute | solution.py:44
  90.9 1.6 %collective-permute-start.33 = (bf16[384,128]{1,0:T(8,128)(2,1)S(1)}, bf16[384,128]{1,0:T(8,128)(2,1)S(1)}, u32[]{:S(2)}, u32[]{:S(2)}) collective-permute-start(bf16[384,128]{1,0:T(8,128)(2,1)S(1)} %get-tuple-element.198), channel_id=1, source_target_pairs={{0,2},{2,0},{1,3},{3,1},{4,6},{6,4},{5,7},{7,5},{8,10},{10,8},{9,1... | collective-permute-start | bytes 294920 | tf_op jit(solution)/shard_map/ppermute | solution.py:34
  92.6 4.2 %collective-permute-start.36 = (bf16[512,1024]{1,0:T(8,128)(2,1)S(1)}, bf16[512,1024]{1,0:T(8,128)(2,1)S(1)}, u32[]{:S(2)}, u32[]{:S(2)}) collective-permute-start(bf16[512,1024]{1,0:T(8,128)(2,1)S(1)} %get-tuple-element.206.refs_0_), channel_id=1, source_target_pairs={{0,2},{2,0},{1,3},{3,1},{4,6},{6,4},{5,7},{7,5},{8,10},{10,8},{9,1... | collective-permute-start | bytes 3145736 | tf_op jit(solution)/shard_map/ppermute | solution.py:34
  93.1 6.4 %collective-permute-start.35 = (bf16[768,128]{1,0:T(8,128)(2,1)S(1)}, bf16[768,128]{1,0:T(8,128)(2,1)S(1)}, u32[]{:S(2)}, u32[]{:S(2)}) collective-permute-start(bf16[768,128]{1,0:T(8,128)(2,1)S(1)} %get-tuple-element.205), channel_id=1, source_target_pairs={{0,16},{16,0},{1,17},{17,1},{2,18},{18,2},{3,19},{19,3},{4,20},{20... | collective-permute-start | bytes 589832 | tf_op jit(solution)/shard_map/ppermute | solution.py:34
  94.6 1.6 %collective-permute-start.22 = (bf16[128,512]{1,0:T(8,128)(2,1)S(1)}, bf16[128,512]{1,0:T(8,128)(2,1)S(1)}, u32[]{:S(2)}, u32[]{:S(2)}) collective-permute-start(bf16[128,512]{1,0:T(8,128)(2,1)S(1)} %get-tuple-element.166), channel_id=1, source_target_pairs={{0,2},{2,0},{1,3},{3,1},{4,6},{6,4},{5,7},{7,5},{8,10},{10,8},{9,1... | collective-permute-start | bytes 393224 | tf_op jit(solution)/shard_map/ppermute | solution.py:34
  95.2 4.0 %collective-permute-start.34 = (bf16[384,128]{1,0:T(8,128)(2,1)S(1)}, bf16[384,128]{1,0:T(8,128)(2,1)S(1)}, u32[]{:S(2)}, u32[]{:S(2)}) collective-permute-start(bf16[384,128]{1,0:T(8,128)(2,1)S(1)} %get-tuple-element.204), channel_id=1, source_target_pairs={{0,2},{2,0},{1,3},{3,1},{4,6},{6,4},{5,7},{7,5},{8,10},{10,8},{9,1... | collective-permute-start | bytes 294920 | tf_op jit(solution)/shard_map/ppermute | solution.py:34
